TPU v7x, 32 devices: a whole 2x2x4 slice. The times are simulated.
32 devices in a mesh: hyp: 2 (over y), row: 4 (over z), col: 4 (over x, core).
Axes of the slice: x: 2, y: 2, z: 4, core: 2. Of those that a mesh axis runs over, the one named last changes fastest.
Arguments:
- inverse_tile: float32 [16384, 8192], P(('hyp', 'row'), 'col'), parts along dimension 0, may hold values from -32768 to 262144, as said below
- panels: float32 [2, 2, 8192, 512], P('hyp', None, ('col', 'row')), parts along dimension 0, may hold values from -0.0007324219 to 0.0007324219
- link_panel: float32 [2, 512, 512], P('hyp'), parts along dimension 0, may hold values from -0.09375 to 0.09375
- diag_inverse: float32 [2, 2, 512, 512], P('hyp', None, 'row', 'col'), parts along dimension 0, may hold values from -3 to 3
- ancestor_tiles: int32 [1, 2, 64], replicated, may hold values 0 or 1
Outputs:
- ancestor_block: float32 [2, 2, 8192, 512], P('hyp', None, ('row', 'col')), parts along dimension 0
- diag_block: float32 [2, 2, 512, 512], P('hyp', None, 'row', 'col'), parts along dimension 0
- cross_block: float32 [2, 512, 512], P('hyp', 'row', 'col'), parts along dimension 0
There are 2 independent parts, one for each index of `hyp`. A program takes and returns all parts, laid end to end along the dimension named above; an argument that names none is the same for every part. Nothing has to cross between parts.
Inputs may be any that keep to these rules, and one draw needn't show every extreme that they name: `inverse_tile`: symmetric.
All inputs are finite; a program needn't handle non-finite values.
Results may differ from a plain program's by a relative error of at most 0.000075.
Values sent between devices are 32-bit elements; how exact they have to be, the bound alone decides.
No kernel may reach another device: no remote copies, remote signals or barrier semaphores. Data moves between devices by JAX's collectives and lax.ppermute only.
A program may use at most 128 MiB of HBM per device.

v0:
```python
import jax
import jax.numpy as jnp
from jax import lax
from jax.experimental import pallas as pl
from jax.experimental.pallas import tpu as pltpu
from jax.sharding import PartitionSpec as P

TILE = 128

precise = lax.Precision.HIGHEST
three_pass = lax.Precision.HIGH


def swap(block, axis, bit):
    pairs = [(i, i ^ bit) for i in range(lax.axis_size(axis))]
    return lax.ppermute(block, axis, pairs)


def parts(values):
    high = values.astype(jnp.bfloat16)
    return high, (values - high.astype(jnp.float32)).astype(jnp.bfloat16)


def product_kernel(place, tile_ref, *refs):
    *block_refs, out_ref, high_ref, low_ref = refs
    height = block_refs[0].shape[0]

    @pl.when((pl.program_id(0) == 0) & (pl.program_id(1) == 0))
    def _():
        for j, block_ref in enumerate(block_refs):
            rows = pl.ds(pl.multiple_of((place[0] ^ j) * height, height), height)
            high_ref[rows], low_ref[rows] = parts(block_ref[...])

    high, low = parts(tile_ref[0])
    out_ref[0] = (jnp.dot(high, high_ref[...], preferred_element_type=jnp.float32)
                  + (jnp.dot(high, low_ref[...], preferred_element_type=jnp.float32)
                     + jnp.dot(low, high_ref[...], preferred_element_type=jnp.float32)))


def product(tile, blocks, parity):
    count, out_rows, width = tile.shape
    columns = blocks[0].shape[1]
    step = min(out_rows, 256)
    chunks = lax.axis_index("col") ^ (2 * jnp.arange(count // 2) + parity)
    place = jnp.concatenate([lax.axis_index("row")[None], chunks]).astype(jnp.int32)
    whole = pl.BlockSpec(blocks[0].shape, lambda i, t, place: (0, 0))
    return pl.pallas_call(
        product_kernel,
        grid_spec=pltpu.PrefetchScalarGridSpec(
            num_scalar_prefetch=1,
            grid=(count // 2, out_rows // step),
            in_specs=[pl.BlockSpec((1, step, width), lambda i, t, place: (place[1 + i], t, 0))]
            + [whole] * len(blocks),
            out_specs=pl.BlockSpec((1, step, columns), lambda i, t, place: (i, t, 0)),
            scratch_shapes=[pltpu.VMEM((width, columns), jnp.bfloat16)] * 2,
        ),
        out_shape=jax.ShapeDtypeStruct((count // 2, out_rows, columns), jnp.float32),
        compiler_params=pltpu.CompilerParams(vmem_limit_bytes=40 * 2**20),
    )(place, tile, *blocks)


def after(block, *others):
    return lax.optimization_barrier((block, *others))[0]


def dot(a, b, precision):
    return jnp.matmul(a, b, precision=precision)


def dot_tn(a, b, precision):
    return lax.dot_general(a, b, (((0,), (0,)), ((), ())), precision=precision)


def sum_scatter(blocks, axis, bit=1):
    while blocks.shape[0] > 1:
        pairs = blocks.reshape((blocks.shape[0] // 2, 2) + blocks.shape[1:])
        blocks = pairs[:, 0] + swap(pairs[:, 1], axis, bit)
        bit *= 2
    return blocks[0]


def by_xor(blocks, axis):
    index = lax.axis_index(axis)
    return jnp.stack([lax.dynamic_index_in_dim(blocks, index ^ j, 0, keepdims=False)
                      for j in range(blocks.shape[0])])


def gather_blocks(block, axis):
    blocks = {0: block}
    bit = lax.axis_size(axis) // 2
    while bit >= 1:
        blocks.update({j ^ bit: swap(held, axis, bit) for j, held in list(blocks.items())})
        bit //= 2
    return [blocks[j] for j in range(len(blocks))]


def placed(blocks, axis):
    index = lax.axis_index(axis)
    height = blocks[0].shape[0]
    whole = jnp.zeros((len(blocks) * height,) + blocks[0].shape[1:], blocks[0].dtype)
    for j, block in enumerate(blocks):
        whole = lax.dynamic_update_slice_in_dim(whole, block, (index ^ j) * height, 0)
    return whole


def all_sum(block, axis):
    bit = 1
    while bit < lax.axis_size(axis):
        block = block + swap(block, axis, bit)
        bit *= 2
    return block


def source_col(row):
    return row * lax.axis_size("col") // lax.axis_size("row")


def own_output_rows(blocks):
    rows, cols = lax.axis_size("row"), lax.axis_size("col")
    row_id, col_id = lax.axis_index("row"), lax.axis_index("col")
    offset = col_id ^ source_col(row_id)
    held = []
    for d in range(cols):
        wanted = [((r * cols + (source_col(r) ^ d)) % rows) ^ r for r in range(rows)]
        if len(set(wanted)) == 1:
            held.append(blocks[wanted[0]])
        else:
            held.append(lax.dynamic_index_in_dim(jnp.stack(blocks), jnp.array(wanted)[row_id], 0, keepdims=False))
    bit = cols // 2
    while bit >= 1:
        pairs = [(r * cols + c, r * cols + (c ^ bit)) for r in range(rows) for c in range(cols)
                 if (c ^ source_col(r)) % (2 * bit) == 0]
        moved = lax.ppermute(jnp.stack(held[bit:]), ("row", "col"), pairs)
        held = [jnp.where(offset & bit != 0, moved[j], held[j]) for j in range(bit)]
        bit //= 2
    return held[0]


def own_output_rows_direct(block):
    rows, cols = lax.axis_size("row"), lax.axis_size("col")
    pairs = [(r * cols + c, c * rows + r) for r in range(rows) for c in range(cols)]
    return lax.ppermute(block, ("row", "col"), pairs)


def local(inverse_tile, panels, link_panel, diag_inverse, ancestor_tiles):
    rows_axis, cols_axis = lax.axis_size("row"), lax.axis_size("col")
    row_id, col_id = lax.axis_index("row"), lax.axis_index("col")
    siblings, _, local_rows, width = panels.shape
    height, span = diag_inverse.shape[2:]
    row_start = (col_id * rows_axis + row_id) * local_rows
    tile_mask = jnp.repeat(ancestor_tiles, TILE, axis=2)
    kept_rows = lax.dynamic_slice_in_dim(tile_mask, row_start, local_rows, 2).astype(jnp.float32)
    masked = panels * kept_rows[..., None]

    tile = inverse_tile.reshape(cols_axis, inverse_tile.shape[0] // cols_axis, -1)

    def output_rows(blocks):
        sent = swap(product(tile, blocks, 1), "col", 1)
        return -sum_scatter(product(tile, blocks, 0) + sent, "col", 2)

    def by_cols(terms):
        return terms.reshape(width, cols_axis, -1).swapaxes(0, 1)

    def by_rows(terms):
        return terms.reshape(rows_axis, height, -1)

    def spread_sum(terms):
        terms = jnp.concatenate([by_cols(term) for term in terms], axis=2)
        terms = sum_scatter(by_xor(terms, "col"), "col")
        terms = sum_scatter(by_xor(by_rows(terms), "row"), "row")
        return [terms[:, start:start + span] for start in range(0, terms.shape[1], span)]

    late = 2 * span
    sent = []
    ancestor, diagonals, crosses = [], [], []
    for s in range(siblings):
        link = link_panel[s]
        first = masked[s, 0]
        second = masked[s, 1] - dot(first, link, precise)

        def gathered(panel, start, stop):
            piece = panel[:, start:stop]
            if len(sent) >= 2:
                piece = after(piece, sent[-2])
            blocks = gather_blocks(piece, "row")
            sent.append(blocks[rows_axis // 2])
            return blocks

        def joined(groups):
            return [jnp.concatenate(group, axis=1) for group in zip(*groups)]

        first_blocks = [gathered(first, i, i + late) for i in range(0, width, late)]
        second_blocks = [gathered(second, i, i + late) for i in range(0, width - late, late)]
        last_blocks = [gathered(second, i, i + span) for i in range(width - late, width, span)]
        own_last = own_output_rows_direct(after(second[:, width - late:], sent[1]))

        link_cols = lax.dynamic_slice_in_dim(link, col_id * span, span, 1)
        link_rows = lax.dynamic_slice_in_dim(link, row_id * height, height, 0)
        given = placed([block.T for block in gather_blocks(diag_inverse[s, 0], "col")], "col")
        given_link = dot_tn(given, link_cols, precise)

        out_first = jnp.concatenate([output_rows(blocks) for blocks in first_blocks], axis=1)
        own_first = own_output_rows(joined(first_blocks))
        (first_sum,) = spread_sum([dot_tn(own_first, out_first, three_pass)])

        out_early = jnp.concatenate([output_rows(blocks) for blocks in second_blocks], axis=1)
        own_early = own_output_rows(joined(second_blocks))
        own_second = jnp.concatenate([own_early, own_last], axis=1)
        cross_terms = dot_tn(out_first, own_second, three_pass)
        early_terms = jnp.concatenate([
            dot_tn(own_second, out_early, three_pass),
            jnp.pad(dot_tn(out_early, own_last, three_pass), ((0, late), (0, 0)))], axis=1)
        cross_sum, early_sum = spread_sum([cross_terms, early_terms])

        link_terms = sum_scatter(by_xor(by_rows(dot_tn(link_rows, given_link, precise)), "row"), "row")

        out_a = output_rows(last_blocks[0])
        terms_a = all_sum(all_sum(dot_tn(own_last, out_a, three_pass), "col"), "row")
        out_b = output_rows(last_blocks[1])
        terms_b = all_sum(all_sum(dot_tn(own_last[:, span:], out_b, three_pass), "col"), "row")
        last_terms = jnp.concatenate([
            terms_a, jnp.concatenate([terms_a[span:].T, terms_b], axis=0)], axis=1)
        padded = jnp.pad(last_terms, ((height, 0), (span, 0)))
        corner = width - late
        last_sum = lax.dynamic_slice(
            padded,
            (jnp.maximum(row_id * height - corner + height, 0), jnp.maximum(col_id * span - corner + span, 0)),
            (height, span))

        ancestor.append(jnp.stack([out_first, jnp.concatenate([out_early, out_a, out_b], axis=1)]))
        diagonals.append(jnp.stack([
            diag_inverse[s, 0] - first_sum,
            diag_inverse[s, 1] - early_sum - last_sum + link_terms]))
        crosses.append(-(cross_sum + given_link))
    return jnp.stack(ancestor), jnp.stack(diagonals), jnp.stack(crosses)


def solution(mesh):
    in_specs = (
        P(("hyp", "row"), "col"),
        P("hyp", None, ("col", "row"), None),
        P("hyp", None, None),
        P("hyp", None, "row", "col"),
        P(),
    )
    out_specs = (
        P("hyp", None, ("row", "col"), None),
        P("hyp", None, "row", "col"),
        P("hyp", "row", "col"),
    )
    return jax.shard_map(local, mesh=mesh, in_specs=in_specs, out_specs=out_specs, check_vma=False)
```

profile of v0, /device:TPU:0, one launch (start us, length us, event | category | flops | bytes accessed | tf_op | source)
XLA Modules:
  0.0 360.4 jit_solution(2833872579827107251)
XLA Ops:
  4.7 4.0 %collective-permute-start.1 = (f32[512,256]{1,0:T(8,128)S(1)}, f32[512,256]{1,0:T(8,128)}, u32[]{:S(2)}, u32[]{:S(2)}) collective-permute-start(f32[512,256]{1,0:T(8,128)S(1)} %get-tuple-element.32.refs_0_), channel_id=1, source_target_pairs={{0,8},{4,12},{8,0},{12,4},{1,9},{5,13},{9,1},{13,5},{2,10},{6,14},... | collective-permute-start | bytes 1572872 | tf_op jit(solution)/shard_map/ppermute | solution.py:16
  26.4 28.1 %collective-permute-done.6.refs_2_ = f32[512,256]{1,0:T(8,128)} collective-permute-done((f32[512,256]{1,0:T(8,128)S(1)}, f32[512,256]{1,0:T(8,128)}, u32[]{:S(2)}, u32[]{:S(2)}) %collective-permute-start.6) | collective-permute-done | bytes 524320 | tf_op jit(solution)/shard_map/ppermute | solution.py:16
  60.1 21.7 %collective-permute-done.16.refs_2_ = f32[512,128]{1,0:T(8,128)S(1)} collective-permute-done((f32[512,128]{1,0:T(8,128)}, f32[512,128]{1,0:T(8,128)S(1)}, u32[]{:S(2)}, u32[]{:S(2)}) %collective-permute-start.16) | collective-permute-done | bytes 262176 | tf_op jit(solution)/shard_map/ppermute | solution.py:16
  88.9 8.1 %collective-permute-done.17.refs_3_ = f32[512,128]{1,0:T(8,128)} collective-permute-done((f32[512,128]{1,0:T(8,128)S(1)}, f32[512,128]{1,0:T(8,128)}, u32[]{:S(2)}, u32[]{:S(2)}) %collective-permute-start.17) | collective-permute-done | bytes 262176 | tf_op jit(solution)/shard_map/ppermute | solution.py:16
  98.9 7.1 %shard_map.86 = f32[2,512,128]{2,1,0:T(8,128)S(1)} custom-call(s32[3]{0:T(128)S(1)} %pad_add_fusion.1.place, f32[4,512,2048]{2,1,0:T(8,128)} %bitcast.281, f32[512,128]{1,0:T(8,128)} %get-tuple-element.8.refs_0_, f32[512,128]{1,0:T(8,128)S(1)} %copy-done.7, f32[512,128]{1,0:T(8,128)S(1)} %copy-done.5, f32[512,128]{1,0:T(8,128)} %collective-permute-done.17.refs_3_), custom_call_target="tpu_custom_call" | custom-call | tf_op jit(solution)/shard_map/pallas_call | solution.py:47
  113.0 7.5 %shard_map.80 = f32[2,512,256]{2,1,0:T(8,128)S(1)} custom-call(s32[3]{0:T(128)S(1)} %pad_add_fusion.1.place, f32[4,512,2048]{2,1,0:T(8,128)} %bitcast.282, f32[512,256]{1,0:T(8,128)S(1)} %get-tuple-element.32.refs_0_, f32[512,256]{1,0:T(8,128)S(1)} %collective-permute-done.refs_1_, f32[512,256]{1,0:T(8,128)} %collective-permute-done.1.refs_2_, ...), custom_call_target="tpu_custom_call" | custom-call | tf_op jit(solution)/shard_map/pallas_call | solution.py:47
  120.6 7.5 %shard_map.79 = f32[2,512,256]{2,1,0:T(8,128)S(1)} custom-call(s32[3]{0:T(128)S(1)} %pad_add_fusion.place, f32[4,512,2048]{2,1,0:T(8,128)} %bitcast.283, f32[512,256]{1,0:T(8,128)S(1)} %get-tuple-element.32.refs_0_, f32[512,256]{1,0:T(8,128)S(1)} %collective-permute-done.refs_1_, f32[512,256]{1,0:T(8,128)} %collective-permute-done.1.refs_2_, ...), custom_call_target="tpu_custom_call" | custom-call | tf_op jit(solution)/shard_map/pallas_call | solution.py:47
  129.0 12.8 %collective-permute-done.7.refs_3_ = f32[512,256]{1,0:T(8,128)S(1)} collective-permute-done((f32[512,256]{1,0:T(8,128)}, f32[512,256]{1,0:T(8,128)S(1)}, u32[]{:S(2)}, u32[]{:S(2)}) %collective-permute-start.7) | collective-permute-done | bytes 524320 | tf_op jit(solution)/shard_map/ppermute | solution.py:16
  141.8 7.4 %shard_map.82 = f32[2,512,256]{2,1,0:T(8,128)S(1)} custom-call(s32[3]{0:T(128)S(1)} %pad_add_fusion.1.place, f32[4,512,2048]{2,1,0:T(8,128)} %bitcast.284, f32[512,256]{1,0:T(8,128)S(1)} %get-tuple-element.31.refs_0_, f32[512,256]{1,0:T(8,128)S(1)} %collective-permute-done.5.refs_1_, f32[512,256]{1,0:T(8,128)} %collective-permute-done.6.refs_2_, ...), custom_call_target="tpu_custom_call" | custom-call | tf_op jit(solution)/shard_map/pallas_call | solution.py:47
  149.2 7.4 %shard_map.81 = f32[2,512,256]{2,1,0:T(8,128)S(1)} custom-call(s32[3]{0:T(128)S(1)} %pad_add_fusion.place, f32[4,512,2048]{2,1,0:T(8,128)} %bitcast.285, f32[512,256]{1,0:T(8,128)S(1)} %get-tuple-element.31.refs_0_, f32[512,256]{1,0:T(8,128)S(1)} %collective-permute-done.5.refs_1_, f32[512,256]{1,0:T(8,128)} %collective-permute-done.6.refs_2_, ...), custom_call_target="tpu_custom_call" | custom-call | tf_op jit(solution)/shard_map/pallas_call | solution.py:47
  156.6 7.1 %shard_map.85 = f32[2,512,128]{2,1,0:T(8,128)S(1)} custom-call(s32[3]{0:T(128)S(1)} %pad_add_fusion.place, f32[4,512,2048]{2,1,0:T(8,128)} %bitcast.286, f32[512,128]{1,0:T(8,128)} %get-tuple-element.8.refs_0_, f32[512,128]{1,0:T(8,128)S(1)} %copy-done.7, f32[512,128]{1,0:T(8,128)S(1)} %copy-done.5, f32[512,128]{1,0:T(8,128)} %collective-permute-done.17.refs_3_), custom_call_target="tpu_custom_call" | custom-call | tf_op jit(solution)/shard_map/pallas_call | solution.py:47
  168.8 17.9 %collective-permute-done.12.refs_3_ = f32[512,256]{1,0:T(8,128)S(1)} collective-permute-done((f32[512,256]{1,0:T(8,128)S(1)}, f32[512,256]{1,0:T(8,128)S(1)}, u32[]{:S(2)}, u32[]{:S(2)}) %collective-permute-start.12) | collective-permute-done | bytes 524320 | tf_op jit(solution)/shard_map/ppermute | solution.py:16
  186.7 8.1 %shard_map.84 = f32[2,512,256]{2,1,0:T(8,128)} custom-call(s32[3]{0:T(128)S(1)} %pad_add_fusion.1.place, f32[4,512,2048]{2,1,0:T(8,128)} %bitcast.287, f32[512,256]{1,0:T(8,128)S(1)} %get-tuple-element.7.refs_0_, f32[512,256]{1,0:T(8,128)S(1)} %collective-permute-done.10.refs_1_, f32[512,256]{1,0:T(8,128)S(1)} %copy-done.3, ...), custom_call_target="tpu_custom_call" | custom-call | tf_op jit(solution)/shard_map/pallas_call | solution.py:47
  194.8 7.3 %shard_map.83 = f32[2,512,256]{2,1,0:T(8,128)S(1)} custom-call(s32[3]{0:T(128)S(1)} %pad_add_fusion.place, f32[4,512,2048]{2,1,0:T(8,128)} %bitcast.288, f32[512,256]{1,0:T(8,128)S(1)} %get-tuple-element.7.refs_0_, f32[512,256]{1,0:T(8,128)S(1)} %collective-permute-done.10.refs_1_, f32[512,256]{1,0:T(8,128)S(1)} %copy-done.3, ...), custom_call_target="tpu_custom_call" | custom-call | tf_op jit(solution)/shard_map/pallas_call | solution.py:47
  205.2 7.0 %shard_map.88 = f32[2,512,128]{2,1,0:T(8,128)S(1)} custom-call(s32[3]{0:T(128)S(1)} %pad_add_fusion.1.place, f32[4,512,2048]{2,1,0:T(8,128)} %bitcast.289, f32[512,128]{1,0:T(8,128)S(1)} %get-tuple-element.9.refs_0_, f32[512,128]{1,0:T(8,128)S(1)} %collective-permute-done.20.refs_1_, f32[512,128]{1,0:T(8,128)S(1)} %collective-permute-done.21.refs_2_, ...), custom_call_target="tpu_custom_call" | custom-call | tf_op jit(solution)/shard_map/pallas_call | solution.py:47
  214.5 7.0 %shard_map.87 = f32[2,512,128]{2,1,0:T(8,128)S(1)} custom-call(s32[3]{0:T(128)S(1)} %pad_add_fusion.place, f32[4,512,2048]{2,1,0:T(8,128)} %bitcast.290, f32[512,128]{1,0:T(8,128)S(1)} %get-tuple-element.9.refs_0_, f32[512,128]{1,0:T(8,128)S(1)} %collective-permute-done.20.refs_1_, f32[512,128]{1,0:T(8,128)S(1)} %collective-permute-done.21.refs_2_, ...), custom_call_target="tpu_custom_call" | custom-call | tf_op jit(solution)/shard_map/pallas_call | solution.py:47
  224.0 17.8 %collective-permute-done.39 = f32[256,128]{0,1:T(8,128)S(1)} collective-permute-done((f32[256,128]{0,1:T(8,128)S(1)}, f32[256,128]{0,1:T(8,128)S(1)}, u32[]{:S(2)}, u32[]{:S(2)}) %collective-permute-start.39) | collective-permute-done | bytes 131104 | tf_op jit(solution)/shard_map/ppermute | solution.py:16
  244.5 6.8 %collective-permute-done.24 = f32[1,512,128]{2,1,0:T(8,128)S(1)} collective-permute-done((f32[1,512,128]{2,1,0:T(8,128)S(1)}, f32[1,512,128]{2,1,0:T(8,128)S(1)}, u32[]{:S(2)}, u32[]{:S(2)}) %collective-permute-start.24) | collective-permute-done | bytes 262176 | tf_op jit(solution)/shard_map/ppermute | solution.py:16
  261.0 4.5 %collective-permute-done.41 = f32[256,128]{0,1:T(8,128)S(1)} collective-permute-done((f32[256,128]{0,1:T(8,128)S(1)}, f32[256,128]{0,1:T(8,128)S(1)}, u32[]{:S(2)}, u32[]{:S(2)}) %collective-permute-start.41) | collective-permute-done | bytes 131104 | tf_op jit(solution)/shard_map/ppermute | solution.py:16
  276.8 6.0 %collective-permute-done.4 = f32[1,512,256]{2,1,0:T(8,128)S(1)} collective-permute-done((f32[1,512,256]{2,1,0:T(8,128)}, f32[1,512,256]{2,1,0:T(8,128)S(1)}, u32[]{:S(2)}, u32[]{:S(2)}) %collective-permute-start.4) | collective-permute-done | bytes 524320 | tf_op jit(solution)/shard_map/ppermute | solution.py:16
  284.2 7.3 %collective-permute-done.9 = f32[1,512,256]{2,1,0:T(8,128)S(1)} collective-permute-done((f32[1,512,256]{2,1,0:T(8,128)}, f32[1,512,256]{2,1,0:T(8,128)S(1)}, u32[]{:S(2)}, u32[]{:S(2)}) %collective-permute-start.9) | collective-permute-done | bytes 524320 | tf_op jit(solution)/shard_map/ppermute | solution.py:16
  298.0 6.0 %collective-permute-done.14 = f32[1,512,256]{2,1,0:T(8,128)S(1)} collective-permute-done((f32[1,512,256]{2,1,0:T(8,128)S(1)}, f32[1,512,256]{2,1,0:T(8,128)S(1)}, u32[]{:S(2)}, u32[]{:S(2)}) %collective-permute-start.14) | collective-permute-done | bytes 524320 | tf_op jit(solution)/shard_map/ppermute | solution.py:16
  328.4 10.5 %collective-permute-done.35 = f32[1,512,256]{2,1,0:T(8,128)S(1)} collective-permute-done((f32[1,512,256]{2,1,0:T(8,128)S(1)}, f32[1,512,256]{2,1,0:T(8,128)S(1)}, u32[]{:S(2)}, u32[]{:S(2)}) %collective-permute-start.35) | collective-permute-done | bytes 524320 | tf_op jit(solution)/shard_map/ppermute | solution.py:16
  353.5 4.2 %collective-permute-done.37 = f32[1,128,256]{1,2,0:T(8,128)S(1)} collective-permute-done((f32[1,128,256]{1,2,0:T(8,128)S(1)}, f32[1,128,256]{1,2,0:T(8,128)S(1)}, u32[]{:S(2)}, u32[]{:S(2)}) %collective-permute-start.37) | collective-permute-done | bytes 131104 | tf_op jit(solution)/shard_map/ppermute | solution.py:16
  (257 shorter events, 129.6 us)
Async XLA Ops:
  4.7 51.2 %collective-permute-start.1 = (f32[512,256]{1,0:T(8,128)S(1)}, f32[512,256]{1,0:T(8,128)}, u32[]{:S(2)}, u32[]{:S(2)}) collective-permute-start(f32[512,256]{1,0:T(8,128)S(1)} %get-tuple-element.32.refs_0_), channel_id=1, source_target_pairs={{0,8},{4,12},{8,0},{12,4},{1,9},{5,13},{9,1},{13,5},{2,10},{6,14},... | collective-permute-start | bytes 1572872 | tf_op jit(solution)/shard_map/ppermute | solution.py:16
  8.7 100.5 %collective-permute-start = (f32[512,256]{1,0:T(8,128)S(1)}, f32[512,256]{1,0:T(8,128)S(1)}, u32[]{:S(2)}, u32[]{:S(2)}) collective-permute-start(f32[512,256]{1,0:T(8,128)S(1)} %get-tuple-element.32.refs_0_), channel_id=1, source_target_pairs={{0,4},{4,0},{8,12},{12,8},{1,5},{5,1},{9,13},{13,9},{2,6},{6,2},{1... | collective-permute-start | bytes 1572872 | tf_op jit(solution)/shard_map/ppermute | solution.py:16
  12.1 42.4 %collective-permute-start.6 = (f32[512,256]{1,0:T(8,128)S(1)}, f32[512,256]{1,0:T(8,128)}, u32[]{:S(2)}, u32[]{:S(2)}) collective-permute-start(f32[512,256]{1,0:T(8,128)S(1)} %get-tuple-element.31.refs_0_), channel_id=1, source_target_pairs={{0,8},{4,12},{8,0},{12,4},{1,9},{5,13},{9,1},{13,5},{2,10},{6,14},... | collective-permute-start | bytes 1572872 | tf_op jit(solution)/shard_map/ppermute | solution.py:16
  54.5 27.3 %collective-permute-start.16 = (f32[512,128]{1,0:T(8,128)}, f32[512,128]{1,0:T(8,128)S(1)}, u32[]{:S(2)}, u32[]{:S(2)}) collective-permute-start(f32[512,128]{1,0:T(8,128)} %get-tuple-element.8.refs_0_), channel_id=1, source_target_pairs={{0,8},{4,12},{8,0},{12,4},{1,9},{5,13},{9,1},{13,5},{2,10},{6,14},... | collective-permute-start | bytes 786440 | tf_op jit(solution)/shard_map/ppermute | solution.py:16
  55.9 52.3 %collective-permute-start.11 = (f32[512,256]{1,0:T(8,128)S(1)}, f32[512,256]{1,0:T(8,128)S(1)}, u32[]{:S(2)}, u32[]{:S(2)}) collective-permute-start(f32[512,256]{1,0:T(8,128)S(1)} %get-tuple-element.7.refs_0_), channel_id=1, source_target_pairs={{0,8},{4,12},{8,0},{12,4},{1,9},{5,13},{9,1},{13,5},{2,10},{6,14},... | collective-permute-start | bytes 1572872 | tf_op jit(solution)/shard_map/ppermute | solution.py:16
  58.9 28.1 %collective-permute-start.15 = (f32[512,128]{1,0:T(8,128)}, f32[512,128]{1,0:T(8,128)S(1)}, u32[]{:S(2)}, u32[]{:S(2)}) collective-permute-start(f32[512,128]{1,0:T(8,128)} %get-tuple-element.8.refs_0_), channel_id=1, source_target_pairs={{0,4},{4,0},{8,12},{12,8},{1,5},{5,1},{9,13},{13,9},{2,6},{6,2},{1... | collective-permute-start | bytes 786440 | tf_op jit(solution)/shard_map/ppermute | solution.py:16
  87.0 24.1 %collective-permute-start.2 = (f32[512,256]{1,0:T(8,128)}, f32[512,256]{1,0:T(8,128)}, u32[]{:S(2)}, u32[]{:S(2)}) collective-permute-start(f32[512,256]{1,0:T(8,128)} %collective-permute-done.1.refs_2_), channel_id=1, source_target_pairs={{0,4},{4,0},{8,12},{12,8},{1,5},{5,1},{9,13},{13,9},{2,6},{6,2},{1... | collective-permute-start | bytes 1572872 | tf_op jit(solution)/shard_map/ppermute | solution.py:16
  97.0 31.1 %collective-permute-start.5 = (f32[512,256]{1,0:T(8,128)S(1)}, f32[512,256]{1,0:T(8,128)S(1)}, u32[]{:S(2)}, u32[]{:S(2)}) collective-permute-start(f32[512,256]{1,0:T(8,128)S(1)} %get-tuple-element.31.refs_0_), channel_id=1, source_target_pairs={{0,4},{4,0},{8,12},{12,8},{1,5},{5,1},{9,13},{13,9},{2,6},{6,2},{1... | collective-permute-start | bytes 1572872 | tf_op jit(solution)/shard_map/ppermute | solution.py:16
  106.1 35.8 %collective-permute-start.7 = (f32[512,256]{1,0:T(8,128)}, f32[512,256]{1,0:T(8,128)S(1)}, u32[]{:S(2)}, u32[]{:S(2)}) collective-permute-start(f32[512,256]{1,0:T(8,128)} %collective-permute-done.6.refs_2_), channel_id=1, source_target_pairs={{0,4},{4,0},{8,12},{12,8},{1,5},{5,1},{9,13},{13,9},{2,6},{6,2},{1... | collective-permute-start | bytes 1572872 | tf_op jit(solution)/shard_map/ppermute | solution.py:16
  108.2 57.7 %collective-permute-start.18 = (f32[2,512,128]{2,1,0:T(8,128)S(1)}, f32[2,512,128]{2,1,0:T(8,128)S(1)}, u32[]{:S(2)}, u32[]{:S(2)}) collective-permute-start(f32[2,512,128]{2,1,0:T(8,128)S(1)} %shard_map.86), channel_id=1, source_target_pairs={{0,1},{1,0},{2,3},{3,2},{4,5},{5,4},{6,7},{7,6},{8,9},{9,8},{10,11... | collective-permute-start | bytes 1572872 | tf_op jit(solution)/shard_map/ppermute | solution.py:16
  109.3 54.5 %collective-permute-start.21 = (f32[512,128]{1,0:T(8,128)S(1)}, f32[512,128]{1,0:T(8,128)S(1)}, u32[]{:S(2)}, u32[]{:S(2)}) collective-permute-start(f32[512,128]{1,0:T(8,128)S(1)} %get-tuple-element.9.refs_0_), channel_id=1, source_target_pairs={{0,8},{4,12},{8,0},{12,4},{1,9},{5,13},{9,1},{13,5},{2,10},{6,14},... | collective-permute-start | bytes 786440 | tf_op jit(solution)/shard_map/ppermute | solution.py:16
  111.1 55.0 %collective-permute-start.10 = (f32[512,256]{1,0:T(8,128)S(1)}, f32[512,256]{1,0:T(8,128)S(1)}, u32[]{:S(2)}, u32[]{:S(2)}) collective-permute-start(f32[512,256]{1,0:T(8,128)S(1)} %get-tuple-element.7.refs_0_), channel_id=1, source_target_pairs={{0,4},{4,0},{8,12},{12,8},{1,5},{5,1},{9,13},{13,9},{2,6},{6,2},{1... | collective-permute-start | bytes 1572872 | tf_op jit(solution)/shard_map/ppermute | solution.py:16
  128.2 84.3 %collective-permute-start.33 = (f32[512,256]{1,0:T(8,128)S(1)}, f32[512,256]{1,0:T(8,128)S(1)}, u32[]{:S(2)}, u32[]{:S(2)}) collective-permute-start(f32[512,256]{1,0:T(8,128)S(1)} %copy-done.25), channel_id=1, source_target_pairs={{0,0},{1,4},{2,8},{3,12},{4,1},{5,5},{6,9},{7,13},{8,2},{9,6},{10,... | collective-permute-start | bytes 1572872 | tf_op jit(solution)/shard_map/ppermute | solution.py:142
  141.8 60.3 %collective-permute-start.20 = (f32[512,128]{1,0:T(8,128)S(1)}, f32[512,128]{1,0:T(8,128)S(1)}, u32[]{:S(2)}, u32[]{:S(2)}) collective-permute-start(f32[512,128]{1,0:T(8,128)S(1)} %get-tuple-element.9.refs_0_), channel_id=1, source_target_pairs={{0,4},{4,0},{8,12},{12,8},{1,5},{5,1},{9,13},{13,9},{2,6},{6,2},{1... | collective-permute-start | bytes 786440 | tf_op jit(solution)/shard_map/ppermute | solution.py:16
  163.8 22.9 %collective-permute-start.12 = (f32[512,256]{1,0:T(8,128)S(1)}, f32[512,256]{1,0:T(8,128)S(1)}, u32[]{:S(2)}, u32[]{:S(2)}) collective-permute-start(f32[512,256]{1,0:T(8,128)S(1)} %copy-done.3), channel_id=1, source_target_pairs={{0,4},{4,0},{8,12},{12,8},{1,5},{5,1},{9,13},{13,9},{2,6},{6,2},{1... | collective-permute-start | bytes 1572872 | tf_op jit(solution)/shard_map/ppermute | solution.py:16
  165.9 36.8 %collective-permute-start.22 = (f32[512,128]{1,0:T(8,128)S(1)}, f32[512,128]{1,0:T(8,128)S(1)}, u32[]{:S(2)}, u32[]{:S(2)}) collective-permute-start(f32[512,128]{1,0:T(8,128)S(1)} %collective-permute-done.21.refs_2_), channel_id=1, source_target_pairs={{0,4},{4,0},{8,12},{12,8},{1,5},{5,1},{9,13},{13,9},{2,6},{6,2},{1... | collective-permute-start | bytes 786440 | tf_op jit(solution)/shard_map/ppermute | solution.py:16
  166.1 46.2 %collective-permute-start.19 = (f32[1,512,128]{2,1,0:T(8,128)S(1)}, f32[1,512,128]{2,1,0:T(8,128)S(1)}, u32[]{:S(2)}, u32[]{:S(2)}) collective-permute-start(f32[1,512,128]{2,1,0:T(8,128)S(1)} %slice_bitcast_fusion.18), channel_id=1, source_target_pairs={{0,2},{1,3},{2,0},{3,1},{4,6},{5,7},{6,4},{7,5},{8,10},{9,11},{10,... | collective-permute-start | bytes 786440 | tf_op jit(solution)/shard_map/ppermute | solution.py:16
  186.7 55.1 %collective-permute-start.3 = (f32[2,512,256]{2,1,0:T(8,128)S(1)}, f32[2,512,256]{2,1,0:T(8,128)S(1)}, u32[]{:S(2)}, u32[]{:S(2)}) collective-permute-start(f32[2,512,256]{2,1,0:T(8,128)S(1)} %shard_map.80), channel_id=1, source_target_pairs={{0,1},{1,0},{2,3},{3,2},{4,5},{5,4},{6,7},{7,6},{8,9},{9,8},{10,11... | collective-permute-start | bytes 3145736 | tf_op jit(solution)/shard_map/ppermute | solution.py:16
  202.1 49.7 %collective-permute-start.8 = (f32[2,512,256]{2,1,0:T(8,128)S(1)}, f32[2,512,256]{2,1,0:T(8,128)S(1)}, u32[]{:S(2)}, u32[]{:S(2)}) collective-permute-start(f32[2,512,256]{2,1,0:T(8,128)S(1)} %shard_map.82), channel_id=1, source_target_pairs={{0,1},{1,0},{2,3},{3,2},{4,5},{5,4},{6,7},{7,6},{8,9},{9,8},{10,11... | collective-permute-start | bytes 3145736 | tf_op jit(solution)/shard_map/ppermute | solution.py:16
  202.7 90.7 %collective-permute-start.25 = (f32[2,512,512]{2,1,0:T(8,128)}, f32[2,512,512]{2,1,0:T(8,128)}, u32[]{:S(2)}, u32[]{:S(2)}) collective-permute-start(f32[2,512,512]{2,1,0:T(8,128)} %pad_maximum_fusion), channel_id=1, source_target_pairs={{0,2},{5,7},{10,8},{15,13},{16,18},{21,23},{26,24},{31,29}} | collective-permute-start | bytes 6291464 | tf_op jit(solution)/shard_map/ppermute | solution.py:133
  221.5 51.2 %collective-permute-start.31 = (f32[2,512,256]{2,1,0:T(8,128)}, f32[2,512,256]{2,1,0:T(8,128)}, u32[]{:S(2)}, u32[]{:S(2)}) collective-permute-start(f32[2,512,256]{2,1,0:T(8,128)} %pad_maximum_fusion.4), channel_id=1, source_target_pairs={{0,2},{5,7},{10,8},{15,13},{16,18},{21,23},{26,24},{31,29}} | collective-permute-start | bytes 3145736 | tf_op jit(solution)/shard_map/ppermute | solution.py:133
  241.7 28.2 %collective-permute-start.13 = (f32[2,512,256]{2,1,0:T(8,128)}, f32[2,512,256]{2,1,0:T(8,128)}, u32[]{:S(2)}, u32[]{:S(2)}) collective-permute-start(f32[2,512,256]{2,1,0:T(8,128)} %shard_map.84), channel_id=1, source_target_pairs={{0,1},{1,0},{2,3},{3,2},{4,5},{5,4},{6,7},{7,6},{8,9},{9,8},{10,11... | collective-permute-start | bytes 3145736 | tf_op jit(solution)/shard_map/ppermute | solution.py:16
  265.5 92.3 %collective-permute-start.50 = (f32[1,128,128]{1,2,0:T(8,128)}, f32[1,128,128]{1,2,0:T(8,128)}, u32[]{:S(2)}, u32[]{:S(2)}) collective-permute-start(f32[1,128,128]{1,2,0:T(8,128)} %slice_bitcast_fusion.22), channel_id=1, source_target_pairs={{0,8},{4,12},{8,0},{12,4},{1,9},{5,13},{9,1},{13,5},{2,10},{6,14},... | collective-permute-start | bytes 196616 | tf_op jit(solution)/shard_map/ppermute | solution.py:16
  272.7 40.6 %collective-permute-start.45 = (f32[128,128]{0,1:T(8,128)}, f32[128,128]{0,1:T(8,128)}, u32[]{:S(2)}, u32[]{:S(2)}) collective-permute-start(f32[128,128]{0,1:T(8,128)} %add.213), channel_id=1, source_target_pairs={{0,8},{4,12},{8,0},{12,4},{1,9},{5,13},{9,1},{13,5},{2,10},{6,14},... | collective-permute-start | bytes 196616 | tf_op jit(solution)/shard_map/ppermute | solution.py:16
  (57 other events, 590.6 us)
where the time goes:
time: 362 us; the launch traced here: 360 us
  waiting for transfers between devices  159 us (44%)
  Pallas kernels  73.5 us (20%)
  starting transfers between devices  55.4 us (15%)
  local copies, waits for them, and re-layouts  33.9 us (9%)
  other arithmetic  24.1 us (7%)
  matrix products  12.4 us (3%)
    ppermute x46, waiting for transfers between devices, swap(): return lax.ppermute(block, axis, pairs)  159 us
    pallas_call x10, Pallas kernels, product(): pl.pallas_call(product_kernel, grid_spec=pltpu.PrefetchScalarGridSpec(num...  73.5 us
    ppermute x46, starting transfers between devices, swap(): return lax.ppermute(block, axis, pairs)  46.1 us
    unnamed x75, local copies, waits for them, and re-layouts  16.4 us
    dot_general x8, matrix products, dot_tn(): return lax.dot_general(a, b, (((0,), (0,)), ((), ())), precision=precision)  9.04 us
    ppermute x4, starting transfers between devices, own_output_rows(): moved = lax.ppermute(jnp.stack(held[bit:]), ('row', 'col'), pairs)  8.45 us
  transfers between devices with their start and end apart: 51, of which 20 were waited for; matrix products, arithmetic and copies ran while one was open for 17% of the time, Pallas kernels for 20%

commit v1 on v0

--- a/solution.py
+++ b/solution.py
@@ -59,10 +59,6 @@
     )(place, tile, *blocks)
 
 
-def after(block, *others):
-    return lax.optimization_barrier((block, *others))[0]
-
-
 def dot(a, b, precision):
     return jnp.matmul(a, b, precision=precision)
 
@@ -83,15 +79,6 @@
     index = lax.axis_index(axis)
     return jnp.stack([lax.dynamic_index_in_dim(blocks, index ^ j, 0, keepdims=False)
                       for j in range(blocks.shape[0])])
-
-
-def gather_blocks(block, axis):
-    blocks = {0: block}
-    bit = lax.axis_size(axis) // 2
-    while bit >= 1:
-        blocks.update({j ^ bit: swap(held, axis, bit) for j, held in list(blocks.items())})
-        bit //= 2
-    return [blocks[j] for j in range(len(blocks))]
 
 
 def placed(blocks, axis):
@@ -103,10 +90,14 @@
     return whole
 
 
-def all_sum(block, axis):
+def sum_to_last(block, axis, count):
+    size = lax.axis_size(axis)
     bit = 1
-    while bit < lax.axis_size(axis):
-        block = block + swap(block, axis, bit)
+    while bit < size:
+        if bit * count >= size:
+            block = block + lax.ppermute(block, axis, [(i, i ^ bit) for i in range(size) if not i & bit])
+        else:
+            block = block + swap(block, axis, bit)
         bit *= 2
     return block
 
@@ -151,88 +142,143 @@
     tile_mask = jnp.repeat(ancestor_tiles, TILE, axis=2)
     kept_rows = lax.dynamic_slice_in_dim(tile_mask, row_start, local_rows, 2).astype(jnp.float32)
     masked = panels * kept_rows[..., None]
-
     tile = inverse_tile.reshape(cols_axis, inverse_tile.shape[0] // cols_axis, -1)
 
-    def output_rows(blocks):
-        sent = swap(product(tile, blocks, 1), "col", 1)
-        return -sum_scatter(product(tile, blocks, 0) + sent, "col", 2)
-
-    def by_cols(terms):
-        return terms.reshape(width, cols_axis, -1).swapaxes(0, 1)
+    def by_cols(*terms):
+        terms = jnp.concatenate([term.reshape(width, cols_axis, span).swapaxes(0, 1) for term in terms], axis=2)
+        return by_xor(terms, "col")
 
     def by_rows(terms):
-        return terms.reshape(rows_axis, height, -1)
-
-    def spread_sum(terms):
-        terms = jnp.concatenate([by_cols(term) for term in terms], axis=2)
-        terms = sum_scatter(by_xor(terms, "col"), "col")
-        terms = sum_scatter(by_xor(by_rows(terms), "row"), "row")
-        return [terms[:, start:start + span] for start in range(0, terms.shape[1], span)]
-
-    late = 2 * span
-    sent = []
-    ancestor, diagonals, crosses = [], [], []
-    for s in range(siblings):
-        link = link_panel[s]
-        first = masked[s, 0]
-        second = masked[s, 1] - dot(first, link, precise)
-
-        def gathered(panel, start, stop):
-            piece = panel[:, start:stop]
-            if len(sent) >= 2:
-                piece = after(piece, sent[-2])
-            blocks = gather_blocks(piece, "row")
-            sent.append(blocks[rows_axis // 2])
-            return blocks
-
-        def joined(groups):
-            return [jnp.concatenate(group, axis=1) for group in zip(*groups)]
-
-        first_blocks = [gathered(first, i, i + late) for i in range(0, width, late)]
-        second_blocks = [gathered(second, i, i + late) for i in range(0, width - late, late)]
-        last_blocks = [gathered(second, i, i + span) for i in range(width - late, width, span)]
-        own_last = own_output_rows_direct(after(second[:, width - late:], sent[1]))
-
-        link_cols = lax.dynamic_slice_in_dim(link, col_id * span, span, 1)
-        link_rows = lax.dynamic_slice_in_dim(link, row_id * height, height, 0)
-        given = placed([block.T for block in gather_blocks(diag_inverse[s, 0], "col")], "col")
-        given_link = dot_tn(given, link_cols, precise)
-
-        out_first = jnp.concatenate([output_rows(blocks) for blocks in first_blocks], axis=1)
-        own_first = own_output_rows(joined(first_blocks))
-        (first_sum,) = spread_sum([dot_tn(own_first, out_first, three_pass)])
-
-        out_early = jnp.concatenate([output_rows(blocks) for blocks in second_blocks], axis=1)
-        own_early = own_output_rows(joined(second_blocks))
-        own_second = jnp.concatenate([own_early, own_last], axis=1)
-        cross_terms = dot_tn(out_first, own_second, three_pass)
-        early_terms = jnp.concatenate([
-            dot_tn(own_second, out_early, three_pass),
-            jnp.pad(dot_tn(out_early, own_last, three_pass), ((0, late), (0, 0)))], axis=1)
-        cross_sum, early_sum = spread_sum([cross_terms, early_terms])
-
-        link_terms = sum_scatter(by_xor(by_rows(dot_tn(link_rows, given_link, precise)), "row"), "row")
-
-        out_a = output_rows(last_blocks[0])
-        terms_a = all_sum(all_sum(dot_tn(own_last, out_a, three_pass), "col"), "row")
-        out_b = output_rows(last_blocks[1])
-        terms_b = all_sum(all_sum(dot_tn(own_last[:, span:], out_b, three_pass), "col"), "row")
-        last_terms = jnp.concatenate([
-            terms_a, jnp.concatenate([terms_a[span:].T, terms_b], axis=0)], axis=1)
-        padded = jnp.pad(last_terms, ((height, 0), (span, 0)))
+        return by_xor(terms.reshape(rows_axis, height, -1), "row")
+
+    def one_pair(first, panel_second, link, given_first, given_second):
+        live = {"first": first, "second": panel_second - dot(first, link, precise)}
+        slots = {}
+
+        def at(slot, *steps):
+            slots.setdefault(slot, []).extend(steps)
+
+        late = 2 * span
+        pieces = [("first", i, i + late) for i in range(0, width, late)]
+        count_first = len(pieces)
+        pieces += [("second", i, i + late) for i in range(0, width - late, late)]
+        count_early = len(pieces)
+        pieces += [("second", i, i + span) for i in range(width - late, width, span)]
+        stages = rows_axis.bit_length() - 1
+
+        def fetch(k, stage):
+            if stage == 0:
+                panel, start, stop = pieces[k]
+                live[k, 0] = live[panel][:, start:stop]
+            for j in range(1, rows_axis):
+                if j.bit_count() == stage + 1:
+                    live[k, j] = swap(live[k, j & (j - 1)], "row", j & -j)
+
+        def blocks(k):
+            return [live[k, j] for j in range(rows_axis)]
+
+        def multiply(k):
+            sent = swap(product(tile, blocks(k), 1), "col", 1)
+            live["sums", k] = product(tile, blocks(k), 0) + sent
+
+        def reduce(k):
+            live["out", k] = -sum_scatter(live.pop(("sums", k)), "col", 2)
+
+        def own(name, start, stop):
+            groups = zip(*(blocks(k) for k in range(start, stop)))
+            live[name] = own_output_rows([jnp.concatenate(group, axis=1) for group in groups])
+            for k in range(start, stop):
+                for j in range(rows_axis):
+                    del live[k, j]
+
+        def outs(start, stop):
+            return jnp.concatenate([live["out", k] for k in range(start, stop)], axis=1)
+
+        for k in range(len(pieces)):
+            for stage in range(stages):
+                at(k + stage, lambda k=k, stage=stage: fetch(k, stage))
+
+        def own_last():
+            live["own_last"] = own_output_rows_direct(live["second"][:, width - late:])
+
+        def given_link():
+            link_cols = lax.dynamic_slice_in_dim(link, col_id * span, span, 1)
+            given = {0: given_first}
+            bit = cols_axis // 2
+            while bit >= 1:
+                given.update({j ^ bit: swap(block, "col", bit) for j, block in list(given.items())})
+                bit //= 2
+            given = [given[j].T for j in range(cols_axis)]
+            live["given_link"] = dot_tn(placed(given, "col"), link_cols, precise)
+
+        def first_terms():
+            live["first_terms"] = sum_scatter(
+                by_cols(dot_tn(live["own_first"], outs(0, count_first), three_pass)), "col")
+
+        def first_sum():
+            live["first_sum"] = sum_scatter(by_rows(live.pop("first_terms")), "row")
+
+        def early_terms():
+            out_early = outs(count_first, count_early)
+            own_second = jnp.concatenate([live["own_early"], live["own_last"]], axis=1)
+            cross = dot_tn(outs(0, count_first), own_second, three_pass)
+            early = jnp.concatenate([
+                dot_tn(own_second, out_early, three_pass),
+                jnp.pad(dot_tn(out_early, live["own_last"], three_pass), ((0, late), (0, 0)))], axis=1)
+            live["early_terms"] = sum_scatter(by_cols(cross, early), "col")
+
+        def early_sum():
+            link_rows = lax.dynamic_slice_in_dim(link, row_id * height, height, 0)
+            terms = live.pop("early_terms")
+            terms = terms.at[:, span:].add(-dot_tn(link_rows, live["given_link"], precise))
+            live["early_sum"] = sum_scatter(by_rows(terms), "row")
+
+        def last_terms(k):
+            start = (k - count_early) * span
+            terms = dot_tn(live["own_last"][:, start:], live["out", k], three_pass)
+            count = cols_axis * terms.shape[1] // terms.shape[0]
+            live["last", k] = sum_to_last(sum_to_last(terms, "col", count), "row", count)
+
+        end = len(pieces) - 1 + stages
+        for k in range(len(pieces)):
+            at(k + stages, lambda k=k: multiply(k))
+            at(min(k + stages + 1, end), lambda k=k: reduce(k))
+            if k == 0:
+                at(1, own_last)
+                at(1, given_link)
+            if k == count_first - 1:
+                at(k + stages, lambda: own("own_first", 0, count_first))
+                at(k + stages + 1, first_terms)
+                at(k + stages + 2, first_sum)
+            if k == count_early - 1:
+                at(k + stages, lambda: own("own_early", count_first, count_early))
+                at(k + stages + 1, early_terms)
+                at(k + stages + 2, early_sum)
+            if k >= count_early:
+                at(end, lambda k=k: last_terms(k))
+
+        for slot in range(end + 1):
+            if slot > 0:
+                live = dict(zip(live, lax.optimization_barrier(tuple(live.values()))))
+            for step in slots[slot]:
+                step()
+
+        last_a, last_b = live["last", end - stages - 1], live["last", end - stages]
+        last = jnp.concatenate([last_a, jnp.concatenate([last_a[span:].T, last_b], axis=0)], axis=1)
+        padded = jnp.pad(last, ((height, 0), (span, 0)))
         corner = width - late
         last_sum = lax.dynamic_slice(
             padded,
             (jnp.maximum(row_id * height - corner + height, 0), jnp.maximum(col_id * span - corner + span, 0)),
             (height, span))
-
-        ancestor.append(jnp.stack([out_first, jnp.concatenate([out_early, out_a, out_b], axis=1)]))
-        diagonals.append(jnp.stack([
-            diag_inverse[s, 0] - first_sum,
-            diag_inverse[s, 1] - early_sum - last_sum + link_terms]))
-        crosses.append(-(cross_sum + given_link))
-    return jnp.stack(ancestor), jnp.stack(diagonals), jnp.stack(crosses)
+        cross_sum, early = live["early_sum"][:, :span], live["early_sum"][:, span:]
+        ancestor = jnp.stack([outs(0, count_first), outs(count_first, len(pieces))])
+        diagonal = jnp.stack([given_first - live["first_sum"], given_second - early - last_sum])
+        return ancestor, diagonal, -(cross_sum + live["given_link"])
+
+    results = [one_pair(masked[s, 0], masked[s, 1], link_panel[s], diag_inverse[s, 0], diag_inverse[s, 1])
+               for s in range(siblings)]
+    return tuple(jnp.stack(group) for group in zip(*results))
 
 
 def solution(mesh):

time: 362 us -> 391 us (1.080)
  starting transfers between devices: 55.4 us -> 71.1 us
  other arithmetic: 24.1 us -> 34 us
    ppermute x46 -> x38, waiting for transfers between devices: 159 us -> 136 us  [swap(): return lax.ppermute(block, axis, pairs)]
    ppermute x0 -> x6, starting transfers between devices: none -> 19.6 us  [sum_to_last(): lax.ppermute(block, axis, [(i, i ^ bit) for i in range(size) if not i & b...]
    ppermute x4, waiting for transfers between devices: 0.01 us -> 16.9 us  [own_output_rows(): moved = lax.ppermute(jnp.stack(held[bit:]), ('row', 'col'), pairs)]
    ppermute x0 -> x6, waiting for transfers between devices: none -> 8.32 us  [sum_to_last(): lax.ppermute(block, axis, [(i, i ^ bit) for i in range(size) if not i & b...]
    another operation x0 -> x5, local copies, waits for them, and re-layouts: none -> 6.22 us
    ppermute x46 -> x38, starting transfers between devices: 46.1 us -> 40 us  [swap(): return lax.ppermute(block, axis, pairs)]
    reshape x0 -> x2, local copies, waits for them, and re-layouts: none -> 5.08 us  [by_cols(): term.reshape(width, cols_axis, span).swapaxes(0, 1)]
    dot_general x4 -> x0, local copies, waits for them, and re-layouts: 4.58 us -> none  [dot_tn(): return lax.dot_general(a, b, (((0,), (0,)), ((), ())), precision=precision)]
  transfers between devices with their start and end apart: 51 -> 49, of which waited for: 20 -> 27; matrix products, arithmetic and copies ran while one was open for 17% -> 13% of each run, Pallas kernels for 20% -> 13%
where the time goes in v1:
time: 391 us; the launch traced here: 388 us
  waiting for transfers between devices  161 us (41%)
  Pallas kernels  73 us (19%)
  starting transfers between devices  71.1 us (18%)
  local copies, waits for them, and re-layouts  36.9 us (9%)
  other arithmetic  34 us (9%)
  matrix products  10.4 us (3%)
    ppermute x38, waiting for transfers between devices, swap(): return lax.ppermute(block, axis, pairs)  136 us
    pallas_call x10, Pallas kernels, product(): pl.pallas_call(product_kernel, grid_spec=pltpu.PrefetchScalarGridSpec(num...  73 us
    ppermute x38, starting transfers between devices, swap(): return lax.ppermute(block, axis, pairs)  40 us
    ppermute x6, starting transfers between devices, sum_to_last(): lax.ppermute(block, axis, [(i, i ^ bit) for i in range(size) if not i & b...  19.6 us
    ppermute x4, waiting for transfers between devices, own_output_rows(): moved = lax.ppermute(jnp.stack(held[bit:]), ('row', 'col'), pairs)  16.9 us
    unnamed x113, local copies, waits for them, and re-layouts  16.3 us
    ppermute x4, starting transfers between devices, own_output_rows(): moved = lax.ppermute(jnp.stack(held[bit:]), ('row', 'col'), pairs)  10.9 us
    ppermute x6, waiting for transfers between devices, sum_to_last(): lax.ppermute(block, axis, [(i, i ^ bit) for i in range(size) if not i & b...  8.32 us
  transfers between devices with their start and end apart: 49, of which 27 were waited for; matrix products, arithmetic and copies ran while one was open for 13% of the time, Pallas kernels for 13%

profile of v1, /device:TPU:0, one launch (start us, length us, event | category | flops | bytes accessed | tf_op | source)
XLA Modules:
  0.0 388.4 jit_solution(16588114206188317110)
XLA Ops:
  16.7 14.1 %collective-permute-done.refs_1_ = f32[512,256]{1,0:T(8,128)S(1)} collective-permute-done((f32[512,256]{1,0:T(8,128)S(1)}, f32[512,256]{1,0:T(8,128)S(1)}, u32[]{:S(2)}, u32[]{:S(2)}) %collective-permute-start) | collective-permute-done | bytes 524320 | tf_op jit(solution)/shard_map/ppermute | solution.py:16
  41.4 17.3 %collective-permute-done.3.refs_1_ = f32[512,256]{1,0:T(8,128)S(1)} collective-permute-done((f32[512,256]{1,0:T(8,128)S(1)}, f32[512,256]{1,0:T(8,128)S(1)}, u32[]{:S(2)}, u32[]{:S(2)}) %collective-permute-start.3) | collective-permute-done | bytes 524320 | tf_op jit(solution)/shard_map/ppermute | solution.py:16
  59.5 13.8 %collective-permute-done.4.refs_2_ = f32[512,256]{1,0:T(8,128)S(1)} collective-permute-done((f32[512,256]{1,0:T(8,128)S(1)}, f32[512,256]{1,0:T(8,128)S(1)}, u32[]{:S(2)}, u32[]{:S(2)}) %collective-permute-start.4) | collective-permute-done | bytes 524320 | tf_op jit(solution)/shard_map/ppermute | solution.py:16
  73.3 12.1 %collective-permute-done.2.refs_3_ = f32[512,256]{1,0:T(8,128)S(1)} collective-permute-done((f32[512,256]{1,0:T(8,128)S(1)}, f32[512,256]{1,0:T(8,128)S(1)}, u32[]{:S(2)}, u32[]{:S(2)}) %collective-permute-start.2) | collective-permute-done | bytes 524320 | tf_op jit(solution)/shard_map/ppermute | solution.py:16
  85.4 7.3 %shard_map.80 = f32[2,512,256]{2,1,0:T(8,128)S(1)} custom-call(s32[3]{0:T(128)S(1)} %pad_add_fusion.1.place, f32[4,512,2048]{2,1,0:T(8,128)} %bitcast.279, f32[512,256]{1,0:T(8,128)S(1)} %slice.198.refs_0_, f32[512,256]{1,0:T(8,128)S(1)} %collective-permute-done.refs_1_, f32[512,256]{1,0:T(8,128)S(1)} %collective-permute-done.1.refs_2_, ...), custom_call_target="tpu_custom_call" | custom-call | tf_op jit(solution)/shard_map/pallas_call | solution.py:47
  97.1 7.3 %shard_map.79 = f32[2,512,256]{2,1,0:T(8,128)S(1)} custom-call(s32[3]{0:T(128)S(1)} %pad_add_fusion.place, f32[4,512,2048]{2,1,0:T(8,128)} %bitcast.280, f32[512,256]{1,0:T(8,128)S(1)} %slice.198.refs_0_, f32[512,256]{1,0:T(8,128)S(1)} %copy-done.5, f32[512,256]{1,0:T(8,128)S(1)} %copy-done.8, f32[512,256]{1,0:T(8,128)S(1)} %collective-permute-done.2.refs_3_), custom_call_target="tpu_custom_call" | custom-call | tf_op jit(solution)/shard_map/pallas_call | solution.py:47
  105.5 11.6 %collective-permute-done.10.refs_1_ = f32[512,256]{1,0:T(8,128)S(1)} collective-permute-done((f32[512,256]{1,0:T(8,128)S(1)}, f32[512,256]{1,0:T(8,128)S(1)}, u32[]{:S(2)}, u32[]{:S(2)}) %collective-permute-start.10) | collective-permute-done | bytes 524320 | tf_op jit(solution)/shard_map/ppermute | solution.py:16
  119.6 10.1 %collective-permute-done.9.refs_3_ = f32[512,256]{1,0:T(8,128)S(1)} collective-permute-done((f32[512,256]{1,0:T(8,128)S(1)}, f32[512,256]{1,0:T(8,128)S(1)}, u32[]{:S(2)}, u32[]{:S(2)}) %collective-permute-start.9) | collective-permute-done | bytes 524320 | tf_op jit(solution)/shard_map/ppermute | solution.py:16
  137.7 8.1 %shard_map.82 = f32[2,512,256]{2,1,0:T(8,128)} custom-call(s32[3]{0:T(128)S(1)} %pad_add_fusion.1.place, f32[4,512,2048]{2,1,0:T(8,128)} %bitcast.281, f32[512,256]{1,0:T(8,128)S(1)} %slice.154.refs_0_, f32[512,256]{1,0:T(8,128)S(1)} %copy-done.10, f32[512,256]{1,0:T(8,128)S(1)} %copy-done.13, f32[512,256]{1,0:T(8,128)S(1)} %copy-done.18), custom_call_target="tpu_custom_call" | custom-call | tf_op jit(solution)/shard_map/pallas_call | solution.py:47
  145.8 16.8 %collective-permute-done.18 = f32[2,512,512]{2,1,0:T(8,128)} collective-permute-done((f32[2,512,512]{2,1,0:T(8,128)}, f32[2,512,512]{2,1,0:T(8,128)}, u32[]{:S(2)}, u32[]{:S(2)}) %collective-permute-start.18) | collective-permute-done | bytes 2097184 | tf_op jit(solution)/shard_map/ppermute | solution.py:124
  173.7 7.3 %shard_map.81 = f32[2,512,256]{2,1,0:T(8,128)S(1)} custom-call(s32[3]{0:T(128)S(1)} %pad_add_fusion.place, f32[4,512,2048]{2,1,0:T(8,128)} %bitcast.282, f32[512,256]{1,0:T(8,128)S(1)} %slice.154.refs_0_, f32[512,256]{1,0:T(8,128)S(1)} %copy-done.11, f32[512,256]{1,0:T(8,128)S(1)} %copy-done.14, f32[512,256]{1,0:T(8,128)S(1)} %copy-done.19), custom_call_target="tpu_custom_call" | custom-call | tf_op jit(solution)/shard_map/pallas_call | solution.py:47
  195.9 8.0 %collective-permute-done.13.refs_3_ = f32[512,256]{1,0:T(8,128)S(1)} collective-permute-done((f32[512,256]{1,0:T(8,128)S(1)}, f32[512,256]{1,0:T(8,128)S(1)}, u32[]{:S(2)}, u32[]{:S(2)}) %collective-permute-start.13) | collective-permute-done | bytes 524320 | tf_op jit(solution)/shard_map/ppermute | solution.py:16
  212.8 4.4 %collective-permute-done.23 = f32[1,512,256]{2,1,0:T(8,128)S(1)} collective-permute-done((f32[1,512,256]{2,1,0:T(8,128)}, f32[1,512,256]{2,1,0:T(8,128)S(1)}, u32[]{:S(2)}, u32[]{:S(2)}) %collective-permute-start.23) | collective-permute-done | bytes 524320 | tf_op jit(solution)/shard_map/ppermute | solution.py:16
  227.0 7.3 %shard_map.84 = f32[2,512,256]{2,1,0:T(8,128)S(1)} custom-call(s32[3]{0:T(128)S(1)} %pad_add_fusion.1.place, f32[4,512,2048]{2,1,0:T(8,128)} %bitcast.283, f32[512,256]{1,0:T(8,128)S(1)} %slice.157.refs_0_, f32[512,256]{1,0:T(8,128)S(1)} %collective-permute-done.10.refs_1_, f32[512,256]{1,0:T(8,128)S(1)} %copy-done.3, f32[512,256]{1,0:T(8,128)S(1)} %copy-done.16), custom_call_target="tpu_custom_call" | custom-call | tf_op jit(solution)/shard_map/pallas_call | solution.py:47
  238.8 7.3 %shard_map.83 = f32[2,512,256]{2,1,0:T(8,128)S(1)} custom-call(s32[3]{0:T(128)S(1)} %pad_add_fusion.place, f32[4,512,2048]{2,1,0:T(8,128)} %bitcast.284, f32[512,256]{1,0:T(8,128)S(1)} %slice.157.refs_0_, f32[512,256]{1,0:T(8,128)S(1)} %collective-permute-done.10.refs_1_, f32[512,256]{1,0:T(8,128)S(1)} %copy-done.3, f32[512,256]{1,0:T(8,128)S(1)} %copy-done.16), custom_call_target="tpu_custom_call" | custom-call | tf_op jit(solution)/shard_map/pallas_call | solution.py:47
  255.5 7.2 %collective-permute-done.21.refs_1_ = f32[512,128]{1,0:T(8,128)S(1)} collective-permute-done((f32[512,128]{1,0:T(8,128)S(1)}, f32[512,128]{1,0:T(8,128)S(1)}, u32[]{:S(2)}, u32[]{:S(2)}) %collective-permute-start.21) | collective-permute-done | bytes 262176 | tf_op jit(solution)/shard_map/ppermute | solution.py:16
  275.1 9.5 %collective-permute-done.32 = f32[1,512,256]{2,1,0:T(8,128)} collective-permute-done((f32[1,512,256]{2,1,0:T(8,128)}, f32[1,512,256]{2,1,0:T(8,128)}, u32[]{:S(2)}, u32[]{:S(2)}) %collective-permute-start.32) | collective-permute-done | bytes 524320 | tf_op jit(solution)/shard_map/ppermute | solution.py:16
  295.0 7.2 %shard_map.86 = f32[2,512,128]{2,1,0:T(8,128)S(1)} custom-call(s32[3]{0:T(128)S(1)} %pad_add_fusion.1.place, f32[4,512,2048]{2,1,0:T(8,128)} %bitcast.285, f32[512,128]{1,0:T(8,128)S(1)} %slice.158.refs_0_, f32[512,128]{1,0:T(8,128)S(1)} %copy-done.21, f32[512,128]{1,0:T(8,128)S(1)} %copy-done.24, f32[512,128]{1,0:T(8,128)S(1)} %collective-permute-done.20.refs_3_), custom_call_target="tpu_custom_call" | custom-call | tf_op jit(solution)/shard_map/pallas_call | solution.py:47
  312.7 7.0 %shard_map.85 = f32[2,512,128]{2,1,0:T(8,128)S(1)} custom-call(s32[3]{0:T(128)S(1)} %pad_add_fusion.place, f32[4,512,2048]{2,1,0:T(8,128)} %bitcast.286, f32[512,128]{1,0:T(8,128)S(1)} %slice.158.refs_0_, f32[512,128]{1,0:T(8,128)S(1)} %copy-done.21, f32[512,128]{1,0:T(8,128)S(1)} %copy-done.24, f32[512,128]{1,0:T(8,128)S(1)} %collective-permute-done.20.refs_3_), custom_call_target="tpu_custom_call" | custom-call | tf_op jit(solution)/shard_map/pallas_call | solution.py:47
  327.2 7.0 %shard_map.88 = f32[2,512,128]{2,1,0:T(8,128)S(1)} custom-call(s32[3]{0:T(128)S(1)} %pad_add_fusion.1.place, f32[4,512,2048]{2,1,0:T(8,128)} %bitcast.287, f32[512,128]{1,0:T(8,128)S(1)} %slice.163.refs_0_, f32[512,128]{1,0:T(8,128)S(1)} %collective-permute-done.21.refs_1_, f32[512,128]{1,0:T(8,128)S(1)} %collective-permute-done.22.refs_2_, ...), custom_call_target="tpu_custom_call" | custom-call | tf_op jit(solution)/shard_map/pallas_call | solution.py:47
  334.3 7.3 %shard_map.87 = f32[2,512,128]{2,1,0:T(8,128)S(1)} custom-call(s32[3]{0:T(128)S(1)} %pad_add_fusion.place, f32[4,512,2048]{2,1,0:T(8,128)} %bitcast.288, f32[512,128]{1,0:T(8,128)S(1)} %slice.163.refs_0_, f32[512,128]{1,0:T(8,128)S(1)} %collective-permute-done.21.refs_1_, f32[512,128]{1,0:T(8,128)S(1)} %collective-permute-done.22.refs_2_, ...), custom_call_target="tpu_custom_call" | custom-call | tf_op jit(solution)/shard_map/pallas_call | solution.py:47
  358.2 4.4 %collective-permute-done.43 = f32[256,128]{0,1:T(8,128)S(1)} collective-permute-done((f32[256,128]{0,1:T(8,128)S(1)}, f32[256,128]{0,1:T(8,128)S(1)}, u32[]{:S(2)}, u32[]{:S(2)}) %collective-permute-start.43) | collective-permute-done | bytes 131104 | tf_op jit(solution)/shard_map/ppermute | solution.py:16
  367.5 4.4 %collective-permute-start.46 = (f32[128,128]{1,0:T(8,128)S(1)}, f32[128,128]{1,0:T(8,128)S(1)}, u32[]{:S(2)}, u32[]{:S(2)}) collective-permute-start(f32[128,128]{1,0:T(8,128)S(1)} %add.211), channel_id=1, source_target_pairs={{0,2},{1,3},{4,6},{5,7},{8,10},{9,11},{12,14},{13,15},{16,18},{17,... | collective-permute-start | bytes 196616 | tf_op jit(solution)/shard_map/ppermute | solution.py:98
  379.6 5.4 %collective-permute-start.48 = (f32[128,128]{1,0:T(8,128)S(1)}, f32[128,128]{1,0:T(8,128)S(1)}, u32[]{:S(2)}, u32[]{:S(2)}) collective-permute-start(f32[128,128]{1,0:T(8,128)S(1)} %add.213), channel_id=1, source_target_pairs={{0,8},{4,12},{1,9},{5,13},{2,10},{6,14},{3,11},{7,15},{16,24},{20,... | collective-permute-start | bytes 196616 | tf_op jit(solution)/shard_map/ppermute | solution.py:98
  (294 shorter events, 174.6 us)
Async XLA Ops:
  4.7 26.1 %collective-permute-start = (f32[512,256]{1,0:T(8,128)S(1)}, f32[512,256]{1,0:T(8,128)S(1)}, u32[]{:S(2)}, u32[]{:S(2)}) collective-permute-start(f32[512,256]{1,0:T(8,128)S(1)} %slice.198.refs_0_), channel_id=1, source_target_pairs={{0,4},{4,0},{8,12},{12,8},{1,5},{5,1},{9,13},{13,9},{2,6},{6,2},{1... | collective-permute-start | bytes 1572872 | tf_op jit(solution)/shard_map/ppermute | solution.py:16
  7.7 25.6 %collective-permute-start.1 = (f32[512,256]{1,0:T(8,128)S(1)}, f32[512,256]{1,0:T(8,128)S(1)}, u32[]{:S(2)}, u32[]{:S(2)}) collective-permute-start(f32[512,256]{1,0:T(8,128)S(1)} %slice.198.refs_0_), channel_id=1, source_target_pairs={{0,8},{4,12},{8,0},{12,4},{1,9},{5,13},{9,1},{13,5},{2,10},{6,14},... | collective-permute-start | bytes 1572872 | tf_op jit(solution)/shard_map/ppermute | solution.py:16
  16.5 24.6 %collective-permute-start.8 = (f32[128,128]{1,0:T(8,128)S(1)}, f32[128,128]{1,0:T(8,128)S(1)}, u32[]{:S(2)}, u32[]{:S(2)}) collective-permute-start(f32[128,128]{1,0:T(8,128)S(1)} %collective-permute-done.7), channel_id=1, source_target_pairs={{0,1},{1,0},{2,3},{3,2},{4,5},{5,4},{6,7},{7,6},{8,9},{9,8},{10,11... | collective-permute-start | bytes 196616 | tf_op jit(solution)/shard_map/ppermute | solution.py:16
  34.6 24.1 %collective-permute-start.3 = (f32[512,256]{1,0:T(8,128)S(1)}, f32[512,256]{1,0:T(8,128)S(1)}, u32[]{:S(2)}, u32[]{:S(2)}) collective-permute-start(f32[512,256]{1,0:T(8,128)S(1)} %slice.154.refs_0_), channel_id=1, source_target_pairs={{0,4},{4,0},{8,12},{12,8},{1,5},{5,1},{9,13},{13,9},{2,6},{6,2},{1... | collective-permute-start | bytes 1572872 | tf_op jit(solution)/shard_map/ppermute | solution.py:16
  35.1 38.2 %collective-permute-start.4 = (f32[512,256]{1,0:T(8,128)S(1)}, f32[512,256]{1,0:T(8,128)S(1)}, u32[]{:S(2)}, u32[]{:S(2)}) collective-permute-start(f32[512,256]{1,0:T(8,128)S(1)} %slice.154.refs_0_), channel_id=1, source_target_pairs={{0,8},{4,12},{8,0},{12,4},{1,9},{5,13},{9,1},{13,5},{2,10},{6,14},... | collective-permute-start | bytes 1572872 | tf_op jit(solution)/shard_map/ppermute | solution.py:16
  38.9 34.4 %collective-permute-start.5 = (f32[512,256]{1,0:T(8,128)S(1)}, f32[512,256]{1,0:T(8,128)S(1)}, u32[]{:S(2)}, u32[]{:S(2)}) collective-permute-start(f32[512,256]{1,0:T(8,128)S(1)} %slice.155), channel_id=1, source_target_pairs={{0,0},{1,4},{2,8},{3,12},{4,1},{5,5},{6,9},{7,13},{8,2},{9,6},{10,... | collective-permute-start | bytes 1572872 | tf_op jit(solution)/shard_map/ppermute | solution.py:133
  39.6 45.8 %collective-permute-start.2 = (f32[512,256]{1,0:T(8,128)S(1)}, f32[512,256]{1,0:T(8,128)S(1)}, u32[]{:S(2)}, u32[]{:S(2)}) collective-permute-start(f32[512,256]{1,0:T(8,128)S(1)} %collective-permute-done.1.refs_2_), channel_id=1, source_target_pairs={{0,4},{4,0},{8,12},{12,8},{1,5},{5,1},{9,13},{13,9},{2,6},{6,2},{1... | collective-permute-start | bytes 1572872 | tf_op jit(solution)/shard_map/ppermute | solution.py:16
  92.8 24.3 %collective-permute-start.10 = (f32[512,256]{1,0:T(8,128)S(1)}, f32[512,256]{1,0:T(8,128)S(1)}, u32[]{:S(2)}, u32[]{:S(2)}) collective-permute-start(f32[512,256]{1,0:T(8,128)S(1)} %slice.157.refs_0_), channel_id=1, source_target_pairs={{0,4},{4,0},{8,12},{12,8},{1,5},{5,1},{9,13},{13,9},{2,6},{6,2},{1... | collective-permute-start | bytes 1572872 | tf_op jit(solution)/shard_map/ppermute | solution.py:16
  92.9 26.7 %collective-permute-start.11 = (f32[512,256]{1,0:T(8,128)S(1)}, f32[512,256]{1,0:T(8,128)S(1)}, u32[]{:S(2)}, u32[]{:S(2)}) collective-permute-start(f32[512,256]{1,0:T(8,128)S(1)} %slice.157.refs_0_), channel_id=1, source_target_pairs={{0,8},{4,12},{8,0},{12,4},{1,9},{5,13},{9,1},{13,5},{2,10},{6,14},... | collective-permute-start | bytes 1572872 | tf_op jit(solution)/shard_map/ppermute | solution.py:16
  93.0 36.7 %collective-permute-start.9 = (f32[512,256]{1,0:T(8,128)S(1)}, f32[512,256]{1,0:T(8,128)S(1)}, u32[]{:S(2)}, u32[]{:S(2)}) collective-permute-start(f32[512,256]{1,0:T(8,128)S(1)} %collective-permute-done.4.refs_2_), channel_id=1, source_target_pairs={{0,4},{4,0},{8,12},{12,8},{1,5},{5,1},{9,13},{13,9},{2,6},{6,2},{1... | collective-permute-start | bytes 1572872 | tf_op jit(solution)/shard_map/ppermute | solution.py:16
  132.0 30.7 %collective-permute-start.18 = (f32[2,512,512]{2,1,0:T(8,128)}, f32[2,512,512]{2,1,0:T(8,128)}, u32[]{:S(2)}, u32[]{:S(2)}) collective-permute-start(f32[2,512,512]{2,1,0:T(8,128)} %pad_maximum_fusion), channel_id=1, source_target_pairs={{0,2},{5,7},{10,8},{15,13},{16,18},{21,23},{26,24},{31,29}} | collective-permute-start | bytes 6291464 | tf_op jit(solution)/shard_map/ppermute | solution.py:124
  145.8 41.8 %collective-permute-start.17 = (f32[2,512,256]{2,1,0:T(8,128)}, f32[2,512,256]{2,1,0:T(8,128)}, u32[]{:S(2)}, u32[]{:S(2)}) collective-permute-start(f32[2,512,256]{2,1,0:T(8,128)} %shard_map.82), channel_id=1, source_target_pairs={{0,1},{1,0},{2,3},{3,2},{4,5},{5,4},{6,7},{7,6},{8,9},{9,8},{10,11... | collective-permute-start | bytes 3145736 | tf_op jit(solution)/shard_map/ppermute | solution.py:16
  165.0 24.0 %collective-permute-start.19 = (f32[1,512,512]{2,1,0:T(8,128)}, f32[1,512,512]{2,1,0:T(8,128)}, u32[]{:S(2)}, u32[]{:S(2)}) collective-permute-start(f32[1,512,512]{2,1,0:T(8,128)} %slice_select_fusion), channel_id=1, source_target_pairs={{0,1},{2,3},{5,4},{7,6},{8,9},{10,11},{13,12},{15,14},{16,17},{18,... | collective-permute-start | bytes 3145736 | tf_op jit(solution)/shard_map/ppermute | solution.py:124
  168.1 15.6 %collective-permute-start.16 = (f32[1,512,256]{2,1,0:T(8,128)}, f32[1,512,256]{2,1,0:T(8,128)}, u32[]{:S(2)}, u32[]{:S(2)}) collective-permute-start(f32[1,512,256]{2,1,0:T(8,128)} %slice_bitcast_fusion.15), channel_id=1, source_target_pairs={{0,2},{1,3},{2,0},{3,1},{4,6},{5,7},{6,4},{7,5},{8,10},{9,11},{10,... | collective-permute-start | bytes 1572872 | tf_op jit(solution)/shard_map/ppermute | solution.py:16
  183.8 20.1 %collective-permute-start.13 = (f32[512,256]{1,0:T(8,128)S(1)}, f32[512,256]{1,0:T(8,128)S(1)}, u32[]{:S(2)}, u32[]{:S(2)}) collective-permute-start(f32[512,256]{1,0:T(8,128)S(1)} %copy-done.2), channel_id=1, source_target_pairs={{0,4},{4,0},{8,12},{12,8},{1,5},{5,1},{9,13},{13,9},{2,6},{6,2},{1... | collective-permute-start | bytes 1572872 | tf_op jit(solution)/shard_map/ppermute | solution.py:16
  208.8 26.1 %collective-permute-start.27 = (f32[2,512,256]{2,1,0:T(8,128)}, f32[2,512,256]{2,1,0:T(8,128)}, u32[]{:S(2)}, u32[]{:S(2)}) collective-permute-start(f32[2,512,256]{2,1,0:T(8,128)} %pad_maximum_fusion.3), channel_id=1, source_target_pairs={{0,2},{5,7},{10,8},{15,13},{16,18},{21,23},{26,24},{31,29}} | collective-permute-start | bytes 3145736 | tf_op jit(solution)/shard_map/ppermute | solution.py:124
  234.3 18.9 %collective-permute-start.26 = (f32[2,512,256]{2,1,0:T(8,128)S(1)}, f32[2,512,256]{2,1,0:T(8,128)S(1)}, u32[]{:S(2)}, u32[]{:S(2)}) collective-permute-start(f32[2,512,256]{2,1,0:T(8,128)S(1)} %shard_map.84), channel_id=1, source_target_pairs={{0,1},{1,0},{2,3},{3,2},{4,5},{5,4},{6,7},{7,6},{8,9},{9,8},{10,11... | collective-permute-start | bytes 3145736 | tf_op jit(solution)/shard_map/ppermute | solution.py:16
  236.0 18.2 %collective-permute-start.28 = (f32[1,512,256]{2,1,0:T(8,128)S(1)}, f32[1,512,256]{2,1,0:T(8,128)S(1)}, u32[]{:S(2)}, u32[]{:S(2)}) collective-permute-start(f32[1,512,256]{2,1,0:T(8,128)S(1)} %fusion.25), channel_id=1, source_target_pairs={{0,1},{2,3},{5,4},{7,6},{8,9},{10,11},{13,12},{15,14},{16,17},{18,... | collective-permute-start | bytes 1572872 | tf_op jit(solution)/shard_map/ppermute | solution.py:124
  238.1 15.4 %collective-permute-start.25 = (f32[1,512,128]{2,1,0:T(8,128)S(1)}, f32[1,512,128]{2,1,0:T(8,128)S(1)}, u32[]{:S(2)}, u32[]{:S(2)}) collective-permute-start(f32[1,512,128]{2,1,0:T(8,128)S(1)} %slice_bitcast_fusion.23), channel_id=1, source_target_pairs={{0,2},{1,3},{2,0},{3,1},{4,6},{5,7},{6,4},{7,5},{8,10},{9,11},{10,... | collective-permute-start | bytes 786440 | tf_op jit(solution)/shard_map/ppermute | solution.py:16
  247.1 15.7 %collective-permute-start.21 = (f32[512,128]{1,0:T(8,128)S(1)}, f32[512,128]{1,0:T(8,128)S(1)}, u32[]{:S(2)}, u32[]{:S(2)}) collective-permute-start(f32[512,128]{1,0:T(8,128)S(1)} %slice.163.refs_0_), channel_id=1, source_target_pairs={{0,4},{4,0},{8,12},{12,8},{1,5},{5,1},{9,13},{13,9},{2,6},{6,2},{1... | collective-permute-start | bytes 786440 | tf_op jit(solution)/shard_map/ppermute | solution.py:16
  251.3 15.5 %collective-permute-start.22 = (f32[512,128]{1,0:T(8,128)S(1)}, f32[512,128]{1,0:T(8,128)S(1)}, u32[]{:S(2)}, u32[]{:S(2)}) collective-permute-start(f32[512,128]{1,0:T(8,128)S(1)} %slice.163.refs_0_), channel_id=1, source_target_pairs={{0,8},{4,12},{8,0},{12,4},{1,9},{5,13},{9,1},{13,5},{2,10},{6,14},... | collective-permute-start | bytes 786440 | tf_op jit(solution)/shard_map/ppermute | solution.py:16
  253.2 16.3 %collective-permute-start.20 = (f32[512,128]{1,0:T(8,128)S(1)}, f32[512,128]{1,0:T(8,128)S(1)}, u32[]{:S(2)}, u32[]{:S(2)}) collective-permute-start(f32[512,128]{1,0:T(8,128)S(1)} %copy-done.23), channel_id=1, source_target_pairs={{0,4},{4,0},{8,12},{12,8},{1,5},{5,1},{9,13},{13,9},{2,6},{6,2},{1... | collective-permute-start | bytes 786440 | tf_op jit(solution)/shard_map/ppermute | solution.py:16
  270.4 14.3 %collective-permute-start.32 = (f32[1,512,256]{2,1,0:T(8,128)}, f32[1,512,256]{2,1,0:T(8,128)}, u32[]{:S(2)}, u32[]{:S(2)}) collective-permute-start(f32[1,512,256]{2,1,0:T(8,128)} %slice_bitcast_fusion.7), channel_id=1, source_target_pairs={{0,2},{1,3},{2,0},{3,1},{4,6},{5,7},{6,4},{7,5},{8,10},{9,11},{10,... | collective-permute-start | bytes 1572872 | tf_op jit(solution)/shard_map/ppermute | solution.py:16
  302.2 19.0 %collective-permute-start.35 = (f32[2,512,128]{2,1,0:T(8,128)S(1)}, f32[2,512,128]{2,1,0:T(8,128)}, u32[]{:S(2)}, u32[]{:S(2)}) collective-permute-start(f32[2,512,128]{2,1,0:T(8,128)S(1)} %shard_map.86), channel_id=1, source_target_pairs={{0,1},{1,0},{2,3},{3,2},{4,5},{5,4},{6,7},{7,6},{8,9},{9,8},{10,11... | collective-permute-start | bytes 1572872 | tf_op jit(solution)/shard_map/ppermute | solution.py:16
  (80 other events, 759.8 us)

commit v2 on v1

--- a/solution.py
+++ b/solution.py
@@ -21,42 +21,70 @@
     return high, (values - high.astype(jnp.float32)).astype(jnp.bfloat16)
 
 
-def product_kernel(place, tile_ref, *refs):
-    *block_refs, out_ref, high_ref, low_ref = refs
+def split_kernel(tile_ref, high_ref, low_ref):
+    high_ref[...], low_ref[...] = parts(tile_ref[...])
+
+
+def split(tile):
+    rows, width = tile.shape
+    step = min(rows, 256)
+    block = pl.BlockSpec((step, width), lambda t: (t, 0))
+    return pl.pallas_call(
+        split_kernel,
+        grid=(rows // step,),
+        in_specs=[block],
+        out_specs=[block, block],
+        out_shape=[jax.ShapeDtypeStruct(tile.shape, jnp.bfloat16)] * 2,
+        compiler_params=pltpu.CompilerParams(vmem_limit_bytes=40 * 2**20),
+    )(tile)
+
+
+def product_kernel(place, tile_high_ref, tile_low_ref, *refs):
+    *block_refs, send_ref, keep_ref, high_ref, low_ref = refs
     height = block_refs[0].shape[0]
-
-    @pl.when((pl.program_id(0) == 0) & (pl.program_id(1) == 0))
+    i = pl.program_id(0)
+
+    @pl.when(i == 0)
     def _():
         for j, block_ref in enumerate(block_refs):
             rows = pl.ds(pl.multiple_of((place[0] ^ j) * height, height), height)
             high_ref[rows], low_ref[rows] = parts(block_ref[...])
 
-    high, low = parts(tile_ref[0])
-    out_ref[0] = (jnp.dot(high, high_ref[...], preferred_element_type=jnp.float32)
-                  + (jnp.dot(high, low_ref[...], preferred_element_type=jnp.float32)
-                     + jnp.dot(low, high_ref[...], preferred_element_type=jnp.float32)))
-
-
-def product(tile, blocks, parity):
-    count, out_rows, width = tile.shape
+    def times(a_ref, b_ref):
+        return jnp.dot(a_ref[0], b_ref[...], preferred_element_type=jnp.float32)
+
+    result = times(tile_high_ref, high_ref) + (times(tile_high_ref, low_ref) + times(tile_low_ref, high_ref))
+
+    @pl.when(i < pl.num_programs(0) // 2)
+    def _():
+        send_ref[0] = result
+
+    @pl.when(i >= pl.num_programs(0) // 2)
+    def _():
+        keep_ref[0] = result
+
+
+def product(tiles, blocks):
+    count, out_rows, width = tiles[0].shape
     columns = blocks[0].shape[1]
-    step = min(out_rows, 256)
-    chunks = lax.axis_index("col") ^ (2 * jnp.arange(count // 2) + parity)
+    half = count // 2
+    chunks = lax.axis_index("col") ^ jnp.concatenate([2 * jnp.arange(half) + 1, 2 * jnp.arange(half)])
     place = jnp.concatenate([lax.axis_index("row")[None], chunks]).astype(jnp.int32)
-    whole = pl.BlockSpec(blocks[0].shape, lambda i, t, place: (0, 0))
+    whole = pl.BlockSpec(blocks[0].shape, lambda i, place: (0, 0))
+    rows = pl.BlockSpec((1, out_rows, width), lambda i, place: (place[1 + i], 0, 0))
     return pl.pallas_call(
         product_kernel,
         grid_spec=pltpu.PrefetchScalarGridSpec(
             num_scalar_prefetch=1,
-            grid=(count // 2, out_rows // step),
-            in_specs=[pl.BlockSpec((1, step, width), lambda i, t, place: (place[1 + i], t, 0))]
-            + [whole] * len(blocks),
-            out_specs=pl.BlockSpec((1, step, columns), lambda i, t, place: (i, t, 0)),
+            grid=(count,),
+            in_specs=[rows, rows] + [whole] * len(blocks),
+            out_specs=[pl.BlockSpec((1, out_rows, columns), lambda i, place: (jnp.minimum(i, half - 1), 0, 0)),
+                       pl.BlockSpec((1, out_rows, columns), lambda i, place: (jnp.maximum(i - half, 0), 0, 0))],
             scratch_shapes=[pltpu.VMEM((width, columns), jnp.bfloat16)] * 2,
         ),
-        out_shape=jax.ShapeDtypeStruct((count // 2, out_rows, columns), jnp.float32),
+        out_shape=[jax.ShapeDtypeStruct((half, out_rows, columns), jnp.float32)] * 2,
         compiler_params=pltpu.CompilerParams(vmem_limit_bytes=40 * 2**20),
-    )(place, tile, *blocks)
+    )(place, *tiles, *blocks)
 
 
 def dot(a, b, precision):
@@ -106,25 +134,26 @@
     return row * lax.axis_size("col") // lax.axis_size("row")
 
 
-def own_output_rows(blocks):
+def blocks_to_send(blocks):
     rows, cols = lax.axis_size("row"), lax.axis_size("col")
-    row_id, col_id = lax.axis_index("row"), lax.axis_index("col")
-    offset = col_id ^ source_col(row_id)
     held = []
     for d in range(cols):
         wanted = [((r * cols + (source_col(r) ^ d)) % rows) ^ r for r in range(rows)]
         if len(set(wanted)) == 1:
             held.append(blocks[wanted[0]])
         else:
-            held.append(lax.dynamic_index_in_dim(jnp.stack(blocks), jnp.array(wanted)[row_id], 0, keepdims=False))
-    bit = cols // 2
-    while bit >= 1:
-        pairs = [(r * cols + c, r * cols + (c ^ bit)) for r in range(rows) for c in range(cols)
-                 if (c ^ source_col(r)) % (2 * bit) == 0]
-        moved = lax.ppermute(jnp.stack(held[bit:]), ("row", "col"), pairs)
-        held = [jnp.where(offset & bit != 0, moved[j], held[j]) for j in range(bit)]
-        bit //= 2
-    return held[0]
+            held.append(lax.dynamic_index_in_dim(jnp.stack(blocks), jnp.array(wanted)[lax.axis_index("row")], 0, keepdims=False))
+    return held
+
+
+def spread_step(held):
+    rows, cols = lax.axis_size("row"), lax.axis_size("col")
+    bit = len(held) // 2
+    pairs = [(r * cols + c, r * cols + (c ^ bit)) for r in range(rows) for c in range(cols)
+             if (c ^ source_col(r)) % (2 * bit) == 0]
+    moved = lax.ppermute(jnp.stack(held[bit:]), ("row", "col"), pairs)
+    offset = lax.axis_index("col") ^ source_col(lax.axis_index("row"))
+    return [jnp.where(offset & bit != 0, moved[j], held[j]) for j in range(bit)]
 
 
 def own_output_rows_direct(block):
@@ -142,7 +171,7 @@
     tile_mask = jnp.repeat(ancestor_tiles, TILE, axis=2)
     kept_rows = lax.dynamic_slice_in_dim(tile_mask, row_start, local_rows, 2).astype(jnp.float32)
     masked = panels * kept_rows[..., None]
-    tile = inverse_tile.reshape(cols_axis, inverse_tile.shape[0] // cols_axis, -1)
+    tiles = [half.reshape(cols_axis, -1, half.shape[1]) for half in split(inverse_tile)]
 
     def by_cols(*terms):
         terms = jnp.concatenate([term.reshape(width, cols_axis, span).swapaxes(0, 1) for term in terms], axis=2)
@@ -152,7 +181,7 @@
         return by_xor(terms.reshape(rows_axis, height, -1), "row")
 
     def one_pair(first, panel_second, link, given_first, given_second):
-        live = {"first": first, "second": panel_second - dot(first, link, precise)}
+        live = {"tiles": tiles, "first": first, "second": panel_second - dot(first, link, precise)}
         slots = {}
 
         def at(slot, *steps):
@@ -178,18 +207,31 @@
             return [live[k, j] for j in range(rows_axis)]
 
         def multiply(k):
-            sent = swap(product(tile, blocks(k), 1), "col", 1)
-            live["sums", k] = product(tile, blocks(k), 0) + sent
-
-        def reduce(k):
+            live["send", k], live["keep", k] = product(live["tiles"], blocks(k))
+            if k >= count_early:
+                live["products", k] = jnp.concatenate([live["send", k], live["keep", k]]).reshape(-1, span)
+
+        def add_core(k):
+            live["sums", k] = live.pop(("keep", k)) + swap(live.pop(("send", k)), "col", 1)
+
+        def add_rest(k):
             live["out", k] = -sum_scatter(live.pop(("sums", k)), "col", 2)
 
-        def own(name, start, stop):
+        def collect(name, start, stop):
             groups = zip(*(blocks(k) for k in range(start, stop)))
-            live[name] = own_output_rows([jnp.concatenate(group, axis=1) for group in groups])
+            live[name] = blocks_to_send([jnp.concatenate(group, axis=1) for group in groups])
+            spread(name)
             for k in range(start, stop):
                 for j in range(rows_axis):
                     del live[k, j]
+
+        def spread(name):
+            live[name] = spread_step(live[name])
+
+        def own(name, slot, start, stop):
+            at(slot, lambda: collect(name, start, stop))
+            for step in range(1, cols_axis.bit_length() - 1):
+                at(slot + step, lambda: spread(name))
 
         def outs(start, stop):
             return jnp.concatenate([live["out", k] for k in range(start, stop)], axis=1)
@@ -213,14 +255,14 @@
 
         def first_terms():
             live["first_terms"] = sum_scatter(
-                by_cols(dot_tn(live["own_first"], outs(0, count_first), three_pass)), "col")
+                by_cols(dot_tn(live["own_first"][0], outs(0, count_first), three_pass)), "col")
 
         def first_sum():
             live["first_sum"] = sum_scatter(by_rows(live.pop("first_terms")), "row")
 
         def early_terms():
             out_early = outs(count_first, count_early)
-            own_second = jnp.concatenate([live["own_early"], live["own_last"]], axis=1)
+            own_second = jnp.concatenate([live["own_early"][0], live["own_last"]], axis=1)
             cross = dot_tn(outs(0, count_first), own_second, three_pass)
             early = jnp.concatenate([
                 dot_tn(own_second, out_early, three_pass),
@@ -233,33 +275,43 @@
             terms = terms.at[:, span:].add(-dot_tn(link_rows, live["given_link"], precise))
             live["early_sum"] = sum_scatter(by_rows(terms), "row")
 
+        def own_last_rows(bit):
+            rows = live.setdefault("last_rows", {0: live["own_last"]})
+            rows.update({j ^ bit: swap(block, "col", bit) for j, block in list(rows.items())})
+            if bit == 1:
+                order = [*range(1, cols_axis, 2), *range(0, cols_axis, 2)]
+                live["last_rows"] = jnp.concatenate([rows[j] for j in order])
+
         def last_terms(k):
             start = (k - count_early) * span
-            terms = dot_tn(live["own_last"][:, start:], live["out", k], three_pass)
+            terms = -dot_tn(live["last_rows"][:, start:], live["products", k], three_pass)
             count = cols_axis * terms.shape[1] // terms.shape[0]
             live["last", k] = sum_to_last(sum_to_last(terms, "col", count), "row", count)
 
         end = len(pieces) - 1 + stages
         for k in range(len(pieces)):
             at(k + stages, lambda k=k: multiply(k))
-            at(min(k + stages + 1, end), lambda k=k: reduce(k))
+            if k >= count_early:
+                at(end, lambda k=k: last_terms(k))
+            at(min(k + stages + 1, end), lambda k=k: add_core(k))
+            at(min(k + stages + 2, end), lambda k=k: add_rest(k))
             if k == 0:
                 at(1, own_last)
                 at(1, given_link)
+                for step in range(cols_axis.bit_length() - 1):
+                    at(2 + step, lambda bit=cols_axis >> (step + 1): own_last_rows(bit))
             if k == count_first - 1:
-                at(k + stages, lambda: own("own_first", 0, count_first))
-                at(k + stages + 1, first_terms)
-                at(k + stages + 2, first_sum)
+                own("own_first", k + stages, 0, count_first)
+                at(k + stages + 2, first_terms)
+                at(k + stages + 3, first_sum)
             if k == count_early - 1:
-                at(k + stages, lambda: own("own_early", count_first, count_early))
-                at(k + stages + 1, early_terms)
-                at(k + stages + 2, early_sum)
-            if k >= count_early:
-                at(end, lambda k=k: last_terms(k))
+                own("own_early", k + stages, count_first, count_early)
+                at(end, early_terms)
+                at(end, early_sum)
 
         for slot in range(end + 1):
             if slot > 0:
-                live = dict(zip(live, lax.optimization_barrier(tuple(live.values()))))
+                live = dict(zip(live, lax.optimization_barrier(list(live.values()))))
             for step in slots[slot]:
                 step()
 

time: 391 us -> 364 us (0.931)
  waiting for transfers between devices: 161 us -> 126 us
  local copies, waits for them, and re-layouts: 36.9 us -> 53.1 us
  other arithmetic: 34 us -> 45.2 us
  Pallas kernels: 73 us -> 62.7 us
  starting transfers between devices: 71.1 us -> 60.9 us
    pallas_call x10 -> x5, Pallas kernels: 73 us -> 51.4 us  [product(): pl.pallas_call(product_kernel, grid_spec=pltpu.PrefetchScalarGridSpec(num...]
    ppermute x4, waiting for transfers between devices: 16.9 us -> 0.01 us  [spread_step(): moved = lax.ppermute(jnp.stack(held[bit:]), ('row', 'col'), pairs)]
    unnamed x113 -> x145, local copies, waits for them, and re-layouts: 16.3 us -> 30.7 us
    pallas_call x0 -> x1, Pallas kernels: none -> 11.3 us  [split(): pl.pallas_call(split_kernel, grid=(rows // step,), in_specs=[block], out_...]
    ppermute x38 -> x41, waiting for transfers between devices: 136 us -> 126 us  [swap(): return lax.ppermute(block, axis, pairs)]
    ppermute x38 -> x41, starting transfers between devices: 40 us -> 31.3 us  [swap(): return lax.ppermute(block, axis, pairs)]
    ppermute x6, waiting for transfers between devices: 8.32 us -> 0.02 us  [sum_to_last(): lax.ppermute(block, axis, [(i, i ^ bit) for i in range(size) if not i & b...]
    select_n x3 -> x4, other arithmetic: 6.86 us -> 8.93 us  [spread_step(): return [jnp.where(offset & bit != 0, moved[j], held[j]) for j in range(bit)]]
  transfers between devices with their start and end apart: 49 -> 52, of which waited for: 27 -> 19; matrix products, arithmetic and copies ran while one was open for 13% -> 18% of each run, Pallas kernels for 13% -> 17%
where the time goes in v2:
time: 364 us; the launch traced here: 362 us
  waiting for transfers between devices  126 us (35%)
  Pallas kernels  62.7 us (17%)
  starting transfers between devices  60.9 us (17%)
  local copies, waits for them, and re-layouts  53.1 us (15%)
  other arithmetic  45.2 us (12%)
  matrix products  11.8 us (3%)
    ppermute x41, waiting for transfers between devices, swap(): return lax.ppermute(block, axis, pairs)  126 us
    pallas_call x5, Pallas kernels, product(): pl.pallas_call(product_kernel, grid_spec=pltpu.PrefetchScalarGridSpec(num...  51.4 us
    ppermute x41, starting transfers between devices, swap(): return lax.ppermute(block, axis, pairs)  31.3 us
    unnamed x145, local copies, waits for them, and re-layouts  30.7 us
    ppermute x6, starting transfers between devices, sum_to_last(): lax.ppermute(block, axis, [(i, i ^ bit) for i in range(size) if not i & b...  16.9 us
    pallas_call x1, Pallas kernels, split(): pl.pallas_call(split_kernel, grid=(rows // step,), in_specs=[block], out_...  11.3 us
    ppermute x4, starting transfers between devices, spread_step(): moved = lax.ppermute(jnp.stack(held[bit:]), ('row', 'col'), pairs)  11.2 us
    dot_general x8, matrix products, dot_tn(): return lax.dot_general(a, b, (((0,), (0,)), ((), ())), precision=precision)  8.97 us
  transfers between devices with their start and end apart: 52, of which 19 were waited for; matrix products, arithmetic and copies ran while one was open for 18% of the time, Pallas kernels for 17%

profile of v2, /device:TPU:0, one launch (start us, length us, event | category | flops | bytes accessed | tf_op | source)
XLA Modules:
  0.0 361.9 jit_solution(1033088530170494920)
XLA Ops:
  14.6 11.3 %shard_map.79 = (bf16[2048,2048]{1,0:T(8,128)(2,1)S(1)}, bf16[2048,2048]{1,0:T(8,128)(2,1)}) custom-call(f32[2048,2048]{1,0:T(8,128)} %tile_ref.1), custom_call_target="tpu_custom_call" | custom-call | tf_op jit(solution)/shard_map/pallas_call | solution.py:32
  41.7 16.8 %collective-permute-done.3.refs_1_ = f32[512,256]{1,0:T(8,128)S(1)} collective-permute-done((f32[512,256]{1,0:T(8,128)S(1)}, f32[512,256]{1,0:T(8,128)S(1)}, u32[]{:S(2)}, u32[]{:S(2)}) %collective-permute-start.3) | collective-permute-done | bytes 524320 | tf_op jit(solution)/shard_map/ppermute | solution.py:16
  59.2 14.5 %collective-permute-done.4.refs_2_ = f32[512,256]{1,0:T(8,128)S(1)} collective-permute-done((f32[512,256]{1,0:T(8,128)S(1)}, f32[512,256]{1,0:T(8,128)S(1)}, u32[]{:S(2)}, u32[]{:S(2)}) %collective-permute-start.4) | collective-permute-done | bytes 524320 | tf_op jit(solution)/shard_map/ppermute | solution.py:16
  73.7 21.9 %collective-permute-done.2.refs_3_ = f32[512,256]{1,0:T(8,128)S(1)} collective-permute-done((f32[512,256]{1,0:T(8,128)S(1)}, f32[512,256]{1,0:T(8,128)S(1)}, u32[]{:S(2)}, u32[]{:S(2)}) %collective-permute-start.2) | collective-permute-done | bytes 524320 | tf_op jit(solution)/shard_map/ppermute | solution.py:16
  98.0 3.4 copy-done.2
  101.3 10.8 %shard_map.80 = (f32[2,512,256]{2,1,0:T(8,128)}, f32[2,512,256]{2,1,0:T(8,128)S(1)}) custom-call(s32[5]{0:T(128)S(1)} %pad_add_fusion.place, bf16[4,512,2048]{2,1,0:T(8,128)(2,1)S(1)} %bitcast.274, bf16[4,512,2048]{2,1,0:T(8,128)(2,1)} %bitcast.281, f32[512,256]{1,0:T(8,128)S(1)} %slice.198.refs_0_, f32[512,256]{1,0:T(8,128)S(1)} %collective-permute-done.refs_1_, ...), custom_call_target="tpu_custom_call" | custom-call | tf_op jit(solution)/shard_map/pallas_call | solution.py:75
  113.9 5.6 %collective-permute-done.9.refs_3_ = f32[512,256]{1,0:T(8,128)S(1)} collective-permute-done((f32[512,256]{1,0:T(8,128)S(1)}, f32[512,256]{1,0:T(8,128)S(1)}, u32[]{:S(2)}, u32[]{:S(2)}) %collective-permute-start.9) | collective-permute-done | bytes 524320 | tf_op jit(solution)/shard_map/ppermute | solution.py:16
  132.5 10.7 %shard_map.81 = (f32[2,512,256]{2,1,0:T(8,128)}, f32[2,512,256]{2,1,0:T(8,128)S(1)}) custom-call(s32[5]{0:T(128)S(1)} %pad_add_fusion.place, bf16[4,512,2048]{2,1,0:T(8,128)(2,1)S(1)} %bitcast.275, bf16[4,512,2048]{2,1,0:T(8,128)(2,1)} %bitcast.282, f32[512,256]{1,0:T(8,128)S(1)} %slice.154.refs_0_, f32[512,256]{1,0:T(8,128)S(1)} %copy-done.7, ...), custom_call_target="tpu_custom_call" | custom-call | tf_op jit(solution)/shard_map/pallas_call | solution.py:75
  149.8 3.7 %fusion.2 = (f32[512,512]{1,0:T(8,128)}, f32[512,512]{1,0:T(8,128)}) fusion(f32[2,512,512]{2,1,0:T(8,128)} %collective-permute-done.19, f32[512,256]{1,0:T(8,128)S(1)} %copy-done.7, f32[512,256]{1,0:T(8,128)S(1)} %collective-permute-done.refs_1_, pred[]{:T(512)S(6)} %ne.26, f32[512,256]{1,0:T(8,128)S(1)} %slice.154.refs_0_, f32[512,256]{1,0:T(8,128)S(1)} %slice.198.refs_0_), kind=kLoop, calls=%fused_computation.23 | loop fusion | flops 1048576 | bytes 6291457 | tf_op jit(solution)/shard_map/jit(_where)/select_n | solution.py:156
  153.5 5.2 %collective-permute-done.17.refs_2_ = f32[512,128]{1,0:T(8,128)S(1)} collective-permute-done((f32[512,128]{1,0:T(8,128)S(1)}, f32[512,128]{1,0:T(8,128)S(1)}, u32[]{:S(2)}, u32[]{:S(2)}) %collective-permute-start.17) | collective-permute-done | bytes 262176 | tf_op jit(solution)/shard_map/ppermute | solution.py:16
  158.7 4.7 %collective-permute-done.15.refs_3_ = f32[512,256]{1,0:T(8,128)S(1)} collective-permute-done((f32[512,256]{1,0:T(8,128)S(1)}, f32[512,256]{1,0:T(8,128)S(1)}, u32[]{:S(2)}, u32[]{:S(2)}) %collective-permute-start.15) | collective-permute-done | bytes 524320 | tf_op jit(solution)/shard_map/ppermute | solution.py:16
  163.4 3.4 collective-permute-start.20
  179.2 10.7 %shard_map.82 = (f32[2,512,256]{2,1,0:T(8,128)}, f32[2,512,256]{2,1,0:T(8,128)S(1)}) custom-call(s32[5]{0:T(128)S(1)} %pad_add_fusion.place, bf16[4,512,2048]{2,1,0:T(8,128)(2,1)S(1)} %bitcast.276, bf16[4,512,2048]{2,1,0:T(8,128)(2,1)} %bitcast.283, f32[512,256]{1,0:T(8,128)S(1)} %slice.157.refs_0_, f32[512,256]{1,0:T(8,128)S(1)} %copy-done.9, ...), custom_call_target="tpu_custom_call" | custom-call | tf_op jit(solution)/shard_map/pallas_call | solution.py:75
  200.2 4.8 %collective-permute-done.23.refs_2_ = f32[512,128]{1,0:T(8,128)} collective-permute-done((f32[512,128]{1,0:T(8,128)S(1)}, f32[512,128]{1,0:T(8,128)}, u32[]{:S(2)}, u32[]{:S(2)}) %collective-permute-start.23) | collective-permute-done | bytes 262176 | tf_op jit(solution)/shard_map/ppermute | solution.py:16
  209.8 12.2 %collective-permute-done.29 = f32[1,512,256]{2,1,0:T(8,128)} collective-permute-done((f32[1,512,256]{2,1,0:T(8,128)}, f32[1,512,256]{2,1,0:T(8,128)}, u32[]{:S(2)}, u32[]{:S(2)}) %collective-permute-start.29) | collective-permute-done | bytes 524320 | tf_op jit(solution)/shard_map/ppermute | solution.py:16
  236.2 9.6 %shard_map.83 = (f32[2,512,128]{2,1,0:T(8,128)S(1)}, f32[2,512,128]{2,1,0:T(8,128)S(1)}) custom-call(s32[5]{0:T(128)S(1)} %pad_add_fusion.place, bf16[4,512,2048]{2,1,0:T(8,128)(2,1)S(1)} %bitcast.277, bf16[4,512,2048]{2,1,0:T(8,128)(2,1)} %bitcast.284, f32[512,128]{1,0:T(8,128)S(1)} %slice.158.refs_0_, f32[512,128]{1,0:T(8,128)S(1)} %copy-done.30, ...), custom_call_target="tpu_custom_call" | custom-call | tf_op jit(solution)/shard_map/pallas_call | solution.py:75
  251.8 4.6 %collective-permute-done.31 = f32[1,512,128]{2,1,0:T(8,128)S(1)} collective-permute-done((f32[1,512,128]{2,1,0:T(8,128)S(1)}, f32[1,512,128]{2,1,0:T(8,128)S(1)}, u32[]{:S(2)}, u32[]{:S(2)}) %collective-permute-start.31) | collective-permute-done | bytes 262176 | tf_op jit(solution)/shard_map/ppermute | solution.py:16
  260.2 9.6 %shard_map.84 = (f32[2,512,128]{2,1,0:T(8,128)S(1)}, f32[2,512,128]{2,1,0:T(8,128)S(1)}) custom-call(s32[5]{0:T(128)S(1)} %pad_add_fusion.place, bf16[4,512,2048]{2,1,0:T(8,128)(2,1)S(1)} %bitcast.278, bf16[4,512,2048]{2,1,0:T(8,128)(2,1)} %bitcast.285, f32[512,128]{1,0:T(8,128)S(1)} %slice.161.refs_0_, f32[512,128]{1,0:T(8,128)S(1)} %copy-done.32, ...), custom_call_target="tpu_custom_call" | custom-call | tf_op jit(solution)/shard_map/pallas_call | solution.py:75
  308.1 4.8 %collective-permute-start.51 = (f32[128,128]{1,0:T(8,128)S(1)}, f32[128,128]{1,0:T(8,128)S(1)}, u32[]{:S(2)}, u32[]{:S(2)}) collective-permute-start(f32[128,128]{1,0:T(8,128)S(1)} %add.213), channel_id=1, source_target_pairs={{0,8},{4,12},{1,9},{5,13},{2,10},{6,14},{3,11},{7,15},{16,24},{20,... | collective-permute-start | bytes 196616 | tf_op jit(solution)/shard_map/ppermute | solution.py:126
  315.5 3.6 collective-permute-done.46
  328.5 3.6 %collective-permute-done.35 = f32[1,512,128]{2,1,0:T(8,128)} collective-permute-done((f32[1,512,128]{2,1,0:T(8,128)}, f32[1,512,128]{2,1,0:T(8,128)}, u32[]{:S(2)}, u32[]{:S(2)}) %collective-permute-start.35) | collective-permute-done | bytes 262176 | tf_op jit(solution)/shard_map/ppermute | solution.py:16
  333.1 10.2 %collective-permute-done.41 = f32[1,512,256]{2,1,0:T(8,128)} collective-permute-done((f32[1,512,256]{2,1,0:T(8,128)}, f32[1,512,256]{2,1,0:T(8,128)}, u32[]{:S(2)}, u32[]{:S(2)}) %collective-permute-start.41) | collective-permute-done | bytes 524320 | tf_op jit(solution)/shard_map/ppermute | solution.py:16
  346.9 6.1 %collective-permute-done.42 = f32[2,128,256]{2,1,0:T(8,128)S(1)} collective-permute-done((f32[2,128,256]{2,1,0:T(8,128)S(1)}, f32[2,128,256]{2,1,0:T(8,128)S(1)}, u32[]{:S(2)}, u32[]{:S(2)}) %collective-permute-start.42) | collective-permute-done | bytes 262176 | tf_op jit(solution)/shard_map/ppermute | solution.py:16
  354.6 5.7 %collective-permute-done.43 = f32[1,128,256]{2,1,0:T(8,128)S(1)} collective-permute-done((f32[1,128,256]{2,1,0:T(8,128)S(1)}, f32[1,128,256]{2,1,0:T(8,128)S(1)}, u32[]{:S(2)}, u32[]{:S(2)}) %collective-permute-start.43) | collective-permute-done | bytes 131104 | tf_op jit(solution)/shard_map/ppermute | solution.py:16
  (331 shorter events, 162.5 us)
Async XLA Ops:
  4.4 26.1 %collective-permute-start = (f32[512,256]{1,0:T(8,128)S(1)}, f32[512,256]{1,0:T(8,128)S(1)}, u32[]{:S(2)}, u32[]{:S(2)}) collective-permute-start(f32[512,256]{1,0:T(8,128)S(1)} %slice.198.refs_0_), channel_id=1, source_target_pairs={{0,4},{4,0},{8,12},{12,8},{1,5},{5,1},{9,13},{13,9},{2,6},{6,2},{1... | collective-permute-start | bytes 1572872 | tf_op jit(solution)/shard_map/ppermute | solution.py:16
  7.5 25.6 %collective-permute-start.1 = (f32[512,256]{1,0:T(8,128)S(1)}, f32[512,256]{1,0:T(8,128)S(1)}, u32[]{:S(2)}, u32[]{:S(2)}) collective-permute-start(f32[512,256]{1,0:T(8,128)S(1)} %slice.198.refs_0_), channel_id=1, source_target_pairs={{0,8},{4,12},{8,0},{12,4},{1,9},{5,13},{9,1},{13,5},{2,10},{6,14},... | collective-permute-start | bytes 1572872 | tf_op jit(solution)/shard_map/ppermute | solution.py:16
  35.0 23.5 %collective-permute-start.3 = (f32[512,256]{1,0:T(8,128)S(1)}, f32[512,256]{1,0:T(8,128)S(1)}, u32[]{:S(2)}, u32[]{:S(2)}) collective-permute-start(f32[512,256]{1,0:T(8,128)S(1)} %slice.154.refs_0_), channel_id=1, source_target_pairs={{0,4},{4,0},{8,12},{12,8},{1,5},{5,1},{9,13},{13,9},{2,6},{6,2},{1... | collective-permute-start | bytes 1572872 | tf_op jit(solution)/shard_map/ppermute | solution.py:16
  35.5 38.2 %collective-permute-start.4 = (f32[512,256]{1,0:T(8,128)S(1)}, f32[512,256]{1,0:T(8,128)S(1)}, u32[]{:S(2)}, u32[]{:S(2)}) collective-permute-start(f32[512,256]{1,0:T(8,128)S(1)} %slice.154.refs_0_), channel_id=1, source_target_pairs={{0,8},{4,12},{8,0},{12,4},{1,9},{5,13},{9,1},{13,5},{2,10},{6,14},... | collective-permute-start | bytes 1572872 | tf_op jit(solution)/shard_map/ppermute | solution.py:16
  39.2 34.6 %collective-permute-start.5 = (f32[512,256]{1,0:T(8,128)S(1)}, f32[512,256]{1,0:T(8,128)}, u32[]{:S(2)}, u32[]{:S(2)}) collective-permute-start(f32[512,256]{1,0:T(8,128)S(1)} %slice.155), channel_id=1, source_target_pairs={{0,0},{1,4},{2,8},{3,12},{4,1},{5,5},{6,9},{7,13},{8,2},{9,6},{10,... | collective-permute-start | bytes 1572872 | tf_op jit(solution)/shard_map/ppermute | solution.py:162
  40.6 55.0 %collective-permute-start.2 = (f32[512,256]{1,0:T(8,128)S(1)}, f32[512,256]{1,0:T(8,128)S(1)}, u32[]{:S(2)}, u32[]{:S(2)}) collective-permute-start(f32[512,256]{1,0:T(8,128)S(1)} %copy-done.14), channel_id=1, source_target_pairs={{0,4},{4,0},{8,12},{12,8},{1,5},{5,1},{9,13},{13,9},{2,6},{6,2},{1... | collective-permute-start | bytes 1572872 | tf_op jit(solution)/shard_map/ppermute | solution.py:16
  95.9 23.6 %collective-permute-start.9 = (f32[512,256]{1,0:T(8,128)S(1)}, f32[512,256]{1,0:T(8,128)S(1)}, u32[]{:S(2)}, u32[]{:S(2)}) collective-permute-start(f32[512,256]{1,0:T(8,128)S(1)} %collective-permute-done.4.refs_2_), channel_id=1, source_target_pairs={{0,4},{4,0},{8,12},{12,8},{1,5},{5,1},{9,13},{13,9},{2,6},{6,2},{1... | collective-permute-start | bytes 1572872 | tf_op jit(solution)/shard_map/ppermute | solution.py:16
  121.8 28.0 %collective-permute-start.19 = (f32[2,512,512]{2,1,0:T(8,128)}, f32[2,512,512]{2,1,0:T(8,128)}, u32[]{:S(2)}, u32[]{:S(2)}) collective-permute-start(f32[2,512,512]{2,1,0:T(8,128)} %pad_maximum_fusion.1), channel_id=1, source_target_pairs={{0,2},{5,7},{10,8},{15,13},{16,18},{21,23},{26,24},{31,29}} | collective-permute-start | bytes 6291464 | tf_op jit(solution)/shard_map/ppermute | solution.py:154
  124.5 24.0 %collective-permute-start.18 = (f32[2,512,256]{2,1,0:T(8,128)}, f32[2,512,256]{2,1,0:T(8,128)}, u32[]{:S(2)}, u32[]{:S(2)}) collective-permute-start(f32[2,512,256]{2,1,0:T(8,128)} %get-tuple-element.154), channel_id=1, source_target_pairs={{0,1},{1,0},{2,3},{3,2},{4,5},{5,4},{6,7},{7,6},{8,9},{9,8},{10,11... | collective-permute-start | bytes 3145736 | tf_op jit(solution)/shard_map/ppermute | solution.py:16
  126.0 27.6 %collective-permute-start.16 = (f32[512,128]{1,0:T(8,128)S(1)}, f32[512,128]{1,0:T(8,128)S(1)}, u32[]{:S(2)}, u32[]{:S(2)}) collective-permute-start(f32[512,128]{1,0:T(8,128)S(1)} %slice.158.refs_0_), channel_id=1, source_target_pairs={{0,4},{4,0},{8,12},{12,8},{1,5},{5,1},{9,13},{13,9},{2,6},{6,2},{1... | collective-permute-start | bytes 786440 | tf_op jit(solution)/shard_map/ppermute | solution.py:16
  143.4 20.0 %collective-permute-start.15 = (f32[512,256]{1,0:T(8,128)S(1)}, f32[512,256]{1,0:T(8,128)S(1)}, u32[]{:S(2)}, u32[]{:S(2)}) collective-permute-start(f32[512,256]{1,0:T(8,128)S(1)} %copy-done.11), channel_id=1, source_target_pairs={{0,4},{4,0},{8,12},{12,8},{1,5},{5,1},{9,13},{13,9},{2,6},{6,2},{1... | collective-permute-start | bytes 1572872 | tf_op jit(solution)/shard_map/ppermute | solution.py:16
  163.4 28.1 %collective-permute-start.25 = (f32[2,512,256]{2,1,0:T(8,128)}, f32[2,512,256]{2,1,0:T(8,128)}, u32[]{:S(2)}, u32[]{:S(2)}) collective-permute-start(f32[2,512,256]{2,1,0:T(8,128)} %get-tuple-element.178), channel_id=1, source_target_pairs={{0,1},{1,0},{2,3},{3,2},{4,5},{5,4},{6,7},{7,6},{8,9},{9,8},{10,11... | collective-permute-start | bytes 3145736 | tf_op jit(solution)/shard_map/ppermute | solution.py:16
  163.4 31.6 %collective-permute-start.20 = (f32[1,512,512]{2,1,0:T(8,128)}, f32[1,512,512]{2,1,0:T(8,128)}, u32[]{:S(2)}, u32[]{:S(2)}) collective-permute-start(f32[1,512,512]{2,1,0:T(8,128)} %bitcast.17), channel_id=1, source_target_pairs={{0,1},{2,3},{5,4},{7,6},{8,9},{10,11},{13,12},{15,14},{16,17},{18,... | collective-permute-start | bytes 3145736 | tf_op jit(solution)/shard_map/ppermute | solution.py:154
  167.7 22.2 %collective-permute-start.24 = (f32[1,512,256]{2,1,0:T(8,128)}, f32[1,512,256]{2,1,0:T(8,128)}, u32[]{:S(2)}, u32[]{:S(2)}) collective-permute-start(f32[1,512,256]{2,1,0:T(8,128)} %slice_bitcast_fusion.16), channel_id=1, source_target_pairs={{0,2},{1,3},{2,0},{3,1},{4,6},{5,7},{6,4},{7,5},{8,10},{9,11},{10,... | collective-permute-start | bytes 1572872 | tf_op jit(solution)/shard_map/ppermute | solution.py:16
  170.4 27.4 %collective-permute-start.26 = (f32[2,512,256]{2,1,0:T(8,128)}, f32[2,512,256]{2,1,0:T(8,128)}, u32[]{:S(2)}, u32[]{:S(2)}) collective-permute-start(f32[2,512,256]{2,1,0:T(8,128)} %pad_maximum_fusion.3), channel_id=1, source_target_pairs={{0,2},{5,7},{10,8},{15,13},{16,18},{21,23},{26,24},{31,29}} | collective-permute-start | bytes 3145736 | tf_op jit(solution)/shard_map/ppermute | solution.py:154
  174.7 25.6 %collective-permute-start.22 = (f32[512,128]{1,0:T(8,128)S(1)}, f32[512,128]{1,0:T(8,128)S(1)}, u32[]{:S(2)}, u32[]{:S(2)}) collective-permute-start(f32[512,128]{1,0:T(8,128)S(1)} %slice.161.refs_0_), channel_id=1, source_target_pairs={{0,4},{4,0},{8,12},{12,8},{1,5},{5,1},{9,13},{13,9},{2,6},{6,2},{1... | collective-permute-start | bytes 786440 | tf_op jit(solution)/shard_map/ppermute | solution.py:16
  230.3 20.0 %collective-permute-start.32 = (f32[2,512,256]{2,1,0:T(8,128)}, f32[2,512,256]{2,1,0:T(8,128)}, u32[]{:S(2)}, u32[]{:S(2)}) collective-permute-start(f32[2,512,256]{2,1,0:T(8,128)} %get-tuple-element.203), channel_id=1, source_target_pairs={{0,1},{1,0},{2,3},{3,2},{4,5},{5,4},{6,7},{7,6},{8,9},{9,8},{10,11... | collective-permute-start | bytes 3145736 | tf_op jit(solution)/shard_map/ppermute | solution.py:16
  230.8 19.4 %collective-permute-start.27 = (f32[1,512,256]{2,1,0:T(8,128)}, f32[1,512,256]{2,1,0:T(8,128)S(1)}, u32[]{:S(2)}, u32[]{:S(2)}) collective-permute-start(f32[1,512,256]{2,1,0:T(8,128)} %bitcast.315), channel_id=1, source_target_pairs={{0,1},{2,3},{5,4},{7,6},{8,9},{10,11},{13,12},{15,14},{16,17},{18,... | collective-permute-start | bytes 1572872 | tf_op jit(solution)/shard_map/ppermute | solution.py:154
  232.8 23.7 %collective-permute-start.28 = (f32[512,128]{1,0:T(8,128)}, f32[512,128]{1,0:T(8,128)S(1)}, u32[]{:S(2)}, u32[]{:S(2)}) collective-permute-start(f32[512,128]{1,0:T(8,128)} %collective-permute-done.23.refs_2_), channel_id=1, source_target_pairs={{0,4},{4,0},{8,12},{12,8},{1,5},{5,1},{9,13},{13,9},{2,6},{6,2},{1... | collective-permute-start | bytes 786440 | tf_op jit(solution)/shard_map/ppermute | solution.py:16
  257.2 29.6 %collective-permute-start.38 = (f32[2,128,128]{2,1,0:T(8,128)}, f32[2,128,128]{2,1,0:T(8,128)}, u32[]{:S(2)}, u32[]{:S(2)}) collective-permute-start(f32[2,128,128]{2,1,0:T(8,128)} %slice_bitcast_fusion.29), channel_id=1, source_target_pairs={{0,4},{4,0},{8,12},{12,8},{1,5},{5,1},{9,13},{13,9},{2,6},{6,2},{1... | collective-permute-start | bytes 393224 | tf_op jit(solution)/shard_map/ppermute | solution.py:16
  260.2 28.2 %collective-permute-start.44 = (f32[256,128]{0,1:T(8,128)}, f32[256,128]{0,1:T(8,128)}, u32[]{:S(2)}, u32[]{:S(2)}) collective-permute-start(f32[256,128]{0,1:T(8,128)} %convolution_negate_fusion.1), channel_id=1, source_target_pairs={{0,1},{1,0},{2,3},{3,2},{4,5},{5,4},{6,7},{7,6},{8,9},{9,8},{10,11... | collective-permute-start | bytes 393224 | tf_op jit(solution)/shard_map/ppermute | solution.py:16
  275.0 20.3 %collective-permute-start.33 = (f32[1,512,256]{2,1,0:T(8,128)}, f32[1,512,256]{2,1,0:T(8,128)}, u32[]{:S(2)}, u32[]{:S(2)}) collective-permute-start(f32[1,512,256]{2,1,0:T(8,128)} %slice_bitcast_fusion.8), channel_id=1, source_target_pairs={{0,2},{1,3},{2,0},{3,1},{4,6},{5,7},{6,4},{7,5},{8,10},{9,11},{10,... | collective-permute-start | bytes 1572872 | tf_op jit(solution)/shard_map/ppermute | solution.py:16
  283.7 37.0 %collective-permute-start.34 = (f32[2,512,128]{2,1,0:T(8,128)S(1)}, f32[2,512,128]{2,1,0:T(8,128)}, u32[]{:S(2)}, u32[]{:S(2)}) collective-permute-start(f32[2,512,128]{2,1,0:T(8,128)S(1)} %copy-done.28), channel_id=1, source_target_pairs={{0,1},{1,0},{2,3},{3,2},{4,5},{5,4},{6,7},{7,6},{8,9},{9,8},{10,11... | collective-permute-start | bytes 1572872 | tf_op jit(solution)/shard_map/ppermute | solution.py:16
  288.4 25.4 %collective-permute-start.39 = (f32[1,128,128]{2,1,0:T(8,128)}, f32[1,128,128]{2,1,0:T(8,128)}, u32[]{:S(2)}, u32[]{:S(2)}) collective-permute-start(f32[1,128,128]{2,1,0:T(8,128)} %slice_bitcast_fusion.32), channel_id=1, source_target_pairs={{0,8},{4,12},{8,0},{12,4},{1,9},{5,13},{9,1},{13,5},{2,10},{6,14},... | collective-permute-start | bytes 196616 | tf_op jit(solution)/shard_map/ppermute | solution.py:16
  (98 other events, 964.6 us)

commit v3 on v2

v3 whole, which is shorter than its diff:
```python
import jax
import jax.numpy as jnp
from jax import lax
from jax.experimental import pallas as pl
from jax.experimental.pallas import tpu as pltpu
from jax.sharding import PartitionSpec as P

TILE = 128

precise = lax.Precision.HIGHEST
three_pass = lax.Precision.HIGH


def swap(block, axis, bit):
    pairs = [(i, i ^ bit) for i in range(lax.axis_size(axis))]
    return lax.ppermute(block, axis, pairs)


def parts(values):
    high = values.astype(jnp.bfloat16)
    return high, (values - high.astype(jnp.float32)).astype(jnp.bfloat16)


def split_kernel(tile_ref, high_ref, low_ref):
    high_ref[...], low_ref[...] = parts(tile_ref[...])


def split(tile):
    rows, width = tile.shape
    step = min(rows, 256)
    block = pl.BlockSpec((step, width), lambda t: (t, 0))
    return pl.pallas_call(
        split_kernel,
        grid=(rows // step,),
        in_specs=[block],
        out_specs=[block, block],
        out_shape=[jax.ShapeDtypeStruct(tile.shape, jnp.bfloat16)] * 2,
        compiler_params=pltpu.CompilerParams(vmem_limit_bytes=40 * 2**20),
    )(tile)


def product_kernel(place, tile_high_ref, tile_low_ref, *refs):
    *block_refs, send_ref, keep_ref, high_ref, low_ref = refs
    height = block_refs[0].shape[0]
    half = send_ref.shape[0]
    for j, block_ref in enumerate(block_refs):
        rows = pl.ds(pl.multiple_of((place[0] ^ j) * height, height), height)
        high_ref[rows], low_ref[rows] = parts(block_ref[...])

    def times(a, b_ref):
        return jnp.dot(a, b_ref[...], preferred_element_type=jnp.float32)

    for first, out_ref in ((1, send_ref), (1 + half, keep_ref)):
        def step(i, carry):
            chunk = place[first + i]
            high, low = tile_high_ref[chunk], tile_low_ref[chunk]
            out_ref[i] = times(high, high_ref) + (times(high, low_ref) + times(low, high_ref))
            return carry

        lax.fori_loop(0, half, step, 0)


def product(tiles, blocks):
    count, out_rows, width = tiles[0].shape
    columns = blocks[0].shape[1]
    half = count // 2
    chunks = lax.axis_index("col") ^ jnp.concatenate([2 * jnp.arange(half) + 1, 2 * jnp.arange(half)])
    place = jnp.concatenate([lax.axis_index("row")[None], chunks]).astype(jnp.int32)
    vmem = pl.BlockSpec(memory_space=pltpu.VMEM)
    return pl.pallas_call(
        product_kernel,
        in_specs=[pl.BlockSpec(memory_space=pltpu.SMEM)] + [vmem] * (2 + len(blocks)),
        out_specs=[vmem, vmem],
        out_shape=[jax.ShapeDtypeStruct((half, out_rows, columns), jnp.float32)] * 2,
        scratch_shapes=[pltpu.VMEM((width, columns), jnp.bfloat16)] * 2,
        compiler_params=pltpu.CompilerParams(vmem_limit_bytes=40 * 2**20),
    )(place, *tiles, *blocks)


def dot(a, b, precision):
    return jnp.matmul(a, b, precision=precision)


def dot_tn(a, b, precision):
    return lax.dot_general(a, b, (((0,), (0,)), ((), ())), precision=precision)


def sum_scatter(blocks, axis, bit=1):
    while blocks.shape[0] > 1:
        pairs = blocks.reshape((blocks.shape[0] // 2, 2) + blocks.shape[1:])
        blocks = pairs[:, 0] + swap(pairs[:, 1], axis, bit)
        bit *= 2
    return blocks[0]


def sum_rows(blocks, axis):
    bit = 1
    while blocks.shape[0] > 1:
        mine = lax.axis_index(axis) // bit % 2
        pairs = blocks.reshape((blocks.shape[0] // 2, 2) + blocks.shape[1:])
        keep = lax.dynamic_index_in_dim(pairs, mine, 1, keepdims=False)
        blocks = keep + swap(lax.dynamic_index_in_dim(pairs, 1 - mine, 1, keepdims=False), axis, bit)
        bit *= 2
    return blocks[0]


def columns_by_xor(array, odd):
    cols, col_id = lax.axis_size("col"), lax.axis_index("col")
    span = array.shape[1] // cols
    return [lax.dynamic_slice_in_dim(array, (col_id ^ j) * span, span, 1) for j in range(odd, cols, 2)]


def source_col(row):
    return row * lax.axis_size("col") // lax.axis_size("row")


def blocks_to_send(blocks):
    rows, cols = lax.axis_size("row"), lax.axis_size("col")
    held = []
    for d in range(cols):
        wanted = [((r * cols + (source_col(r) ^ d)) % rows) ^ r for r in range(rows)]
        if len(set(wanted)) == 1:
            held.append(blocks[wanted[0]])
        else:
            held.append(lax.dynamic_index_in_dim(jnp.stack(blocks), jnp.array(wanted)[lax.axis_index("row")], 0, keepdims=False))
    return held


def spread_step(held):
    rows, cols = lax.axis_size("row"), lax.axis_size("col")
    bit = len(held) // 2
    pairs = [(r * cols + c, r * cols + (c ^ bit)) for r in range(rows) for c in range(cols)
             if (c ^ source_col(r)) % (2 * bit) == 0]
    moved = lax.ppermute(jnp.stack(held[bit:]), ("row", "col"), pairs)
    offset = lax.axis_index("col") ^ source_col(lax.axis_index("row"))
    return [jnp.where(offset & bit != 0, moved[j], held[j]) for j in range(bit)]


def local(inverse_tile, panels, link_panel, diag_inverse, ancestor_tiles):
    rows_axis, cols_axis = lax.axis_size("row"), lax.axis_size("col")
    row_id, col_id = lax.axis_index("row"), lax.axis_index("col")
    siblings, _, local_rows, width = panels.shape
    height, span = diag_inverse.shape[2:]
    row_start = (col_id * rows_axis + row_id) * local_rows
    tile_mask = jnp.repeat(ancestor_tiles, TILE, axis=2)
    kept_rows = lax.dynamic_slice_in_dim(tile_mask, row_start, local_rows, 2).astype(jnp.float32)
    masked = panels * kept_rows[..., None]
    tiles = [half.reshape(cols_axis, -1, half.shape[1]) for half in split(inverse_tile)]

    def one_pair(first, panel_second, link, given_first, given_second):
        live = {"tiles": tiles, "given": given_first, "first": first, "second": panel_second - dot(first, link, precise)}
        slots = {}

        def at(slot, *steps):
            slots.setdefault(slot, []).extend(steps)

        late = 2 * span
        pieces = [("first", i, i + late) for i in range(0, width, late)]
        count_first = len(pieces)
        pieces += [("second", i, i + late) for i in range(0, width, late)]
        count_early = len(pieces) - 1
        stages = rows_axis.bit_length() - 1

        def fetch(k, stage):
            if stage == 0:
                panel, start, stop = pieces[k]
                live[k, 0] = live[panel][:, start:stop]
            for j in range(1, rows_axis):
                if j.bit_count() == stage + 1:
                    live[k, j] = swap(live[k, j & (j - 1)], "row", j & -j)

        def blocks(k):
            return [live[k, j] for j in range(rows_axis)]

        def multiply(k):
            live["send", k], live["keep", k] = product(live["tiles"], blocks(k))

        def add_core(k):
            live["sums", k] = live.pop(("keep", k)) + swap(live.pop(("send", k)), "col", 1)

        def add_rest(k):
            live["out", k] = -sum_scatter(live.pop(("sums", k)), "col", 2)

        def collect(name, start, stop):
            groups = zip(*(blocks(k) for k in range(start, stop)))
            live[name] = blocks_to_send([jnp.concatenate(group, axis=1) for group in groups])
            spread(name)
            for k in range(start, stop):
                for j in range(rows_axis):
                    del live[k, j]

        def spread(name):
            live[name] = spread_step(live[name])

        def own(name, slot, start, stop):
            at(slot, lambda: collect(name, start, stop))
            for step in range(1, cols_axis.bit_length() - 1):
                at(slot + step, lambda: spread(name))

        def outs(start, stop):
            return jnp.concatenate([live["out", k] for k in range(start, stop)], axis=1)

        for k in range(len(pieces)):
            for stage in range(stages):
                at(k + stage, lambda k=k, stage=stage: fetch(k, stage))

        def link_terms():
            link_rows = lax.dynamic_slice_in_dim(link, row_id * height, height, 0)
            link_cols = lax.dynamic_slice_in_dim(link, col_id * span, span, 0)
            given = dot(live["given"], link_cols, precise)
            live["link_cross"] = lax.dynamic_update_slice_in_dim(jnp.zeros_like(link), given, row_id * height, 0)
            live["link_second"] = -dot_tn(link_rows, given, precise)

        def own_second():
            return jnp.concatenate([live["own_early"][0], live["own_last"][0]], axis=1)

        def first_terms():
            out_first = outs(0, count_first)
            terms = jnp.stack([dot_tn(out_first, live["own_first"][0], three_pass),
                               dot_tn(out_first, own_second(), three_pass) + live["link_cross"]])
            terms = terms.reshape(2 * width, cols_axis, span).swapaxes(0, 1)
            terms = lax.psum_scatter(terms, "col", scatter_dimension=0)
            terms = terms.reshape(2, rows_axis, height, span).swapaxes(0, 1)
            live["first_sums"] = lax.psum_scatter(terms, "row", scatter_dimension=0)

        def second_terms():
            out_second = outs(count_first, len(pieces))

            def terms(odd):
                own_columns, link_columns = (jnp.concatenate(columns_by_xor(array, odd), axis=1)
                                             for array in (own_second(), live["link_second"]))
                return dot_tn(out_second, own_columns, three_pass) + link_columns

            sent = swap(terms(1), "col", 1)
            sums = (terms(0) + sent).reshape(width, cols_axis // 2, span).swapaxes(0, 1)
            sums = sum_scatter(sums, "col", 2)
            live["second_sum"] = sum_rows(sums.reshape(rows_axis, height, span), "row")

        end = len(pieces) - 1 + stages
        for k in range(len(pieces)):
            at(k + stages, lambda k=k: multiply(k))
            at(min(k + stages + 1, end), lambda k=k: add_core(k))
            at(min(k + stages + 1, end), lambda k=k: add_rest(k))
            if k == 0:
                at(1, link_terms)
            if k == count_first - 1:
                own("own_first", k + stages, 0, count_first)
            if k == count_early - 1:
                own("own_early", k + stages, count_first, count_early)
        at(end, lambda: collect("own_last", count_early, len(pieces)))
        for step in range(1, cols_axis.bit_length() - 1):
            at(end, lambda: spread("own_last"))
        at(end, first_terms)
        at(end, second_terms)

        for slot in range(end + 1):
            if slot > 0:
                live = dict(zip(live, lax.optimization_barrier(list(live.values()))))
            for step in slots[slot]:
                step()

        first_sum, cross_sum = live["first_sums"]
        ancestor = jnp.stack([outs(0, count_first), outs(count_first, len(pieces))])
        diagonal = jnp.stack([given_first - first_sum, given_second - live["second_sum"]])
        return ancestor, diagonal, -cross_sum

    results = [one_pair(masked[s, 0], masked[s, 1], link_panel[s], diag_inverse[s, 0], diag_inverse[s, 1])
               for s in range(siblings)]
    return tuple(jnp.stack(group) for group in zip(*results))


def solution(mesh):
    in_specs = (
        P(("hyp", "row"), "col"),
        P("hyp", None, ("col", "row"), None),
        P("hyp", None, None),
        P("hyp", None, "row", "col"),
        P(),
    )
    out_specs = (
        P("hyp", None, ("row", "col"), None),
        P("hyp", None, "row", "col"),
        P("hyp", "row", "col"),
    )
    return jax.shard_map(local, mesh=mesh, in_specs=in_specs, out_specs=out_specs, check_vma=False)
```

time: 364 us -> 343 us (0.942)
  waiting for transfers between devices: 126 us -> 157 us
  starting transfers between devices: 60.9 us -> 42.2 us
  local copies, waits for them, and re-layouts: 53.1 us -> 34.9 us
  other arithmetic: 45.2 us -> 27.7 us
  between operations: 1.83 us -> 14.8 us
  Pallas kernels: 62.7 us -> 56.5 us
    unnamed x0 -> x3, waiting for transfers between devices: none -> 27.3 us
    ppermute x7 -> x0, starting transfers between devices: 18.4 us -> none  [the longest x6 16.9 us: sum_to_last(): lax.ppermute(block, axis, [(i, i ^ bit) for i in range(size) if not i & b...]
    ppermute x4 -> x6, waiting for transfers between devices: 0.01 us -> 10.8 us  [spread_step(): moved = lax.ppermute(jnp.stack(held[bit:]), ('row', 'col'), pairs)]
    add x11 -> x1, other arithmetic: 8.69 us -> 0.92 us  [sum_rows(): keep + swap(lax.dynamic_index_in_dim(pairs, 1 - mine, 1, keepdims=False),...]
    ppermute x41 -> x24, starting transfers between devices: 31.3 us -> 23.6 us  [swap(): return lax.ppermute(block, axis, pairs)]
    ppermute x41 -> x24, waiting for transfers between devices: 126 us -> 119 us  [swap(): return lax.ppermute(block, axis, pairs)]
    ppermute x4 -> x6, starting transfers between devices: 11.2 us -> 18.5 us  [spread_step(): moved = lax.ppermute(jnp.stack(held[bit:]), ('row', 'col'), pairs)]
    squeeze x13 -> x4, local copies, waits for them, and re-layouts: 8.22 us -> 0.96 us  [sum_scatter(): blocks = pairs[:, 0] + swap(pairs[:, 1], axis, bit)]
  transfers between devices with their start and end apart: 52 -> 32, of which waited for: 19 -> 16; matrix products, arithmetic and copies ran while one was open for 18% -> 12% of each run, Pallas kernels for 17% -> 17%
where the time goes in v3:
time: 343 us; the launch traced here: 342 us
  waiting for transfers between devices  157 us (46%)
  Pallas kernels  56.5 us (16%)
  starting transfers between devices  42.2 us (12%)
  local copies, waits for them, and re-layouts  34.9 us (10%)
  other arithmetic  27.7 us (8%)
  between operations  14.8 us (4%)
  matrix products  9.39 us (3%)
    ppermute x24, waiting for transfers between devices, swap(): return lax.ppermute(block, axis, pairs)  119 us
    pallas_call x4, Pallas kernels, product(): pl.pallas_call(product_kernel, in_specs=[pl.BlockSpec(memory_space=pltpu....  45.1 us
    unnamed x3, waiting for transfers between devices  27.3 us
    unnamed x88, local copies, waits for them, and re-layouts  25 us
    ppermute x24, starting transfers between devices, swap(): return lax.ppermute(block, axis, pairs)  23.6 us
    ppermute x6, starting transfers between devices, spread_step(): moved = lax.ppermute(jnp.stack(held[bit:]), ('row', 'col'), pairs)  18.5 us
    pallas_call x1, Pallas kernels, split(): pl.pallas_call(split_kernel, grid=(rows // step,), in_specs=[block], out_...  11.4 us
    ppermute x6, waiting for transfers between devices, spread_step(): moved = lax.ppermute(jnp.stack(held[bit:]), ('row', 'col'), pairs)  10.8 us
  transfers between devices with their start and end apart: 32, of which 16 were waited for; matrix products, arithmetic and copies ran while one was open for 12% of the time, Pallas kernels for 17%

profile of v3, /device:TPU:0, one launch (start us, length us, event | category | flops | bytes accessed | tf_op | source)
XLA Modules:
  0.0 342.2 jit_solution(13851526799379842670)
XLA Ops:
  15.8 11.4 %shard_map.79 = (bf16[2048,2048]{1,0:T(8,128)(2,1)S(1)}, bf16[2048,2048]{1,0:T(8,128)(2,1)}) custom-call(f32[2048,2048]{1,0:T(8,128)} %tile_ref.1), custom_call_target="tpu_custom_call" | custom-call | tf_op jit(solution)/shard_map/pallas_call | solution.py:32
  44.7 19.5 %collective-permute-done.3.refs_1_ = f32[512,256]{1,0:T(8,128)S(1)} collective-permute-done((f32[512,256]{1,0:T(8,128)S(1)}, f32[512,256]{1,0:T(8,128)S(1)}, u32[]{:S(2)}, u32[]{:S(2)}) %collective-permute-start.3) | collective-permute-done | bytes 524320 | tf_op jit(solution)/shard_map/ppermute | solution.py:16
  64.2 8.8 %collective-permute-done.2.refs_3_ = f32[512,256]{1,0:T(8,128)} collective-permute-done((f32[512,256]{1,0:T(8,128)}, f32[512,256]{1,0:T(8,128)}, u32[]{:S(2)}, u32[]{:S(2)}) %collective-permute-start.2) | collective-permute-done | bytes 524320 | tf_op jit(solution)/shard_map/ppermute | solution.py:16
  76.9 3.4 copy-done.3
  80.3 11.2 %shard_map.80 = (f32[2,512,256]{2,1,0:T(8,128)S(1)}, f32[2,512,256]{2,1,0:T(8,128)S(1)}) custom-call(s32[5]{0:T(128)S(1)} %pad_add_fusion.place, bf16[4,512,2048]{2,1,0:T(8,128)(2,1)S(1)} %bitcast.183, bf16[4,512,2048]{2,1,0:T(8,128)(2,1)} %bitcast.191, f32[512,256]{1,0:T(8,128)S(1)} %slice.101.refs_0_, f32[512,256]{1,0:T(8,128)S(1)} %collective-permute-done.refs_1_, ...), custom_call_target="tpu_custom_call" | custom-call | tf_op jit(solution)/shard_map/pallas_call | solution.py:70
  91.6 7.1 %collective-permute-done.6.refs_1_ = f32[512,256]{1,0:T(8,128)S(1)} collective-permute-done((f32[512,256]{1,0:T(8,128)S(1)}, f32[512,256]{1,0:T(8,128)S(1)}, u32[]{:S(2)}, u32[]{:S(2)}) %collective-permute-start.6) | collective-permute-done | bytes 524320 | tf_op jit(solution)/shard_map/ppermute | solution.py:16
  98.7 8.7 %collective-permute-done.5.refs_3_ = f32[512,256]{1,0:T(8,128)S(1)} collective-permute-done((f32[512,256]{1,0:T(8,128)}, f32[512,256]{1,0:T(8,128)S(1)}, u32[]{:S(2)}, u32[]{:S(2)}) %collective-permute-start.5) | collective-permute-done | bytes 524320 | tf_op jit(solution)/shard_map/ppermute | solution.py:16
  111.6 4.7 %collective-permute-start.13 = (f32[2,512,512]{2,1,0:T(8,128)}, f32[2,512,512]{2,1,0:T(8,128)}, u32[]{:S(2)}, u32[]{:S(2)}) collective-permute-start(f32[2,512,512]{2,1,0:T(8,128)} %pad_maximum_fusion), channel_id=1, source_target_pairs={{0,2},{5,7},{10,8},{15,13},{16,18},{21,23},{26,24},{31,29}} | collective-permute-start | bytes 6291464 | tf_op jit(solution)/shard_map/ppermute | solution.py:134
  123.3 3.4 copy-done.4
  127.7 11.2 %shard_map.81 = (f32[2,512,256]{2,1,0:T(8,128)}, f32[2,512,256]{2,1,0:T(8,128)S(1)}) custom-call(s32[5]{0:T(128)S(1)} %pad_add_fusion.place, bf16[4,512,2048]{2,1,0:T(8,128)(2,1)S(1)} %bitcast.184, bf16[4,512,2048]{2,1,0:T(8,128)(2,1)} %bitcast.192, f32[512,256]{1,0:T(8,128)S(1)} %slice.78.refs_0_, f32[512,256]{1,0:T(8,128)S(1)} %collective-permute-done.3.refs_1_, ...), custom_call_target="tpu_custom_call" | custom-call | tf_op jit(solution)/shard_map/pallas_call | solution.py:70
  138.9 11.2 %collective-permute-done.12 = f32[1,512,256]{2,1,0:T(8,128)} collective-permute-done((f32[1,512,256]{2,1,0:T(8,128)}, f32[1,512,256]{2,1,0:T(8,128)}, u32[]{:S(2)}, u32[]{:S(2)}) %collective-permute-start.12) | collective-permute-done | bytes 524320 | tf_op jit(solution)/shard_map/ppermute | solution.py:16
  156.3 3.4 collective-permute-start.14
  160.8 5.3 %collective-permute-start.18 = (f32[2,512,256]{2,1,0:T(8,128)}, f32[2,512,256]{2,1,0:T(8,128)}, u32[]{:S(2)}, u32[]{:S(2)}) collective-permute-start(f32[2,512,256]{2,1,0:T(8,128)} %pad_maximum_fusion.4), channel_id=1, source_target_pairs={{0,2},{5,7},{10,8},{15,13},{16,18},{21,23},{26,24},{31,29}} | collective-permute-start | bytes 3145736 | tf_op jit(solution)/shard_map/ppermute | solution.py:134
  170.6 11.0 %shard_map.82 = (f32[2,512,256]{2,1,0:T(8,128)}, f32[2,512,256]{2,1,0:T(8,128)S(1)}) custom-call(s32[5]{0:T(128)S(1)} %pad_add_fusion.place, bf16[4,512,2048]{2,1,0:T(8,128)(2,1)S(1)} %bitcast.185, bf16[4,512,2048]{2,1,0:T(8,128)(2,1)} %bitcast.193, f32[512,256]{1,0:T(8,128)S(1)} %slice.79.refs_0_, f32[512,256]{1,0:T(8,128)S(1)} %copy-done.10, ...), custom_call_target="tpu_custom_call" | custom-call | tf_op jit(solution)/shard_map/pallas_call | solution.py:70
  186.3 11.5 %collective-permute-done.17 = f32[1,512,256]{2,1,0:T(8,128)S(1)} collective-permute-done((f32[1,512,256]{2,1,0:T(8,128)S(1)}, f32[1,512,256]{2,1,0:T(8,128)S(1)}, u32[]{:S(2)}, u32[]{:S(2)}) %collective-permute-start.17) | collective-permute-done | bytes 524320 | tf_op jit(solution)/shard_map/ppermute | solution.py:16
  201.8 10.8 %collective-permute-done.24 = f32[2,512,256]{2,1,0:T(8,128)S(1)} collective-permute-done((f32[2,512,256]{2,1,0:T(8,128)S(1)}, f32[2,512,256]{2,1,0:T(8,128)S(1)}, u32[]{:S(2)}, u32[]{:S(2)}) %collective-permute-start.24) | collective-permute-done | bytes 1048608 | tf_op jit(solution)/shard_map/ppermute | solution.py:134
  225.6 3.4 copy-done.6
  229.0 11.7 %shard_map.83 = (f32[2,512,256]{2,1,0:T(8,128)}, f32[2,512,256]{2,1,0:T(8,128)S(1)}) custom-call(s32[5]{0:T(128)S(1)} %pad_add_fusion.place, bf16[4,512,2048]{2,1,0:T(8,128)(2,1)S(1)} %bitcast.186, bf16[4,512,2048]{2,1,0:T(8,128)(2,1)} %bitcast.194, f32[512,256]{1,0:T(8,128)S(1)} %slice.80.refs_0_, f32[512,256]{1,0:T(8,128)S(1)} %copy-done.8, ...), custom_call_target="tpu_custom_call" | custom-call | tf_op jit(solution)/shard_map/pallas_call | solution.py:70
  249.0 17.4 %collective-permute-done.20 = f32[1,512,256]{2,1,0:T(8,128)S(1)} collective-permute-done((f32[1,512,256]{2,1,0:T(8,128)S(1)}, f32[1,512,256]{2,1,0:T(8,128)S(1)}, u32[]{:S(2)}, u32[]{:S(2)}) %collective-permute-start.20) | collective-permute-done | bytes 524320 | tf_op jit(solution)/shard_map/ppermute | solution.py:16
  266.5 11.1 %collective-permute-done.22 = f32[1,512,256]{2,1,0:T(8,128)S(1)} collective-permute-done((f32[1,512,256]{2,1,0:T(8,128)S(1)}, f32[1,512,256]{2,1,0:T(8,128)S(1)}, u32[]{:S(2)}, u32[]{:S(2)}) %collective-permute-start.22) | collective-permute-done | bytes 524320 | tf_op jit(solution)/shard_map/ppermute | solution.py:16
  283.5 7.4 %collective-permute-done.27 = f32[1,512,128]{2,1,0:T(8,128)S(1)} collective-permute-done((f32[1,512,128]{2,1,0:T(8,128)S(1)}, f32[1,512,128]{2,1,0:T(8,128)S(1)}, u32[]{:S(2)}, u32[]{:S(2)}) %collective-permute-start.27) | collective-permute-done | bytes 262176 | tf_op jit(solution)/shard_map/ppermute | solution.py:16
  291.7 5.1 %collective-permute-done.28 = f32[2,128,128]{2,1,0:T(8,128)} collective-permute-done((f32[2,128,128]{2,1,0:T(8,128)}, f32[2,128,128]{2,1,0:T(8,128)}, u32[]{:S(2)}, u32[]{:S(2)}) %collective-permute-start.28) | collective-permute-done | bytes 131104 | tf_op jit(solution)/shard_map/ppermute | solution.py:16
  301.7 3.5 %collective-permute-done.29 = f32[1,128,128]{2,1,0:T(8,128)S(1)} collective-permute-done((f32[1,128,128]{2,1,0:T(8,128)S(1)}, f32[1,128,128]{2,1,0:T(8,128)S(1)}, u32[]{:S(2)}, u32[]{:S(2)}) %collective-permute-start.29) | collective-permute-done | bytes 65568 | tf_op jit(solution)/shard_map/ppermute | solution.py:16
  305.2 27.3 %all-reduce.3.cloned.1.call-done = f32[4,2,128,128]{3,2,0,1:T(8,128)} async-done(((f32[4,2,128,128]{3,2,0,1:T(8,128)}), f32[4,2,128,128]{3,2,0,1:T(8,128)}) %all-reduce.3.cloned.1.call-update) | async-done | bytes 524304
  (194 shorter events, 98.1 us)
Async XLA Ops:
  7.2 284.5 %reduce-scatter.5.cloned.1.call-start = ((), (), s32[]{:S(2)}) async-start(), calls=%async_computation.1 | async-start | bytes 2621440 | tf_op jit(solution)/shard_map/reduce_scatter | solution.py:222
  10.1 26.1 %collective-permute-start = (f32[512,256]{1,0:T(8,128)S(1)}, f32[512,256]{1,0:T(8,128)S(1)}, u32[]{:S(2)}, u32[]{:S(2)}) collective-permute-start(f32[512,256]{1,0:T(8,128)S(1)} %slice.101.refs_0_), channel_id=1, source_target_pairs={{0,4},{4,0},{8,12},{12,8},{1,5},{5,1},{9,13},{13,9},{2,6},{6,2},{1... | collective-permute-start | bytes 1572872 | tf_op jit(solution)/shard_map/ppermute | solution.py:16
  13.2 25.7 %collective-permute-start.1 = (f32[512,256]{1,0:T(8,128)S(1)}, f32[512,256]{1,0:T(8,128)}, u32[]{:S(2)}, u32[]{:S(2)}) collective-permute-start(f32[512,256]{1,0:T(8,128)S(1)} %slice.101.refs_0_), channel_id=1, source_target_pairs={{0,8},{4,12},{8,0},{12,4},{1,9},{5,13},{9,1},{13,5},{2,10},{6,14},... | collective-permute-start | bytes 1572872 | tf_op jit(solution)/shard_map/ppermute | solution.py:16
  38.9 25.3 %collective-permute-start.3 = (f32[512,256]{1,0:T(8,128)S(1)}, f32[512,256]{1,0:T(8,128)S(1)}, u32[]{:S(2)}, u32[]{:S(2)}) collective-permute-start(f32[512,256]{1,0:T(8,128)S(1)} %slice.78.refs_0_), channel_id=1, source_target_pairs={{0,4},{4,0},{8,12},{12,8},{1,5},{5,1},{9,13},{13,9},{2,6},{6,2},{1... | collective-permute-start | bytes 1572872 | tf_op jit(solution)/shard_map/ppermute | solution.py:16
  39.4 24.8 %collective-permute-start.4 = (f32[512,256]{1,0:T(8,128)S(1)}, f32[512,256]{1,0:T(8,128)}, u32[]{:S(2)}, u32[]{:S(2)}) collective-permute-start(f32[512,256]{1,0:T(8,128)S(1)} %slice.78.refs_0_), channel_id=1, source_target_pairs={{0,8},{4,12},{8,0},{12,4},{1,9},{5,13},{9,1},{13,5},{2,10},{6,14},... | collective-permute-start | bytes 1572872 | tf_op jit(solution)/shard_map/ppermute | solution.py:16
  42.0 30.9 %collective-permute-start.2 = (f32[512,256]{1,0:T(8,128)}, f32[512,256]{1,0:T(8,128)}, u32[]{:S(2)}, u32[]{:S(2)}) collective-permute-start(f32[512,256]{1,0:T(8,128)} %collective-permute-done.1.refs_2_), channel_id=1, source_target_pairs={{0,4},{4,0},{8,12},{12,8},{1,5},{5,1},{9,13},{13,9},{2,6},{6,2},{1... | collective-permute-start | bytes 1572872 | tf_op jit(solution)/shard_map/ppermute | solution.py:16
  73.0 25.7 %collective-permute-start.6 = (f32[512,256]{1,0:T(8,128)S(1)}, f32[512,256]{1,0:T(8,128)S(1)}, u32[]{:S(2)}, u32[]{:S(2)}) collective-permute-start(f32[512,256]{1,0:T(8,128)S(1)} %slice.79.refs_0_), channel_id=1, source_target_pairs={{0,4},{4,0},{8,12},{12,8},{1,5},{5,1},{9,13},{13,9},{2,6},{6,2},{1... | collective-permute-start | bytes 1572872 | tf_op jit(solution)/shard_map/ppermute | solution.py:16
  74.9 23.8 %collective-permute-start.7 = (f32[512,256]{1,0:T(8,128)S(1)}, f32[512,256]{1,0:T(8,128)S(1)}, u32[]{:S(2)}, u32[]{:S(2)}) collective-permute-start(f32[512,256]{1,0:T(8,128)S(1)} %slice.79.refs_0_), channel_id=1, source_target_pairs={{0,8},{4,12},{8,0},{12,4},{1,9},{5,13},{9,1},{13,5},{2,10},{6,14},... | collective-permute-start | bytes 1572872 | tf_op jit(solution)/shard_map/ppermute | solution.py:16
  75.7 31.7 %collective-permute-start.5 = (f32[512,256]{1,0:T(8,128)}, f32[512,256]{1,0:T(8,128)S(1)}, u32[]{:S(2)}, u32[]{:S(2)}) collective-permute-start(f32[512,256]{1,0:T(8,128)} %collective-permute-done.4.refs_2_), channel_id=1, source_target_pairs={{0,4},{4,0},{8,12},{12,8},{1,5},{5,1},{9,13},{13,9},{2,6},{6,2},{1... | collective-permute-start | bytes 1572872 | tf_op jit(solution)/shard_map/ppermute | solution.py:16
  111.6 40.4 %collective-permute-start.13 = (f32[2,512,512]{2,1,0:T(8,128)}, f32[2,512,512]{2,1,0:T(8,128)}, u32[]{:S(2)}, u32[]{:S(2)}) collective-permute-start(f32[2,512,512]{2,1,0:T(8,128)} %pad_maximum_fusion), channel_id=1, source_target_pairs={{0,2},{5,7},{10,8},{15,13},{16,18},{21,23},{26,24},{31,29}} | collective-permute-start | bytes 6291464 | tf_op jit(solution)/shard_map/ppermute | solution.py:134
  118.3 31.8 %collective-permute-start.12 = (f32[1,512,256]{2,1,0:T(8,128)}, f32[1,512,256]{2,1,0:T(8,128)}, u32[]{:S(2)}, u32[]{:S(2)}) collective-permute-start(f32[1,512,256]{2,1,0:T(8,128)} %slice_bitcast_fusion.14), channel_id=1, source_target_pairs={{0,2},{1,3},{2,0},{3,1},{4,6},{5,7},{6,4},{7,5},{8,10},{9,11},{10,... | collective-permute-start | bytes 1572872 | tf_op jit(solution)/shard_map/ppermute | solution.py:16
  119.5 35.9 %collective-permute-start.10 = (f32[512,256]{1,0:T(8,128)S(1)}, f32[512,256]{1,0:T(8,128)S(1)}, u32[]{:S(2)}, u32[]{:S(2)}) collective-permute-start(f32[512,256]{1,0:T(8,128)S(1)} %slice.80.refs_0_), channel_id=1, source_target_pairs={{0,8},{4,12},{8,0},{12,4},{1,9},{5,13},{9,1},{13,5},{2,10},{6,14},... | collective-permute-start | bytes 1572872 | tf_op jit(solution)/shard_map/ppermute | solution.py:16
  121.2 34.1 %collective-permute-start.9 = (f32[512,256]{1,0:T(8,128)S(1)}, f32[512,256]{1,0:T(8,128)S(1)}, u32[]{:S(2)}, u32[]{:S(2)}) collective-permute-start(f32[512,256]{1,0:T(8,128)S(1)} %slice.80.refs_0_), channel_id=1, source_target_pairs={{0,4},{4,0},{8,12},{12,8},{1,5},{5,1},{9,13},{13,9},{2,6},{6,2},{1... | collective-permute-start | bytes 1572872 | tf_op jit(solution)/shard_map/ppermute | solution.py:16
  121.2 34.9 %collective-permute-start.8 = (f32[512,256]{1,0:T(8,128)}, f32[512,256]{1,0:T(8,128)S(1)}, u32[]{:S(2)}, u32[]{:S(2)}) collective-permute-start(f32[512,256]{1,0:T(8,128)} %copy-done.13), channel_id=1, source_target_pairs={{0,4},{4,0},{8,12},{12,8},{1,5},{5,1},{9,13},{13,9},{2,6},{6,2},{1... | collective-permute-start | bytes 1572872 | tf_op jit(solution)/shard_map/ppermute | solution.py:16
  156.3 25.3 %collective-permute-start.16 = (f32[2,512,256]{2,1,0:T(8,128)}, f32[2,512,256]{2,1,0:T(8,128)}, u32[]{:S(2)}, u32[]{:S(2)}) collective-permute-start(f32[2,512,256]{2,1,0:T(8,128)} %get-tuple-element.137), channel_id=1, source_target_pairs={{0,1},{1,0},{2,3},{3,2},{4,5},{5,4},{6,7},{7,6},{8,9},{9,8},{10,11... | collective-permute-start | bytes 3145736 | tf_op jit(solution)/shard_map/ppermute | solution.py:16
  156.3 27.2 %collective-permute-start.14 = (f32[1,512,512]{2,1,0:T(8,128)}, f32[1,512,512]{2,1,0:T(8,128)}, u32[]{:S(2)}, u32[]{:S(2)}) collective-permute-start(f32[1,512,512]{2,1,0:T(8,128)} %bitcast.19), channel_id=1, source_target_pairs={{0,1},{2,3},{5,4},{7,6},{8,9},{10,11},{13,12},{15,14},{16,17},{18,... | collective-permute-start | bytes 3145736 | tf_op jit(solution)/shard_map/ppermute | solution.py:134
  160.8 24.2 %collective-permute-start.18 = (f32[2,512,256]{2,1,0:T(8,128)}, f32[2,512,256]{2,1,0:T(8,128)}, u32[]{:S(2)}, u32[]{:S(2)}) collective-permute-start(f32[2,512,256]{2,1,0:T(8,128)} %pad_maximum_fusion.4), channel_id=1, source_target_pairs={{0,2},{5,7},{10,8},{15,13},{16,18},{21,23},{26,24},{31,29}} | collective-permute-start | bytes 3145736 | tf_op jit(solution)/shard_map/ppermute | solution.py:134
  166.1 31.8 %collective-permute-start.15 = (f32[512,256]{1,0:T(8,128)S(1)}, f32[512,256]{1,0:T(8,128)S(1)}, u32[]{:S(2)}, u32[]{:S(2)}) collective-permute-start(f32[512,256]{1,0:T(8,128)S(1)} %copy-done.12), channel_id=1, source_target_pairs={{0,4},{4,0},{8,12},{12,8},{1,5},{5,1},{9,13},{13,9},{2,6},{6,2},{1... | collective-permute-start | bytes 1572872 | tf_op jit(solution)/shard_map/ppermute | solution.py:16
  198.0 14.5 %collective-permute-start.24 = (f32[2,512,256]{2,1,0:T(8,128)S(1)}, f32[2,512,256]{2,1,0:T(8,128)S(1)}, u32[]{:S(2)}, u32[]{:S(2)}) collective-permute-start(f32[2,512,256]{2,1,0:T(8,128)S(1)} %pad_maximum_fusion.6), channel_id=1, source_target_pairs={{0,2},{5,7},{10,8},{15,13},{16,18},{21,23},{26,24},{31,29}} | collective-permute-start | bytes 3145736 | tf_op jit(solution)/shard_map/ppermute | solution.py:134
  200.3 15.0 %collective-permute-start.23 = (f32[1,512,256]{2,1,0:T(8,128)S(1)}, f32[1,512,256]{2,1,0:T(8,128)S(1)}, u32[]{:S(2)}, u32[]{:S(2)}) collective-permute-start(f32[1,512,256]{2,1,0:T(8,128)S(1)} %bitcast.202), channel_id=1, source_target_pairs={{0,1},{2,3},{5,4},{7,6},{8,9},{10,11},{13,12},{15,14},{16,17},{18,... | collective-permute-start | bytes 1572872 | tf_op jit(solution)/shard_map/ppermute | solution.py:134
  201.6 40.0 %collective-permute-start.19 = (f32[2,512,256]{2,1,0:T(8,128)}, f32[2,512,256]{2,1,0:T(8,128)}, u32[]{:S(2)}, u32[]{:S(2)}) collective-permute-start(f32[2,512,256]{2,1,0:T(8,128)} %get-tuple-element.147), channel_id=1, source_target_pairs={{0,1},{1,0},{2,3},{3,2},{4,5},{5,4},{6,7},{7,6},{8,9},{9,8},{10,11... | collective-permute-start | bytes 3145736 | tf_op jit(solution)/shard_map/ppermute | solution.py:16
  225.5 107.0 %all-reduce.3.cloned.1.call-start = ((), (), s32[]{:S(2)}) async-start(), calls=%async_computation.2 | async-start | bytes 1048576
  243.2 23.3 %collective-permute-start.20 = (f32[1,512,256]{2,1,0:T(8,128)S(1)}, f32[1,512,256]{2,1,0:T(8,128)S(1)}, u32[]{:S(2)}, u32[]{:S(2)}) collective-permute-start(f32[1,512,256]{2,1,0:T(8,128)S(1)} %slice_bitcast_fusion.8), channel_id=1, source_target_pairs={{0,2},{1,3},{2,0},{3,1},{4,6},{5,7},{6,4},{7,5},{8,10},{9,11},{10,... | collective-permute-start | bytes 1572872 | tf_op jit(solution)/shard_map/ppermute | solution.py:16
  247.2 30.5 %collective-permute-start.22 = (f32[1,512,256]{2,1,0:T(8,128)S(1)}, f32[1,512,256]{2,1,0:T(8,128)S(1)}, u32[]{:S(2)}, u32[]{:S(2)}) collective-permute-start(f32[1,512,256]{2,1,0:T(8,128)S(1)} %slice_bitcast_fusion.6), channel_id=1, source_target_pairs={{0,2},{1,3},{2,0},{3,1},{4,6},{5,7},{6,4},{7,5},{8,10},{9,11},{10,... | collective-permute-start | bytes 1572872 | tf_op jit(solution)/shard_map/ppermute | solution.py:16
  (50 other events, 432.8 us)
Sparse Core Ops, SparseCore 0:
  225.7 38.9 reduce-scatter.4
  291.9 40.6 all-reduce.2

commit v4 on v3

--- a/solution.py
+++ b/solution.py
@@ -35,7 +35,7 @@
         in_specs=[block],
         out_specs=[block, block],
         out_shape=[jax.ShapeDtypeStruct(tile.shape, jnp.bfloat16)] * 2,
-        compiler_params=pltpu.CompilerParams(vmem_limit_bytes=40 * 2**20),
+        compiler_params=pltpu.CompilerParams(vmem_limit_bytes=16 * 2**20),
     )(tile)
 
 
@@ -73,7 +73,7 @@
         out_specs=[vmem, vmem],
         out_shape=[jax.ShapeDtypeStruct((half, out_rows, columns), jnp.float32)] * 2,
         scratch_shapes=[pltpu.VMEM((width, columns), jnp.bfloat16)] * 2,
-        compiler_params=pltpu.CompilerParams(vmem_limit_bytes=40 * 2**20),
+        compiler_params=pltpu.CompilerParams(vmem_limit_bytes=16 * 2**20),
     )(place, *tiles, *blocks)
 
 
@@ -158,7 +158,6 @@
         pieces = [("first", i, i + late) for i in range(0, width, late)]
         count_first = len(pieces)
         pieces += [("second", i, i + late) for i in range(0, width, late)]
-        count_early = len(pieces) - 1
         stages = rows_axis.bit_length() - 1
 
         def fetch(k, stage):
@@ -181,21 +180,15 @@
         def add_rest(k):
             live["out", k] = -sum_scatter(live.pop(("sums", k)), "col", 2)
 
-        def collect(name, start, stop):
-            groups = zip(*(blocks(k) for k in range(start, stop)))
-            live[name] = blocks_to_send([jnp.concatenate(group, axis=1) for group in groups])
-            spread(name)
-            for k in range(start, stop):
-                for j in range(rows_axis):
-                    del live[k, j]
-
-        def spread(name):
-            live[name] = spread_step(live[name])
-
-        def own(name, slot, start, stop):
-            at(slot, lambda: collect(name, start, stop))
-            for step in range(1, cols_axis.bit_length() - 1):
-                at(slot + step, lambda: spread(name))
+        def collect(k):
+            live["own", k] = blocks_to_send(blocks(k))
+            spread(k)
+
+        def spread(k):
+            live["own", k] = spread_step(live["own", k])
+
+        def owns(start, stop):
+            return jnp.concatenate([live["own", k][0] for k in range(start, stop)], axis=1)
 
         def outs(start, stop):
             return jnp.concatenate([live["out", k] for k in range(start, stop)], axis=1)
@@ -211,47 +204,49 @@
             live["link_cross"] = lax.dynamic_update_slice_in_dim(jnp.zeros_like(link), given, row_id * height, 0)
             live["link_second"] = -dot_tn(link_rows, given, precise)
 
-        def own_second():
-            return jnp.concatenate([live["own_early"][0], live["own_last"][0]], axis=1)
+        def core_sum(terms):
+            sent = swap(terms(1), "col", 1)
+            return terms(0) + sent
+
+        def spread_sum(sums):
+            sums = sums.reshape(-1, cols_axis // 2, span).swapaxes(0, 1)
+            sums = sum_scatter(sums, "col", 2)
+            return sum_rows(sums.reshape(-1, rows_axis, height, span).swapaxes(0, 1), "row")
+
+        def by_parity(array, odd):
+            return jnp.concatenate(columns_by_xor(array, odd), axis=1)
 
         def first_terms():
             out_first = outs(0, count_first)
-            terms = jnp.stack([dot_tn(out_first, live["own_first"][0], three_pass),
-                               dot_tn(out_first, own_second(), three_pass) + live["link_cross"]])
-            terms = terms.reshape(2 * width, cols_axis, span).swapaxes(0, 1)
-            terms = lax.psum_scatter(terms, "col", scatter_dimension=0)
-            terms = terms.reshape(2, rows_axis, height, span).swapaxes(0, 1)
-            live["first_sums"] = lax.psum_scatter(terms, "row", scatter_dimension=0)
+            own_first, own_second = owns(0, count_first), owns(count_first, len(pieces))
+
+            def terms(odd):
+                cross = dot_tn(out_first, by_parity(own_second, odd), three_pass) + by_parity(live["link_cross"], odd)
+                return jnp.concatenate([dot_tn(out_first, by_parity(own_first, odd), three_pass), cross])
+
+            live["first_sums"] = core_sum(terms)
+
+        def first_sums():
+            live["first_sums"] = spread_sum(live["first_sums"])
 
         def second_terms():
-            out_second = outs(count_first, len(pieces))
+            out_second, own_second = outs(count_first, len(pieces)), owns(count_first, len(pieces))
 
             def terms(odd):
-                own_columns, link_columns = (jnp.concatenate(columns_by_xor(array, odd), axis=1)
-                                             for array in (own_second(), live["link_second"]))
-                return dot_tn(out_second, own_columns, three_pass) + link_columns
-
-            sent = swap(terms(1), "col", 1)
-            sums = (terms(0) + sent).reshape(width, cols_axis // 2, span).swapaxes(0, 1)
-            sums = sum_scatter(sums, "col", 2)
-            live["second_sum"] = sum_rows(sums.reshape(rows_axis, height, span), "row")
-
-        end = len(pieces) - 1 + stages
+                return dot_tn(out_second, by_parity(own_second, odd), three_pass) + by_parity(live["link_second"], odd)
+
+            live["second_sum"] = spread_sum(core_sum(terms))[0]
+
+        at(1, link_terms)
         for k in range(len(pieces)):
-            at(k + stages, lambda k=k: multiply(k))
-            at(min(k + stages + 1, end), lambda k=k: add_core(k))
-            at(min(k + stages + 1, end), lambda k=k: add_rest(k))
-            if k == 0:
-                at(1, link_terms)
-            if k == count_first - 1:
-                own("own_first", k + stages, 0, count_first)
-            if k == count_early - 1:
-                own("own_early", k + stages, count_first, count_early)
-        at(end, lambda: collect("own_last", count_early, len(pieces)))
-        for step in range(1, cols_axis.bit_length() - 1):
-            at(end, lambda: spread("own_last"))
-        at(end, first_terms)
-        at(end, second_terms)
+            at(k + stages, lambda k=k: collect(k), lambda k=k: multiply(k))
+            for step in range(1, cols_axis.bit_length() - 1):
+                at(k + stages + step, lambda k=k: spread(k))
+            at(k + stages + 1, lambda k=k: add_core(k))
+            at(k + stages + (2 if k + 1 < len(pieces) else 1), lambda k=k: add_rest(k))
+        end = len(pieces) + stages + 1
+        at(end - 1, first_terms)
+        at(end, first_sums, second_terms)
 
         for slot in range(end + 1):
             if slot > 0:

time: 343 us -> 277 us (0.81)
  waiting for transfers between devices: 157 us -> 101 us
  Pallas kernels: 56.5 us -> 35.9 us
  between operations: 14.8 us -> 1.59 us
  local copies, waits for them, and re-layouts: 34.9 us -> 44.8 us
  starting transfers between devices: 42.2 us -> 49.6 us
  matrix products: 9.39 us -> 14.1 us
    ppermute x24 -> x28, waiting for transfers between devices: 119 us -> 90.6 us  [swap(): return lax.ppermute(block, axis, pairs)]
    unnamed x3 -> x0, waiting for transfers between devices: 27.3 us -> none
    unnamed x88 -> x96, local copies, waits for them, and re-layouts: 25 us -> 38 us
    pallas_call x4, Pallas kernels: 45.1 us -> 33.5 us  [product(): pl.pallas_call(product_kernel, in_specs=[pl.BlockSpec(memory_space=pltpu....]
    pallas_call x1, Pallas kernels: 11.4 us -> 2.45 us  [split(): pl.pallas_call(split_kernel, grid=(rows // step,), in_specs=[block], out_...]
    reshape x3 -> x2, local copies, waits for them, and re-layouts: 6.21 us -> 1.46 us  [the longest x1 1.39 us: spread_sum(): sums = sums.reshape(-1, cols_axis // 2, span).swapaxes(0, 1)]
    reshape x4 -> x1, other arithmetic: 4.84 us -> 0.14 us  [sum_scatter(): pairs = blocks.reshape((blocks.shape[0] // 2, 2) + blocks.shape[1:])]
    select_n x5 -> x8, other arithmetic: 6.2 us -> 10.9 us  [spread_step(): return [jnp.where(offset & bit != 0, moved[j], held[j]) for j in range(bit)]]
  transfers between devices with their start and end apart: 32 -> 36, of which waited for: 16 -> 14; matrix products, arithmetic and copies ran while one was open for 12% -> 13% of each run, Pallas kernels for 17% -> 13%
where the time goes in v4:
time: 277 us; the launch traced here: 276 us
  waiting for transfers between devices  101 us (36%)
  starting transfers between devices  49.6 us (18%)
  local copies, waits for them, and re-layouts  44.8 us (16%)
  Pallas kernels  35.9 us (13%)
  other arithmetic  28.5 us (10%)
  matrix products  14.1 us (5%)
    ppermute x28, waiting for transfers between devices, swap(): return lax.ppermute(block, axis, pairs)  90.6 us
    unnamed x96, local copies, waits for them, and re-layouts  38 us
    pallas_call x4, Pallas kernels, product(): pl.pallas_call(product_kernel, in_specs=[pl.BlockSpec(memory_space=pltpu....  33.5 us
    ppermute x28, starting transfers between devices, swap(): return lax.ppermute(block, axis, pairs)  27.5 us
    ppermute x8, starting transfers between devices, spread_step(): moved = lax.ppermute(jnp.stack(held[bit:]), ('row', 'col'), pairs)  22.2 us
    select_n x8, other arithmetic, spread_step(): return [jnp.where(offset & bit != 0, moved[j], held[j]) for j in range(bit)]  10.9 us
    dot_general x7, matrix products, dot_tn(): return lax.dot_general(a, b, (((0,), (0,)), ((), ())), precision=precision)  10.9 us
    ppermute x8, waiting for transfers between devices, spread_step(): moved = lax.ppermute(jnp.stack(held[bit:]), ('row', 'col'), pairs)  10.8 us
  transfers between devices with their start and end apart: 36, of which 14 were waited for; matrix products, arithmetic and copies ran while one was open for 13% of the time, Pallas kernels for 13%

profile of v4, /device:TPU:0, one launch (start us, length us, event | category | flops | bytes accessed | tf_op | source)
XLA Modules:
  0.0 276.0 jit_solution(18050886321241427532)
XLA Ops:
  3.5 3.1 %collective-permute-start = (f32[512,256]{1,0:T(8,128)S(1)}, f32[512,256]{1,0:T(8,128)S(1)}, u32[]{:S(2)}, u32[]{:S(2)}) collective-permute-start(f32[512,256]{1,0:T(8,128)S(1)} %slice.116.refs_0_), channel_id=1, source_target_pairs={{0,4},{4,0},{8,12},{12,8},{1,5},{5,1},{9,13},{13,9},{2,6},{6,2},{1... | collective-permute-start | bytes 1572872 | tf_op jit(solution)/shard_map/ppermute | solution.py:16
  9.2 5.8 %copy-done.10 = f32[2048,2048]{1,0:T(8,128)S(1)} copy-done((f32[2048,2048]{1,0:T(8,128)S(1)}, f32[2048,2048]{1,0:T(8,128)}, u32[]{:S(2)}) %copy-start.10) | copy-done | bytes 16777240
  17.4 3.3 %copy-done.2 = bf16[2048,2048]{1,0:T(8,128)(2,1)} copy-done((bf16[2048,2048]{1,0:T(8,128)(2,1)}, bf16[2048,2048]{1,0:T(8,128)(2,1)S(1)}, u32[]{:S(2)}) %copy-start.2) | copy-done | bytes 8388632
  20.8 3.3 %copy-done.6 = bf16[2048,2048]{1,0:T(8,128)(2,1)} copy-done((bf16[2048,2048]{1,0:T(8,128)(2,1)}, bf16[2048,2048]{1,0:T(8,128)(2,1)S(1)}, u32[]{:S(2)}) %copy-start.6) | copy-done | bytes 8388632
  38.1 19.7 %collective-permute-done.2.refs_3_ = f32[512,256]{1,0:T(8,128)} collective-permute-done((f32[512,256]{1,0:T(8,128)}, f32[512,256]{1,0:T(8,128)}, u32[]{:S(2)}, u32[]{:S(2)}) %collective-permute-start.2) | collective-permute-done | bytes 524320 | tf_op jit(solution)/shard_map/ppermute | solution.py:16
  57.8 8.6 %collective-permute-done.3.refs_1_ = f32[512,256]{1,0:T(8,128)S(1)} collective-permute-done((f32[512,256]{1,0:T(8,128)S(1)}, f32[512,256]{1,0:T(8,128)S(1)}, u32[]{:S(2)}, u32[]{:S(2)}) %collective-permute-start.3) | collective-permute-done | bytes 524320 | tf_op jit(solution)/shard_map/ppermute | solution.py:16
  68.8 4.4 %collective-permute-start.8 = (f32[2,512,256]{2,1,0:T(8,128)}, f32[2,512,256]{2,1,0:T(8,128)}, u32[]{:S(2)}, u32[]{:S(2)}) collective-permute-start(f32[2,512,256]{2,1,0:T(8,128)} %pad_maximum_fusion), channel_id=1, source_target_pairs={{0,2},{5,7},{10,8},{15,13},{16,18},{21,23},{26,24},{31,29}} | collective-permute-start | bytes 3145736 | tf_op jit(solution)/shard_map/ppermute | solution.py:134
  75.5 3.4 %copy-done.3 = bf16[2048,2048]{1,0:T(8,128)(2,1)S(1)} copy-done((bf16[2048,2048]{1,0:T(8,128)(2,1)S(1)}, bf16[2048,2048]{1,0:T(8,128)(2,1)}, u32[]{:S(2)}) %copy-start.3) | copy-done | bytes 8388632
  78.9 3.4 %copy-done.7 = bf16[2048,2048]{1,0:T(8,128)(2,1)S(1)} copy-done((bf16[2048,2048]{1,0:T(8,128)(2,1)S(1)}, bf16[2048,2048]{1,0:T(8,128)(2,1)}, u32[]{:S(2)}) %copy-start.7) | copy-done | bytes 8388632
  83.3 8.7 %shard_map.80 = (f32[2,512,256]{2,1,0:T(8,128)}, f32[2,512,256]{2,1,0:T(8,128)S(1)}) custom-call(s32[5]{0:T(128)S(1)} %pad_add_fusion.place, bf16[4,512,2048]{2,1,0:T(8,128)(2,1)S(1)} %bitcast.194, bf16[4,512,2048]{2,1,0:T(8,128)(2,1)S(1)} %bitcast.198, f32[512,256]{1,0:T(8,128)S(1)} %slice.116.refs_0_, f32[512,256]{1,0:T(8,128)S(1)} %copy-done.19, ...), custom_call_target="tpu_custom_call" | custom-call | tf_op jit(solution)/shard_map/pallas_call | solution.py:70
  94.9 11.7 %collective-permute-done.5.refs_3_ = f32[512,256]{1,0:T(8,128)} collective-permute-done((f32[512,256]{1,0:T(8,128)}, f32[512,256]{1,0:T(8,128)}, u32[]{:S(2)}, u32[]{:S(2)}) %collective-permute-start.5) | collective-permute-done | bytes 524320 | tf_op jit(solution)/shard_map/ppermute | solution.py:16
  116.1 3.4 %copy-done.4 = bf16[2048,2048]{1,0:T(8,128)(2,1)S(1)} copy-done((bf16[2048,2048]{1,0:T(8,128)(2,1)S(1)}, bf16[2048,2048]{1,0:T(8,128)(2,1)}, u32[]{:S(2)}) %copy-start.4) | copy-done | bytes 8388632
  119.5 3.4 %copy-done.8 = bf16[2048,2048]{1,0:T(8,128)(2,1)S(1)} copy-done((bf16[2048,2048]{1,0:T(8,128)(2,1)S(1)}, bf16[2048,2048]{1,0:T(8,128)(2,1)}, u32[]{:S(2)}) %copy-start.8) | copy-done | bytes 8388632
  123.9 8.6 %shard_map.81 = (f32[2,512,256]{2,1,0:T(8,128)S(1)}, f32[2,512,256]{2,1,0:T(8,128)S(1)}) custom-call(s32[5]{0:T(128)S(1)} %pad_add_fusion.place, bf16[4,512,2048]{2,1,0:T(8,128)(2,1)S(1)} %bitcast.195, bf16[4,512,2048]{2,1,0:T(8,128)(2,1)S(1)} %bitcast.199, f32[512,256]{1,0:T(8,128)S(1)} %slice.90.refs_0_, f32[512,256]{1,0:T(8,128)S(1)} %collective-permute-done.3.refs_1_, ...), custom_call_target="tpu_custom_call" | custom-call | tf_op jit(solution)/shard_map/pallas_call | solution.py:70
  139.1 12.2 %collective-permute-done.10.refs_3_ = f32[512,256]{1,0:T(8,128)S(1)} collective-permute-done((f32[512,256]{1,0:T(8,128)S(1)}, f32[512,256]{1,0:T(8,128)S(1)}, u32[]{:S(2)}, u32[]{:S(2)}) %collective-permute-start.10) | collective-permute-done | bytes 524320 | tf_op jit(solution)/shard_map/ppermute | solution.py:16
  151.6 3.9 %collective-permute-start.19 = (f32[2,512,256]{2,1,0:T(8,128)S(1)}, f32[2,512,256]{2,1,0:T(8,128)S(1)}, u32[]{:S(2)}, u32[]{:S(2)}) collective-permute-start(f32[2,512,256]{2,1,0:T(8,128)S(1)} %pad_maximum_fusion.2), channel_id=1, source_target_pairs={{0,2},{5,7},{10,8},{15,13},{16,18},{21,23},{26,24},{31,29}} | collective-permute-start | bytes 3145736 | tf_op jit(solution)/shard_map/ppermute | solution.py:134
  157.0 8.1 %shard_map.82 = (f32[2,512,256]{2,1,0:T(8,128)}, f32[2,512,256]{2,1,0:T(8,128)S(1)}) custom-call(s32[5]{0:T(128)S(1)} %pad_add_fusion.place, bf16[4,512,2048]{2,1,0:T(8,128)(2,1)S(1)} %bitcast.196, bf16[4,512,2048]{2,1,0:T(8,128)(2,1)S(1)} %bitcast.200, f32[512,256]{1,0:T(8,128)S(1)} %slice.91.refs_0_, f32[512,256]{1,0:T(8,128)S(1)} %collective-permute-done.6.refs_1_, ...), custom_call_target="tpu_custom_call" | custom-call | tf_op jit(solution)/shard_map/pallas_call | solution.py:70
  166.4 10.8 %collective-permute-done.19 = f32[2,512,256]{2,1,0:T(8,128)S(1)} collective-permute-done((f32[2,512,256]{2,1,0:T(8,128)S(1)}, f32[2,512,256]{2,1,0:T(8,128)S(1)}, u32[]{:S(2)}, u32[]{:S(2)}) %collective-permute-start.19) | collective-permute-done | bytes 1048608 | tf_op jit(solution)/shard_map/ppermute | solution.py:134
  187.7 3.4 %copy-done.5 = bf16[2048,2048]{1,0:T(8,128)(2,1)S(1)} copy-done((bf16[2048,2048]{1,0:T(8,128)(2,1)S(1)}, bf16[2048,2048]{1,0:T(8,128)(2,1)}, u32[]{:S(2)}) %copy-start.5) | copy-done | bytes 8388632
  191.1 3.4 %copy-done.9 = bf16[2048,2048]{1,0:T(8,128)(2,1)S(1)} copy-done((bf16[2048,2048]{1,0:T(8,128)(2,1)S(1)}, bf16[2048,2048]{1,0:T(8,128)(2,1)}, u32[]{:S(2)}) %copy-start.9) | copy-done | bytes 8388632
  195.5 8.1 %shard_map.83 = (f32[2,512,256]{2,1,0:T(8,128)S(1)}, f32[2,512,256]{2,1,0:T(8,128)S(1)}) custom-call(s32[5]{0:T(128)S(1)} %pad_add_fusion.place, bf16[4,512,2048]{2,1,0:T(8,128)(2,1)S(1)} %bitcast.197, bf16[4,512,2048]{2,1,0:T(8,128)(2,1)S(1)} %bitcast.201, f32[512,256]{1,0:T(8,128)S(1)} %slice.94.refs_0_, f32[512,256]{1,0:T(8,128)S(1)} %collective-permute-done.11.refs_1_, ...), custom_call_target="tpu_custom_call" | custom-call | tf_op jit(solution)/shard_map/pallas_call | solution.py:70
  219.7 6.9 %collective-permute-done.25 = f32[1,512,256]{2,1,0:T(8,128)S(1)} collective-permute-done((f32[1,512,256]{2,1,0:T(8,128)S(1)}, f32[1,512,256]{2,1,0:T(8,128)S(1)}, u32[]{:S(2)}, u32[]{:S(2)}) %collective-permute-start.25) | collective-permute-done | bytes 524320 | tf_op jit(solution)/shard_map/ppermute | solution.py:16
  226.7 9.5 %collective-permute-done.27 = f32[1,512,256]{2,1,0:T(8,128)S(1)} collective-permute-done((f32[1,512,256]{2,1,0:T(8,128)S(1)}, f32[1,512,256]{2,1,0:T(8,128)S(1)}, u32[]{:S(2)}, u32[]{:S(2)}) %collective-permute-start.27) | collective-permute-done | bytes 524320 | tf_op jit(solution)/shard_map/ppermute | solution.py:16
  242.1 7.9 %collective-permute-done.29 = f32[1,1024,128]{2,1,0:T(8,128)} collective-permute-done((f32[1,1024,128]{2,1,0:T(8,128)}, f32[1,1024,128]{2,1,0:T(8,128)}, u32[]{:S(2)}, u32[]{:S(2)}) %collective-permute-start.29) | collective-permute-done | bytes 524320 | tf_op jit(solution)/shard_map/ppermute | solution.py:16
  (223 shorter events, 109.5 us)
Async XLA Ops:
  3.5 26.1 %collective-permute-start = (f32[512,256]{1,0:T(8,128)S(1)}, f32[512,256]{1,0:T(8,128)S(1)}, u32[]{:S(2)}, u32[]{:S(2)}) collective-permute-start(f32[512,256]{1,0:T(8,128)S(1)} %slice.116.refs_0_), channel_id=1, source_target_pairs={{0,4},{4,0},{8,12},{12,8},{1,5},{5,1},{9,13},{13,9},{2,6},{6,2},{1... | collective-permute-start | bytes 1572872 | tf_op jit(solution)/shard_map/ppermute | solution.py:16
  6.6 25.7 %collective-permute-start.1 = (f32[512,256]{1,0:T(8,128)S(1)}, f32[512,256]{1,0:T(8,128)}, u32[]{:S(2)}, u32[]{:S(2)}) collective-permute-start(f32[512,256]{1,0:T(8,128)S(1)} %slice.116.refs_0_), channel_id=1, source_target_pairs={{0,8},{4,12},{8,0},{12,4},{1,9},{5,13},{9,1},{13,5},{2,10},{6,14},... | collective-permute-start | bytes 1572872 | tf_op jit(solution)/shard_map/ppermute | solution.py:16
  32.3 25.5 %collective-permute-start.2 = (f32[512,256]{1,0:T(8,128)}, f32[512,256]{1,0:T(8,128)}, u32[]{:S(2)}, u32[]{:S(2)}) collective-permute-start(f32[512,256]{1,0:T(8,128)} %collective-permute-done.1.refs_2_), channel_id=1, source_target_pairs={{0,4},{4,0},{8,12},{12,8},{1,5},{5,1},{9,13},{13,9},{2,6},{6,2},{1... | collective-permute-start | bytes 1572872 | tf_op jit(solution)/shard_map/ppermute | solution.py:16
  32.8 33.6 %collective-permute-start.3 = (f32[512,256]{1,0:T(8,128)S(1)}, f32[512,256]{1,0:T(8,128)S(1)}, u32[]{:S(2)}, u32[]{:S(2)}) collective-permute-start(f32[512,256]{1,0:T(8,128)S(1)} %slice.90.refs_0_), channel_id=1, source_target_pairs={{0,4},{4,0},{8,12},{12,8},{1,5},{5,1},{9,13},{13,9},{2,6},{6,2},{1... | collective-permute-start | bytes 1572872 | tf_op jit(solution)/shard_map/ppermute | solution.py:16
  34.4 32.0 %collective-permute-start.4 = (f32[512,256]{1,0:T(8,128)S(1)}, f32[512,256]{1,0:T(8,128)S(1)}, u32[]{:S(2)}, u32[]{:S(2)}) collective-permute-start(f32[512,256]{1,0:T(8,128)S(1)} %slice.90.refs_0_), channel_id=1, source_target_pairs={{0,8},{4,12},{8,0},{12,4},{1,9},{5,13},{9,1},{13,5},{2,10},{6,14},... | collective-permute-start | bytes 1572872 | tf_op jit(solution)/shard_map/ppermute | solution.py:16
  68.8 23.3 %collective-permute-start.8 = (f32[2,512,256]{2,1,0:T(8,128)}, f32[2,512,256]{2,1,0:T(8,128)}, u32[]{:S(2)}, u32[]{:S(2)}) collective-permute-start(f32[2,512,256]{2,1,0:T(8,128)} %pad_maximum_fusion), channel_id=1, source_target_pairs={{0,2},{5,7},{10,8},{15,13},{16,18},{21,23},{26,24},{31,29}} | collective-permute-start | bytes 3145736 | tf_op jit(solution)/shard_map/ppermute | solution.py:134
  73.3 33.3 %collective-permute-start.6 = (f32[512,256]{1,0:T(8,128)S(1)}, f32[512,256]{1,0:T(8,128)S(1)}, u32[]{:S(2)}, u32[]{:S(2)}) collective-permute-start(f32[512,256]{1,0:T(8,128)S(1)} %slice.91.refs_0_), channel_id=1, source_target_pairs={{0,4},{4,0},{8,12},{12,8},{1,5},{5,1},{9,13},{13,9},{2,6},{6,2},{1... | collective-permute-start | bytes 1572872 | tf_op jit(solution)/shard_map/ppermute | solution.py:16
  73.3 33.3 %collective-permute-start.7 = (f32[512,256]{1,0:T(8,128)S(1)}, f32[512,256]{1,0:T(8,128)S(1)}, u32[]{:S(2)}, u32[]{:S(2)}) collective-permute-start(f32[512,256]{1,0:T(8,128)S(1)} %slice.91.refs_0_), channel_id=1, source_target_pairs={{0,8},{4,12},{8,0},{12,4},{1,9},{5,13},{9,1},{13,5},{2,10},{6,14},... | collective-permute-start | bytes 1572872 | tf_op jit(solution)/shard_map/ppermute | solution.py:16
  73.4 33.2 %collective-permute-start.5 = (f32[512,256]{1,0:T(8,128)}, f32[512,256]{1,0:T(8,128)}, u32[]{:S(2)}, u32[]{:S(2)}) collective-permute-start(f32[512,256]{1,0:T(8,128)} %copy-done.15), channel_id=1, source_target_pairs={{0,4},{4,0},{8,12},{12,8},{1,5},{5,1},{9,13},{13,9},{2,6},{6,2},{1... | collective-permute-start | bytes 1572872 | tf_op jit(solution)/shard_map/ppermute | solution.py:16
  106.6 29.8 %collective-permute-start.13 = (f32[2,512,256]{2,1,0:T(8,128)}, f32[2,512,256]{2,1,0:T(8,128)}, u32[]{:S(2)}, u32[]{:S(2)}) collective-permute-start(f32[2,512,256]{2,1,0:T(8,128)} %get-tuple-element.141), channel_id=1, source_target_pairs={{0,1},{1,0},{2,3},{3,2},{4,5},{5,4},{6,7},{7,6},{8,9},{9,8},{10,11... | collective-permute-start | bytes 3145736 | tf_op jit(solution)/shard_map/ppermute | solution.py:16
  108.9 28.9 %collective-permute-start.14 = (f32[2,512,256]{2,1,0:T(8,128)}, f32[2,512,256]{2,1,0:T(8,128)}, u32[]{:S(2)}, u32[]{:S(2)}) collective-permute-start(f32[2,512,256]{2,1,0:T(8,128)} %pad_maximum_fusion.1), channel_id=1, source_target_pairs={{0,2},{5,7},{10,8},{15,13},{16,18},{21,23},{26,24},{31,29}} | collective-permute-start | bytes 3145736 | tf_op jit(solution)/shard_map/ppermute | solution.py:134
  111.4 21.1 %collective-permute-start.9 = (f32[1,512,256]{2,1,0:T(8,128)}, f32[1,512,256]{2,1,0:T(8,128)}, u32[]{:S(2)}, u32[]{:S(2)}) collective-permute-start(f32[1,512,256]{2,1,0:T(8,128)} %bitcast.14), channel_id=1, source_target_pairs={{0,1},{2,3},{5,4},{7,6},{8,9},{10,11},{13,12},{15,14},{16,17},{18,... | collective-permute-start | bytes 1572872 | tf_op jit(solution)/shard_map/ppermute | solution.py:134
  114.9 36.5 %collective-permute-start.11 = (f32[512,256]{1,0:T(8,128)S(1)}, f32[512,256]{1,0:T(8,128)S(1)}, u32[]{:S(2)}, u32[]{:S(2)}) collective-permute-start(f32[512,256]{1,0:T(8,128)S(1)} %slice.94.refs_0_), channel_id=1, source_target_pairs={{0,4},{4,0},{8,12},{12,8},{1,5},{5,1},{9,13},{13,9},{2,6},{6,2},{1... | collective-permute-start | bytes 1572872 | tf_op jit(solution)/shard_map/ppermute | solution.py:16
  115.1 36.3 %collective-permute-start.12 = (f32[512,256]{1,0:T(8,128)S(1)}, f32[512,256]{1,0:T(8,128)S(1)}, u32[]{:S(2)}, u32[]{:S(2)}) collective-permute-start(f32[512,256]{1,0:T(8,128)S(1)} %slice.94.refs_0_), channel_id=1, source_target_pairs={{0,8},{4,12},{8,0},{12,4},{1,9},{5,13},{9,1},{13,5},{2,10},{6,14},... | collective-permute-start | bytes 1572872 | tf_op jit(solution)/shard_map/ppermute | solution.py:16
  132.5 18.8 %collective-permute-start.10 = (f32[512,256]{1,0:T(8,128)S(1)}, f32[512,256]{1,0:T(8,128)S(1)}, u32[]{:S(2)}, u32[]{:S(2)}) collective-permute-start(f32[512,256]{1,0:T(8,128)S(1)} %copy-done.12), channel_id=1, source_target_pairs={{0,4},{4,0},{8,12},{12,8},{1,5},{5,1},{9,13},{13,9},{2,6},{6,2},{1... | collective-permute-start | bytes 1572872 | tf_op jit(solution)/shard_map/ppermute | solution.py:16
  151.6 25.5 %collective-permute-start.19 = (f32[2,512,256]{2,1,0:T(8,128)S(1)}, f32[2,512,256]{2,1,0:T(8,128)S(1)}, u32[]{:S(2)}, u32[]{:S(2)}) collective-permute-start(f32[2,512,256]{2,1,0:T(8,128)S(1)} %pad_maximum_fusion.2), channel_id=1, source_target_pairs={{0,2},{5,7},{10,8},{15,13},{16,18},{21,23},{26,24},{31,29}} | collective-permute-start | bytes 3145736 | tf_op jit(solution)/shard_map/ppermute | solution.py:134
  156.9 21.4 %collective-permute-start.16 = (f32[512,256]{1,0:T(8,128)S(1)}, f32[512,256]{1,0:T(8,128)S(1)}, u32[]{:S(2)}, u32[]{:S(2)}) collective-permute-start(f32[512,256]{1,0:T(8,128)S(1)} %collective-permute-done.12.refs_2_), channel_id=1, source_target_pairs={{0,4},{4,0},{8,12},{12,8},{1,5},{5,1},{9,13},{13,9},{2,6},{6,2},{1... | collective-permute-start | bytes 1572872 | tf_op jit(solution)/shard_map/ppermute | solution.py:16
  179.2 24.4 %collective-permute-start.21 = (f32[1,512,256]{2,1,0:T(8,128)}, f32[1,512,256]{2,1,0:T(8,128)}, u32[]{:S(2)}, u32[]{:S(2)}) collective-permute-start(f32[1,512,256]{2,1,0:T(8,128)} %slice_bitcast_fusion.10), channel_id=1, source_target_pairs={{0,2},{1,3},{2,0},{3,1},{4,6},{5,7},{6,4},{7,5},{8,10},{9,11},{10,... | collective-permute-start | bytes 1572872 | tf_op jit(solution)/shard_map/ppermute | solution.py:16
  182.7 23.4 %collective-permute-start.23 = (f32[2,512,256]{2,1,0:T(8,128)}, f32[2,512,256]{2,1,0:T(8,128)}, u32[]{:S(2)}, u32[]{:S(2)}) collective-permute-start(f32[2,512,256]{2,1,0:T(8,128)} %pad_maximum_fusion.3), channel_id=1, source_target_pairs={{0,2},{5,7},{10,8},{15,13},{16,18},{21,23},{26,24},{31,29}} | collective-permute-start | bytes 3145736 | tf_op jit(solution)/shard_map/ppermute | solution.py:134
  185.6 19.2 %collective-permute-start.20 = (f32[1,512,256]{2,1,0:T(8,128)}, f32[1,512,256]{2,1,0:T(8,128)}, u32[]{:S(2)}, u32[]{:S(2)}) collective-permute-start(f32[1,512,256]{2,1,0:T(8,128)} %bitcast.30), channel_id=1, source_target_pairs={{0,1},{2,3},{5,4},{7,6},{8,9},{10,11},{13,12},{15,14},{16,17},{18,... | collective-permute-start | bytes 1572872 | tf_op jit(solution)/shard_map/ppermute | solution.py:134
  187.7 19.8 %collective-permute-start.22 = (f32[2,512,256]{2,1,0:T(8,128)}, f32[2,512,256]{2,1,0:T(8,128)}, u32[]{:S(2)}, u32[]{:S(2)}) collective-permute-start(f32[2,512,256]{2,1,0:T(8,128)} %get-tuple-element.178), channel_id=1, source_target_pairs={{0,1},{1,0},{2,3},{3,2},{4,5},{5,4},{6,7},{7,6},{8,9},{9,8},{10,11... | collective-permute-start | bytes 3145736 | tf_op jit(solution)/shard_map/ppermute | solution.py:16
  211.7 14.9 %collective-permute-start.25 = (f32[1,512,256]{2,1,0:T(8,128)S(1)}, f32[1,512,256]{2,1,0:T(8,128)S(1)}, u32[]{:S(2)}, u32[]{:S(2)}) collective-permute-start(f32[1,512,256]{2,1,0:T(8,128)S(1)} %slice_bitcast_fusion.6), channel_id=1, source_target_pairs={{0,2},{1,3},{2,0},{3,1},{4,6},{5,7},{6,4},{7,5},{8,10},{9,11},{10,... | collective-permute-start | bytes 1572872 | tf_op jit(solution)/shard_map/ppermute | solution.py:16
  216.7 19.6 %collective-permute-start.28 = (f32[1024,256]{1,0:T(8,128)S(1)}, f32[1024,256]{1,0:T(8,128)S(1)}, u32[]{:S(2)}, u32[]{:S(2)}) collective-permute-start(f32[1024,256]{1,0:T(8,128)S(1)} %pad_maximum_fusion.4), channel_id=1, source_target_pairs={{0,1},{1,0},{2,3},{3,2},{4,5},{5,4},{6,7},{7,6},{8,9},{9,8},{10,11... | collective-permute-start | bytes 3145736 | tf_op jit(solution)/shard_map/ppermute | solution.py:16
  217.0 19.2 %collective-permute-start.27 = (f32[1,512,256]{2,1,0:T(8,128)S(1)}, f32[1,512,256]{2,1,0:T(8,128)S(1)}, u32[]{:S(2)}, u32[]{:S(2)}) collective-permute-start(f32[1,512,256]{2,1,0:T(8,128)S(1)} %slice_bitcast_fusion.4), channel_id=1, source_target_pairs={{0,2},{1,3},{2,0},{3,1},{4,6},{5,7},{6,4},{7,5},{8,10},{9,11},{10,... | collective-permute-start | bytes 1572872 | tf_op jit(solution)/shard_map/ppermute | solution.py:16
  (57 other events, 547.0 us)

commit v5 on v4

--- a/solution.py
+++ b/solution.py
@@ -21,20 +21,31 @@
     return high, (values - high.astype(jnp.float32)).astype(jnp.bfloat16)
 
 
-def split_kernel(tile_ref, high_ref, low_ref):
-    high_ref[...], low_ref[...] = parts(tile_ref[...])
+def split_kernel(tile_ref, high_ref, low_ref, held, arrived):
+    step = held.shape[1]
+
+    def fetch(t):
+        return pltpu.make_async_copy(tile_ref.at[pl.ds(t * step, step)], held.at[t % 2], arrived.at[t % 2])
+
+    count = tile_ref.shape[0] // step
+    fetch(0).start()
+    for t in range(count):
+        if t + 1 < count:
+            fetch(t + 1).start()
+        fetch(t).wait()
+        rows = pl.ds(t * step, step)
+        high_ref[rows], low_ref[rows] = parts(held[t % 2])
 
 
 def split(tile):
     rows, width = tile.shape
     step = min(rows, 256)
-    block = pl.BlockSpec((step, width), lambda t: (t, 0))
     return pl.pallas_call(
         split_kernel,
-        grid=(rows // step,),
-        in_specs=[block],
-        out_specs=[block, block],
+        in_specs=[pl.BlockSpec(memory_space=pltpu.HBM)],
+        out_specs=[pl.BlockSpec(memory_space=pltpu.VMEM)] * 2,
         out_shape=[jax.ShapeDtypeStruct(tile.shape, jnp.bfloat16)] * 2,
+        scratch_shapes=[pltpu.VMEM((2, step, width), jnp.float32), pltpu.SemaphoreType.DMA((2,))],
         compiler_params=pltpu.CompilerParams(vmem_limit_bytes=16 * 2**20),
     )(tile)
 
@@ -172,7 +183,9 @@
             return [live[k, j] for j in range(rows_axis)]
 
         def multiply(k):
-            live["send", k], live["keep", k] = product(live["tiles"], blocks(k))
+            if "tiles" in live:
+                tiles[:] = live.pop("tiles")
+            live["send", k], live["keep", k] = product(tiles, blocks(k))
 
         def add_core(k):
             live["sums", k] = live.pop(("keep", k)) + swap(live.pop(("send", k)), "col", 1)
@@ -243,7 +256,7 @@
             for step in range(1, cols_axis.bit_length() - 1):
                 at(k + stages + step, lambda k=k: spread(k))
             at(k + stages + 1, lambda k=k: add_core(k))
-            at(k + stages + (2 if k + 1 < len(pieces) else 1), lambda k=k: add_rest(k))
+            at(k + stages + 1, lambda k=k: add_rest(k))
         end = len(pieces) + stages + 1
         at(end - 1, first_terms)
         at(end, first_sums, second_terms)

time: 277 us -> 277 us (level)
  waiting for transfers between devices: 101 us -> 105 us
    ppermute x28, waiting for transfers between devices: 90.6 us -> 103 us  [swap(): return lax.ppermute(block, axis, pairs)]
    ppermute x8, waiting for transfers between devices: 10.8 us -> 1.87 us  [spread_step(): moved = lax.ppermute(jnp.stack(held[bit:]), ('row', 'col'), pairs)]
    reshape x1 -> x4, other arithmetic: 0.14 us -> 3.09 us  [sum_scatter(): pairs = blocks.reshape((blocks.shape[0] // 2, 2) + blocks.shape[1:])]
    add x3 -> x0, other arithmetic: 2.91 us -> none  [add_core(): live.pop(('keep', k)) + swap(live.pop(('send', k)), 'col', 1)]
    unnamed x96 -> x88, local copies, waits for them, and re-layouts: 38 us -> 38.6 us
  transfers between devices with their start and end apart: 36 -> 36, of which waited for: 14 -> 16; matrix products, arithmetic and copies ran while one was open for 13% -> 13% of each run, Pallas kernels for 13% -> 13%
where the time goes in v5:
time: 277 us; the launch traced here: 276 us
  waiting for transfers between devices  105 us (38%)
  starting transfers between devices  47.3 us (17%)
  local copies, waits for them, and re-layouts  44.4 us (16%)
  Pallas kernels  37.1 us (13%)
  other arithmetic  26.1 us (9%)
  matrix products  14.1 us (5%)
    ppermute x28, waiting for transfers between devices, swap(): return lax.ppermute(block, axis, pairs)  103 us
    unnamed x88, local copies, waits for them, and re-layouts  38.6 us
    pallas_call x4, Pallas kernels, product(): pl.pallas_call(product_kernel, in_specs=[pl.BlockSpec(memory_space=pltpu....  33.6 us
    ppermute x28, starting transfers between devices, swap(): return lax.ppermute(block, axis, pairs)  25.4 us
    ppermute x8, starting transfers between devices, spread_step(): moved = lax.ppermute(jnp.stack(held[bit:]), ('row', 'col'), pairs)  22 us
    dot_general x7, matrix products, dot_tn(): return lax.dot_general(a, b, (((0,), (0,)), ((), ())), precision=precision)  10.9 us
    select_n x8, other arithmetic, spread_step(): return [jnp.where(offset & bit != 0, moved[j], held[j]) for j in range(bit)]  8.51 us
    another operation x4, other arithmetic, spread_step(): moved = lax.ppermute(jnp.stack(held[bit:]), ('row', 'col'), pairs)  5.77 us
  transfers between devices with their start and end apart: 36, of which 16 were waited for; matrix products, arithmetic and copies ran while one was open for 13% of the time, Pallas kernels for 13%

profile of v5, /device:TPU:0, one launch (start us, length us, event | category | flops | bytes accessed | tf_op | source)
XLA Modules:
  0.0 275.7 jit_solution(8938380451998512635)
XLA Ops:
  9.2 5.8 %copy-done.10 = f32[2048,2048]{1,0:T(8,128)S(1)} copy-done((f32[2048,2048]{1,0:T(8,128)S(1)}, f32[2048,2048]{1,0:T(8,128)}, u32[]{:S(2)}) %copy-start.10) | copy-done | bytes 16777240
  15.0 3.5 %shard_map.79 = (bf16[2048,2048]{1,0:T(8,128)(2,1)S(1)}, bf16[2048,2048]{1,0:T(8,128)(2,1)S(1)}) custom-call(f32[2048,2048]{1,0:T(8,128)S(1)} %copy-done.10), custom_call_target="tpu_custom_call" | custom-call | tf_op jit(solution)/shard_map/pallas_call | solution.py:43
  18.5 3.3 %copy-done.2 = bf16[2048,2048]{1,0:T(8,128)(2,1)} copy-done((bf16[2048,2048]{1,0:T(8,128)(2,1)}, bf16[2048,2048]{1,0:T(8,128)(2,1)S(1)}, u32[]{:S(2)}) %copy-start.2) | copy-done | bytes 8388632
  38.1 19.7 %collective-permute-done.2.refs_3_ = f32[512,256]{1,0:T(8,128)} collective-permute-done((f32[512,256]{1,0:T(8,128)}, f32[512,256]{1,0:T(8,128)}, u32[]{:S(2)}, u32[]{:S(2)}) %collective-permute-start.2) | collective-permute-done | bytes 524320 | tf_op jit(solution)/shard_map/ppermute | solution.py:16
  57.8 8.6 %collective-permute-done.3.refs_1_ = f32[512,256]{1,0:T(8,128)S(1)} collective-permute-done((f32[512,256]{1,0:T(8,128)S(1)}, f32[512,256]{1,0:T(8,128)S(1)}, u32[]{:S(2)}, u32[]{:S(2)}) %collective-permute-start.3) | collective-permute-done | bytes 524320 | tf_op jit(solution)/shard_map/ppermute | solution.py:16
  68.8 4.4 %collective-permute-start.8 = (f32[2,512,256]{2,1,0:T(8,128)}, f32[2,512,256]{2,1,0:T(8,128)}, u32[]{:S(2)}, u32[]{:S(2)}) collective-permute-start(f32[2,512,256]{2,1,0:T(8,128)} %pad_maximum_fusion), channel_id=1, source_target_pairs={{0,2},{5,7},{10,8},{15,13},{16,18},{21,23},{26,24},{31,29}} | collective-permute-start | bytes 3145736 | tf_op jit(solution)/shard_map/ppermute | solution.py:145
  75.5 3.4 %copy-done.3 = bf16[2048,2048]{1,0:T(8,128)(2,1)S(1)} copy-done((bf16[2048,2048]{1,0:T(8,128)(2,1)S(1)}, bf16[2048,2048]{1,0:T(8,128)(2,1)}, u32[]{:S(2)}) %copy-start.3) | copy-done | bytes 8388632
  78.9 3.4 %copy-done.7 = bf16[2048,2048]{1,0:T(8,128)(2,1)S(1)} copy-done((bf16[2048,2048]{1,0:T(8,128)(2,1)S(1)}, bf16[2048,2048]{1,0:T(8,128)(2,1)}, u32[]{:S(2)}) %copy-start.7) | copy-done | bytes 8388632
  83.3 8.7 %shard_map.80 = (f32[2,512,256]{2,1,0:T(8,128)}, f32[2,512,256]{2,1,0:T(8,128)S(1)}) custom-call(s32[5]{0:T(128)S(1)} %pad_add_fusion.place, bf16[4,512,2048]{2,1,0:T(8,128)(2,1)S(1)} %bitcast.197, bf16[4,512,2048]{2,1,0:T(8,128)(2,1)S(1)} %bitcast.201, f32[512,256]{1,0:T(8,128)S(1)} %slice.116.refs_0_, f32[512,256]{1,0:T(8,128)S(1)} %copy-done.19, ...), custom_call_target="tpu_custom_call" | custom-call | tf_op jit(solution)/shard_map/pallas_call | solution.py:81
  94.9 11.7 %collective-permute-done.5.refs_3_ = f32[512,256]{1,0:T(8,128)} collective-permute-done((f32[512,256]{1,0:T(8,128)}, f32[512,256]{1,0:T(8,128)}, u32[]{:S(2)}, u32[]{:S(2)}) %collective-permute-start.5) | collective-permute-done | bytes 524320 | tf_op jit(solution)/shard_map/ppermute | solution.py:16
  116.3 3.4 %copy-done.4 = bf16[2048,2048]{1,0:T(8,128)(2,1)S(1)} copy-done((bf16[2048,2048]{1,0:T(8,128)(2,1)S(1)}, bf16[2048,2048]{1,0:T(8,128)(2,1)}, u32[]{:S(2)}) %copy-start.4) | copy-done | bytes 8388632
  119.6 3.4 %copy-done.8 = bf16[2048,2048]{1,0:T(8,128)(2,1)S(1)} copy-done((bf16[2048,2048]{1,0:T(8,128)(2,1)S(1)}, bf16[2048,2048]{1,0:T(8,128)(2,1)}, u32[]{:S(2)}) %copy-start.8) | copy-done | bytes 8388632
  124.1 8.7 %shard_map.81 = (f32[2,512,256]{2,1,0:T(8,128)S(1)}, f32[2,512,256]{2,1,0:T(8,128)S(1)}) custom-call(s32[5]{0:T(128)S(1)} %pad_add_fusion.place, bf16[4,512,2048]{2,1,0:T(8,128)(2,1)S(1)} %bitcast.198, bf16[4,512,2048]{2,1,0:T(8,128)(2,1)S(1)} %bitcast.202, f32[512,256]{1,0:T(8,128)S(1)} %slice.90.refs_0_, f32[512,256]{1,0:T(8,128)S(1)} %collective-permute-done.3.refs_1_, ...), custom_call_target="tpu_custom_call" | custom-call | tf_op jit(solution)/shard_map/pallas_call | solution.py:81
  139.9 10.3 %collective-permute-done.14 = f32[1,512,256]{2,1,0:T(8,128)S(1)} collective-permute-done((f32[1,512,256]{2,1,0:T(8,128)S(1)}, f32[1,512,256]{2,1,0:T(8,128)S(1)}, u32[]{:S(2)}, u32[]{:S(2)}) %collective-permute-start.14) | collective-permute-done | bytes 524320 | tf_op jit(solution)/shard_map/ppermute | solution.py:16
  150.6 4.0 %collective-permute-start.20 = (f32[2,512,256]{2,1,0:T(8,128)S(1)}, f32[2,512,256]{2,1,0:T(8,128)S(1)}, u32[]{:S(2)}, u32[]{:S(2)}) collective-permute-start(f32[2,512,256]{2,1,0:T(8,128)S(1)} %pad_maximum_fusion.2), channel_id=1, source_target_pairs={{0,2},{5,7},{10,8},{15,13},{16,18},{21,23},{26,24},{31,29}} | collective-permute-start | bytes 3145736 | tf_op jit(solution)/shard_map/ppermute | solution.py:145
  156.0 8.1 %shard_map.82 = (f32[2,512,256]{2,1,0:T(8,128)}, f32[2,512,256]{2,1,0:T(8,128)S(1)}) custom-call(s32[5]{0:T(128)S(1)} %pad_add_fusion.place, bf16[4,512,2048]{2,1,0:T(8,128)(2,1)S(1)} %bitcast.199, bf16[4,512,2048]{2,1,0:T(8,128)(2,1)S(1)} %bitcast.203, f32[512,256]{1,0:T(8,128)S(1)} %slice.91.refs_0_, f32[512,256]{1,0:T(8,128)S(1)} %collective-permute-done.6.refs_1_, ...), custom_call_target="tpu_custom_call" | custom-call | tf_op jit(solution)/shard_map/pallas_call | solution.py:81
  168.9 10.2 %collective-permute-done.19 = f32[1,512,256]{2,1,0:T(8,128)S(1)} collective-permute-done((f32[1,512,256]{2,1,0:T(8,128)S(1)}, f32[1,512,256]{2,1,0:T(8,128)S(1)}, u32[]{:S(2)}, u32[]{:S(2)}) %collective-permute-start.19) | collective-permute-done | bytes 524320 | tf_op jit(solution)/shard_map/ppermute | solution.py:16
  181.1 4.3 %collective-permute-start.24 = (f32[2,512,256]{2,1,0:T(8,128)}, f32[2,512,256]{2,1,0:T(8,128)}, u32[]{:S(2)}, u32[]{:S(2)}) collective-permute-start(f32[2,512,256]{2,1,0:T(8,128)} %pad_maximum_fusion.3), channel_id=1, source_target_pairs={{0,2},{5,7},{10,8},{15,13},{16,18},{21,23},{26,24},{31,29}} | collective-permute-start | bytes 3145736 | tf_op jit(solution)/shard_map/ppermute | solution.py:145
  186.7 3.4 %copy-done.5 = bf16[2048,2048]{1,0:T(8,128)(2,1)S(1)} copy-done((bf16[2048,2048]{1,0:T(8,128)(2,1)S(1)}, bf16[2048,2048]{1,0:T(8,128)(2,1)}, u32[]{:S(2)}) %copy-start.5) | copy-done | bytes 8388632
  190.1 3.4 %copy-done.9 = bf16[2048,2048]{1,0:T(8,128)(2,1)S(1)} copy-done((bf16[2048,2048]{1,0:T(8,128)(2,1)S(1)}, bf16[2048,2048]{1,0:T(8,128)(2,1)}, u32[]{:S(2)}) %copy-start.9) | copy-done | bytes 8388632
  194.5 8.1 %shard_map.83 = (f32[2,512,256]{2,1,0:T(8,128)S(1)}, f32[2,512,256]{2,1,0:T(8,128)S(1)}) custom-call(s32[5]{0:T(128)S(1)} %pad_add_fusion.place, bf16[4,512,2048]{2,1,0:T(8,128)(2,1)S(1)} %bitcast.200, bf16[4,512,2048]{2,1,0:T(8,128)(2,1)S(1)} %bitcast.204, f32[512,256]{1,0:T(8,128)S(1)} %slice.94.refs_0_, f32[512,256]{1,0:T(8,128)S(1)} %collective-permute-done.11.refs_1_, ...), custom_call_target="tpu_custom_call" | custom-call | tf_op jit(solution)/shard_map/pallas_call | solution.py:81
  205.6 10.2 %collective-permute-done.23 = f32[1,512,256]{2,1,0:T(8,128)S(1)} collective-permute-done((f32[1,512,256]{2,1,0:T(8,128)S(1)}, f32[1,512,256]{2,1,0:T(8,128)S(1)}, u32[]{:S(2)}, u32[]{:S(2)}) %collective-permute-start.23) | collective-permute-done | bytes 524320 | tf_op jit(solution)/shard_map/ppermute | solution.py:16
  225.6 10.4 %collective-permute-done.27 = f32[1,512,256]{2,1,0:T(8,128)S(1)} collective-permute-done((f32[1,512,256]{2,1,0:T(8,128)S(1)}, f32[1,512,256]{2,1,0:T(8,128)S(1)}, u32[]{:S(2)}, u32[]{:S(2)}) %collective-permute-start.27) | collective-permute-done | bytes 524320 | tf_op jit(solution)/shard_map/ppermute | solution.py:16
  242.8 7.8 %collective-permute-done.29 = f32[1,1024,128]{2,1,0:T(8,128)} collective-permute-done((f32[1,1024,128]{2,1,0:T(8,128)}, f32[1,1024,128]{2,1,0:T(8,128)}, u32[]{:S(2)}, u32[]{:S(2)}) %collective-permute-start.29) | collective-permute-done | bytes 524320 | tf_op jit(solution)/shard_map/ppermute | solution.py:16
  (215 shorter events, 106.0 us)
Async XLA Ops:
  3.5 26.1 %collective-permute-start = (f32[512,256]{1,0:T(8,128)S(1)}, f32[512,256]{1,0:T(8,128)S(1)}, u32[]{:S(2)}, u32[]{:S(2)}) collective-permute-start(f32[512,256]{1,0:T(8,128)S(1)} %slice.116.refs_0_), channel_id=1, source_target_pairs={{0,4},{4,0},{8,12},{12,8},{1,5},{5,1},{9,13},{13,9},{2,6},{6,2},{1... | collective-permute-start | bytes 1572872 | tf_op jit(solution)/shard_map/ppermute | solution.py:16
  6.6 25.7 %collective-permute-start.1 = (f32[512,256]{1,0:T(8,128)S(1)}, f32[512,256]{1,0:T(8,128)}, u32[]{:S(2)}, u32[]{:S(2)}) collective-permute-start(f32[512,256]{1,0:T(8,128)S(1)} %slice.116.refs_0_), channel_id=1, source_target_pairs={{0,8},{4,12},{8,0},{12,4},{1,9},{5,13},{9,1},{13,5},{2,10},{6,14},... | collective-permute-start | bytes 1572872 | tf_op jit(solution)/shard_map/ppermute | solution.py:16
  32.3 25.5 %collective-permute-start.2 = (f32[512,256]{1,0:T(8,128)}, f32[512,256]{1,0:T(8,128)}, u32[]{:S(2)}, u32[]{:S(2)}) collective-permute-start(f32[512,256]{1,0:T(8,128)} %collective-permute-done.1.refs_2_), channel_id=1, source_target_pairs={{0,4},{4,0},{8,12},{12,8},{1,5},{5,1},{9,13},{13,9},{2,6},{6,2},{1... | collective-permute-start | bytes 1572872 | tf_op jit(solution)/shard_map/ppermute | solution.py:16
  32.8 33.6 %collective-permute-start.3 = (f32[512,256]{1,0:T(8,128)S(1)}, f32[512,256]{1,0:T(8,128)S(1)}, u32[]{:S(2)}, u32[]{:S(2)}) collective-permute-start(f32[512,256]{1,0:T(8,128)S(1)} %slice.90.refs_0_), channel_id=1, source_target_pairs={{0,4},{4,0},{8,12},{12,8},{1,5},{5,1},{9,13},{13,9},{2,6},{6,2},{1... | collective-permute-start | bytes 1572872 | tf_op jit(solution)/shard_map/ppermute | solution.py:16
  34.4 32.0 %collective-permute-start.4 = (f32[512,256]{1,0:T(8,128)S(1)}, f32[512,256]{1,0:T(8,128)S(1)}, u32[]{:S(2)}, u32[]{:S(2)}) collective-permute-start(f32[512,256]{1,0:T(8,128)S(1)} %slice.90.refs_0_), channel_id=1, source_target_pairs={{0,8},{4,12},{8,0},{12,4},{1,9},{5,13},{9,1},{13,5},{2,10},{6,14},... | collective-permute-start | bytes 1572872 | tf_op jit(solution)/shard_map/ppermute | solution.py:16
  68.8 23.3 %collective-permute-start.8 = (f32[2,512,256]{2,1,0:T(8,128)}, f32[2,512,256]{2,1,0:T(8,128)}, u32[]{:S(2)}, u32[]{:S(2)}) collective-permute-start(f32[2,512,256]{2,1,0:T(8,128)} %pad_maximum_fusion), channel_id=1, source_target_pairs={{0,2},{5,7},{10,8},{15,13},{16,18},{21,23},{26,24},{31,29}} | collective-permute-start | bytes 3145736 | tf_op jit(solution)/shard_map/ppermute | solution.py:145
  73.3 33.3 %collective-permute-start.6 = (f32[512,256]{1,0:T(8,128)S(1)}, f32[512,256]{1,0:T(8,128)S(1)}, u32[]{:S(2)}, u32[]{:S(2)}) collective-permute-start(f32[512,256]{1,0:T(8,128)S(1)} %slice.91.refs_0_), channel_id=1, source_target_pairs={{0,4},{4,0},{8,12},{12,8},{1,5},{5,1},{9,13},{13,9},{2,6},{6,2},{1... | collective-permute-start | bytes 1572872 | tf_op jit(solution)/shard_map/ppermute | solution.py:16
  73.3 33.3 %collective-permute-start.7 = (f32[512,256]{1,0:T(8,128)S(1)}, f32[512,256]{1,0:T(8,128)S(1)}, u32[]{:S(2)}, u32[]{:S(2)}) collective-permute-start(f32[512,256]{1,0:T(8,128)S(1)} %slice.91.refs_0_), channel_id=1, source_target_pairs={{0,8},{4,12},{8,0},{12,4},{1,9},{5,13},{9,1},{13,5},{2,10},{6,14},... | collective-permute-start | bytes 1572872 | tf_op jit(solution)/shard_map/ppermute | solution.py:16
  73.4 33.2 %collective-permute-start.5 = (f32[512,256]{1,0:T(8,128)}, f32[512,256]{1,0:T(8,128)}, u32[]{:S(2)}, u32[]{:S(2)}) collective-permute-start(f32[512,256]{1,0:T(8,128)} %copy-done.15), channel_id=1, source_target_pairs={{0,4},{4,0},{8,12},{12,8},{1,5},{5,1},{9,13},{13,9},{2,6},{6,2},{1... | collective-permute-start | bytes 1572872 | tf_op jit(solution)/shard_map/ppermute | solution.py:16
  106.6 26.2 %collective-permute-start.13 = (f32[2,512,256]{2,1,0:T(8,128)}, f32[2,512,256]{2,1,0:T(8,128)}, u32[]{:S(2)}, u32[]{:S(2)}) collective-permute-start(f32[2,512,256]{2,1,0:T(8,128)} %get-tuple-element.133), channel_id=1, source_target_pairs={{0,1},{1,0},{2,3},{3,2},{4,5},{5,4},{6,7},{7,6},{8,9},{9,8},{10,11... | collective-permute-start | bytes 3145736 | tf_op jit(solution)/shard_map/ppermute | solution.py:16
  108.9 29.7 %collective-permute-start.15 = (f32[2,512,256]{2,1,0:T(8,128)}, f32[2,512,256]{2,1,0:T(8,128)}, u32[]{:S(2)}, u32[]{:S(2)}) collective-permute-start(f32[2,512,256]{2,1,0:T(8,128)} %pad_maximum_fusion.1), channel_id=1, source_target_pairs={{0,2},{5,7},{10,8},{15,13},{16,18},{21,23},{26,24},{31,29}} | collective-permute-start | bytes 3145736 | tf_op jit(solution)/shard_map/ppermute | solution.py:145
  112.3 38.0 %collective-permute-start.11 = (f32[512,256]{1,0:T(8,128)S(1)}, f32[512,256]{1,0:T(8,128)S(1)}, u32[]{:S(2)}, u32[]{:S(2)}) collective-permute-start(f32[512,256]{1,0:T(8,128)S(1)} %slice.94.refs_0_), channel_id=1, source_target_pairs={{0,4},{4,0},{8,12},{12,8},{1,5},{5,1},{9,13},{13,9},{2,6},{6,2},{1... | collective-permute-start | bytes 1572872 | tf_op jit(solution)/shard_map/ppermute | solution.py:16
  113.4 36.9 %collective-permute-start.12 = (f32[512,256]{1,0:T(8,128)S(1)}, f32[512,256]{1,0:T(8,128)S(1)}, u32[]{:S(2)}, u32[]{:S(2)}) collective-permute-start(f32[512,256]{1,0:T(8,128)S(1)} %slice.94.refs_0_), channel_id=1, source_target_pairs={{0,8},{4,12},{8,0},{12,4},{1,9},{5,13},{9,1},{13,5},{2,10},{6,14},... | collective-permute-start | bytes 1572872 | tf_op jit(solution)/shard_map/ppermute | solution.py:16
  113.4 20.9 %collective-permute-start.9 = (f32[1,512,256]{2,1,0:T(8,128)}, f32[1,512,256]{2,1,0:T(8,128)S(1)}, u32[]{:S(2)}, u32[]{:S(2)}) collective-permute-start(f32[1,512,256]{2,1,0:T(8,128)} %bitcast.218), channel_id=1, source_target_pairs={{0,1},{2,3},{5,4},{7,6},{8,9},{10,11},{13,12},{15,14},{16,17},{18,... | collective-permute-start | bytes 1572872 | tf_op jit(solution)/shard_map/ppermute | solution.py:145
  132.8 17.5 %collective-permute-start.10 = (f32[512,256]{1,0:T(8,128)S(1)}, f32[512,256]{1,0:T(8,128)S(1)}, u32[]{:S(2)}, u32[]{:S(2)}) collective-permute-start(f32[512,256]{1,0:T(8,128)S(1)} %copy-done.12), channel_id=1, source_target_pairs={{0,4},{4,0},{8,12},{12,8},{1,5},{5,1},{9,13},{13,9},{2,6},{6,2},{1... | collective-permute-start | bytes 1572872 | tf_op jit(solution)/shard_map/ppermute | solution.py:16
  134.4 15.9 %collective-permute-start.14 = (f32[1,512,256]{2,1,0:T(8,128)S(1)}, f32[1,512,256]{2,1,0:T(8,128)S(1)}, u32[]{:S(2)}, u32[]{:S(2)}) collective-permute-start(f32[1,512,256]{2,1,0:T(8,128)S(1)} %slice_bitcast_fusion.16), channel_id=1, source_target_pairs={{0,2},{1,3},{2,0},{3,1},{4,6},{5,7},{6,4},{7,5},{8,10},{9,11},{10,... | collective-permute-start | bytes 1572872 | tf_op jit(solution)/shard_map/ppermute | solution.py:16
  150.6 17.2 %collective-permute-start.20 = (f32[2,512,256]{2,1,0:T(8,128)S(1)}, f32[2,512,256]{2,1,0:T(8,128)S(1)}, u32[]{:S(2)}, u32[]{:S(2)}) collective-permute-start(f32[2,512,256]{2,1,0:T(8,128)S(1)} %pad_maximum_fusion.2), channel_id=1, source_target_pairs={{0,2},{5,7},{10,8},{15,13},{16,18},{21,23},{26,24},{31,29}} | collective-permute-start | bytes 3145736 | tf_op jit(solution)/shard_map/ppermute | solution.py:145
  155.9 24.1 %collective-permute-start.17 = (f32[512,256]{1,0:T(8,128)S(1)}, f32[512,256]{1,0:T(8,128)S(1)}, u32[]{:S(2)}, u32[]{:S(2)}) collective-permute-start(f32[512,256]{1,0:T(8,128)S(1)} %collective-permute-done.12.refs_2_), channel_id=1, source_target_pairs={{0,4},{4,0},{8,12},{12,8},{1,5},{5,1},{9,13},{13,9},{2,6},{6,2},{1... | collective-permute-start | bytes 1572872 | tf_op jit(solution)/shard_map/ppermute | solution.py:16
  165.1 14.1 %collective-permute-start.19 = (f32[1,512,256]{2,1,0:T(8,128)S(1)}, f32[1,512,256]{2,1,0:T(8,128)S(1)}, u32[]{:S(2)}, u32[]{:S(2)}) collective-permute-start(f32[1,512,256]{2,1,0:T(8,128)S(1)} %slice_bitcast_fusion.12), channel_id=1, source_target_pairs={{0,2},{1,3},{2,0},{3,1},{4,6},{5,7},{6,4},{7,5},{8,10},{9,11},{10,... | collective-permute-start | bytes 1572872 | tf_op jit(solution)/shard_map/ppermute | solution.py:16
  180.0 22.6 %collective-permute-start.22 = (f32[2,512,256]{2,1,0:T(8,128)}, f32[2,512,256]{2,1,0:T(8,128)}, u32[]{:S(2)}, u32[]{:S(2)}) collective-permute-start(f32[2,512,256]{2,1,0:T(8,128)} %get-tuple-element.166), channel_id=1, source_target_pairs={{0,1},{1,0},{2,3},{3,2},{4,5},{5,4},{6,7},{7,6},{8,9},{9,8},{10,11... | collective-permute-start | bytes 3145736 | tf_op jit(solution)/shard_map/ppermute | solution.py:16
  181.1 23.1 %collective-permute-start.24 = (f32[2,512,256]{2,1,0:T(8,128)}, f32[2,512,256]{2,1,0:T(8,128)}, u32[]{:S(2)}, u32[]{:S(2)}) collective-permute-start(f32[2,512,256]{2,1,0:T(8,128)} %pad_maximum_fusion.3), channel_id=1, source_target_pairs={{0,2},{5,7},{10,8},{15,13},{16,18},{21,23},{26,24},{31,29}} | collective-permute-start | bytes 3145736 | tf_op jit(solution)/shard_map/ppermute | solution.py:145
  185.4 18.8 %collective-permute-start.21 = (f32[1,512,256]{2,1,0:T(8,128)}, f32[1,512,256]{2,1,0:T(8,128)S(1)}, u32[]{:S(2)}, u32[]{:S(2)}) collective-permute-start(f32[1,512,256]{2,1,0:T(8,128)} %bitcast.34), channel_id=1, source_target_pairs={{0,1},{2,3},{5,4},{7,6},{8,9},{10,11},{13,12},{15,14},{16,17},{18,... | collective-permute-start | bytes 1572872 | tf_op jit(solution)/shard_map/ppermute | solution.py:145
  221.3 14.7 %collective-permute-start.28 = (f32[1024,256]{1,0:T(8,128)S(1)}, f32[1024,256]{1,0:T(8,128)S(1)}, u32[]{:S(2)}, u32[]{:S(2)}) collective-permute-start(f32[1024,256]{1,0:T(8,128)S(1)} %pad_maximum_fusion.4), channel_id=1, source_target_pairs={{0,1},{1,0},{2,3},{3,2},{4,5},{5,4},{6,7},{7,6},{8,9},{9,8},{10,11... | collective-permute-start | bytes 3145736 | tf_op jit(solution)/shard_map/ppermute | solution.py:16
  222.1 13.9 %collective-permute-start.27 = (f32[1,512,256]{2,1,0:T(8,128)S(1)}, f32[1,512,256]{2,1,0:T(8,128)S(1)}, u32[]{:S(2)}, u32[]{:S(2)}) collective-permute-start(f32[1,512,256]{2,1,0:T(8,128)S(1)} %slice_bitcast_fusion.4), channel_id=1, source_target_pairs={{0,2},{1,3},{2,0},{3,1},{4,6},{5,7},{6,4},{7,5},{8,10},{9,11},{10,... | collective-permute-start | bytes 1572872 | tf_op jit(solution)/shard_map/ppermute | solution.py:16
  (53 other events, 514.2 us)

commit v6 on v4

--- a/solution.py
+++ b/solution.py
@@ -35,14 +35,21 @@
         in_specs=[block],
         out_specs=[block, block],
         out_shape=[jax.ShapeDtypeStruct(tile.shape, jnp.bfloat16)] * 2,
-        compiler_params=pltpu.CompilerParams(vmem_limit_bytes=16 * 2**20),
+        compiler_params=pltpu.CompilerParams(vmem_limit_bytes=24 * 2**20),
     )(tile)
 
 
 def product_kernel(place, tile_high_ref, tile_low_ref, *refs):
-    *block_refs, send_ref, keep_ref, high_ref, low_ref = refs
+    *block_refs, send_ref, keep_ref, high_ref, low_ref, held_high, held_low, arrived = refs
     height = block_refs[0].shape[0]
     half = send_ref.shape[0]
+
+    def fetch(i, run):
+        slot = i % 2
+        run(pltpu.make_async_copy(tile_high_ref.at[place[1 + i]], held_high.at[slot], arrived.at[0, slot]))
+        run(pltpu.make_async_copy(tile_low_ref.at[place[1 + i]], held_low.at[slot], arrived.at[1, slot]))
+
+    fetch(0, lambda copy: copy.start())
     for j, block_ref in enumerate(block_refs):
         rows = pl.ds(pl.multiple_of((place[0] ^ j) * height, height), height)
         high_ref[rows], low_ref[rows] = parts(block_ref[...])
@@ -50,10 +57,14 @@
     def times(a, b_ref):
         return jnp.dot(a, b_ref[...], preferred_element_type=jnp.float32)
 
-    for first, out_ref in ((1, send_ref), (1 + half, keep_ref)):
+    for base, out_ref in ((0, send_ref), (half, keep_ref)):
         def step(i, carry):
-            chunk = place[first + i]
-            high, low = tile_high_ref[chunk], tile_low_ref[chunk]
+            @pl.when(base + i + 1 < 2 * half)
+            def _():
+                fetch(base + i + 1, lambda copy: copy.start())
+
+            fetch(base + i, lambda copy: copy.wait())
+            high, low = held_high[(base + i) % 2], held_low[(base + i) % 2]
             out_ref[i] = times(high, high_ref) + (times(high, low_ref) + times(low, high_ref))
             return carry
 
@@ -66,14 +77,16 @@
     half = count // 2
     chunks = lax.axis_index("col") ^ jnp.concatenate([2 * jnp.arange(half) + 1, 2 * jnp.arange(half)])
     place = jnp.concatenate([lax.axis_index("row")[None], chunks]).astype(jnp.int32)
-    vmem = pl.BlockSpec(memory_space=pltpu.VMEM)
+    vmem, hbm = (pl.BlockSpec(memory_space=space) for space in (pltpu.VMEM, pltpu.HBM))
     return pl.pallas_call(
         product_kernel,
-        in_specs=[pl.BlockSpec(memory_space=pltpu.SMEM)] + [vmem] * (2 + len(blocks)),
+        in_specs=[pl.BlockSpec(memory_space=pltpu.SMEM), hbm, hbm] + [vmem] * len(blocks),
         out_specs=[vmem, vmem],
         out_shape=[jax.ShapeDtypeStruct((half, out_rows, columns), jnp.float32)] * 2,
-        scratch_shapes=[pltpu.VMEM((width, columns), jnp.bfloat16)] * 2,
-        compiler_params=pltpu.CompilerParams(vmem_limit_bytes=16 * 2**20),
+        scratch_shapes=[pltpu.VMEM((width, columns), jnp.bfloat16)] * 2
+        + [pltpu.VMEM((2, out_rows, width), jnp.bfloat16)] * 2
+        + [pltpu.SemaphoreType.DMA((2, 2))],
+        compiler_params=pltpu.CompilerParams(vmem_limit_bytes=24 * 2**20),
     )(place, *tiles, *blocks)
 
 
@@ -172,7 +185,12 @@
             return [live[k, j] for j in range(rows_axis)]
 
         def multiply(k):
-            live["send", k], live["keep", k] = product(live["tiles"], blocks(k))
+            if "tiles" in live:
+                tiles[:] = live.pop("tiles")
+            gathered = blocks(k)
+            if ("sums", k - 1) in live:
+                live["sums", k - 1], gathered = lax.optimization_barrier((live["sums", k - 1], gathered))
+            live["send", k], live["keep", k] = product(tiles, gathered)
 
         def add_core(k):
             live["sums", k] = live.pop(("keep", k)) + swap(live.pop(("send", k)), "col", 1)
@@ -239,11 +257,14 @@
 
         at(1, link_terms)
         for k in range(len(pieces)):
-            at(k + stages, lambda k=k: collect(k), lambda k=k: multiply(k))
+            at(k + stages, lambda k=k: collect(k))
             for step in range(1, cols_axis.bit_length() - 1):
                 at(k + stages + step, lambda k=k: spread(k))
+        for k in range(len(pieces)):
             at(k + stages + 1, lambda k=k: add_core(k))
-            at(k + stages + (2 if k + 1 < len(pieces) else 1), lambda k=k: add_rest(k))
+            at(k + stages, lambda k=k: multiply(k))
+        for k in range(len(pieces)):
+            at(k + stages + 1, lambda k=k: add_rest(k))
         end = len(pieces) + stages + 1
         at(end - 1, first_terms)
         at(end, first_sums, second_terms)

time: 277 us -> 269 us (0.971)
  Pallas kernels: 35.9 us -> 47.5 us
  local copies, waits for them, and re-layouts: 44.8 us -> 34.6 us
  starting transfers between devices: 49.6 us -> 45 us
  matrix products: 14.1 us -> 11.3 us
    unnamed x96 -> x70, local copies, waits for them, and re-layouts: 38 us -> 30.6 us
    pallas_call x1, Pallas kernels: 2.45 us -> 8.65 us  [split(): pl.pallas_call(split_kernel, grid=(rows // step,), in_specs=[block], out_...]
    ppermute x8, waiting for transfers between devices: 10.8 us -> 4.98 us  [spread_step(): moved = lax.ppermute(jnp.stack(held[bit:]), ('row', 'col'), pairs)]
    pallas_call x4, Pallas kernels: 33.5 us -> 38.9 us  [product(): pl.pallas_call(product_kernel, in_specs=[pl.BlockSpec(memory_space=pltpu....]
    ppermute x28, starting transfers between devices: 27.5 us -> 23 us  [swap(): return lax.ppermute(block, axis, pairs)]
    dot_general x7, matrix products: 10.9 us -> 8.09 us  [dot_tn(): return lax.dot_general(a, b, (((0,), (0,)), ((), ())), precision=precision)]
  transfers between devices with their start and end apart: 36 -> 36, of which waited for: 14 -> 20; matrix products, arithmetic and copies ran while one was open for 13% -> 14% of each run, Pallas kernels for 13% -> 18%
where the time goes in v6:
time: 269 us; the launch traced here: 268 us
  waiting for transfers between devices  98.3 us (37%)
  Pallas kernels  47.5 us (18%)
  starting transfers between devices  45 us (17%)
  local copies, waits for them, and re-layouts  34.6 us (13%)
  other arithmetic  29.9 us (11%)
  matrix products  11.3 us (4%)
    ppermute x28, waiting for transfers between devices, swap(): return lax.ppermute(block, axis, pairs)  93.3 us
    pallas_call x4, Pallas kernels, product(): pl.pallas_call(product_kernel, in_specs=[pl.BlockSpec(memory_space=pltpu....  38.9 us
    unnamed x70, local copies, waits for them, and re-layouts  30.6 us
    ppermute x28, starting transfers between devices, swap(): return lax.ppermute(block, axis, pairs)  23 us
    ppermute x8, starting transfers between devices, spread_step(): moved = lax.ppermute(jnp.stack(held[bit:]), ('row', 'col'), pairs)  22 us
    select_n x8, other arithmetic, spread_step(): return [jnp.where(offset & bit != 0, moved[j], held[j]) for j in range(bit)]  10.5 us
    pallas_call x1, Pallas kernels, split(): pl.pallas_call(split_kernel, grid=(rows // step,), in_specs=[block], out_...  8.65 us
    dot_general x7, matrix products, dot_tn(): return lax.dot_general(a, b, (((0,), (0,)), ((), ())), precision=precision)  8.09 us
  transfers between devices with their start and end apart: 36, of which 20 were waited for; matrix products, arithmetic and copies ran while one was open for 14% of the time, Pallas kernels for 18%

profile of v6, /device:TPU:0, one launch (start us, length us, event | category | flops | bytes accessed | tf_op | source)
XLA Modules:
  0.0 268.1 jit_solution(12800469221694346934)
XLA Ops:
  9.2 8.6 %shard_map.79 = (bf16[2048,2048]{1,0:T(8,128)(2,1)S(1)}, bf16[2048,2048]{1,0:T(8,128)(2,1)S(1)}) custom-call(f32[2048,2048]{1,0:T(8,128)} %tile_ref.1), custom_call_target="tpu_custom_call" | custom-call | tf_op jit(solution)/shard_map/pallas_call | solution.py:32
  17.9 3.3 %copy-done.2 = bf16[2048,2048]{1,0:T(8,128)(2,1)} copy-done((bf16[2048,2048]{1,0:T(8,128)(2,1)}, bf16[2048,2048]{1,0:T(8,128)(2,1)S(1)}, u32[]{:S(2)}) %copy-start.2) | copy-done | bytes 8388632
  38.0 19.5 %collective-permute-done.3.refs_1_ = f32[512,256]{1,0:T(8,128)S(1)} collective-permute-done((f32[512,256]{1,0:T(8,128)S(1)}, f32[512,256]{1,0:T(8,128)S(1)}, u32[]{:S(2)}, u32[]{:S(2)}) %collective-permute-start.3) | collective-permute-done | bytes 524320 | tf_op jit(solution)/shard_map/ppermute | solution.py:16
  57.6 8.8 %collective-permute-done.2.refs_3_ = f32[512,256]{1,0:T(8,128)} collective-permute-done((f32[512,256]{1,0:T(8,128)}, f32[512,256]{1,0:T(8,128)}, u32[]{:S(2)}, u32[]{:S(2)}) %collective-permute-start.2) | collective-permute-done | bytes 524320 | tf_op jit(solution)/shard_map/ppermute | solution.py:16
  68.7 4.4 %collective-permute-start.8 = (f32[2,512,256]{2,1,0:T(8,128)}, f32[2,512,256]{2,1,0:T(8,128)}, u32[]{:S(2)}, u32[]{:S(2)}) collective-permute-start(f32[2,512,256]{2,1,0:T(8,128)} %pad_maximum_fusion), channel_id=1, source_target_pairs={{0,2},{5,7},{10,8},{15,13},{16,18},{21,23},{26,24},{31,29}} | collective-permute-start | bytes 3145736 | tf_op jit(solution)/shard_map/ppermute | solution.py:147
  75.4 3.4 %copy-done.3 = bf16[2048,2048]{1,0:T(8,128)(2,1)S(1)} copy-done((bf16[2048,2048]{1,0:T(8,128)(2,1)S(1)}, bf16[2048,2048]{1,0:T(8,128)(2,1)}, u32[]{:S(2)}) %copy-start.3) | copy-done | bytes 8388632
  78.7 3.4 %copy-done.7 = bf16[2048,2048]{1,0:T(8,128)(2,1)S(1)} copy-done((bf16[2048,2048]{1,0:T(8,128)(2,1)S(1)}, bf16[2048,2048]{1,0:T(8,128)(2,1)}, u32[]{:S(2)}) %copy-start.7) | copy-done | bytes 8388632
  83.2 10.0 %shard_map.80 = (f32[2,512,256]{2,1,0:T(8,128)}, f32[2,512,256]{2,1,0:T(8,128)S(1)}) custom-call(s32[5]{0:T(128)S(1)} %pad_add_fusion.place, bf16[4,512,2048]{2,1,0:T(8,128)(2,1)S(1)} %bitcast.194, bf16[4,512,2048]{2,1,0:T(8,128)(2,1)S(1)} %bitcast.198, f32[512,256]{1,0:T(8,128)S(1)} %slice.116.refs_0_, f32[512,256]{1,0:T(8,128)S(1)} %copy-done.16, ...), custom_call_target="tpu_custom_call" | custom-call | tf_op jit(solution)/shard_map/pallas_call | solution.py:81
  98.6 8.7 %collective-permute-done.5.refs_3_ = f32[512,256]{1,0:T(8,128)} collective-permute-done((f32[512,256]{1,0:T(8,128)}, f32[512,256]{1,0:T(8,128)}, u32[]{:S(2)}, u32[]{:S(2)}) %collective-permute-start.5) | collective-permute-done | bytes 524320 | tf_op jit(solution)/shard_map/ppermute | solution.py:16
  123.2 3.4 %copy-done.4 = bf16[2048,2048]{1,0:T(8,128)(2,1)S(1)} copy-done((bf16[2048,2048]{1,0:T(8,128)(2,1)S(1)}, bf16[2048,2048]{1,0:T(8,128)(2,1)}, u32[]{:S(2)}) %copy-start.4) | copy-done | bytes 8388632
  126.6 3.4 %copy-done.8 = bf16[2048,2048]{1,0:T(8,128)(2,1)S(1)} copy-done((bf16[2048,2048]{1,0:T(8,128)(2,1)S(1)}, bf16[2048,2048]{1,0:T(8,128)(2,1)}, u32[]{:S(2)}) %copy-start.8) | copy-done | bytes 8388632
  129.9 9.8 %shard_map.81 = (f32[2,512,256]{2,1,0:T(8,128)S(1)}, f32[2,512,256]{2,1,0:T(8,128)S(1)}) custom-call(s32[5]{0:T(128)S(1)} %pad_add_fusion.place, bf16[4,512,2048]{2,1,0:T(8,128)(2,1)S(1)} %bitcast.195, bf16[4,512,2048]{2,1,0:T(8,128)(2,1)S(1)} %bitcast.199, f32[512,256]{1,0:T(8,128)S(1)} %slice.90.refs_0_, f32[512,256]{1,0:T(8,128)S(1)} %copy-done.11, ...), custom_call_target="tpu_custom_call" | custom-call | tf_op jit(solution)/shard_map/pallas_call | solution.py:81
  142.2 9.5 %collective-permute-done.10.refs_3_ = f32[512,256]{1,0:T(8,128)S(1)} collective-permute-done((f32[512,256]{1,0:T(8,128)}, f32[512,256]{1,0:T(8,128)S(1)}, u32[]{:S(2)}, u32[]{:S(2)}) %collective-permute-start.10) | collective-permute-done | bytes 524320 | tf_op jit(solution)/shard_map/ppermute | solution.py:16
  158.4 9.8 %shard_map.82 = (f32[2,512,256]{2,1,0:T(8,128)}, f32[2,512,256]{2,1,0:T(8,128)S(1)}) custom-call(s32[5]{0:T(128)S(1)} %pad_add_fusion.place, bf16[4,512,2048]{2,1,0:T(8,128)(2,1)S(1)} %bitcast.196, bf16[4,512,2048]{2,1,0:T(8,128)(2,1)S(1)} %bitcast.200, f32[512,256]{1,0:T(8,128)S(1)} %slice.91.refs_0_, f32[512,256]{1,0:T(8,128)S(1)} %collective-permute-done.6.refs_1_, ...), custom_call_target="tpu_custom_call" | custom-call | tf_op jit(solution)/shard_map/pallas_call | solution.py:81
  168.2 3.8 %collective-permute-done.18 = f32[2,512,256]{2,1,0:T(8,128)S(1)} collective-permute-done((f32[2,512,256]{2,1,0:T(8,128)S(1)}, f32[2,512,256]{2,1,0:T(8,128)S(1)}, u32[]{:S(2)}, u32[]{:S(2)}) %collective-permute-start.18) | collective-permute-done | bytes 1048608 | tf_op jit(solution)/shard_map/ppermute | solution.py:147
  173.2 4.5 %collective-permute-done.20 = f32[1,512,256]{2,1,0:T(8,128)S(1)} collective-permute-done((f32[1,512,256]{2,1,0:T(8,128)S(1)}, f32[1,512,256]{2,1,0:T(8,128)S(1)}, u32[]{:S(2)}, u32[]{:S(2)}) %collective-permute-start.20) | collective-permute-done | bytes 524320 | tf_op jit(solution)/shard_map/ppermute | solution.py:16
  179.7 5.4 %collective-permute-start.22 = (f32[2,512,256]{2,1,0:T(8,128)}, f32[2,512,256]{2,1,0:T(8,128)}, u32[]{:S(2)}, u32[]{:S(2)}) collective-permute-start(f32[2,512,256]{2,1,0:T(8,128)} %pad_maximum_fusion.3), channel_id=1, source_target_pairs={{0,2},{5,7},{10,8},{15,13},{16,18},{21,23},{26,24},{31,29}} | collective-permute-start | bytes 3145736 | tf_op jit(solution)/shard_map/ppermute | solution.py:147
  189.9 3.4 %copy-done.5 = bf16[2048,2048]{1,0:T(8,128)(2,1)S(1)} copy-done((bf16[2048,2048]{1,0:T(8,128)(2,1)S(1)}, bf16[2048,2048]{1,0:T(8,128)(2,1)}, u32[]{:S(2)}) %copy-start.5) | copy-done | bytes 8388632
  193.2 3.4 %copy-done.9 = bf16[2048,2048]{1,0:T(8,128)(2,1)S(1)} copy-done((bf16[2048,2048]{1,0:T(8,128)(2,1)S(1)}, bf16[2048,2048]{1,0:T(8,128)(2,1)}, u32[]{:S(2)}) %copy-start.9) | copy-done | bytes 8388632
  196.6 9.3 %shard_map.83 = (f32[2,512,256]{2,1,0:T(8,128)S(1)}, f32[2,512,256]{2,1,0:T(8,128)S(1)}) custom-call(s32[5]{0:T(128)S(1)} %pad_add_fusion.place, bf16[4,512,2048]{2,1,0:T(8,128)(2,1)S(1)} %bitcast.197, bf16[4,512,2048]{2,1,0:T(8,128)(2,1)S(1)} %bitcast.201, f32[512,256]{1,0:T(8,128)S(1)} %slice.94.refs_0_, f32[512,256]{1,0:T(8,128)S(1)} %collective-permute-done.11.refs_1_, ...), custom_call_target="tpu_custom_call" | custom-call | tf_op jit(solution)/shard_map/pallas_call | solution.py:81
  218.1 10.2 %collective-permute-done.27 = f32[1,512,256]{2,1,0:T(8,128)S(1)} collective-permute-done((f32[1,512,256]{2,1,0:T(8,128)S(1)}, f32[1,512,256]{2,1,0:T(8,128)S(1)}, u32[]{:S(2)}, u32[]{:S(2)}) %collective-permute-start.27) | collective-permute-done | bytes 524320 | tf_op jit(solution)/shard_map/ppermute | solution.py:16
  237.0 10.1 %collective-permute-done.29 = f32[1,1024,128]{2,1,0:T(8,128)} collective-permute-done((f32[1,1024,128]{2,1,0:T(8,128)}, f32[1,1024,128]{2,1,0:T(8,128)}, u32[]{:S(2)}, u32[]{:S(2)}) %collective-permute-start.29) | collective-permute-done | bytes 524320 | tf_op jit(solution)/shard_map/ppermute | solution.py:16
  252.4 4.7 %collective-permute-done.30 = f32[2,2,128,128]{3,2,1,0:T(8,128)S(1)} collective-permute-done((f32[2,2,128,128]{3,2,1,0:T(8,128)S(1)}, f32[2,2,128,128]{3,2,1,0:T(8,128)S(1)}, u32[]{:S(2)}, u32[]{:S(2)}) %collective-permute-start.30) | collective-permute-done | bytes 262176 | tf_op jit(solution)/shard_map/ppermute | solution.py:16
  261.5 4.5 %collective-permute-done.31 = f32[1,2,128,128]{3,2,1,0:T(8,128)S(1)} collective-permute-done((f32[1,2,128,128]{3,2,1,0:T(8,128)S(1)}, f32[1,2,128,128]{3,2,1,0:T(8,128)S(1)}, u32[]{:S(2)}, u32[]{:S(2)}) %collective-permute-start.31) | collective-permute-done | bytes 131104 | tf_op jit(solution)/shard_map/ppermute | solution.py:16
  (197 shorter events, 101.3 us)
Async XLA Ops:
  3.5 26.1 %collective-permute-start = (f32[512,256]{1,0:T(8,128)S(1)}, f32[512,256]{1,0:T(8,128)S(1)}, u32[]{:S(2)}, u32[]{:S(2)}) collective-permute-start(f32[512,256]{1,0:T(8,128)S(1)} %slice.116.refs_0_), channel_id=1, source_target_pairs={{0,4},{4,0},{8,12},{12,8},{1,5},{5,1},{9,13},{13,9},{2,6},{6,2},{1... | collective-permute-start | bytes 1572872 | tf_op jit(solution)/shard_map/ppermute | solution.py:16
  6.6 25.7 %collective-permute-start.1 = (f32[512,256]{1,0:T(8,128)S(1)}, f32[512,256]{1,0:T(8,128)}, u32[]{:S(2)}, u32[]{:S(2)}) collective-permute-start(f32[512,256]{1,0:T(8,128)S(1)} %slice.116.refs_0_), channel_id=1, source_target_pairs={{0,8},{4,12},{8,0},{12,4},{1,9},{5,13},{9,1},{13,5},{2,10},{6,14},... | collective-permute-start | bytes 1572872 | tf_op jit(solution)/shard_map/ppermute | solution.py:16
  32.3 25.3 %collective-permute-start.3 = (f32[512,256]{1,0:T(8,128)S(1)}, f32[512,256]{1,0:T(8,128)S(1)}, u32[]{:S(2)}, u32[]{:S(2)}) collective-permute-start(f32[512,256]{1,0:T(8,128)S(1)} %slice.90.refs_0_), channel_id=1, source_target_pairs={{0,4},{4,0},{8,12},{12,8},{1,5},{5,1},{9,13},{13,9},{2,6},{6,2},{1... | collective-permute-start | bytes 1572872 | tf_op jit(solution)/shard_map/ppermute | solution.py:16
  32.8 24.8 %collective-permute-start.4 = (f32[512,256]{1,0:T(8,128)S(1)}, f32[512,256]{1,0:T(8,128)S(1)}, u32[]{:S(2)}, u32[]{:S(2)}) collective-permute-start(f32[512,256]{1,0:T(8,128)S(1)} %slice.90.refs_0_), channel_id=1, source_target_pairs={{0,8},{4,12},{8,0},{12,4},{1,9},{5,13},{9,1},{13,5},{2,10},{6,14},... | collective-permute-start | bytes 1572872 | tf_op jit(solution)/shard_map/ppermute | solution.py:16
  35.4 31.0 %collective-permute-start.2 = (f32[512,256]{1,0:T(8,128)}, f32[512,256]{1,0:T(8,128)}, u32[]{:S(2)}, u32[]{:S(2)}) collective-permute-start(f32[512,256]{1,0:T(8,128)} %collective-permute-done.1.refs_2_), channel_id=1, source_target_pairs={{0,4},{4,0},{8,12},{12,8},{1,5},{5,1},{9,13},{13,9},{2,6},{6,2},{1... | collective-permute-start | bytes 1572872 | tf_op jit(solution)/shard_map/ppermute | solution.py:16
  68.7 24.5 %collective-permute-start.8 = (f32[2,512,256]{2,1,0:T(8,128)}, f32[2,512,256]{2,1,0:T(8,128)}, u32[]{:S(2)}, u32[]{:S(2)}) collective-permute-start(f32[2,512,256]{2,1,0:T(8,128)} %pad_maximum_fusion), channel_id=1, source_target_pairs={{0,2},{5,7},{10,8},{15,13},{16,18},{21,23},{26,24},{31,29}} | collective-permute-start | bytes 3145736 | tf_op jit(solution)/shard_map/ppermute | solution.py:147
  73.1 25.4 %collective-permute-start.6 = (f32[512,256]{1,0:T(8,128)S(1)}, f32[512,256]{1,0:T(8,128)S(1)}, u32[]{:S(2)}, u32[]{:S(2)}) collective-permute-start(f32[512,256]{1,0:T(8,128)S(1)} %slice.91.refs_0_), channel_id=1, source_target_pairs={{0,4},{4,0},{8,12},{12,8},{1,5},{5,1},{9,13},{13,9},{2,6},{6,2},{1... | collective-permute-start | bytes 1572872 | tf_op jit(solution)/shard_map/ppermute | solution.py:16
  73.2 25.4 %collective-permute-start.7 = (f32[512,256]{1,0:T(8,128)S(1)}, f32[512,256]{1,0:T(8,128)}, u32[]{:S(2)}, u32[]{:S(2)}) collective-permute-start(f32[512,256]{1,0:T(8,128)S(1)} %slice.91.refs_0_), channel_id=1, source_target_pairs={{0,8},{4,12},{8,0},{12,4},{1,9},{5,13},{9,1},{13,5},{2,10},{6,14},... | collective-permute-start | bytes 1572872 | tf_op jit(solution)/shard_map/ppermute | solution.py:16
  73.3 34.1 %collective-permute-start.5 = (f32[512,256]{1,0:T(8,128)}, f32[512,256]{1,0:T(8,128)}, u32[]{:S(2)}, u32[]{:S(2)}) collective-permute-start(f32[512,256]{1,0:T(8,128)} %copy-done.12), channel_id=1, source_target_pairs={{0,4},{4,0},{8,12},{12,8},{1,5},{5,1},{9,13},{13,9},{2,6},{6,2},{1... | collective-permute-start | bytes 1572872 | tf_op jit(solution)/shard_map/ppermute | solution.py:16
  109.4 30.3 %collective-permute-start.13 = (f32[2,512,256]{2,1,0:T(8,128)}, f32[2,512,256]{2,1,0:T(8,128)}, u32[]{:S(2)}, u32[]{:S(2)}) collective-permute-start(f32[2,512,256]{2,1,0:T(8,128)} %pad_maximum_fusion.1), channel_id=1, source_target_pairs={{0,2},{5,7},{10,8},{15,13},{16,18},{21,23},{26,24},{31,29}} | collective-permute-start | bytes 3145736 | tf_op jit(solution)/shard_map/ppermute | solution.py:147
  115.4 26.7 %collective-permute-start.11 = (f32[512,256]{1,0:T(8,128)S(1)}, f32[512,256]{1,0:T(8,128)S(1)}, u32[]{:S(2)}, u32[]{:S(2)}) collective-permute-start(f32[512,256]{1,0:T(8,128)S(1)} %slice.94.refs_0_), channel_id=1, source_target_pairs={{0,4},{4,0},{8,12},{12,8},{1,5},{5,1},{9,13},{13,9},{2,6},{6,2},{1... | collective-permute-start | bytes 1572872 | tf_op jit(solution)/shard_map/ppermute | solution.py:16
  115.4 26.8 %collective-permute-start.12 = (f32[512,256]{1,0:T(8,128)S(1)}, f32[512,256]{1,0:T(8,128)S(1)}, u32[]{:S(2)}, u32[]{:S(2)}) collective-permute-start(f32[512,256]{1,0:T(8,128)S(1)} %slice.94.refs_0_), channel_id=1, source_target_pairs={{0,8},{4,12},{8,0},{12,4},{1,9},{5,13},{9,1},{13,5},{2,10},{6,14},... | collective-permute-start | bytes 1572872 | tf_op jit(solution)/shard_map/ppermute | solution.py:16
  115.5 36.2 %collective-permute-start.10 = (f32[512,256]{1,0:T(8,128)}, f32[512,256]{1,0:T(8,128)S(1)}, u32[]{:S(2)}, u32[]{:S(2)}) collective-permute-start(f32[512,256]{1,0:T(8,128)} %collective-permute-done.7.refs_2_), channel_id=1, source_target_pairs={{0,4},{4,0},{8,12},{12,8},{1,5},{5,1},{9,13},{13,9},{2,6},{6,2},{1... | collective-permute-start | bytes 1572872 | tf_op jit(solution)/shard_map/ppermute | solution.py:16
  119.2 21.9 %collective-permute-start.15 = (f32[1,512,256]{2,1,0:T(8,128)S(1)}, f32[1,512,256]{2,1,0:T(8,128)S(1)}, u32[]{:S(2)}, u32[]{:S(2)}) collective-permute-start(f32[1,512,256]{2,1,0:T(8,128)S(1)} %slice_bitcast_fusion.14), channel_id=1, source_target_pairs={{0,2},{1,3},{2,0},{3,1},{4,6},{5,7},{6,4},{7,5},{8,10},{9,11},{10,... | collective-permute-start | bytes 1572872 | tf_op jit(solution)/shard_map/ppermute | solution.py:16
  152.9 19.2 %collective-permute-start.18 = (f32[2,512,256]{2,1,0:T(8,128)S(1)}, f32[2,512,256]{2,1,0:T(8,128)S(1)}, u32[]{:S(2)}, u32[]{:S(2)}) collective-permute-start(f32[2,512,256]{2,1,0:T(8,128)S(1)} %pad_maximum_fusion.2), channel_id=1, source_target_pairs={{0,2},{5,7},{10,8},{15,13},{16,18},{21,23},{26,24},{31,29}} | collective-permute-start | bytes 3145736 | tf_op jit(solution)/shard_map/ppermute | solution.py:147
  156.0 22.6 %collective-permute-start.17 = (f32[512,256]{1,0:T(8,128)S(1)}, f32[512,256]{1,0:T(8,128)S(1)}, u32[]{:S(2)}, u32[]{:S(2)}) collective-permute-start(f32[512,256]{1,0:T(8,128)S(1)} %collective-permute-done.12.refs_2_), channel_id=1, source_target_pairs={{0,4},{4,0},{8,12},{12,8},{1,5},{5,1},{9,13},{13,9},{2,6},{6,2},{1... | collective-permute-start | bytes 1572872 | tf_op jit(solution)/shard_map/ppermute | solution.py:16
  156.3 21.4 %collective-permute-start.20 = (f32[1,512,256]{2,1,0:T(8,128)S(1)}, f32[1,512,256]{2,1,0:T(8,128)S(1)}, u32[]{:S(2)}, u32[]{:S(2)}) collective-permute-start(f32[1,512,256]{2,1,0:T(8,128)S(1)} %slice_bitcast_fusion.10), channel_id=1, source_target_pairs={{0,2},{1,3},{2,0},{3,1},{4,6},{5,7},{6,4},{7,5},{8,10},{9,11},{10,... | collective-permute-start | bytes 1572872 | tf_op jit(solution)/shard_map/ppermute | solution.py:16
  179.7 26.2 %collective-permute-start.22 = (f32[2,512,256]{2,1,0:T(8,128)}, f32[2,512,256]{2,1,0:T(8,128)}, u32[]{:S(2)}, u32[]{:S(2)}) collective-permute-start(f32[2,512,256]{2,1,0:T(8,128)} %pad_maximum_fusion.3), channel_id=1, source_target_pairs={{0,2},{5,7},{10,8},{15,13},{16,18},{21,23},{26,24},{31,29}} | collective-permute-start | bytes 3145736 | tf_op jit(solution)/shard_map/ppermute | solution.py:147
  188.7 19.2 %collective-permute-start.24 = (f32[1,512,256]{2,1,0:T(8,128)S(1)}, f32[1,512,256]{2,1,0:T(8,128)S(1)}, u32[]{:S(2)}, u32[]{:S(2)}) collective-permute-start(f32[1,512,256]{2,1,0:T(8,128)S(1)} %slice_bitcast_fusion.6), channel_id=1, source_target_pairs={{0,2},{1,3},{2,0},{3,1},{4,6},{5,7},{6,4},{7,5},{8,10},{9,11},{10,... | collective-permute-start | bytes 1572872 | tf_op jit(solution)/shard_map/ppermute | solution.py:16
  213.6 14.7 %collective-permute-start.28 = (f32[1024,256]{1,0:T(8,128)S(1)}, f32[1024,256]{1,0:T(8,128)S(1)}, u32[]{:S(2)}, u32[]{:S(2)}) collective-permute-start(f32[1024,256]{1,0:T(8,128)S(1)} %pad_maximum_fusion.4), channel_id=1, source_target_pairs={{0,1},{1,0},{2,3},{3,2},{4,5},{5,4},{6,7},{7,6},{8,9},{9,8},{10,11... | collective-permute-start | bytes 3145736 | tf_op jit(solution)/shard_map/ppermute | solution.py:16
  214.4 13.9 %collective-permute-start.27 = (f32[1,512,256]{2,1,0:T(8,128)S(1)}, f32[1,512,256]{2,1,0:T(8,128)S(1)}, u32[]{:S(2)}, u32[]{:S(2)}) collective-permute-start(f32[1,512,256]{2,1,0:T(8,128)S(1)} %slice_bitcast_fusion.4), channel_id=1, source_target_pairs={{0,2},{1,3},{2,0},{3,1},{4,6},{5,7},{6,4},{7,5},{8,10},{9,11},{10,... | collective-permute-start | bytes 1572872 | tf_op jit(solution)/shard_map/ppermute | solution.py:16
  232.1 15.0 %collective-permute-start.29 = (f32[1,1024,128]{2,1,0:T(8,128)}, f32[1,1024,128]{2,1,0:T(8,128)}, u32[]{:S(2)}, u32[]{:S(2)}) collective-permute-start(f32[1,1024,128]{2,1,0:T(8,128)} %slice_bitcast_fusion.2), channel_id=1, source_target_pairs={{0,2},{1,3},{2,0},{3,1},{4,6},{5,7},{6,4},{7,5},{8,10},{9,11},{10,... | collective-permute-start | bytes 1572872 | tf_op jit(solution)/shard_map/ppermute | solution.py:16
  236.6 15.7 %collective-permute-start.33 = (f32[1,512,128]{2,1,0:T(8,128)S(1)}, f32[1,512,128]{2,1,0:T(8,128)S(1)}, u32[]{:S(2)}, u32[]{:S(2)}) collective-permute-start(f32[1,512,128]{2,1,0:T(8,128)S(1)} %bitcast.222), channel_id=1, source_target_pairs={{0,2},{1,3},{2,0},{3,1},{4,6},{5,7},{6,4},{7,5},{8,10},{9,11},{10,... | collective-permute-start | bytes 786440 | tf_op jit(solution)/shard_map/ppermute | solution.py:16
  257.1 8.9 %collective-permute-start.31 = (f32[1,2,128,128]{3,2,1,0:T(8,128)S(1)}, f32[1,2,128,128]{3,2,1,0:T(8,128)S(1)}, u32[]{:S(2)}, u32[]{:S(2)}) collective-permute-start(f32[1,2,128,128]{3,2,1,0:T(8,128)S(1)} %constant_dynamic-slice_fusion.9), channel_id=1, source_target_pairs={{0,8},{4,12},{8,0},{12,4},{1,9},{5,13},{9,1},{13,5},{2,10},{6,14},... | collective-permute-start | bytes 393224 | tf_op jit(solution)/shard_map/ppermute | solution.py:16
  (44 other events, 344.9 us)

commit v7 on v6

--- a/solution.py
+++ b/solution.py
@@ -21,33 +21,35 @@
     return high, (values - high.astype(jnp.float32)).astype(jnp.bfloat16)
 
 
-def split_kernel(tile_ref, high_ref, low_ref):
-    high_ref[...], low_ref[...] = parts(tile_ref[...])
+PARTS = 6
+
+
+def split_kernel(tile_ref, parts_ref):
+    parts_ref[0], parts_ref[1] = parts(tile_ref[...])
 
 
 def split(tile):
     rows, width = tile.shape
     step = min(rows, 256)
-    block = pl.BlockSpec((step, width), lambda t: (t, 0))
     return pl.pallas_call(
         split_kernel,
         grid=(rows // step,),
-        in_specs=[block],
-        out_specs=[block, block],
-        out_shape=[jax.ShapeDtypeStruct(tile.shape, jnp.bfloat16)] * 2,
+        in_specs=[pl.BlockSpec((step, width), lambda t: (t, 0))],
+        out_specs=pl.BlockSpec((2, step, width), lambda t: (0, t, 0)),
+        out_shape=jax.ShapeDtypeStruct((PARTS, rows, width), jnp.bfloat16),
         compiler_params=pltpu.CompilerParams(vmem_limit_bytes=24 * 2**20),
     )(tile)
 
 
-def product_kernel(place, tile_high_ref, tile_low_ref, *refs):
-    *block_refs, send_ref, keep_ref, high_ref, low_ref, held_high, held_low, arrived = refs
+def product_kernel(place, tile_ref, *refs):
+    *block_refs, send_ref, keep_ref, high_ref, low_ref, held, arrived = refs
     height = block_refs[0].shape[0]
     half = send_ref.shape[0]
 
     def fetch(i, run):
         slot = i % 2
-        run(pltpu.make_async_copy(tile_high_ref.at[place[1 + i]], held_high.at[slot], arrived.at[0, slot]))
-        run(pltpu.make_async_copy(tile_low_ref.at[place[1 + i]], held_low.at[slot], arrived.at[1, slot]))
+        for part in range(2):
+            run(pltpu.make_async_copy(tile_ref.at[part, place[1 + i]], held.at[part, slot], arrived.at[part, slot]))
 
     fetch(0, lambda copy: copy.start())
     for j, block_ref in enumerate(block_refs):
@@ -64,15 +66,15 @@
                 fetch(base + i + 1, lambda copy: copy.start())
 
             fetch(base + i, lambda copy: copy.wait())
-            high, low = held_high[(base + i) % 2], held_low[(base + i) % 2]
+            high, low = held[0, (base + i) % 2], held[1, (base + i) % 2]
             out_ref[i] = times(high, high_ref) + (times(high, low_ref) + times(low, high_ref))
             return carry
 
         lax.fori_loop(0, half, step, 0)
 
 
-def product(tiles, blocks):
-    count, out_rows, width = tiles[0].shape
+def product(tile, blocks):
+    _, count, out_rows, width = tile.shape
     columns = blocks[0].shape[1]
     half = count // 2
     chunks = lax.axis_index("col") ^ jnp.concatenate([2 * jnp.arange(half) + 1, 2 * jnp.arange(half)])
@@ -80,14 +82,13 @@
     vmem, hbm = (pl.BlockSpec(memory_space=space) for space in (pltpu.VMEM, pltpu.HBM))
     return pl.pallas_call(
         product_kernel,
-        in_specs=[pl.BlockSpec(memory_space=pltpu.SMEM), hbm, hbm] + [vmem] * len(blocks),
+        in_specs=[pl.BlockSpec(memory_space=pltpu.SMEM), hbm] + [vmem] * len(blocks),
         out_specs=[vmem, vmem],
         out_shape=[jax.ShapeDtypeStruct((half, out_rows, columns), jnp.float32)] * 2,
         scratch_shapes=[pltpu.VMEM((width, columns), jnp.bfloat16)] * 2
-        + [pltpu.VMEM((2, out_rows, width), jnp.bfloat16)] * 2
-        + [pltpu.SemaphoreType.DMA((2, 2))],
+        + [pltpu.VMEM((2, 2, out_rows, width), jnp.bfloat16), pltpu.SemaphoreType.DMA((2, 2))],
         compiler_params=pltpu.CompilerParams(vmem_limit_bytes=24 * 2**20),
-    )(place, *tiles, *blocks)
+    )(place, tile, *blocks)
 
 
 def dot(a, b, precision):
@@ -106,13 +107,16 @@
     return blocks[0]
 
 
-def sum_rows(blocks, axis):
-    bit = 1
+def sum_step(blocks, axis, bit):
+    mine = lax.axis_index(axis) // bit % 2
+    pairs = blocks.reshape((blocks.shape[0] // 2, 2) + blocks.shape[1:])
+    keep = lax.dynamic_index_in_dim(pairs, mine, 1, keepdims=False)
+    return keep + swap(lax.dynamic_index_in_dim(pairs, 1 - mine, 1, keepdims=False), axis, bit)
+
+
+def sum_rows(blocks, axis, bit=1):
     while blocks.shape[0] > 1:
-        mine = lax.axis_index(axis) // bit % 2
-        pairs = blocks.reshape((blocks.shape[0] // 2, 2) + blocks.shape[1:])
-        keep = lax.dynamic_index_in_dim(pairs, mine, 1, keepdims=False)
-        blocks = keep + swap(lax.dynamic_index_in_dim(pairs, 1 - mine, 1, keepdims=False), axis, bit)
+        blocks = sum_step(blocks, axis, bit)
         bit *= 2
     return blocks[0]
 
@@ -158,10 +162,10 @@
     tile_mask = jnp.repeat(ancestor_tiles, TILE, axis=2)
     kept_rows = lax.dynamic_slice_in_dim(tile_mask, row_start, local_rows, 2).astype(jnp.float32)
     masked = panels * kept_rows[..., None]
-    tiles = [half.reshape(cols_axis, -1, half.shape[1]) for half in split(inverse_tile)]
+    tile = split(inverse_tile).reshape(PARTS, cols_axis, -1, inverse_tile.shape[1])
 
     def one_pair(first, panel_second, link, given_first, given_second):
-        live = {"tiles": tiles, "given": given_first, "first": first, "second": panel_second - dot(first, link, precise)}
+        live = {"tile": tile, "given": given_first, "first": first, "second": panel_second - dot(first, link, precise)}
         slots = {}
 
         def at(slot, *steps):
@@ -185,12 +189,10 @@
             return [live[k, j] for j in range(rows_axis)]
 
         def multiply(k):
-            if "tiles" in live:
-                tiles[:] = live.pop("tiles")
             gathered = blocks(k)
             if ("sums", k - 1) in live:
                 live["sums", k - 1], gathered = lax.optimization_barrier((live["sums", k - 1], gathered))
-            live["send", k], live["keep", k] = product(tiles, gathered)
+            live["send", k], live["keep", k] = product(live["tile"], gathered)
 
         def add_core(k):
             live["sums", k] = live.pop(("keep", k)) + swap(live.pop(("send", k)), "col", 1)
@@ -226,10 +228,11 @@
             sent = swap(terms(1), "col", 1)
             return terms(0) + sent
 
-        def spread_sum(sums):
-            sums = sums.reshape(-1, cols_axis // 2, span).swapaxes(0, 1)
-            sums = sum_scatter(sums, "col", 2)
-            return sum_rows(sums.reshape(-1, rows_axis, height, span).swapaxes(0, 1), "row")
+        def by_rows(sums):
+            return sums.reshape(-1, rows_axis, height, sums.shape[1]).swapaxes(0, 1)
+
+        def rest_of_cols(sums):
+            return sum_scatter(sums.reshape(-1, cols_axis // 2, span).swapaxes(0, 1), "col", 2)
 
         def by_parity(array, odd):
             return jnp.concatenate(columns_by_xor(array, odd), axis=1)
@@ -242,10 +245,11 @@
                 cross = dot_tn(out_first, by_parity(own_second, odd), three_pass) + by_parity(live["link_cross"], odd)
                 return jnp.concatenate([dot_tn(out_first, by_parity(own_first, odd), three_pass), cross])
 
-            live["first_sums"] = core_sum(terms)
+            live["first_sums"] = sum_step(by_rows(core_sum(terms)), "row", 1)
 
         def first_sums():
-            live["first_sums"] = spread_sum(live["first_sums"])
+            sums = sum_rows(live["first_sums"], "row", 2)
+            live["first_sums"] = rest_of_cols(sums.reshape(-1, sums.shape[2])).reshape(-1, height, span)
 
         def second_terms():
             out_second, own_second = outs(count_first, len(pieces)), owns(count_first, len(pieces))
@@ -253,7 +257,7 @@
             def terms(odd):
                 return dot_tn(out_second, by_parity(own_second, odd), three_pass) + by_parity(live["link_second"], odd)
 
-            live["second_sum"] = spread_sum(core_sum(terms))[0]
+            live["second_sum"] = sum_rows(by_rows(rest_of_cols(core_sum(terms))), "row")[0]
 
         at(1, link_terms)
         for k in range(len(pieces)):

time: 269 us -> 268 us (level)
  local copies, waits for them, and re-layouts: 34.6 us -> 14.8 us
  waiting for transfers between devices: 98.3 us -> 113 us
  Pallas kernels: 47.5 us -> 51.2 us
    unnamed x70 -> x67, local copies, waits for them, and re-layouts: 30.6 us -> 8.44 us
    ppermute x28, waiting for transfers between devices: 93.3 us -> 108 us  [swap(): return lax.ppermute(block, axis, pairs)]
    pallas_call x4, Pallas kernels: 38.9 us -> 44 us  [product(): pl.pallas_call(product_kernel, in_specs=[pl.BlockSpec(memory_space=pltpu....]
  transfers between devices with their start and end apart: 36 -> 36, of which waited for: 20 -> 21; matrix products, arithmetic and copies ran while one was open for 14% -> 15% of each run, Pallas kernels for 18% -> 19%
where the time goes in v7:
time: 268 us; the launch traced here: 267 us
  waiting for transfers between devices  113 us (42%)
  Pallas kernels  51.2 us (19%)
  starting transfers between devices  42.7 us (16%)
  other arithmetic  30.5 us (11%)
  local copies, waits for them, and re-layouts  14.8 us (6%)
  matrix products  13.2 us (5%)
    ppermute x28, waiting for transfers between devices, swap(): return lax.ppermute(block, axis, pairs)  108 us
    pallas_call x4, Pallas kernels, product(): pl.pallas_call(product_kernel, in_specs=[pl.BlockSpec(memory_space=pltpu....  44 us
    ppermute x8, starting transfers between devices, spread_step(): moved = lax.ppermute(jnp.stack(held[bit:]), ('row', 'col'), pairs)  21.6 us
    ppermute x28, starting transfers between devices, swap(): return lax.ppermute(block, axis, pairs)  21.1 us
    select_n x8, other arithmetic, spread_step(): return [jnp.where(offset & bit != 0, moved[j], held[j]) for j in range(bit)]  10.4 us
    dot_general x7, matrix products, dot_tn(): return lax.dot_general(a, b, (((0,), (0,)), ((), ())), precision=precision)  9.97 us
    unnamed x67, local copies, waits for them, and re-layouts  8.44 us
    pallas_call x1, Pallas kernels, split(): pl.pallas_call(split_kernel, grid=(rows // step,), in_specs=[pl.BlockSpec...  7.14 us
  transfers between devices with their start and end apart: 36, of which 21 were waited for; matrix products, arithmetic and copies ran while one was open for 15% of the time, Pallas kernels for 19%

profile of v7, /device:TPU:0, one launch (start us, length us, event | category | flops | bytes accessed | tf_op | source)
XLA Modules:
  0.0 267.0 jit_solution(5737954970491864637)
XLA Ops:
  3.5 3.1 %collective-permute-start = (f32[512,256]{1,0:T(8,128)S(1)}, f32[512,256]{1,0:T(8,128)S(1)}, u32[]{:S(2)}, u32[]{:S(2)}) collective-permute-start(f32[512,256]{1,0:T(8,128)S(1)} %slice.116.refs_0_), channel_id=1, source_target_pairs={{0,4},{4,0},{8,12},{12,8},{1,5},{5,1},{9,13},{13,9},{2,6},{6,2},{1... | collective-permute-start | bytes 1572872 | tf_op jit(solution)/shard_map/ppermute | solution.py:16
  9.2 5.8 %copy-done.2 = f32[2048,2048]{1,0:T(8,128)S(1)} copy-done((f32[2048,2048]{1,0:T(8,128)S(1)}, f32[2048,2048]{1,0:T(8,128)}, u32[]{:S(2)}) %copy-start.2) | copy-done | bytes 16777240
  15.0 7.1 %shard_map.79 = bf16[6,2048,2048]{2,1,0:T(8,128)(2,1)} custom-call(f32[2048,2048]{1,0:T(8,128)S(1)} %copy-done.2), custom_call_target="tpu_custom_call" | custom-call | tf_op jit(solution)/shard_map/pallas_call | solution.py:34
  22.1 2.8 %convolution_subtract_fusion = f32[512,512]{1,0:T(8,128)} fusion(f32[1,2,512,512]{3,2,1,0:T(8,128)S(1)} %broadcast_multiply_fusion, f32[1,512,512]{2,1,0:T(8,128)S(1)} %copy-done), kind=kOutput, calls=%fused_computation.10 | convolution fusion | flops 1610874880 | bytes 4194304 | tf_op jit(solution)/shard_map/dot_general | solution.py:95
  24.9 4.7 %collective-permute-done.refs_1_ = f32[512,256]{1,0:T(8,128)S(1)} collective-permute-done((f32[512,256]{1,0:T(8,128)S(1)}, f32[512,256]{1,0:T(8,128)S(1)}, u32[]{:S(2)}, u32[]{:S(2)}) %collective-permute-start) | collective-permute-done | bytes 524320 | tf_op jit(solution)/shard_map/ppermute | solution.py:16
  38.1 19.5 %collective-permute-done.3.refs_1_ = f32[512,256]{1,0:T(8,128)S(1)} collective-permute-done((f32[512,256]{1,0:T(8,128)S(1)}, f32[512,256]{1,0:T(8,128)S(1)}, u32[]{:S(2)}, u32[]{:S(2)}) %collective-permute-start.3) | collective-permute-done | bytes 524320 | tf_op jit(solution)/shard_map/ppermute | solution.py:16
  57.6 8.8 %collective-permute-done.2.refs_3_ = f32[512,256]{1,0:T(8,128)} collective-permute-done((f32[512,256]{1,0:T(8,128)}, f32[512,256]{1,0:T(8,128)}, u32[]{:S(2)}, u32[]{:S(2)}) %collective-permute-start.2) | collective-permute-done | bytes 524320 | tf_op jit(solution)/shard_map/ppermute | solution.py:16
  68.7 4.4 %collective-permute-start.8 = (f32[2,512,256]{2,1,0:T(8,128)}, f32[2,512,256]{2,1,0:T(8,128)}, u32[]{:S(2)}, u32[]{:S(2)}) collective-permute-start(f32[2,512,256]{2,1,0:T(8,128)} %pad_maximum_fusion), channel_id=1, source_target_pairs={{0,2},{5,7},{10,8},{15,13},{16,18},{21,23},{26,24},{31,29}} | collective-permute-start | bytes 3145736 | tf_op jit(solution)/shard_map/ppermute | solution.py:151
  76.4 11.2 %shard_map.80 = (f32[2,512,256]{2,1,0:T(8,128)}, f32[2,512,256]{2,1,0:T(8,128)S(1)}) custom-call(s32[5]{0:T(128)S(1)} %pad_add_fusion.place, bf16[6,4,512,2048]{3,2,1,0:T(8,128)(2,1)} %bitcast.193, f32[512,256]{1,0:T(8,128)S(1)} %slice.116.refs_0_, f32[512,256]{1,0:T(8,128)S(1)} %copy-done.9, f32[512,256]{1,0:T(8,128)} %collective-permute-done.1.refs_2_, ...), custom_call_target="tpu_custom_call" | custom-call | tf_op jit(solution)/shard_map/pallas_call | solution.py:83
  87.7 2.7 %fusion.20 = (f32[512,256]{1,0:T(8,128)}, f32[512,256]{1,0:T(8,128)}) fusion(f32[512,256]{1,0:T(8,128)S(1)} %copy-done.9, f32[2,512,256]{2,1,0:T(8,128)} %collective-permute-done.8, pred[]{:T(512)S(6)} %ne.64, f32[512,256]{1,0:T(8,128)S(1)} %slice.116.refs_0_), kind=kLoop, calls=%fused_computation.61 | loop fusion | flops 262144 | bytes 3145729 | tf_op jit(solution)/shard_map/jit(_where)/select_n | solution.py:153
  90.4 8.1 %collective-permute-done.6.refs_1_ = f32[512,256]{1,0:T(8,128)S(1)} collective-permute-done((f32[512,256]{1,0:T(8,128)S(1)}, f32[512,256]{1,0:T(8,128)S(1)}, u32[]{:S(2)}, u32[]{:S(2)}) %collective-permute-start.6) | collective-permute-done | bytes 524320 | tf_op jit(solution)/shard_map/ppermute | solution.py:16
  98.6 8.7 %collective-permute-done.5.refs_3_ = f32[512,256]{1,0:T(8,128)} collective-permute-done((f32[512,256]{1,0:T(8,128)}, f32[512,256]{1,0:T(8,128)}, u32[]{:S(2)}, u32[]{:S(2)}) %collective-permute-start.5) | collective-permute-done | bytes 524320 | tf_op jit(solution)/shard_map/ppermute | solution.py:16
  123.2 11.1 %shard_map.81 = (f32[2,512,256]{2,1,0:T(8,128)S(1)}, f32[2,512,256]{2,1,0:T(8,128)S(1)}) custom-call(s32[5]{0:T(128)S(1)} %pad_add_fusion.place, bf16[6,4,512,2048]{3,2,1,0:T(8,128)(2,1)} %bitcast.194, f32[512,256]{1,0:T(8,128)S(1)} %slice.90.refs_0_, f32[512,256]{1,0:T(8,128)S(1)} %copy-done.4, f32[512,256]{1,0:T(8,128)S(1)} %copy-done.7, ...), custom_call_target="tpu_custom_call" | custom-call | tf_op jit(solution)/shard_map/pallas_call | solution.py:83
  137.6 4.7 %collective-permute-done.12.refs_2_ = f32[512,256]{1,0:T(8,128)S(1)} collective-permute-done((f32[512,256]{1,0:T(8,128)S(1)}, f32[512,256]{1,0:T(8,128)S(1)}, u32[]{:S(2)}, u32[]{:S(2)}) %collective-permute-start.12) | collective-permute-done | bytes 524320 | tf_op jit(solution)/shard_map/ppermute | solution.py:16
  142.3 9.5 %collective-permute-done.10.refs_3_ = f32[512,256]{1,0:T(8,128)S(1)} collective-permute-done((f32[512,256]{1,0:T(8,128)}, f32[512,256]{1,0:T(8,128)S(1)}, u32[]{:S(2)}, u32[]{:S(2)}) %collective-permute-start.10) | collective-permute-done | bytes 524320 | tf_op jit(solution)/shard_map/ppermute | solution.py:16
  158.5 11.1 %shard_map.82 = (f32[2,512,256]{2,1,0:T(8,128)}, f32[2,512,256]{2,1,0:T(8,128)S(1)}) custom-call(s32[5]{0:T(128)S(1)} %pad_add_fusion.place, bf16[6,4,512,2048]{3,2,1,0:T(8,128)(2,1)} %bitcast.195, f32[512,256]{1,0:T(8,128)S(1)} %slice.91.refs_0_, f32[512,256]{1,0:T(8,128)S(1)} %collective-permute-done.6.refs_1_, f32[512,256]{1,0:T(8,128)} %collective-permute-done.7.refs_2_, ...), custom_call_target="tpu_custom_call" | custom-call | tf_op jit(solution)/shard_map/pallas_call | solution.py:83
  173.3 4.5 %collective-permute-done.20 = f32[1,512,256]{2,1,0:T(8,128)S(1)} collective-permute-done((f32[1,512,256]{2,1,0:T(8,128)S(1)}, f32[1,512,256]{2,1,0:T(8,128)S(1)}, u32[]{:S(2)}, u32[]{:S(2)}) %collective-permute-start.20) | collective-permute-done | bytes 524320 | tf_op jit(solution)/shard_map/ppermute | solution.py:16
  179.8 5.4 %collective-permute-start.22 = (f32[2,512,256]{2,1,0:T(8,128)}, f32[2,512,256]{2,1,0:T(8,128)}, u32[]{:S(2)}, u32[]{:S(2)}) collective-permute-start(f32[2,512,256]{2,1,0:T(8,128)} %pad_maximum_fusion.3), channel_id=1, source_target_pairs={{0,2},{5,7},{10,8},{15,13},{16,18},{21,23},{26,24},{31,29}} | collective-permute-start | bytes 3145736 | tf_op jit(solution)/shard_map/ppermute | solution.py:151
  190.0 10.6 %shard_map.83 = (f32[2,512,256]{2,1,0:T(8,128)S(1)}, f32[2,512,256]{2,1,0:T(8,128)S(1)}) custom-call(s32[5]{0:T(128)S(1)} %pad_add_fusion.place, bf16[6,4,512,2048]{3,2,1,0:T(8,128)(2,1)} %bitcast.196, f32[512,256]{1,0:T(8,128)S(1)} %slice.94.refs_0_, f32[512,256]{1,0:T(8,128)S(1)} %collective-permute-done.11.refs_1_, ...), custom_call_target="tpu_custom_call" | custom-call | tf_op jit(solution)/shard_map/pallas_call | solution.py:83
  203.8 4.2 %collective-permute-done.24 = f32[1,512,256]{2,1,0:T(8,128)S(1)} collective-permute-done((f32[1,512,256]{2,1,0:T(8,128)S(1)}, f32[1,512,256]{2,1,0:T(8,128)S(1)}, u32[]{:S(2)}, u32[]{:S(2)}) %collective-permute-start.24) | collective-permute-done | bytes 524320 | tf_op jit(solution)/shard_map/ppermute | solution.py:16
  218.6 11.8 %collective-permute-done.27 = f32[1,512,256]{2,1,0:T(8,128)S(1)} collective-permute-done((f32[1,512,256]{2,1,0:T(8,128)S(1)}, f32[1,512,256]{2,1,0:T(8,128)S(1)}, u32[]{:S(2)}, u32[]{:S(2)}) %collective-permute-start.27) | collective-permute-done | bytes 524320 | tf_op jit(solution)/shard_map/ppermute | solution.py:16
  244.4 8.8 %collective-permute-done.30 = f32[1,2,128,256]{3,2,1,0:T(8,128)} collective-permute-done((f32[1,2,128,256]{3,2,1,0:T(8,128)}, f32[1,2,128,256]{3,2,1,0:T(8,128)}, u32[]{:S(2)}, u32[]{:S(2)}) %collective-permute-start.30) | collective-permute-done | bytes 262176 | tf_op jit(solution)/shard_map/ppermute | solution.py:16
  256.9 3.2 %collective-permute-done.31 = f32[1,256,128]{2,1,0:T(8,128)S(1)} collective-permute-done((f32[1,256,128]{2,1,0:T(8,128)S(1)}, f32[1,256,128]{2,1,0:T(8,128)S(1)}, u32[]{:S(2)}, u32[]{:S(2)}) %collective-permute-start.31) | collective-permute-done | bytes 131104 | tf_op jit(solution)/shard_map/ppermute | solution.py:16
  261.3 4.9 %collective-permute-done.35 = f32[1,1,128,128]{3,2,1,0:T(8,128)S(1)} collective-permute-done((f32[1,1,128,128]{3,2,1,0:T(8,128)S(1)}, f32[1,1,128,128]{3,2,1,0:T(8,128)S(1)}, u32[]{:S(2)}, u32[]{:S(2)}) %collective-permute-start.35) | collective-permute-done | bytes 65568 | tf_op jit(solution)/shard_map/ppermute | solution.py:16
  (194 shorter events, 88.6 us)
Async XLA Ops:
  3.5 26.1 %collective-permute-start = (f32[512,256]{1,0:T(8,128)S(1)}, f32[512,256]{1,0:T(8,128)S(1)}, u32[]{:S(2)}, u32[]{:S(2)}) collective-permute-start(f32[512,256]{1,0:T(8,128)S(1)} %slice.116.refs_0_), channel_id=1, source_target_pairs={{0,4},{4,0},{8,12},{12,8},{1,5},{5,1},{9,13},{13,9},{2,6},{6,2},{1... | collective-permute-start | bytes 1572872 | tf_op jit(solution)/shard_map/ppermute | solution.py:16
  6.6 25.7 %collective-permute-start.1 = (f32[512,256]{1,0:T(8,128)S(1)}, f32[512,256]{1,0:T(8,128)}, u32[]{:S(2)}, u32[]{:S(2)}) collective-permute-start(f32[512,256]{1,0:T(8,128)S(1)} %slice.116.refs_0_), channel_id=1, source_target_pairs={{0,8},{4,12},{8,0},{12,4},{1,9},{5,13},{9,1},{13,5},{2,10},{6,14},... | collective-permute-start | bytes 1572872 | tf_op jit(solution)/shard_map/ppermute | solution.py:16
  32.3 25.3 %collective-permute-start.3 = (f32[512,256]{1,0:T(8,128)S(1)}, f32[512,256]{1,0:T(8,128)S(1)}, u32[]{:S(2)}, u32[]{:S(2)}) collective-permute-start(f32[512,256]{1,0:T(8,128)S(1)} %slice.90.refs_0_), channel_id=1, source_target_pairs={{0,4},{4,0},{8,12},{12,8},{1,5},{5,1},{9,13},{13,9},{2,6},{6,2},{1... | collective-permute-start | bytes 1572872 | tf_op jit(solution)/shard_map/ppermute | solution.py:16
  32.8 24.8 %collective-permute-start.4 = (f32[512,256]{1,0:T(8,128)S(1)}, f32[512,256]{1,0:T(8,128)S(1)}, u32[]{:S(2)}, u32[]{:S(2)}) collective-permute-start(f32[512,256]{1,0:T(8,128)S(1)} %slice.90.refs_0_), channel_id=1, source_target_pairs={{0,8},{4,12},{8,0},{12,4},{1,9},{5,13},{9,1},{13,5},{2,10},{6,14},... | collective-permute-start | bytes 1572872 | tf_op jit(solution)/shard_map/ppermute | solution.py:16
  35.4 31.0 %collective-permute-start.2 = (f32[512,256]{1,0:T(8,128)}, f32[512,256]{1,0:T(8,128)}, u32[]{:S(2)}, u32[]{:S(2)}) collective-permute-start(f32[512,256]{1,0:T(8,128)} %collective-permute-done.1.refs_2_), channel_id=1, source_target_pairs={{0,4},{4,0},{8,12},{12,8},{1,5},{5,1},{9,13},{13,9},{2,6},{6,2},{1... | collective-permute-start | bytes 1572872 | tf_op jit(solution)/shard_map/ppermute | solution.py:16
  68.7 19.0 %collective-permute-start.8 = (f32[2,512,256]{2,1,0:T(8,128)}, f32[2,512,256]{2,1,0:T(8,128)}, u32[]{:S(2)}, u32[]{:S(2)}) collective-permute-start(f32[2,512,256]{2,1,0:T(8,128)} %pad_maximum_fusion), channel_id=1, source_target_pairs={{0,2},{5,7},{10,8},{15,13},{16,18},{21,23},{26,24},{31,29}} | collective-permute-start | bytes 3145736 | tf_op jit(solution)/shard_map/ppermute | solution.py:151
  73.1 25.4 %collective-permute-start.6 = (f32[512,256]{1,0:T(8,128)S(1)}, f32[512,256]{1,0:T(8,128)S(1)}, u32[]{:S(2)}, u32[]{:S(2)}) collective-permute-start(f32[512,256]{1,0:T(8,128)S(1)} %slice.91.refs_0_), channel_id=1, source_target_pairs={{0,4},{4,0},{8,12},{12,8},{1,5},{5,1},{9,13},{13,9},{2,6},{6,2},{1... | collective-permute-start | bytes 1572872 | tf_op jit(solution)/shard_map/ppermute | solution.py:16
  73.2 25.4 %collective-permute-start.7 = (f32[512,256]{1,0:T(8,128)S(1)}, f32[512,256]{1,0:T(8,128)}, u32[]{:S(2)}, u32[]{:S(2)}) collective-permute-start(f32[512,256]{1,0:T(8,128)S(1)} %slice.91.refs_0_), channel_id=1, source_target_pairs={{0,8},{4,12},{8,0},{12,4},{1,9},{5,13},{9,1},{13,5},{2,10},{6,14},... | collective-permute-start | bytes 1572872 | tf_op jit(solution)/shard_map/ppermute | solution.py:16
  73.3 34.1 %collective-permute-start.5 = (f32[512,256]{1,0:T(8,128)}, f32[512,256]{1,0:T(8,128)}, u32[]{:S(2)}, u32[]{:S(2)}) collective-permute-start(f32[512,256]{1,0:T(8,128)} %copy-done.5), channel_id=1, source_target_pairs={{0,4},{4,0},{8,12},{12,8},{1,5},{5,1},{9,13},{13,9},{2,6},{6,2},{1... | collective-permute-start | bytes 1572872 | tf_op jit(solution)/shard_map/ppermute | solution.py:16
  109.5 24.8 %collective-permute-start.13 = (f32[2,512,256]{2,1,0:T(8,128)}, f32[2,512,256]{2,1,0:T(8,128)}, u32[]{:S(2)}, u32[]{:S(2)}) collective-permute-start(f32[2,512,256]{2,1,0:T(8,128)} %pad_maximum_fusion.1), channel_id=1, source_target_pairs={{0,2},{5,7},{10,8},{15,13},{16,18},{21,23},{26,24},{31,29}} | collective-permute-start | bytes 3145736 | tf_op jit(solution)/shard_map/ppermute | solution.py:151
  115.4 22.1 %collective-permute-start.11 = (f32[512,256]{1,0:T(8,128)S(1)}, f32[512,256]{1,0:T(8,128)S(1)}, u32[]{:S(2)}, u32[]{:S(2)}) collective-permute-start(f32[512,256]{1,0:T(8,128)S(1)} %slice.94.refs_0_), channel_id=1, source_target_pairs={{0,4},{4,0},{8,12},{12,8},{1,5},{5,1},{9,13},{13,9},{2,6},{6,2},{1... | collective-permute-start | bytes 1572872 | tf_op jit(solution)/shard_map/ppermute | solution.py:16
  115.5 26.8 %collective-permute-start.12 = (f32[512,256]{1,0:T(8,128)S(1)}, f32[512,256]{1,0:T(8,128)S(1)}, u32[]{:S(2)}, u32[]{:S(2)}) collective-permute-start(f32[512,256]{1,0:T(8,128)S(1)} %slice.94.refs_0_), channel_id=1, source_target_pairs={{0,8},{4,12},{8,0},{12,4},{1,9},{5,13},{9,1},{13,5},{2,10},{6,14},... | collective-permute-start | bytes 1572872 | tf_op jit(solution)/shard_map/ppermute | solution.py:16
  115.6 36.2 %collective-permute-start.10 = (f32[512,256]{1,0:T(8,128)}, f32[512,256]{1,0:T(8,128)S(1)}, u32[]{:S(2)}, u32[]{:S(2)}) collective-permute-start(f32[512,256]{1,0:T(8,128)} %collective-permute-done.7.refs_2_), channel_id=1, source_target_pairs={{0,4},{4,0},{8,12},{12,8},{1,5},{5,1},{9,13},{13,9},{2,6},{6,2},{1... | collective-permute-start | bytes 1572872 | tf_op jit(solution)/shard_map/ppermute | solution.py:16
  119.3 16.3 %collective-permute-start.15 = (f32[1,512,256]{2,1,0:T(8,128)S(1)}, f32[1,512,256]{2,1,0:T(8,128)S(1)}, u32[]{:S(2)}, u32[]{:S(2)}) collective-permute-start(f32[1,512,256]{2,1,0:T(8,128)S(1)} %slice_bitcast_fusion.12), channel_id=1, source_target_pairs={{0,2},{1,3},{2,0},{3,1},{4,6},{5,7},{6,4},{7,5},{8,10},{9,11},{10,... | collective-permute-start | bytes 1572872 | tf_op jit(solution)/shard_map/ppermute | solution.py:16
  152.9 19.2 %collective-permute-start.18 = (f32[2,512,256]{2,1,0:T(8,128)S(1)}, f32[2,512,256]{2,1,0:T(8,128)S(1)}, u32[]{:S(2)}, u32[]{:S(2)}) collective-permute-start(f32[2,512,256]{2,1,0:T(8,128)S(1)} %pad_maximum_fusion.2), channel_id=1, source_target_pairs={{0,2},{5,7},{10,8},{15,13},{16,18},{21,23},{26,24},{31,29}} | collective-permute-start | bytes 3145736 | tf_op jit(solution)/shard_map/ppermute | solution.py:151
  156.1 22.5 %collective-permute-start.17 = (f32[512,256]{1,0:T(8,128)S(1)}, f32[512,256]{1,0:T(8,128)S(1)}, u32[]{:S(2)}, u32[]{:S(2)}) collective-permute-start(f32[512,256]{1,0:T(8,128)S(1)} %collective-permute-done.12.refs_2_), channel_id=1, source_target_pairs={{0,4},{4,0},{8,12},{12,8},{1,5},{5,1},{9,13},{13,9},{2,6},{6,2},{1... | collective-permute-start | bytes 1572872 | tf_op jit(solution)/shard_map/ppermute | solution.py:16
  156.4 21.4 %collective-permute-start.20 = (f32[1,512,256]{2,1,0:T(8,128)S(1)}, f32[1,512,256]{2,1,0:T(8,128)S(1)}, u32[]{:S(2)}, u32[]{:S(2)}) collective-permute-start(f32[1,512,256]{2,1,0:T(8,128)S(1)} %slice_bitcast_fusion.8), channel_id=1, source_target_pairs={{0,2},{1,3},{2,0},{3,1},{4,6},{5,7},{6,4},{7,5},{8,10},{9,11},{10,... | collective-permute-start | bytes 1572872 | tf_op jit(solution)/shard_map/ppermute | solution.py:16
  178.7 8.6 %collective-permute-start.23 = (f32[2,512,256]{2,1,0:T(8,128)}, f32[2,512,256]{2,1,0:T(8,128)}, u32[]{:S(2)}, u32[]{:S(2)}) collective-permute-start(f32[2,512,256]{2,1,0:T(8,128)} %get-tuple-element.189), channel_id=1, source_target_pairs={{0,1},{1,0},{2,3},{3,2},{4,5},{5,4},{6,7},{7,6},{8,9},{9,8},{10,11... | collective-permute-start | bytes 3145736 | tf_op jit(solution)/shard_map/ppermute | solution.py:16
  179.8 22.6 %collective-permute-start.22 = (f32[2,512,256]{2,1,0:T(8,128)}, f32[2,512,256]{2,1,0:T(8,128)}, u32[]{:S(2)}, u32[]{:S(2)}) collective-permute-start(f32[2,512,256]{2,1,0:T(8,128)} %pad_maximum_fusion.3), channel_id=1, source_target_pairs={{0,2},{5,7},{10,8},{15,13},{16,18},{21,23},{26,24},{31,29}} | collective-permute-start | bytes 3145736 | tf_op jit(solution)/shard_map/ppermute | solution.py:151
  188.8 19.2 %collective-permute-start.24 = (f32[1,512,256]{2,1,0:T(8,128)S(1)}, f32[1,512,256]{2,1,0:T(8,128)S(1)}, u32[]{:S(2)}, u32[]{:S(2)}) collective-permute-start(f32[1,512,256]{2,1,0:T(8,128)S(1)} %slice_bitcast_fusion.4), channel_id=1, source_target_pairs={{0,2},{1,3},{2,0},{3,1},{4,6},{5,7},{6,4},{7,5},{8,10},{9,11},{10,... | collective-permute-start | bytes 1572872 | tf_op jit(solution)/shard_map/ppermute | solution.py:16
  215.7 14.7 %collective-permute-start.27 = (f32[1,512,256]{2,1,0:T(8,128)S(1)}, f32[1,512,256]{2,1,0:T(8,128)S(1)}, u32[]{:S(2)}, u32[]{:S(2)}) collective-permute-start(f32[1,512,256]{2,1,0:T(8,128)S(1)} %slice_bitcast_fusion.2), channel_id=1, source_target_pairs={{0,2},{1,3},{2,0},{3,1},{4,6},{5,7},{6,4},{7,5},{8,10},{9,11},{10,... | collective-permute-start | bytes 1572872 | tf_op jit(solution)/shard_map/ppermute | solution.py:16
  218.5 13.7 %collective-permute-start.29 = (f32[2,2,128,256]{3,2,1,0:T(8,128)S(1)}, f32[2,2,128,256]{3,2,1,0:T(8,128)S(1)}, u32[]{:S(2)}, u32[]{:S(2)}) collective-permute-start(f32[2,2,128,256]{3,2,1,0:T(8,128)S(1)} %bitcast.210), channel_id=1, source_target_pairs={{0,4},{4,0},{8,12},{12,8},{1,5},{5,1},{9,13},{13,9},{2,6},{6,2},{1... | collective-permute-start | bytes 1572872 | tf_op jit(solution)/shard_map/ppermute | solution.py:16
  238.0 15.3 %collective-permute-start.30 = (f32[1,2,128,256]{3,2,1,0:T(8,128)}, f32[1,2,128,256]{3,2,1,0:T(8,128)}, u32[]{:S(2)}, u32[]{:S(2)}) collective-permute-start(f32[1,2,128,256]{3,2,1,0:T(8,128)} %constant_dynamic-slice_fusion.9), channel_id=1, source_target_pairs={{0,8},{4,12},{8,0},{12,4},{1,9},{5,13},{9,1},{13,5},{2,10},{6,14},... | collective-permute-start | bytes 786440 | tf_op jit(solution)/shard_map/ppermute | solution.py:16
  243.0 12.2 %collective-permute-start.33 = (f32[1,512,128]{2,1,0:T(8,128)}, f32[1,512,128]{2,1,0:T(8,128)S(1)}, u32[]{:S(2)}, u32[]{:S(2)}) collective-permute-start(f32[1,512,128]{2,1,0:T(8,128)} %bitcast.69), channel_id=1, source_target_pairs={{0,2},{1,3},{2,0},{3,1},{4,6},{5,7},{6,4},{7,5},{8,10},{9,11},{10,... | collective-permute-start | bytes 786440 | tf_op jit(solution)/shard_map/ppermute | solution.py:16
  (42 other events, 333.8 us)

commit v8 on v7

--- a/solution.py
+++ b/solution.py
@@ -161,11 +161,10 @@
     row_start = (col_id * rows_axis + row_id) * local_rows
     tile_mask = jnp.repeat(ancestor_tiles, TILE, axis=2)
     kept_rows = lax.dynamic_slice_in_dim(tile_mask, row_start, local_rows, 2).astype(jnp.float32)
-    masked = panels * kept_rows[..., None]
     tile = split(inverse_tile).reshape(PARTS, cols_axis, -1, inverse_tile.shape[1])
 
-    def one_pair(first, panel_second, link, given_first, given_second):
-        live = {"tile": tile, "given": given_first, "first": first, "second": panel_second - dot(first, link, precise)}
+    def one_pair(panels, kept_first, kept_second, link, given_first, given_second):
+        live = {"tile": tile, "given": given_first}
         slots = {}
 
         def at(slot, *steps):
@@ -176,12 +175,14 @@
         count_first = len(pieces)
         pieces += [("second", i, i + late) for i in range(0, width, late)]
         stages = rows_axis.bit_length() - 1
+        second = panels[1] * kept_second - dot(panels[0] * kept_first, link, precise)
+        for k, (panel, start, stop) in enumerate(pieces):
+            live["piece", k] = panels[0][:, start:stop] * kept_first if panel == "first" else second[:, start:stop]
 
         def fetch(k, stage):
             if stage == 0:
-                panel, start, stop = pieces[k]
-                live[k, 0] = live[panel][:, start:stop]
-            for j in range(1, rows_axis):
+                live[k, 0] = live.pop(("piece", k))
+            for j in reversed(range(1, rows_axis)):
                 if j.bit_count() == stage + 1:
                     live[k, j] = swap(live[k, j & (j - 1)], "row", j & -j)
 
@@ -260,6 +261,7 @@
             live["second_sum"] = sum_rows(by_rows(rest_of_cols(core_sum(terms))), "row")[0]
 
         at(1, link_terms)
+        last = len(pieces) - 1 + stages
         for k in range(len(pieces)):
             at(k + stages, lambda k=k: collect(k))
             for step in range(1, cols_axis.bit_length() - 1):
@@ -269,8 +271,8 @@
             at(k + stages, lambda k=k: multiply(k))
         for k in range(len(pieces)):
             at(k + stages + 1, lambda k=k: add_rest(k))
-        end = len(pieces) + stages + 1
-        at(end - 1, first_terms)
+        end = last + 2
+        at(last + 1, first_terms)
         at(end, first_sums, second_terms)
 
         for slot in range(end + 1):
@@ -284,7 +286,8 @@
         diagonal = jnp.stack([given_first - first_sum, given_second - live["second_sum"]])
         return ancestor, diagonal, -cross_sum
 
-    results = [one_pair(masked[s, 0], masked[s, 1], link_panel[s], diag_inverse[s, 0], diag_inverse[s, 1])
+    results = [one_pair(panels[s], kept_rows[s, 0, :, None], kept_rows[s, 1, :, None], link_panel[s],
+                        diag_inverse[s, 0], diag_inverse[s, 1])
                for s in range(siblings)]
     return tuple(jnp.stack(group) for group in zip(*results))
 

time: 268 us -> 268 us (level)
  starting transfers between devices: 42.7 us -> 49.4 us
  other arithmetic: 30.5 us -> 27.1 us
    ppermute x8, starting transfers between devices: 21.6 us -> 25.3 us  [spread_step(): moved = lax.ppermute(jnp.stack(held[bit:]), ('row', 'col'), pairs)]
    ppermute x28, waiting for transfers between devices: 108 us -> 104 us  [swap(): return lax.ppermute(block, axis, pairs)]
    ppermute x28, starting transfers between devices: 21.1 us -> 24.1 us  [swap(): return lax.ppermute(block, axis, pairs)]
    unnamed x67 -> x53, local copies, waits for them, and re-layouts: 8.44 us -> 9.92 us
  transfers between devices with their start and end apart: 36 -> 36, of which waited for: 21 -> 18; matrix products, arithmetic and copies ran while one was open for 15% -> 14% of each run, Pallas kernels for 19% -> 19%
where the time goes in v8:
time: 268 us; the launch traced here: 267 us
  waiting for transfers between devices  111 us (41%)
  Pallas kernels  50.9 us (19%)
  starting transfers between devices  49.4 us (18%)
  other arithmetic  27.1 us (10%)
  local copies, waits for them, and re-layouts  15.8 us (6%)
  matrix products  12.3 us (5%)
    ppermute x28, waiting for transfers between devices, swap(): return lax.ppermute(block, axis, pairs)  104 us
    pallas_call x4, Pallas kernels, product(): pl.pallas_call(product_kernel, in_specs=[pl.BlockSpec(memory_space=pltpu....  43.8 us
    ppermute x8, starting transfers between devices, spread_step(): moved = lax.ppermute(jnp.stack(held[bit:]), ('row', 'col'), pairs)  25.3 us
    ppermute x28, starting transfers between devices, swap(): return lax.ppermute(block, axis, pairs)  24.1 us
    select_n x8, other arithmetic, spread_step(): return [jnp.where(offset & bit != 0, moved[j], held[j]) for j in range(bit)]  10.7 us
    dot_general x7, matrix products, dot_tn(): return lax.dot_general(a, b, (((0,), (0,)), ((), ())), precision=precision)  10 us
    unnamed x53, local copies, waits for them, and re-layouts  9.92 us
    pallas_call x1, Pallas kernels, split(): pl.pallas_call(split_kernel, grid=(rows // step,), in_specs=[pl.BlockSpec...  7.11 us
  transfers between devices with their start and end apart: 36, of which 18 were waited for; matrix products, arithmetic and copies ran while one was open for 14% of the time, Pallas kernels for 19%

profile of v8, /device:TPU:0, one launch (start us, length us, event | category | flops | bytes accessed | tf_op | source)
XLA Modules:
  0.0 267.5 jit_solution(9625784883245554992)
XLA Ops:
  3.2 4.1 %collective-permute-start = (f32[512,256]{1,0:T(8,128)S(1)}, f32[512,256]{1,0:T(8,128)}, u32[]{:S(2)}, u32[]{:S(2)}) collective-permute-start(f32[512,256]{1,0:T(8,128)S(1)} %get-tuple-element.122.refs_0_), channel_id=1, source_target_pairs={{0,8},{4,12},{8,0},{12,4},{1,9},{5,13},{9,1},{13,5},{2,10},{6,14},... | collective-permute-start | bytes 1572872 | tf_op jit(solution)/shard_map/ppermute | solution.py:16
  10.8 5.8 %copy-done.2 = f32[2048,2048]{1,0:T(8,128)S(1)} copy-done((f32[2048,2048]{1,0:T(8,128)S(1)}, f32[2048,2048]{1,0:T(8,128)}, u32[]{:S(2)}) %copy-start.2) | copy-done | bytes 16777240
  16.6 7.1 %shard_map.79 = bf16[6,2048,2048]{2,1,0:T(8,128)(2,1)} custom-call(f32[2048,2048]{1,0:T(8,128)S(1)} %copy-done.2), custom_call_target="tpu_custom_call" | custom-call | tf_op jit(solution)/shard_map/pallas_call | solution.py:34
  23.8 6.9 %collective-permute-done.refs_2_ = f32[512,256]{1,0:T(8,128)} collective-permute-done((f32[512,256]{1,0:T(8,128)S(1)}, f32[512,256]{1,0:T(8,128)}, u32[]{:S(2)}, u32[]{:S(2)}) %collective-permute-start) | collective-permute-done | bytes 524320 | tf_op jit(solution)/shard_map/ppermute | solution.py:16
  38.0 18.8 %collective-permute-done.3.refs_2_ = f32[512,256]{1,0:T(8,128)} collective-permute-done((f32[512,256]{1,0:T(8,128)S(1)}, f32[512,256]{1,0:T(8,128)}, u32[]{:S(2)}, u32[]{:S(2)}) %collective-permute-start.3) | collective-permute-done | bytes 524320 | tf_op jit(solution)/shard_map/ppermute | solution.py:16
  57.9 10.3 %collective-permute-done.2.refs_3_ = f32[512,256]{1,0:T(8,128)} collective-permute-done((f32[512,256]{1,0:T(8,128)}, f32[512,256]{1,0:T(8,128)}, u32[]{:S(2)}, u32[]{:S(2)}) %collective-permute-start.2) | collective-permute-done | bytes 524320 | tf_op jit(solution)/shard_map/ppermute | solution.py:16
  70.4 4.2 %collective-permute-start.8 = (f32[2,512,256]{2,1,0:T(8,128)}, f32[2,512,256]{2,1,0:T(8,128)}, u32[]{:S(2)}, u32[]{:S(2)}) collective-permute-start(f32[2,512,256]{2,1,0:T(8,128)} %pad_maximum_fusion), channel_id=1, source_target_pairs={{0,2},{5,7},{10,8},{15,13},{16,18},{21,23},{26,24},{31,29}} | collective-permute-start | bytes 3145736 | tf_op jit(solution)/shard_map/ppermute | solution.py:151
  77.8 11.2 %shard_map.80 = (f32[2,512,256]{2,1,0:T(8,128)}, f32[2,512,256]{2,1,0:T(8,128)S(1)}) custom-call(s32[5]{0:T(128)S(1)} %pad_add_fusion.place, bf16[6,4,512,2048]{3,2,1,0:T(8,128)(2,1)} %bitcast.199, f32[512,256]{1,0:T(8,128)S(1)} %get-tuple-element.122.refs_0_, f32[512,256]{1,0:T(8,128)S(1)} %copy-done.6, f32[512,256]{1,0:T(8,128)} %collective-permute-done.refs_2_, ...), custom_call_target="tpu_custom_call" | custom-call | tf_op jit(solution)/shard_map/pallas_call | solution.py:83
  89.1 2.7 %fusion.23 = (f32[512,256]{1,0:T(8,128)}, f32[512,256]{1,0:T(8,128)}) fusion(f32[512,256]{1,0:T(8,128)S(1)} %copy-done.6, f32[2,512,256]{2,1,0:T(8,128)} %collective-permute-done.8, pred[]{:T(512)S(6)} %ne.64, f32[512,256]{1,0:T(8,128)S(1)} %get-tuple-element.122.refs_0_), kind=kLoop, calls=%fused_computation.63 | loop fusion | flops 262144 | bytes 3145729 | tf_op jit(solution)/shard_map/jit(_where)/select_n | solution.py:153
  91.8 16.8 %collective-permute-done.5.refs_3_ = f32[512,256]{1,0:T(8,128)} collective-permute-done((f32[512,256]{1,0:T(8,128)}, f32[512,256]{1,0:T(8,128)}, u32[]{:S(2)}, u32[]{:S(2)}) %collective-permute-start.5) | collective-permute-done | bytes 524320 | tf_op jit(solution)/shard_map/ppermute | solution.py:16
  111.0 4.3 %collective-permute-start.13 = (f32[2,512,256]{2,1,0:T(8,128)}, f32[2,512,256]{2,1,0:T(8,128)}, u32[]{:S(2)}, u32[]{:S(2)}) collective-permute-start(f32[2,512,256]{2,1,0:T(8,128)} %pad_maximum_fusion.1), channel_id=1, source_target_pairs={{0,2},{5,7},{10,8},{15,13},{16,18},{21,23},{26,24},{31,29}} | collective-permute-start | bytes 3145736 | tf_op jit(solution)/shard_map/ppermute | solution.py:151
  125.6 11.4 %shard_map.81 = (f32[2,512,256]{2,1,0:T(8,128)S(1)}, f32[2,512,256]{2,1,0:T(8,128)S(1)}) custom-call(s32[5]{0:T(128)S(1)} %pad_add_fusion.place, bf16[6,4,512,2048]{3,2,1,0:T(8,128)(2,1)} %bitcast.200, f32[512,256]{1,0:T(8,128)S(1)} %get-tuple-element.149.refs_0_, f32[512,256]{1,0:T(8,128)} %collective-permute-done.4.refs_1_, ...), custom_call_target="tpu_custom_call" | custom-call | tf_op jit(solution)/shard_map/pallas_call | solution.py:83
  139.5 12.7 %collective-permute-done.10.refs_3_ = f32[512,256]{1,0:T(8,128)S(1)} collective-permute-done((f32[512,256]{1,0:T(8,128)}, f32[512,256]{1,0:T(8,128)S(1)}, u32[]{:S(2)}, u32[]{:S(2)}) %collective-permute-start.10) | collective-permute-done | bytes 524320 | tf_op jit(solution)/shard_map/ppermute | solution.py:16
  152.3 4.2 %collective-permute-start.18 = (f32[2,512,256]{2,1,0:T(8,128)S(1)}, f32[2,512,256]{2,1,0:T(8,128)S(1)}, u32[]{:S(2)}, u32[]{:S(2)}) collective-permute-start(f32[2,512,256]{2,1,0:T(8,128)S(1)} %pad_maximum_fusion.2), channel_id=1, source_target_pairs={{0,2},{5,7},{10,8},{15,13},{16,18},{21,23},{26,24},{31,29}} | collective-permute-start | bytes 3145736 | tf_op jit(solution)/shard_map/ppermute | solution.py:151
  160.2 10.6 %shard_map.82 = (f32[2,512,256]{2,1,0:T(8,128)}, f32[2,512,256]{2,1,0:T(8,128)S(1)}) custom-call(s32[5]{0:T(128)S(1)} %pad_add_fusion.place, bf16[6,4,512,2048]{3,2,1,0:T(8,128)(2,1)} %bitcast.201, f32[512,256]{1,0:T(8,128)S(1)} %get-tuple-element.172.refs_0_, f32[512,256]{1,0:T(8,128)S(1)} %collective-permute-done.7.refs_1_, f32[512,256]{1,0:T(8,128)S(1)} %copy-done.4, ...), custom_call_target="tpu_custom_call" | custom-call | tf_op jit(solution)/shard_map/pallas_call | solution.py:83
  170.8 3.5 %collective-permute-done.18 = f32[2,512,256]{2,1,0:T(8,128)S(1)} collective-permute-done((f32[2,512,256]{2,1,0:T(8,128)S(1)}, f32[2,512,256]{2,1,0:T(8,128)S(1)}, u32[]{:S(2)}, u32[]{:S(2)}) %collective-permute-start.18) | collective-permute-done | bytes 1048608 | tf_op jit(solution)/shard_map/ppermute | solution.py:151
  175.4 4.5 %collective-permute-done.20 = f32[1,512,256]{2,1,0:T(8,128)S(1)} collective-permute-done((f32[1,512,256]{2,1,0:T(8,128)S(1)}, f32[1,512,256]{2,1,0:T(8,128)S(1)}, u32[]{:S(2)}, u32[]{:S(2)}) %collective-permute-start.20) | collective-permute-done | bytes 524320 | tf_op jit(solution)/shard_map/ppermute | solution.py:16
  181.2 5.4 %collective-permute-start.22 = (f32[2,512,256]{2,1,0:T(8,128)}, f32[2,512,256]{2,1,0:T(8,128)}, u32[]{:S(2)}, u32[]{:S(2)}) collective-permute-start(f32[2,512,256]{2,1,0:T(8,128)} %pad_maximum_fusion.3), channel_id=1, source_target_pairs={{0,2},{5,7},{10,8},{15,13},{16,18},{21,23},{26,24},{31,29}} | collective-permute-start | bytes 3145736 | tf_op jit(solution)/shard_map/ppermute | solution.py:151
  191.7 10.6 %shard_map.83 = (f32[2,512,256]{2,1,0:T(8,128)S(1)}, f32[2,512,256]{2,1,0:T(8,128)S(1)}) custom-call(s32[5]{0:T(128)S(1)} %pad_add_fusion.place, bf16[6,4,512,2048]{3,2,1,0:T(8,128)(2,1)} %bitcast.202, f32[512,256]{1,0:T(8,128)S(1)} %get-tuple-element.194.refs_0_, f32[512,256]{1,0:T(8,128)S(1)} %collective-permute-done.12.refs_1_, ...), custom_call_target="tpu_custom_call" | custom-call | tf_op jit(solution)/shard_map/pallas_call | solution.py:83
  205.2 4.2 %collective-permute-done.24 = f32[1,512,256]{2,1,0:T(8,128)S(1)} collective-permute-done((f32[1,512,256]{2,1,0:T(8,128)S(1)}, f32[1,512,256]{2,1,0:T(8,128)S(1)}, u32[]{:S(2)}, u32[]{:S(2)}) %collective-permute-start.24) | collective-permute-done | bytes 524320 | tf_op jit(solution)/shard_map/ppermute | solution.py:16
  219.9 11.8 %collective-permute-done.27 = f32[1,512,256]{2,1,0:T(8,128)S(1)} collective-permute-done((f32[1,512,256]{2,1,0:T(8,128)S(1)}, f32[1,512,256]{2,1,0:T(8,128)S(1)}, u32[]{:S(2)}, u32[]{:S(2)}) %collective-permute-start.27) | collective-permute-done | bytes 524320 | tf_op jit(solution)/shard_map/ppermute | solution.py:16
  245.9 7.9 %collective-permute-done.30 = f32[1,2,128,256]{3,2,1,0:T(8,128)} collective-permute-done((f32[1,2,128,256]{3,2,1,0:T(8,128)}, f32[1,2,128,256]{3,2,1,0:T(8,128)}, u32[]{:S(2)}, u32[]{:S(2)}) %collective-permute-start.30) | collective-permute-done | bytes 262176 | tf_op jit(solution)/shard_map/ppermute | solution.py:16
  257.4 3.3 %collective-permute-done.31 = f32[1,256,128]{2,1,0:T(8,128)S(1)} collective-permute-done((f32[1,256,128]{2,1,0:T(8,128)S(1)}, f32[1,256,128]{2,1,0:T(8,128)S(1)}, u32[]{:S(2)}, u32[]{:S(2)}) %collective-permute-start.31) | collective-permute-done | bytes 131104 | tf_op jit(solution)/shard_map/ppermute | solution.py:16
  262.7 4.0 %collective-permute-done.35 = f32[1,1,128,128]{3,2,1,0:T(8,128)S(1)} collective-permute-done((f32[1,1,128,128]{3,2,1,0:T(8,128)S(1)}, f32[1,1,128,128]{3,2,1,0:T(8,128)S(1)}, u32[]{:S(2)}, u32[]{:S(2)}) %collective-permute-start.35) | collective-permute-done | bytes 65568 | tf_op jit(solution)/shard_map/ppermute | solution.py:16
  (178 shorter events, 79.9 us)
Async XLA Ops:
  3.2 27.5 %collective-permute-start = (f32[512,256]{1,0:T(8,128)S(1)}, f32[512,256]{1,0:T(8,128)}, u32[]{:S(2)}, u32[]{:S(2)}) collective-permute-start(f32[512,256]{1,0:T(8,128)S(1)} %get-tuple-element.122.refs_0_), channel_id=1, source_target_pairs={{0,8},{4,12},{8,0},{12,4},{1,9},{5,13},{9,1},{13,5},{2,10},{6,14},... | collective-permute-start | bytes 1572872 | tf_op jit(solution)/shard_map/ppermute | solution.py:16
  7.3 23.5 %collective-permute-start.1 = (f32[512,256]{1,0:T(8,128)S(1)}, f32[512,256]{1,0:T(8,128)S(1)}, u32[]{:S(2)}, u32[]{:S(2)}) collective-permute-start(f32[512,256]{1,0:T(8,128)S(1)} %get-tuple-element.122.refs_0_), channel_id=1, source_target_pairs={{0,4},{4,0},{8,12},{12,8},{1,5},{5,1},{9,13},{13,9},{2,6},{6,2},{1... | collective-permute-start | bytes 1572872 | tf_op jit(solution)/shard_map/ppermute | solution.py:16
  31.5 25.3 %collective-permute-start.3 = (f32[512,256]{1,0:T(8,128)S(1)}, f32[512,256]{1,0:T(8,128)}, u32[]{:S(2)}, u32[]{:S(2)}) collective-permute-start(f32[512,256]{1,0:T(8,128)S(1)} %get-tuple-element.149.refs_0_), channel_id=1, source_target_pairs={{0,8},{4,12},{8,0},{12,4},{1,9},{5,13},{9,1},{13,5},{2,10},{6,14},... | collective-permute-start | bytes 1572872 | tf_op jit(solution)/shard_map/ppermute | solution.py:16
  32.9 24.9 %collective-permute-start.4 = (f32[512,256]{1,0:T(8,128)S(1)}, f32[512,256]{1,0:T(8,128)}, u32[]{:S(2)}, u32[]{:S(2)}) collective-permute-start(f32[512,256]{1,0:T(8,128)S(1)} %get-tuple-element.149.refs_0_), channel_id=1, source_target_pairs={{0,4},{4,0},{8,12},{12,8},{1,5},{5,1},{9,13},{13,9},{2,6},{6,2},{1... | collective-permute-start | bytes 1572872 | tf_op jit(solution)/shard_map/ppermute | solution.py:16
  35.5 32.7 %collective-permute-start.2 = (f32[512,256]{1,0:T(8,128)}, f32[512,256]{1,0:T(8,128)}, u32[]{:S(2)}, u32[]{:S(2)}) collective-permute-start(f32[512,256]{1,0:T(8,128)} %collective-permute-done.refs_2_), channel_id=1, source_target_pairs={{0,4},{4,0},{8,12},{12,8},{1,5},{5,1},{9,13},{13,9},{2,6},{6,2},{1... | collective-permute-start | bytes 1572872 | tf_op jit(solution)/shard_map/ppermute | solution.py:16
  70.4 18.7 %collective-permute-start.8 = (f32[2,512,256]{2,1,0:T(8,128)}, f32[2,512,256]{2,1,0:T(8,128)}, u32[]{:S(2)}, u32[]{:S(2)}) collective-permute-start(f32[2,512,256]{2,1,0:T(8,128)} %pad_maximum_fusion), channel_id=1, source_target_pairs={{0,2},{5,7},{10,8},{15,13},{16,18},{21,23},{26,24},{31,29}} | collective-permute-start | bytes 3145736 | tf_op jit(solution)/shard_map/ppermute | solution.py:151
  74.6 34.0 %collective-permute-start.6 = (f32[512,256]{1,0:T(8,128)S(1)}, f32[512,256]{1,0:T(8,128)S(1)}, u32[]{:S(2)}, u32[]{:S(2)}) collective-permute-start(f32[512,256]{1,0:T(8,128)S(1)} %get-tuple-element.172.refs_0_), channel_id=1, source_target_pairs={{0,8},{4,12},{8,0},{12,4},{1,9},{5,13},{9,1},{13,5},{2,10},{6,14},... | collective-permute-start | bytes 1572872 | tf_op jit(solution)/shard_map/ppermute | solution.py:16
  74.6 34.0 %collective-permute-start.7 = (f32[512,256]{1,0:T(8,128)S(1)}, f32[512,256]{1,0:T(8,128)S(1)}, u32[]{:S(2)}, u32[]{:S(2)}) collective-permute-start(f32[512,256]{1,0:T(8,128)S(1)} %get-tuple-element.172.refs_0_), channel_id=1, source_target_pairs={{0,4},{4,0},{8,12},{12,8},{1,5},{5,1},{9,13},{13,9},{2,6},{6,2},{1... | collective-permute-start | bytes 1572872 | tf_op jit(solution)/shard_map/ppermute | solution.py:16
  75.8 32.8 %collective-permute-start.5 = (f32[512,256]{1,0:T(8,128)}, f32[512,256]{1,0:T(8,128)}, u32[]{:S(2)}, u32[]{:S(2)}) collective-permute-start(f32[512,256]{1,0:T(8,128)} %collective-permute-done.3.refs_2_), channel_id=1, source_target_pairs={{0,4},{4,0},{8,12},{12,8},{1,5},{5,1},{9,13},{13,9},{2,6},{6,2},{1... | collective-permute-start | bytes 1572872 | tf_op jit(solution)/shard_map/ppermute | solution.py:16
  108.6 9.0 %collective-permute-start.14 = (f32[2,512,256]{2,1,0:T(8,128)}, f32[2,512,256]{2,1,0:T(8,128)}, u32[]{:S(2)}, u32[]{:S(2)}) collective-permute-start(f32[2,512,256]{2,1,0:T(8,128)} %get-tuple-element.148), channel_id=1, source_target_pairs={{0,1},{1,0},{2,3},{3,2},{4,5},{5,4},{6,7},{7,6},{8,9},{9,8},{10,11... | collective-permute-start | bytes 3145736 | tf_op jit(solution)/shard_map/ppermute | solution.py:16
  111.0 26.0 %collective-permute-start.13 = (f32[2,512,256]{2,1,0:T(8,128)}, f32[2,512,256]{2,1,0:T(8,128)}, u32[]{:S(2)}, u32[]{:S(2)}) collective-permute-start(f32[2,512,256]{2,1,0:T(8,128)} %pad_maximum_fusion.1), channel_id=1, source_target_pairs={{0,2},{5,7},{10,8},{15,13},{16,18},{21,23},{26,24},{31,29}} | collective-permute-start | bytes 3145736 | tf_op jit(solution)/shard_map/ppermute | solution.py:151
  117.5 34.7 %collective-permute-start.11 = (f32[512,256]{1,0:T(8,128)S(1)}, f32[512,256]{1,0:T(8,128)S(1)}, u32[]{:S(2)}, u32[]{:S(2)}) collective-permute-start(f32[512,256]{1,0:T(8,128)S(1)} %get-tuple-element.194.refs_0_), channel_id=1, source_target_pairs={{0,8},{4,12},{8,0},{12,4},{1,9},{5,13},{9,1},{13,5},{2,10},{6,14},... | collective-permute-start | bytes 1572872 | tf_op jit(solution)/shard_map/ppermute | solution.py:16
  117.6 34.6 %collective-permute-start.12 = (f32[512,256]{1,0:T(8,128)S(1)}, f32[512,256]{1,0:T(8,128)S(1)}, u32[]{:S(2)}, u32[]{:S(2)}) collective-permute-start(f32[512,256]{1,0:T(8,128)S(1)} %get-tuple-element.194.refs_0_), channel_id=1, source_target_pairs={{0,4},{4,0},{8,12},{12,8},{1,5},{5,1},{9,13},{13,9},{2,6},{6,2},{1... | collective-permute-start | bytes 1572872 | tf_op jit(solution)/shard_map/ppermute | solution.py:16
  117.6 34.5 %collective-permute-start.10 = (f32[512,256]{1,0:T(8,128)}, f32[512,256]{1,0:T(8,128)S(1)}, u32[]{:S(2)}, u32[]{:S(2)}) collective-permute-start(f32[512,256]{1,0:T(8,128)} %copy-done.3), channel_id=1, source_target_pairs={{0,4},{4,0},{8,12},{12,8},{1,5},{5,1},{9,13},{13,9},{2,6},{6,2},{1... | collective-permute-start | bytes 1572872 | tf_op jit(solution)/shard_map/ppermute | solution.py:16
  121.4 17.2 %collective-permute-start.15 = (f32[1,512,256]{2,1,0:T(8,128)S(1)}, f32[1,512,256]{2,1,0:T(8,128)S(1)}, u32[]{:S(2)}, u32[]{:S(2)}) collective-permute-start(f32[1,512,256]{2,1,0:T(8,128)S(1)} %slice_bitcast_fusion.11), channel_id=1, source_target_pairs={{0,2},{1,3},{2,0},{3,1},{4,6},{5,7},{6,4},{7,5},{8,10},{9,11},{10,... | collective-permute-start | bytes 1572872 | tf_op jit(solution)/shard_map/ppermute | solution.py:16
  152.3 22.0 %collective-permute-start.18 = (f32[2,512,256]{2,1,0:T(8,128)S(1)}, f32[2,512,256]{2,1,0:T(8,128)S(1)}, u32[]{:S(2)}, u32[]{:S(2)}) collective-permute-start(f32[2,512,256]{2,1,0:T(8,128)S(1)} %pad_maximum_fusion.2), channel_id=1, source_target_pairs={{0,2},{5,7},{10,8},{15,13},{16,18},{21,23},{26,24},{31,29}} | collective-permute-start | bytes 3145736 | tf_op jit(solution)/shard_map/ppermute | solution.py:151
  157.8 22.2 %collective-permute-start.17 = (f32[512,256]{1,0:T(8,128)S(1)}, f32[512,256]{1,0:T(8,128)S(1)}, u32[]{:S(2)}, u32[]{:S(2)}) collective-permute-start(f32[512,256]{1,0:T(8,128)S(1)} %collective-permute-done.11.refs_2_), channel_id=1, source_target_pairs={{0,4},{4,0},{8,12},{12,8},{1,5},{5,1},{9,13},{13,9},{2,6},{6,2},{1... | collective-permute-start | bytes 1572872 | tf_op jit(solution)/shard_map/ppermute | solution.py:16
  158.1 21.9 %collective-permute-start.20 = (f32[1,512,256]{2,1,0:T(8,128)S(1)}, f32[1,512,256]{2,1,0:T(8,128)S(1)}, u32[]{:S(2)}, u32[]{:S(2)}) collective-permute-start(f32[1,512,256]{2,1,0:T(8,128)S(1)} %slice_bitcast_fusion.7), channel_id=1, source_target_pairs={{0,2},{1,3},{2,0},{3,1},{4,6},{5,7},{6,4},{7,5},{8,10},{9,11},{10,... | collective-permute-start | bytes 1572872 | tf_op jit(solution)/shard_map/ppermute | solution.py:16
  181.2 22.6 %collective-permute-start.22 = (f32[2,512,256]{2,1,0:T(8,128)}, f32[2,512,256]{2,1,0:T(8,128)}, u32[]{:S(2)}, u32[]{:S(2)}) collective-permute-start(f32[2,512,256]{2,1,0:T(8,128)} %pad_maximum_fusion.3), channel_id=1, source_target_pairs={{0,2},{5,7},{10,8},{15,13},{16,18},{21,23},{26,24},{31,29}} | collective-permute-start | bytes 3145736 | tf_op jit(solution)/shard_map/ppermute | solution.py:151
  190.4 18.9 %collective-permute-start.24 = (f32[1,512,256]{2,1,0:T(8,128)S(1)}, f32[1,512,256]{2,1,0:T(8,128)S(1)}, u32[]{:S(2)}, u32[]{:S(2)}) collective-permute-start(f32[1,512,256]{2,1,0:T(8,128)S(1)} %slice_bitcast_fusion.3), channel_id=1, source_target_pairs={{0,2},{1,3},{2,0},{3,1},{4,6},{5,7},{6,4},{7,5},{8,10},{9,11},{10,... | collective-permute-start | bytes 1572872 | tf_op jit(solution)/shard_map/ppermute | solution.py:16
  217.0 14.7 %collective-permute-start.27 = (f32[1,512,256]{2,1,0:T(8,128)S(1)}, f32[1,512,256]{2,1,0:T(8,128)S(1)}, u32[]{:S(2)}, u32[]{:S(2)}) collective-permute-start(f32[1,512,256]{2,1,0:T(8,128)S(1)} %slice_bitcast_fusion.1), channel_id=1, source_target_pairs={{0,2},{1,3},{2,0},{3,1},{4,6},{5,7},{6,4},{7,5},{8,10},{9,11},{10,... | collective-permute-start | bytes 1572872 | tf_op jit(solution)/shard_map/ppermute | solution.py:16
  219.9 13.7 %collective-permute-start.29 = (f32[2,2,128,256]{3,2,1,0:T(8,128)S(1)}, f32[2,2,128,256]{3,2,1,0:T(8,128)S(1)}, u32[]{:S(2)}, u32[]{:S(2)}) collective-permute-start(f32[2,2,128,256]{3,2,1,0:T(8,128)S(1)} %bitcast.216), channel_id=1, source_target_pairs={{0,4},{4,0},{8,12},{12,8},{1,5},{5,1},{9,13},{13,9},{2,6},{6,2},{1... | collective-permute-start | bytes 1572872 | tf_op jit(solution)/shard_map/ppermute | solution.py:16
  238.5 15.3 %collective-permute-start.30 = (f32[1,2,128,256]{3,2,1,0:T(8,128)}, f32[1,2,128,256]{3,2,1,0:T(8,128)}, u32[]{:S(2)}, u32[]{:S(2)}) collective-permute-start(f32[1,2,128,256]{3,2,1,0:T(8,128)} %constant_dynamic-slice_fusion.9), channel_id=1, source_target_pairs={{0,8},{4,12},{8,0},{12,4},{1,9},{5,13},{9,1},{13,5},{2,10},{6,14},... | collective-permute-start | bytes 786440 | tf_op jit(solution)/shard_map/ppermute | solution.py:16
  244.4 11.3 %collective-permute-start.33 = (f32[1,512,128]{2,1,0:T(8,128)}, f32[1,512,128]{2,1,0:T(8,128)S(1)}, u32[]{:S(2)}, u32[]{:S(2)}) collective-permute-start(f32[1,512,128]{2,1,0:T(8,128)} %bitcast.73), channel_id=1, source_target_pairs={{0,2},{1,3},{2,0},{3,1},{4,6},{5,7},{6,4},{7,5},{8,10},{9,11},{10,... | collective-permute-start | bytes 786440 | tf_op jit(solution)/shard_map/ppermute | solution.py:16
  (35 other events, 239.4 us)

commit v9 on v8

--- a/solution.py
+++ b/solution.py
@@ -173,7 +173,8 @@
         late = 2 * span
         pieces = [("first", i, i + late) for i in range(0, width, late)]
         count_first = len(pieces)
-        pieces += [("second", i, i + late) for i in range(0, width, late)]
+        pieces += [("second", i, i + late) for i in range(0, width - late, late)]
+        pieces += [("second", i, i + span) for i in range(width - late, width, span)]
         stages = rows_axis.bit_length() - 1
         second = panels[1] * kept_second - dot(panels[0] * kept_first, link, precise)
         for k, (panel, start, stop) in enumerate(pieces):
@@ -239,18 +240,24 @@
             return jnp.concatenate(columns_by_xor(array, odd), axis=1)
 
         def first_terms():
-            out_first = outs(0, count_first)
-            own_first, own_second = owns(0, count_first), owns(count_first, len(pieces))
-
-            def terms(odd):
-                cross = dot_tn(out_first, by_parity(own_second, odd), three_pass) + by_parity(live["link_cross"], odd)
-                return jnp.concatenate([dot_tn(out_first, by_parity(own_first, odd), three_pass), cross])
-
-            live["first_sums"] = sum_step(by_rows(core_sum(terms)), "row", 1)
-
-        def first_sums():
-            sums = sum_rows(live["first_sums"], "row", 2)
-            live["first_sums"] = rest_of_cols(sums.reshape(-1, sums.shape[2])).reshape(-1, height, span)
+            out_first, own_first = outs(0, count_first), owns(0, count_first)
+            sums = core_sum(lambda odd: dot_tn(out_first, by_parity(own_first, odd), three_pass))
+            live["first_sum"] = by_rows(rest_of_cols(sums))
+
+        def first_rows():
+            live["first_sum"] = sum_rows(live["first_sum"], "row")[0]
+
+        def cross_terms():
+            out_first, own_second = outs(0, count_first), owns(count_first, len(pieces))
+            sums = core_sum(lambda odd: dot_tn(out_first, by_parity(own_second, odd), three_pass)
+                            + by_parity(live["link_cross"], odd))
+            live["cross_sum"] = sum_step(by_rows(sums), "row", 1)
+
+        def cross_rows():
+            live["cross_sum"] = sum_rows(live["cross_sum"], "row", 2)[0]
+
+        def cross_cols():
+            live["cross_sum"] = rest_of_cols(live["cross_sum"])
 
         def second_terms():
             out_second, own_second = outs(count_first, len(pieces)), owns(count_first, len(pieces))
@@ -258,7 +265,10 @@
             def terms(odd):
                 return dot_tn(out_second, by_parity(own_second, odd), three_pass) + by_parity(live["link_second"], odd)
 
-            live["second_sum"] = sum_rows(by_rows(rest_of_cols(core_sum(terms))), "row")[0]
+            live["second_sum"] = by_rows(rest_of_cols(core_sum(terms)))
+
+        def second_rows():
+            live["second_sum"] = sum_rows(live["second_sum"], "row")[0]
 
         at(1, link_terms)
         last = len(pieces) - 1 + stages
@@ -271,9 +281,10 @@
             at(k + stages, lambda k=k: multiply(k))
         for k in range(len(pieces)):
             at(k + stages + 1, lambda k=k: add_rest(k))
-        end = last + 2
-        at(last + 1, first_terms)
-        at(end, first_sums, second_terms)
+        end = last + 3
+        at(last + 1, cross_terms, first_terms)
+        at(last + 2, cross_rows, second_terms, first_rows)
+        at(end, second_rows, cross_cols)
 
         for slot in range(end + 1):
             if slot > 0:
@@ -281,10 +292,9 @@
             for step in slots[slot]:
                 step()
 
-        first_sum, cross_sum = live["first_sums"]
         ancestor = jnp.stack([outs(0, count_first), outs(count_first, len(pieces))])
-        diagonal = jnp.stack([given_first - first_sum, given_second - live["second_sum"]])
-        return ancestor, diagonal, -cross_sum
+        diagonal = jnp.stack([given_first - live["first_sum"], given_second - live["second_sum"]])
+        return ancestor, diagonal, -live["cross_sum"]
 
     results = [one_pair(panels[s], kept_rows[s, 0, :, None], kept_rows[s, 1, :, None], link_panel[s],
                         diag_inverse[s, 0], diag_inverse[s, 1])

time: 268 us -> 285 us (1.063)
  waiting for transfers between devices: 111 us -> 92.3 us
  starting transfers between devices: 49.4 us -> 62.5 us
  Pallas kernels: 50.9 us -> 61.4 us
  local copies, waits for them, and re-layouts: 15.8 us -> 25.2 us
    ppermute x28 -> x37, waiting for transfers between devices: 104 us -> 81.1 us  [swap(): return lax.ppermute(block, axis, pairs)]
    pallas_call x4 -> x5, Pallas kernels: 43.8 us -> 54.2 us  [product(): pl.pallas_call(product_kernel, in_specs=[pl.BlockSpec(memory_space=pltpu....]
    ppermute x28 -> x37, starting transfers between devices: 24.1 us -> 31.6 us  [swap(): return lax.ppermute(block, axis, pairs)]
    ppermute x8 -> x10, starting transfers between devices: 25.3 us -> 30.9 us  [spread_step(): moved = lax.ppermute(jnp.stack(held[bit:]), ('row', 'col'), pairs)]
    ppermute x8 -> x10, waiting for transfers between devices: 6.22 us -> 11.1 us  [spread_step(): moved = lax.ppermute(jnp.stack(held[bit:]), ('row', 'col'), pairs)]
    select_n x8 -> x10, other arithmetic: 10.7 us -> 9.35 us  [spread_step(): return [jnp.where(offset & bit != 0, moved[j], held[j]) for j in range(bit)]]
    unnamed x53 -> x57, local copies, waits for them, and re-layouts: 9.92 us -> 10.9 us
    another operation x4 -> x5, other arithmetic: 5.77 us -> 5.5 us  [spread_step(): moved = lax.ppermute(jnp.stack(held[bit:]), ('row', 'col'), pairs)]
  transfers between devices with their start and end apart: 36 -> 47, of which waited for: 18 -> 17; matrix products, arithmetic and copies ran while one was open for 14% -> 16% of each run, Pallas kernels for 19% -> 22%
where the time goes in v9:
time: 285 us; the launch traced here: 284 us
  waiting for transfers between devices  92.3 us (32%)
  starting transfers between devices  62.5 us (22%)
  Pallas kernels  61.4 us (22%)
  other arithmetic  28.8 us (10%)
  local copies, waits for them, and re-layouts  25.2 us (9%)
  matrix products  12.5 us (4%)
    ppermute x37, waiting for transfers between devices, swap(): return lax.ppermute(block, axis, pairs)  81.1 us
    pallas_call x5, Pallas kernels, product(): pl.pallas_call(product_kernel, in_specs=[pl.BlockSpec(memory_space=pltpu....  54.2 us
    ppermute x37, starting transfers between devices, swap(): return lax.ppermute(block, axis, pairs)  31.6 us
    ppermute x10, starting transfers between devices, spread_step(): moved = lax.ppermute(jnp.stack(held[bit:]), ('row', 'col'), pairs)  30.9 us
    ppermute x10, waiting for transfers between devices, spread_step(): moved = lax.ppermute(jnp.stack(held[bit:]), ('row', 'col'), pairs)  11.1 us
    unnamed x57, local copies, waits for them, and re-layouts  10.9 us
    dot_general x7, matrix products, dot_tn(): return lax.dot_general(a, b, (((0,), (0,)), ((), ())), precision=precision)  10.2 us
    select_n x10, other arithmetic, spread_step(): return [jnp.where(offset & bit != 0, moved[j], held[j]) for j in range(bit)]  9.35 us
  transfers between devices with their start and end apart: 47, of which 17 were waited for; matrix products, arithmetic and copies ran while one was open for 16% of the time, Pallas kernels for 22%

profile of v9, /device:TPU:0, one launch (start us, length us, event | category | flops | bytes accessed | tf_op | source)
XLA Modules:
  0.0 284.2 jit_solution(15092250794858022948)
XLA Ops:
  3.2 4.1 %collective-permute-start = (f32[512,256]{1,0:T(8,128)S(1)}, f32[512,256]{1,0:T(8,128)}, u32[]{:S(2)}, u32[]{:S(2)}) collective-permute-start(f32[512,256]{1,0:T(8,128)S(1)} %get-tuple-element.168.refs_0_), channel_id=1, source_target_pairs={{0,8},{4,12},{8,0},{12,4},{1,9},{5,13},{9,1},{13,5},{2,10},{6,14},... | collective-permute-start | bytes 1572872 | tf_op jit(solution)/shard_map/ppermute | solution.py:16
  10.9 5.8 %copy-done.2 = f32[2048,2048]{1,0:T(8,128)S(1)} copy-done((f32[2048,2048]{1,0:T(8,128)S(1)}, f32[2048,2048]{1,0:T(8,128)}, u32[]{:S(2)}) %copy-start.2) | copy-done | bytes 16777240
  16.6 7.2 %shard_map.79 = bf16[6,2048,2048]{2,1,0:T(8,128)(2,1)} custom-call(f32[2048,2048]{1,0:T(8,128)S(1)} %copy-done.2), custom_call_target="tpu_custom_call" | custom-call | tf_op jit(solution)/shard_map/pallas_call | solution.py:34
  23.8 6.8 %collective-permute-done.refs_2_ = f32[512,256]{1,0:T(8,128)} collective-permute-done((f32[512,256]{1,0:T(8,128)S(1)}, f32[512,256]{1,0:T(8,128)}, u32[]{:S(2)}, u32[]{:S(2)}) %collective-permute-start) | collective-permute-done | bytes 524320 | tf_op jit(solution)/shard_map/ppermute | solution.py:16
  38.0 18.8 %collective-permute-done.3.refs_2_ = f32[512,256]{1,0:T(8,128)} collective-permute-done((f32[512,256]{1,0:T(8,128)S(1)}, f32[512,256]{1,0:T(8,128)}, u32[]{:S(2)}, u32[]{:S(2)}) %collective-permute-start.3) | collective-permute-done | bytes 524320 | tf_op jit(solution)/shard_map/ppermute | solution.py:16
  57.9 10.3 %collective-permute-done.2.refs_3_ = f32[512,256]{1,0:T(8,128)} collective-permute-done((f32[512,256]{1,0:T(8,128)}, f32[512,256]{1,0:T(8,128)}, u32[]{:S(2)}, u32[]{:S(2)}) %collective-permute-start.2) | collective-permute-done | bytes 524320 | tf_op jit(solution)/shard_map/ppermute | solution.py:16
  70.4 4.2 %collective-permute-start.8 = (f32[2,512,256]{2,1,0:T(8,128)}, f32[2,512,256]{2,1,0:T(8,128)}, u32[]{:S(2)}, u32[]{:S(2)}) collective-permute-start(f32[2,512,256]{2,1,0:T(8,128)} %pad_maximum_fusion), channel_id=1, source_target_pairs={{0,2},{5,7},{10,8},{15,13},{16,18},{21,23},{26,24},{31,29}} | collective-permute-start | bytes 3145736 | tf_op jit(solution)/shard_map/ppermute | solution.py:151
  77.9 11.2 %shard_map.80 = (f32[2,512,256]{2,1,0:T(8,128)}, f32[2,512,256]{2,1,0:T(8,128)S(1)}) custom-call(s32[5]{0:T(128)S(1)} %pad_add_fusion.place, bf16[6,4,512,2048]{3,2,1,0:T(8,128)(2,1)} %bitcast.244, f32[512,256]{1,0:T(8,128)S(1)} %get-tuple-element.168.refs_0_, f32[512,256]{1,0:T(8,128)S(1)} %copy-done.4, f32[512,256]{1,0:T(8,128)} %collective-permute-done.refs_2_, ...), custom_call_target="tpu_custom_call" | custom-call | tf_op jit(solution)/shard_map/pallas_call | solution.py:83
  91.9 16.7 %collective-permute-done.5.refs_3_ = f32[512,256]{1,0:T(8,128)} collective-permute-done((f32[512,256]{1,0:T(8,128)}, f32[512,256]{1,0:T(8,128)}, u32[]{:S(2)}, u32[]{:S(2)}) %collective-permute-start.5) | collective-permute-done | bytes 524320 | tf_op jit(solution)/shard_map/ppermute | solution.py:16
  110.9 4.3 %collective-permute-start.13 = (f32[2,512,256]{2,1,0:T(8,128)}, f32[2,512,256]{2,1,0:T(8,128)}, u32[]{:S(2)}, u32[]{:S(2)}) collective-permute-start(f32[2,512,256]{2,1,0:T(8,128)} %pad_maximum_fusion.1), channel_id=1, source_target_pairs={{0,2},{5,7},{10,8},{15,13},{16,18},{21,23},{26,24},{31,29}} | collective-permute-start | bytes 3145736 | tf_op jit(solution)/shard_map/ppermute | solution.py:151
  125.5 11.4 %shard_map.81 = (f32[2,512,256]{2,1,0:T(8,128)S(1)}, f32[2,512,256]{2,1,0:T(8,128)S(1)}) custom-call(s32[5]{0:T(128)S(1)} %pad_add_fusion.place, bf16[6,4,512,2048]{3,2,1,0:T(8,128)(2,1)} %bitcast.245, f32[512,256]{1,0:T(8,128)S(1)} %get-tuple-element.196.refs_0_, f32[512,256]{1,0:T(8,128)} %collective-permute-done.4.refs_1_, ...), custom_call_target="tpu_custom_call" | custom-call | tf_op jit(solution)/shard_map/pallas_call | solution.py:83
  141.0 4.2 %collective-permute-start.20 = (f32[2,512,256]{2,1,0:T(8,128)S(1)}, f32[2,512,256]{2,1,0:T(8,128)S(1)}, u32[]{:S(2)}, u32[]{:S(2)}) collective-permute-start(f32[2,512,256]{2,1,0:T(8,128)S(1)} %pad_maximum_fusion.2), channel_id=1, source_target_pairs={{0,2},{5,7},{10,8},{15,13},{16,18},{21,23},{26,24},{31,29}} | collective-permute-start | bytes 3145736 | tf_op jit(solution)/shard_map/ppermute | solution.py:151
  152.5 10.6 %shard_map.82 = (f32[2,512,256]{2,1,0:T(8,128)S(1)}, f32[2,512,256]{2,1,0:T(8,128)S(1)}) custom-call(s32[5]{0:T(128)S(1)} %pad_add_fusion.place, bf16[6,4,512,2048]{3,2,1,0:T(8,128)(2,1)} %bitcast.246, f32[512,256]{1,0:T(8,128)S(1)} %slice.155.refs_0_, f32[512,256]{1,0:T(8,128)S(1)} %collective-permute-done.7.refs_1_, ...), custom_call_target="tpu_custom_call" | custom-call | tf_op jit(solution)/shard_map/pallas_call | solution.py:83
  163.3 5.4 %collective-permute-done.22 = f32[1,512,256]{2,1,0:T(8,128)S(1)} collective-permute-done((f32[1,512,256]{2,1,0:T(8,128)S(1)}, f32[1,512,256]{2,1,0:T(8,128)S(1)}, u32[]{:S(2)}, u32[]{:S(2)}) %collective-permute-start.22) | collective-permute-done | bytes 524320 | tf_op jit(solution)/shard_map/ppermute | solution.py:16
  169.7 4.4 %collective-permute-start.25 = (f32[2,512,128]{2,1,0:T(8,128)S(1)}, f32[2,512,128]{2,1,0:T(8,128)S(1)}, u32[]{:S(2)}, u32[]{:S(2)}) collective-permute-start(f32[2,512,128]{2,1,0:T(8,128)S(1)} %pad_maximum_fusion.4), channel_id=1, source_target_pairs={{0,2},{5,7},{10,8},{15,13},{16,18},{21,23},{26,24},{31,29}} | collective-permute-start | bytes 1572872 | tf_op jit(solution)/shard_map/ppermute | solution.py:151
  175.8 10.5 %collective-permute-done.25 = f32[2,512,128]{2,1,0:T(8,128)S(1)} collective-permute-done((f32[2,512,128]{2,1,0:T(8,128)S(1)}, f32[2,512,128]{2,1,0:T(8,128)S(1)}, u32[]{:S(2)}, u32[]{:S(2)}) %collective-permute-start.25) | collective-permute-done | bytes 524320 | tf_op jit(solution)/shard_map/ppermute | solution.py:151
  187.3 10.5 %shard_map.83 = (f32[2,512,128]{2,1,0:T(8,128)S(1)}, f32[2,512,128]{2,1,0:T(8,128)S(1)}) custom-call(s32[5]{0:T(128)S(1)} %pad_add_fusion.place, bf16[6,4,512,2048]{3,2,1,0:T(8,128)(2,1)} %bitcast.247, f32[512,128]{1,0:T(8,128)S(1)} %get-tuple-element.245.refs_0_, f32[512,128]{1,0:T(8,128)S(1)} %collective-permute-done.12.refs_1_, ...), custom_call_target="tpu_custom_call" | custom-call | tf_op jit(solution)/shard_map/pallas_call | solution.py:83
  199.5 5.2 %collective-permute-start.29 = (f32[2,512,128]{2,1,0:T(8,128)}, f32[2,512,128]{2,1,0:T(8,128)}, u32[]{:S(2)}, u32[]{:S(2)}) collective-permute-start(f32[2,512,128]{2,1,0:T(8,128)} %pad_maximum_fusion.5), channel_id=1, source_target_pairs={{0,2},{5,7},{10,8},{15,13},{16,18},{21,23},{26,24},{31,29}} | collective-permute-start | bytes 1572872 | tf_op jit(solution)/shard_map/ppermute | solution.py:151
  207.5 10.5 %shard_map.84 = (f32[2,512,128]{2,1,0:T(8,128)S(1)}, f32[2,512,128]{2,1,0:T(8,128)S(1)}) custom-call(s32[5]{0:T(128)S(1)} %pad_add_fusion.place, bf16[6,4,512,2048]{3,2,1,0:T(8,128)(2,1)} %bitcast.248, f32[512,128]{1,0:T(8,128)S(1)} %get-tuple-element.269.refs_0_, f32[512,128]{1,0:T(8,128)S(1)} %collective-permute-done.19.refs_1_, ...), custom_call_target="tpu_custom_call" | custom-call | tf_op jit(solution)/shard_map/pallas_call | solution.py:83
  232.9 3.0 %collective-permute-done.34 = f32[1,512,128]{2,1,0:T(8,128)} collective-permute-done((f32[1,512,128]{2,1,0:T(8,128)}, f32[1,512,128]{2,1,0:T(8,128)}, u32[]{:S(2)}, u32[]{:S(2)}) %collective-permute-start.34) | collective-permute-done | bytes 262176 | tf_op jit(solution)/shard_map/ppermute | solution.py:16
  259.2 3.1 %fusion.1 = f32[512,256]{1,0:T(8,128)} fusion(f32[512,256]{1,0:T(8,128)} %collective-permute-done.42, f32[512,512]{1,0:T(8,128)S(1)} %constant_dynamic-update-slice_fusion.4, f32[512,128]{1,0:T(8,128)} %get-tuple-element.321, f32[512,128]{1,0:T(8,128)S(1)} %get-tuple-element.318, f32[512,128]{1,0:T(8,128)} %get-tuple-element.317, ...), kind=kOutput, calls=%fused_computation.9 | convolution fusion | flops 403177472 | bytes 3145728 | tf_op jit(solution)/shard_map/dot_general | solution.py:99
  266.6 5.0 %collective-permute-done.43 = f32[1,512,128]{2,1,0:T(8,128)S(1)} collective-permute-done((f32[1,512,128]{2,1,0:T(8,128)S(1)}, f32[1,512,128]{2,1,0:T(8,128)S(1)}, u32[]{:S(2)}, u32[]{:S(2)}) %collective-permute-start.43) | collective-permute-done | bytes 262176 | tf_op jit(solution)/shard_map/ppermute | solution.py:16
  274.9 2.7 collective-permute-done.44
  279.9 3.6 %collective-permute-done.45 = f32[1,1,128,128]{3,2,1,0:T(8,128)S(1)} collective-permute-done((f32[1,1,128,128]{3,2,1,0:T(8,128)S(1)}, f32[1,1,128,128]{3,2,1,0:T(8,128)S(1)}, u32[]{:S(2)}, u32[]{:S(2)}) %collective-permute-start.45) | collective-permute-done | bytes 65568 | tf_op jit(solution)/shard_map/ppermute | solution.py:16
  (220 shorter events, 103.1 us)
Async XLA Ops:
  3.2 27.5 %collective-permute-start = (f32[512,256]{1,0:T(8,128)S(1)}, f32[512,256]{1,0:T(8,128)}, u32[]{:S(2)}, u32[]{:S(2)}) collective-permute-start(f32[512,256]{1,0:T(8,128)S(1)} %get-tuple-element.168.refs_0_), channel_id=1, source_target_pairs={{0,8},{4,12},{8,0},{12,4},{1,9},{5,13},{9,1},{13,5},{2,10},{6,14},... | collective-permute-start | bytes 1572872 | tf_op jit(solution)/shard_map/ppermute | solution.py:16
  7.3 23.5 %collective-permute-start.1 = (f32[512,256]{1,0:T(8,128)S(1)}, f32[512,256]{1,0:T(8,128)S(1)}, u32[]{:S(2)}, u32[]{:S(2)}) collective-permute-start(f32[512,256]{1,0:T(8,128)S(1)} %get-tuple-element.168.refs_0_), channel_id=1, source_target_pairs={{0,4},{4,0},{8,12},{12,8},{1,5},{5,1},{9,13},{13,9},{2,6},{6,2},{1... | collective-permute-start | bytes 1572872 | tf_op jit(solution)/shard_map/ppermute | solution.py:16
  31.5 25.3 %collective-permute-start.3 = (f32[512,256]{1,0:T(8,128)S(1)}, f32[512,256]{1,0:T(8,128)}, u32[]{:S(2)}, u32[]{:S(2)}) collective-permute-start(f32[512,256]{1,0:T(8,128)S(1)} %get-tuple-element.196.refs_0_), channel_id=1, source_target_pairs={{0,8},{4,12},{8,0},{12,4},{1,9},{5,13},{9,1},{13,5},{2,10},{6,14},... | collective-permute-start | bytes 1572872 | tf_op jit(solution)/shard_map/ppermute | solution.py:16
  32.9 24.9 %collective-permute-start.4 = (f32[512,256]{1,0:T(8,128)S(1)}, f32[512,256]{1,0:T(8,128)}, u32[]{:S(2)}, u32[]{:S(2)}) collective-permute-start(f32[512,256]{1,0:T(8,128)S(1)} %get-tuple-element.196.refs_0_), channel_id=1, source_target_pairs={{0,4},{4,0},{8,12},{12,8},{1,5},{5,1},{9,13},{13,9},{2,6},{6,2},{1... | collective-permute-start | bytes 1572872 | tf_op jit(solution)/shard_map/ppermute | solution.py:16
  35.5 32.7 %collective-permute-start.2 = (f32[512,256]{1,0:T(8,128)}, f32[512,256]{1,0:T(8,128)}, u32[]{:S(2)}, u32[]{:S(2)}) collective-permute-start(f32[512,256]{1,0:T(8,128)} %collective-permute-done.refs_2_), channel_id=1, source_target_pairs={{0,4},{4,0},{8,12},{12,8},{1,5},{5,1},{9,13},{13,9},{2,6},{6,2},{1... | collective-permute-start | bytes 1572872 | tf_op jit(solution)/shard_map/ppermute | solution.py:16
  70.4 18.7 %collective-permute-start.8 = (f32[2,512,256]{2,1,0:T(8,128)}, f32[2,512,256]{2,1,0:T(8,128)}, u32[]{:S(2)}, u32[]{:S(2)}) collective-permute-start(f32[2,512,256]{2,1,0:T(8,128)} %pad_maximum_fusion), channel_id=1, source_target_pairs={{0,2},{5,7},{10,8},{15,13},{16,18},{21,23},{26,24},{31,29}} | collective-permute-start | bytes 3145736 | tf_op jit(solution)/shard_map/ppermute | solution.py:151
  74.6 34.0 %collective-permute-start.6 = (f32[512,256]{1,0:T(8,128)S(1)}, f32[512,256]{1,0:T(8,128)S(1)}, u32[]{:S(2)}, u32[]{:S(2)}) collective-permute-start(f32[512,256]{1,0:T(8,128)S(1)} %slice.155.refs_0_), channel_id=1, source_target_pairs={{0,8},{4,12},{8,0},{12,4},{1,9},{5,13},{9,1},{13,5},{2,10},{6,14},... | collective-permute-start | bytes 1572872 | tf_op jit(solution)/shard_map/ppermute | solution.py:16
  74.6 34.0 %collective-permute-start.7 = (f32[512,256]{1,0:T(8,128)S(1)}, f32[512,256]{1,0:T(8,128)S(1)}, u32[]{:S(2)}, u32[]{:S(2)}) collective-permute-start(f32[512,256]{1,0:T(8,128)S(1)} %slice.155.refs_0_), channel_id=1, source_target_pairs={{0,4},{4,0},{8,12},{12,8},{1,5},{5,1},{9,13},{13,9},{2,6},{6,2},{1... | collective-permute-start | bytes 1572872 | tf_op jit(solution)/shard_map/ppermute | solution.py:16
  75.8 32.8 %collective-permute-start.5 = (f32[512,256]{1,0:T(8,128)}, f32[512,256]{1,0:T(8,128)}, u32[]{:S(2)}, u32[]{:S(2)}) collective-permute-start(f32[512,256]{1,0:T(8,128)} %collective-permute-done.3.refs_2_), channel_id=1, source_target_pairs={{0,4},{4,0},{8,12},{12,8},{1,5},{5,1},{9,13},{13,9},{2,6},{6,2},{1... | collective-permute-start | bytes 1572872 | tf_op jit(solution)/shard_map/ppermute | solution.py:16
  110.9 26.0 %collective-permute-start.13 = (f32[2,512,256]{2,1,0:T(8,128)}, f32[2,512,256]{2,1,0:T(8,128)}, u32[]{:S(2)}, u32[]{:S(2)}) collective-permute-start(f32[2,512,256]{2,1,0:T(8,128)} %pad_maximum_fusion.1), channel_id=1, source_target_pairs={{0,2},{5,7},{10,8},{15,13},{16,18},{21,23},{26,24},{31,29}} | collective-permute-start | bytes 3145736 | tf_op jit(solution)/shard_map/ppermute | solution.py:151
  117.4 21.1 %collective-permute-start.11 = (f32[512,128]{1,0:T(8,128)S(1)}, f32[512,128]{1,0:T(8,128)S(1)}, u32[]{:S(2)}, u32[]{:S(2)}) collective-permute-start(f32[512,128]{1,0:T(8,128)S(1)} %get-tuple-element.245.refs_0_), channel_id=1, source_target_pairs={{0,8},{4,12},{8,0},{12,4},{1,9},{5,13},{9,1},{13,5},{2,10},{6,14},... | collective-permute-start | bytes 786440 | tf_op jit(solution)/shard_map/ppermute | solution.py:16
  117.6 20.9 %collective-permute-start.12 = (f32[512,128]{1,0:T(8,128)S(1)}, f32[512,128]{1,0:T(8,128)S(1)}, u32[]{:S(2)}, u32[]{:S(2)}) collective-permute-start(f32[512,128]{1,0:T(8,128)S(1)} %get-tuple-element.245.refs_0_), channel_id=1, source_target_pairs={{0,4},{4,0},{8,12},{12,8},{1,5},{5,1},{9,13},{13,9},{2,6},{6,2},{1... | collective-permute-start | bytes 786440 | tf_op jit(solution)/shard_map/ppermute | solution.py:16
  117.6 23.3 %collective-permute-start.10 = (f32[512,256]{1,0:T(8,128)S(1)}, f32[512,256]{1,0:T(8,128)S(1)}, u32[]{:S(2)}, u32[]{:S(2)}) collective-permute-start(f32[512,256]{1,0:T(8,128)S(1)} %collective-permute-done.6.refs_2_), channel_id=1, source_target_pairs={{0,4},{4,0},{8,12},{12,8},{1,5},{5,1},{9,13},{13,9},{2,6},{6,2},{1... | collective-permute-start | bytes 1572872 | tf_op jit(solution)/shard_map/ppermute | solution.py:16
  121.4 17.0 %collective-permute-start.15 = (f32[1,512,256]{2,1,0:T(8,128)S(1)}, f32[1,512,256]{2,1,0:T(8,128)S(1)}, u32[]{:S(2)}, u32[]{:S(2)}) collective-permute-start(f32[1,512,256]{2,1,0:T(8,128)S(1)} %slice_bitcast_fusion.7), channel_id=1, source_target_pairs={{0,2},{1,3},{2,0},{3,1},{4,6},{5,7},{6,4},{7,5},{8,10},{9,11},{10,... | collective-permute-start | bytes 1572872 | tf_op jit(solution)/shard_map/ppermute | solution.py:16
  141.0 22.1 %collective-permute-start.20 = (f32[2,512,256]{2,1,0:T(8,128)S(1)}, f32[2,512,256]{2,1,0:T(8,128)S(1)}, u32[]{:S(2)}, u32[]{:S(2)}) collective-permute-start(f32[2,512,256]{2,1,0:T(8,128)S(1)} %pad_maximum_fusion.2), channel_id=1, source_target_pairs={{0,2},{5,7},{10,8},{15,13},{16,18},{21,23},{26,24},{31,29}} | collective-permute-start | bytes 3145736 | tf_op jit(solution)/shard_map/ppermute | solution.py:151
  146.6 23.0 %collective-permute-start.18 = (f32[512,128]{1,0:T(8,128)S(1)}, f32[512,128]{1,0:T(8,128)S(1)}, u32[]{:S(2)}, u32[]{:S(2)}) collective-permute-start(f32[512,128]{1,0:T(8,128)S(1)} %get-tuple-element.269.refs_0_), channel_id=1, source_target_pairs={{0,8},{4,12},{8,0},{12,4},{1,9},{5,13},{9,1},{13,5},{2,10},{6,14},... | collective-permute-start | bytes 786440 | tf_op jit(solution)/shard_map/ppermute | solution.py:16
  147.1 22.5 %collective-permute-start.19 = (f32[512,128]{1,0:T(8,128)S(1)}, f32[512,128]{1,0:T(8,128)S(1)}, u32[]{:S(2)}, u32[]{:S(2)}) collective-permute-start(f32[512,128]{1,0:T(8,128)S(1)} %get-tuple-element.269.refs_0_), channel_id=1, source_target_pairs={{0,4},{4,0},{8,12},{12,8},{1,5},{5,1},{9,13},{13,9},{2,6},{6,2},{1... | collective-permute-start | bytes 786440 | tf_op jit(solution)/shard_map/ppermute | solution.py:16
  148.5 21.1 %collective-permute-start.17 = (f32[512,128]{1,0:T(8,128)S(1)}, f32[512,128]{1,0:T(8,128)S(1)}, u32[]{:S(2)}, u32[]{:S(2)}) collective-permute-start(f32[512,128]{1,0:T(8,128)S(1)} %collective-permute-done.11.refs_2_), channel_id=1, source_target_pairs={{0,4},{4,0},{8,12},{12,8},{1,5},{5,1},{9,13},{13,9},{2,6},{6,2},{1... | collective-permute-start | bytes 786440 | tf_op jit(solution)/shard_map/ppermute | solution.py:16
  149.3 19.4 %collective-permute-start.22 = (f32[1,512,256]{2,1,0:T(8,128)S(1)}, f32[1,512,256]{2,1,0:T(8,128)S(1)}, u32[]{:S(2)}, u32[]{:S(2)}) collective-permute-start(f32[1,512,256]{2,1,0:T(8,128)S(1)} %slice_bitcast_fusion.3), channel_id=1, source_target_pairs={{0,2},{1,3},{2,0},{3,1},{4,6},{5,7},{6,4},{7,5},{8,10},{9,11},{10,... | collective-permute-start | bytes 1572872 | tf_op jit(solution)/shard_map/ppermute | solution.py:16
  169.7 16.6 %collective-permute-start.25 = (f32[2,512,128]{2,1,0:T(8,128)S(1)}, f32[2,512,128]{2,1,0:T(8,128)S(1)}, u32[]{:S(2)}, u32[]{:S(2)}) collective-permute-start(f32[2,512,128]{2,1,0:T(8,128)S(1)} %pad_maximum_fusion.4), channel_id=1, source_target_pairs={{0,2},{5,7},{10,8},{15,13},{16,18},{21,23},{26,24},{31,29}} | collective-permute-start | bytes 1572872 | tf_op jit(solution)/shard_map/ppermute | solution.py:151
  175.7 22.1 %collective-permute-start.27 = (f32[1,512,256]{2,1,0:T(8,128)S(1)}, f32[1,512,256]{2,1,0:T(8,128)S(1)}, u32[]{:S(2)}, u32[]{:S(2)}) collective-permute-start(f32[1,512,256]{2,1,0:T(8,128)S(1)} %slice_bitcast_fusion.1), channel_id=1, source_target_pairs={{0,2},{1,3},{2,0},{3,1},{4,6},{5,7},{6,4},{7,5},{8,10},{9,11},{10,... | collective-permute-start | bytes 1572872 | tf_op jit(solution)/shard_map/ppermute | solution.py:16
  175.8 22.9 %collective-permute-start.24 = (f32[512,128]{1,0:T(8,128)S(1)}, f32[512,128]{1,0:T(8,128)S(1)}, u32[]{:S(2)}, u32[]{:S(2)}) collective-permute-start(f32[512,128]{1,0:T(8,128)S(1)} %collective-permute-done.18.refs_2_), channel_id=1, source_target_pairs={{0,4},{4,0},{8,12},{12,8},{1,5},{5,1},{9,13},{13,9},{2,6},{6,2},{1... | collective-permute-start | bytes 786440 | tf_op jit(solution)/shard_map/ppermute | solution.py:16
  199.5 18.5 %collective-permute-start.29 = (f32[2,512,128]{2,1,0:T(8,128)}, f32[2,512,128]{2,1,0:T(8,128)}, u32[]{:S(2)}, u32[]{:S(2)}) collective-permute-start(f32[2,512,128]{2,1,0:T(8,128)} %pad_maximum_fusion.5), channel_id=1, source_target_pairs={{0,2},{5,7},{10,8},{15,13},{16,18},{21,23},{26,24},{31,29}} | collective-permute-start | bytes 1572872 | tf_op jit(solution)/shard_map/ppermute | solution.py:151
  251.3 13.6 %collective-permute-start.39 = (f32[1,1,128,256]{2,3,1,0:T(8,128)}, f32[1,1,128,256]{2,3,1,0:T(8,128)}, u32[]{:S(2)}, u32[]{:S(2)}) collective-permute-start(f32[1,1,128,256]{2,3,1,0:T(8,128)} %constant_dynamic-slice_fusion.10), channel_id=1, source_target_pairs={{0,8},{4,12},{8,0},{12,4},{1,9},{5,13},{9,1},{13,5},{2,10},{6,14},... | collective-permute-start | bytes 393224 | tf_op jit(solution)/shard_map/ppermute | solution.py:16
  (47 other events, 319.5 us)

commit v10 on v9

--- a/solution.py
+++ b/solution.py
@@ -173,8 +173,7 @@
         late = 2 * span
         pieces = [("first", i, i + late) for i in range(0, width, late)]
         count_first = len(pieces)
-        pieces += [("second", i, i + late) for i in range(0, width - late, late)]
-        pieces += [("second", i, i + span) for i in range(width - late, width, span)]
+        pieces += [("second", i, i + late) for i in range(0, width, late)]
         stages = rows_axis.bit_length() - 1
         second = panels[1] * kept_second - dot(panels[0] * kept_first, link, precise)
         for k, (panel, start, stop) in enumerate(pieces):
@@ -192,7 +191,7 @@
 
         def multiply(k):
             gathered = blocks(k)
-            if ("sums", k - 1) in live:
+            if ("sums", k - 1) in live and k + stages >= len(pieces):
                 live["sums", k - 1], gathered = lax.optimization_barrier((live["sums", k - 1], gathered))
             live["send", k], live["keep", k] = product(live["tile"], gathered)
 
@@ -202,15 +201,17 @@
         def add_rest(k):
             live["out", k] = -sum_scatter(live.pop(("sums", k)), "col", 2)
 
-        def collect(k):
-            live["own", k] = blocks_to_send(blocks(k))
-            spread(k)
-
-        def spread(k):
-            live["own", k] = spread_step(live["own", k])
-
-        def owns(start, stop):
-            return jnp.concatenate([live["own", k][0] for k in range(start, stop)], axis=1)
+        def collect(group):
+            live["own", group] = blocks_to_send([jnp.concatenate(parts, axis=1) for parts in zip(*map(blocks, group))])
+            spread(group)
+
+        def spread(group):
+            live["own", group] = spread_step(live["own", group])
+
+        own_groups = [tuple(range(count_first))] + [(k,) for k in range(count_first, len(pieces))]
+
+        def owns(groups):
+            return jnp.concatenate([live["own", group][0] for group in groups], axis=1)
 
         def outs(start, stop):
             return jnp.concatenate([live["out", k] for k in range(start, stop)], axis=1)
@@ -240,51 +241,48 @@
             return jnp.concatenate(columns_by_xor(array, odd), axis=1)
 
         def first_terms():
-            out_first, own_first = outs(0, count_first), owns(0, count_first)
+            out_first, own_first = outs(0, count_first), owns(own_groups[:1])
             sums = core_sum(lambda odd: dot_tn(out_first, by_parity(own_first, odd), three_pass))
-            live["first_sum"] = by_rows(rest_of_cols(sums))
+            live["first_sum"] = by_rows(sums)
 
         def first_rows():
             live["first_sum"] = sum_rows(live["first_sum"], "row")[0]
 
+        def first_cols():
+            live["first_sum"] = rest_of_cols(live["first_sum"])
+
         def cross_terms():
-            out_first, own_second = outs(0, count_first), owns(count_first, len(pieces))
+            out_first, own_second = outs(0, count_first), owns(own_groups[1:])
             sums = core_sum(lambda odd: dot_tn(out_first, by_parity(own_second, odd), three_pass)
                             + by_parity(live["link_cross"], odd))
             live["cross_sum"] = sum_step(by_rows(sums), "row", 1)
 
-        def cross_rows():
-            live["cross_sum"] = sum_rows(live["cross_sum"], "row", 2)[0]
-
-        def cross_cols():
-            live["cross_sum"] = rest_of_cols(live["cross_sum"])
+        def cross_rest():
+            live["cross_sum"] = rest_of_cols(sum_rows(live["cross_sum"], "row", 2)[0])
 
         def second_terms():
-            out_second, own_second = outs(count_first, len(pieces)), owns(count_first, len(pieces))
+            out_second, own_second = outs(count_first, len(pieces)), owns(own_groups[1:])
 
             def terms(odd):
                 return dot_tn(out_second, by_parity(own_second, odd), three_pass) + by_parity(live["link_second"], odd)
 
-            live["second_sum"] = by_rows(rest_of_cols(core_sum(terms)))
-
-        def second_rows():
-            live["second_sum"] = sum_rows(live["second_sum"], "row")[0]
+            live["second_sum"] = sum_rows(by_rows(rest_of_cols(core_sum(terms))), "row")[0]
 
         at(1, link_terms)
         last = len(pieces) - 1 + stages
-        for k in range(len(pieces)):
-            at(k + stages, lambda k=k: collect(k))
+        for group in own_groups:
+            at(group[-1] + stages, lambda group=group: collect(group))
             for step in range(1, cols_axis.bit_length() - 1):
-                at(k + stages + step, lambda k=k: spread(k))
+                at(group[-1] + stages + step, lambda group=group: spread(group))
         for k in range(len(pieces)):
             at(k + stages + 1, lambda k=k: add_core(k))
             at(k + stages, lambda k=k: multiply(k))
         for k in range(len(pieces)):
             at(k + stages + 1, lambda k=k: add_rest(k))
-        end = last + 3
-        at(last + 1, cross_terms, first_terms)
-        at(last + 2, cross_rows, second_terms, first_rows)
-        at(end, second_rows, cross_cols)
+        end = last + 2
+        at(last, first_terms)
+        at(last + 1, cross_terms, first_rows)
+        at(end, cross_rest, second_terms, first_cols)
 
         for slot in range(end + 1):
             if slot > 0:

time: 285 us -> 284 us (level)
  waiting for transfers between devices: 92.3 us -> 107 us
  starting transfers between devices: 62.5 us -> 48.1 us
  Pallas kernels: 61.4 us -> 50.9 us
  other arithmetic: 28.8 us -> 35.9 us
    ppermute x37 -> x32, waiting for transfers between devices: 81.1 us -> 104 us  [swap(): return lax.ppermute(block, axis, pairs)]
    pallas_call x5 -> x4, Pallas kernels: 54.2 us -> 43.9 us  [product(): pl.pallas_call(product_kernel, in_specs=[pl.BlockSpec(memory_space=pltpu....]
    ppermute x10 -> x6, starting transfers between devices: 30.9 us -> 22.1 us  [spread_step(): moved = lax.ppermute(jnp.stack(held[bit:]), ('row', 'col'), pairs)]
    ppermute x10 -> x6, waiting for transfers between devices: 11.1 us -> 2.85 us  [spread_step(): moved = lax.ppermute(jnp.stack(held[bit:]), ('row', 'col'), pairs)]
    unnamed x57 -> x108, local copies, waits for them, and re-layouts: 10.9 us -> 16.7 us
    ppermute x37 -> x32, starting transfers between devices: 31.6 us -> 26 us  [swap(): return lax.ppermute(block, axis, pairs)]
    select_n x10 -> x6, other arithmetic: 9.35 us -> 13 us  [spread_step(): return [jnp.where(offset & bit != 0, moved[j], held[j]) for j in range(bit)]]
  transfers between devices with their start and end apart: 47 -> 38, of which waited for: 17 -> 17; matrix products, arithmetic and copies ran while one was open for 16% -> 21% of each run, Pallas kernels for 22% -> 18%
where the time goes in v10:
time: 284 us; the launch traced here: 283 us
  waiting for transfers between devices  107 us (38%)
  Pallas kernels  50.9 us (18%)
  starting transfers between devices  48.1 us (17%)
  other arithmetic  35.9 us (13%)
  local copies, waits for them, and re-layouts  27.1 us (10%)
  matrix products  12.7 us (4%)
    ppermute x32, waiting for transfers between devices, swap(): return lax.ppermute(block, axis, pairs)  104 us
    pallas_call x4, Pallas kernels, product(): pl.pallas_call(product_kernel, in_specs=[pl.BlockSpec(memory_space=pltpu....  43.9 us
    ppermute x32, starting transfers between devices, swap(): return lax.ppermute(block, axis, pairs)  26 us
    ppermute x6, starting transfers between devices, spread_step(): moved = lax.ppermute(jnp.stack(held[bit:]), ('row', 'col'), pairs)  22.1 us
    unnamed x108, local copies, waits for them, and re-layouts  16.7 us
    select_n x6, other arithmetic, spread_step(): return [jnp.where(offset & bit != 0, moved[j], held[j]) for j in range(bit)]  13 us
    dot_general x7, matrix products, dot_tn(): return lax.dot_general(a, b, (((0,), (0,)), ((), ())), precision=precision)  10.3 us
    pallas_call x1, Pallas kernels, split(): pl.pallas_call(split_kernel, grid=(rows // step,), in_specs=[pl.BlockSpec...  7.08 us
  transfers between devices with their start and end apart: 38, of which 17 were waited for; matrix products, arithmetic and copies ran while one was open for 21% of the time, Pallas kernels for 18%

profile of v10, /device:TPU:0, one launch (start us, length us, event | category | flops | bytes accessed | tf_op | source)
XLA Modules:
  0.0 283.4 jit_solution(1338848588351130411)
XLA Ops:
  3.1 4.1 %collective-permute-start = (f32[512,256]{1,0:T(8,128)S(1)}, f32[512,256]{1,0:T(8,128)}, u32[]{:S(2)}, u32[]{:S(2)}) collective-permute-start(f32[512,256]{1,0:T(8,128)S(1)} %get-tuple-element.130.refs_0_), channel_id=1, source_target_pairs={{0,8},{4,12},{8,0},{12,4},{1,9},{5,13},{9,1},{13,5},{2,10},{6,14},... | collective-permute-start | bytes 1572872 | tf_op jit(solution)/shard_map/ppermute | solution.py:16
  8.9 5.8 %copy-done.2 = f32[2048,2048]{1,0:T(8,128)S(1)} copy-done((f32[2048,2048]{1,0:T(8,128)S(1)}, f32[2048,2048]{1,0:T(8,128)}, u32[]{:S(2)}) %copy-start.2) | copy-done | bytes 16777240
  14.7 7.1 %shard_map.79 = bf16[6,2048,2048]{2,1,0:T(8,128)(2,1)} custom-call(f32[2048,2048]{1,0:T(8,128)S(1)} %copy-done.2), custom_call_target="tpu_custom_call" | custom-call | tf_op jit(solution)/shard_map/pallas_call | solution.py:34
  23.7 6.8 %collective-permute-done.refs_2_ = f32[512,256]{1,0:T(8,128)} collective-permute-done((f32[512,256]{1,0:T(8,128)S(1)}, f32[512,256]{1,0:T(8,128)}, u32[]{:S(2)}, u32[]{:S(2)}) %collective-permute-start) | collective-permute-done | bytes 524320 | tf_op jit(solution)/shard_map/ppermute | solution.py:16
  37.2 18.8 %collective-permute-done.3.refs_2_ = f32[512,256]{1,0:T(8,128)} collective-permute-done((f32[512,256]{1,0:T(8,128)S(1)}, f32[512,256]{1,0:T(8,128)}, u32[]{:S(2)}, u32[]{:S(2)}) %collective-permute-start.3) | collective-permute-done | bytes 524320 | tf_op jit(solution)/shard_map/ppermute | solution.py:16
  57.0 10.3 %collective-permute-done.2.refs_3_ = f32[512,256]{1,0:T(8,128)} collective-permute-done((f32[512,256]{1,0:T(8,128)}, f32[512,256]{1,0:T(8,128)}, u32[]{:S(2)}, u32[]{:S(2)}) %collective-permute-start.2) | collective-permute-done | bytes 524320 | tf_op jit(solution)/shard_map/ppermute | solution.py:16
  67.6 3.4 %collective-permute-start.6 = (f32[512,256]{1,0:T(8,128)S(1)}, f32[512,256]{1,0:T(8,128)S(1)}, u32[]{:S(2)}, u32[]{:S(2)}) collective-permute-start(f32[512,256]{1,0:T(8,128)S(1)} %get-tuple-element.163.refs_0_), channel_id=1, source_target_pairs={{0,8},{4,12},{8,0},{12,4},{1,9},{5,13},{9,1},{13,5},{2,10},{6,14},... | collective-permute-start | bytes 1572872 | tf_op jit(solution)/shard_map/ppermute | solution.py:16
  71.5 11.4 %shard_map.80 = (f32[2,512,256]{2,1,0:T(8,128)S(1)}, f32[2,512,256]{2,1,0:T(8,128)S(1)}) custom-call(s32[5]{0:T(128)S(1)} %pad_add_fusion.place, bf16[6,4,512,2048]{3,2,1,0:T(8,128)(2,1)} %bitcast.199, f32[512,256]{1,0:T(8,128)S(1)} %get-tuple-element.130.refs_0_, f32[512,256]{1,0:T(8,128)} %collective-permute-done.1.refs_1_, ...), custom_call_target="tpu_custom_call" | custom-call | tf_op jit(solution)/shard_map/pallas_call | solution.py:83
  82.9 9.9 %collective-permute-done.5.refs_3_ = f32[512,256]{1,0:T(8,128)S(1)} collective-permute-done((f32[512,256]{1,0:T(8,128)}, f32[512,256]{1,0:T(8,128)S(1)}, u32[]{:S(2)}, u32[]{:S(2)}) %collective-permute-start.5) | collective-permute-done | bytes 524320 | tf_op jit(solution)/shard_map/ppermute | solution.py:16
  92.7 10.2 %collective-permute-done.7.refs_1_ = f32[512,256]{1,0:T(8,128)S(1)} collective-permute-done((f32[512,256]{1,0:T(8,128)S(1)}, f32[512,256]{1,0:T(8,128)S(1)}, u32[]{:S(2)}, u32[]{:S(2)}) %collective-permute-start.7) | collective-permute-done | bytes 524320 | tf_op jit(solution)/shard_map/ppermute | solution.py:16
  107.1 4.5 %collective-permute-start.11 = (f32[2,512,512]{2,1,0:T(8,128)}, f32[2,512,512]{2,1,0:T(8,128)}, u32[]{:S(2)}, u32[]{:S(2)}) collective-permute-start(f32[2,512,512]{2,1,0:T(8,128)} %pad_maximum_fusion), channel_id=1, source_target_pairs={{0,2},{5,7},{10,8},{15,13},{16,18},{21,23},{26,24},{31,29}} | collective-permute-start | bytes 6291464 | tf_op jit(solution)/shard_map/ppermute | solution.py:151
  118.2 11.3 %shard_map.81 = (f32[2,512,256]{2,1,0:T(8,128)}, f32[2,512,256]{2,1,0:T(8,128)S(1)}) custom-call(s32[5]{0:T(128)S(1)} %pad_add_fusion.place, bf16[6,4,512,2048]{3,2,1,0:T(8,128)(2,1)} %bitcast.200, f32[512,256]{1,0:T(8,128)S(1)} %get-tuple-element.134.refs_0_, f32[512,256]{1,0:T(8,128)} %collective-permute-done.4.refs_1_, ...), custom_call_target="tpu_custom_call" | custom-call | tf_op jit(solution)/shard_map/pallas_call | solution.py:83
  129.5 15.8 %collective-permute-done.13 = f32[1,512,256]{2,1,0:T(8,128)} collective-permute-done((f32[1,512,256]{2,1,0:T(8,128)}, f32[1,512,256]{2,1,0:T(8,128)}, u32[]{:S(2)}, u32[]{:S(2)}) %collective-permute-start.13) | collective-permute-done | bytes 524320 | tf_op jit(solution)/shard_map/ppermute | solution.py:16
  147.3 3.6 %fusion.2 = (f32[512,512]{1,0:T(8,128)}, f32[512,512]{1,0:T(8,128)}) fusion(f32[2,512,512]{2,1,0:T(8,128)} %collective-permute-done.11, f32[512,256]{1,0:T(8,128)} %collective-permute-done.4.refs_1_, f32[512,256]{1,0:T(8,128)} %collective-permute-done.1.refs_1_, pred[]{:T(512)S(6)} %ne.65, f32[512,256]{1,0:T(8,128)S(1)} %get-tuple-element.134.refs_0_, ...), kind=kLoop, calls=%fused_computation.20 | loop fusion | flops 1048576 | bytes 6291457 | tf_op jit(solution)/shard_map/jit(_where)/select_n | solution.py:153
  151.0 3.4 %collective-permute-start.14 = (f32[1,512,512]{2,1,0:T(8,128)}, f32[1,512,512]{2,1,0:T(8,128)}, u32[]{:S(2)}, u32[]{:S(2)}) collective-permute-start(f32[1,512,512]{2,1,0:T(8,128)} %bitcast.21), channel_id=1, source_target_pairs={{0,1},{2,3},{5,4},{7,6},{8,9},{10,11},{13,12},{15,14},{16,17},{18,... | collective-permute-start | bytes 3145736 | tf_op jit(solution)/shard_map/ppermute | solution.py:151
  155.4 5.4 %collective-permute-start.16 = (f32[2,512,256]{2,1,0:T(8,128)}, f32[2,512,256]{2,1,0:T(8,128)}, u32[]{:S(2)}, u32[]{:S(2)}) collective-permute-start(f32[2,512,256]{2,1,0:T(8,128)} %pad_maximum_fusion.1), channel_id=1, source_target_pairs={{0,2},{5,7},{10,8},{15,13},{16,18},{21,23},{26,24},{31,29}} | collective-permute-start | bytes 3145736 | tf_op jit(solution)/shard_map/ppermute | solution.py:151
  162.7 10.6 %shard_map.82 = (f32[2,512,256]{2,1,0:T(8,128)}, f32[2,512,256]{2,1,0:T(8,128)S(1)}) custom-call(s32[5]{0:T(128)S(1)} %pad_add_fusion.place, bf16[6,4,512,2048]{3,2,1,0:T(8,128)(2,1)} %bitcast.201, f32[512,256]{1,0:T(8,128)S(1)} %get-tuple-element.163.refs_0_, f32[512,256]{1,0:T(8,128)S(1)} %copy-done.4, f32[512,256]{1,0:T(8,128)S(1)} %copy-done.7, ...), custom_call_target="tpu_custom_call" | custom-call | tf_op jit(solution)/shard_map/pallas_call | solution.py:83
  188.3 5.4 %collective-permute-start.20 = (f32[2,512,256]{2,1,0:T(8,128)}, f32[2,512,256]{2,1,0:T(8,128)}, u32[]{:S(2)}, u32[]{:S(2)}) collective-permute-start(f32[2,512,256]{2,1,0:T(8,128)} %pad_maximum_fusion.2), channel_id=1, source_target_pairs={{0,2},{5,7},{10,8},{15,13},{16,18},{21,23},{26,24},{31,29}} | collective-permute-start | bytes 3145736 | tf_op jit(solution)/shard_map/ppermute | solution.py:151
  201.3 10.6 %shard_map.83 = (f32[2,512,256]{2,1,0:T(8,128)S(1)}, f32[2,512,256]{2,1,0:T(8,128)S(1)}) custom-call(s32[5]{0:T(128)S(1)} %pad_add_fusion.place, bf16[6,4,512,2048]{3,2,1,0:T(8,128)(2,1)} %bitcast.202, f32[512,256]{1,0:T(8,128)S(1)} %get-tuple-element.184.refs_0_, f32[512,256]{1,0:T(8,128)S(1)} %collective-permute-done.10.refs_1_, ...), custom_call_target="tpu_custom_call" | custom-call | tf_op jit(solution)/shard_map/pallas_call | solution.py:83
  224.1 3.5 %collective-permute-done.25 = f32[2,1,128,256]{2,3,1,0:T(8,128)} collective-permute-done((f32[2,1,128,256]{2,3,1,0:T(8,128)}, f32[2,1,128,256]{2,3,1,0:T(8,128)}, u32[]{:S(2)}, u32[]{:S(2)}) %collective-permute-start.25) | collective-permute-done | bytes 262176 | tf_op jit(solution)/shard_map/ppermute | solution.py:16
  243.7 5.7 %collective-permute-done.30 = f32[2,1,128,256]{2,3,1,0:T(8,128)} collective-permute-done((f32[2,1,128,256]{2,3,1,0:T(8,128)}, f32[2,1,128,256]{2,3,1,0:T(8,128)}, u32[]{:S(2)}, u32[]{:S(2)}) %collective-permute-start.30) | collective-permute-done | bytes 262176 | tf_op jit(solution)/shard_map/ppermute | solution.py:16
  265.6 6.3 %collective-permute-done.33 = f32[1,512,128]{2,1,0:T(8,128)S(1)} collective-permute-done((f32[1,512,128]{2,1,0:T(8,128)S(1)}, f32[1,512,128]{2,1,0:T(8,128)S(1)}, u32[]{:S(2)}, u32[]{:S(2)}) %collective-permute-start.33) | collective-permute-done | bytes 262176 | tf_op jit(solution)/shard_map/ppermute | solution.py:16
  272.7 4.5 %collective-permute-done.34 = f32[2,1,128,128]{2,3,1,0:T(8,128)S(1)} collective-permute-done((f32[2,1,128,128]{2,3,1,0:T(8,128)S(1)}, f32[2,1,128,128]{2,3,1,0:T(8,128)S(1)}, u32[]{:S(2)}, u32[]{:S(2)}) %collective-permute-start.34) | collective-permute-done | bytes 131104 | tf_op jit(solution)/shard_map/ppermute | solution.py:16
  278.7 3.9 %collective-permute-done.35 = f32[1,1,128,128]{2,3,1,0:T(8,128)S(1)} collective-permute-done((f32[1,1,128,128]{2,3,1,0:T(8,128)S(1)}, f32[1,1,128,128]{2,3,1,0:T(8,128)S(1)}, u32[]{:S(2)}, u32[]{:S(2)}) %collective-permute-start.35) | collective-permute-done | bytes 65568 | tf_op jit(solution)/shard_map/ppermute | solution.py:16
  (240 shorter events, 99.8 us)
Async XLA Ops:
  3.1 27.5 %collective-permute-start = (f32[512,256]{1,0:T(8,128)S(1)}, f32[512,256]{1,0:T(8,128)}, u32[]{:S(2)}, u32[]{:S(2)}) collective-permute-start(f32[512,256]{1,0:T(8,128)S(1)} %get-tuple-element.130.refs_0_), channel_id=1, source_target_pairs={{0,8},{4,12},{8,0},{12,4},{1,9},{5,13},{9,1},{13,5},{2,10},{6,14},... | collective-permute-start | bytes 1572872 | tf_op jit(solution)/shard_map/ppermute | solution.py:16
  7.2 23.6 %collective-permute-start.1 = (f32[512,256]{1,0:T(8,128)S(1)}, f32[512,256]{1,0:T(8,128)}, u32[]{:S(2)}, u32[]{:S(2)}) collective-permute-start(f32[512,256]{1,0:T(8,128)S(1)} %get-tuple-element.130.refs_0_), channel_id=1, source_target_pairs={{0,4},{4,0},{8,12},{12,8},{1,5},{5,1},{9,13},{13,9},{2,6},{6,2},{1... | collective-permute-start | bytes 1572872 | tf_op jit(solution)/shard_map/ppermute | solution.py:16
  30.7 25.2 %collective-permute-start.3 = (f32[512,256]{1,0:T(8,128)S(1)}, f32[512,256]{1,0:T(8,128)}, u32[]{:S(2)}, u32[]{:S(2)}) collective-permute-start(f32[512,256]{1,0:T(8,128)S(1)} %get-tuple-element.134.refs_0_), channel_id=1, source_target_pairs={{0,8},{4,12},{8,0},{12,4},{1,9},{5,13},{9,1},{13,5},{2,10},{6,14},... | collective-permute-start | bytes 1572872 | tf_op jit(solution)/shard_map/ppermute | solution.py:16
  32.1 24.8 %collective-permute-start.4 = (f32[512,256]{1,0:T(8,128)S(1)}, f32[512,256]{1,0:T(8,128)}, u32[]{:S(2)}, u32[]{:S(2)}) collective-permute-start(f32[512,256]{1,0:T(8,128)S(1)} %get-tuple-element.134.refs_0_), channel_id=1, source_target_pairs={{0,4},{4,0},{8,12},{12,8},{1,5},{5,1},{9,13},{13,9},{2,6},{6,2},{1... | collective-permute-start | bytes 1572872 | tf_op jit(solution)/shard_map/ppermute | solution.py:16
  34.6 32.7 %collective-permute-start.2 = (f32[512,256]{1,0:T(8,128)}, f32[512,256]{1,0:T(8,128)}, u32[]{:S(2)}, u32[]{:S(2)}) collective-permute-start(f32[512,256]{1,0:T(8,128)} %collective-permute-done.refs_2_), channel_id=1, source_target_pairs={{0,4},{4,0},{8,12},{12,8},{1,5},{5,1},{9,13},{13,9},{2,6},{6,2},{1... | collective-permute-start | bytes 1572872 | tf_op jit(solution)/shard_map/ppermute | solution.py:16
  67.3 25.5 %collective-permute-start.5 = (f32[512,256]{1,0:T(8,128)}, f32[512,256]{1,0:T(8,128)S(1)}, u32[]{:S(2)}, u32[]{:S(2)}) collective-permute-start(f32[512,256]{1,0:T(8,128)} %collective-permute-done.3.refs_2_), channel_id=1, source_target_pairs={{0,4},{4,0},{8,12},{12,8},{1,5},{5,1},{9,13},{13,9},{2,6},{6,2},{1... | collective-permute-start | bytes 1572872 | tf_op jit(solution)/shard_map/ppermute | solution.py:16
  67.6 25.2 %collective-permute-start.6 = (f32[512,256]{1,0:T(8,128)S(1)}, f32[512,256]{1,0:T(8,128)S(1)}, u32[]{:S(2)}, u32[]{:S(2)}) collective-permute-start(f32[512,256]{1,0:T(8,128)S(1)} %get-tuple-element.163.refs_0_), channel_id=1, source_target_pairs={{0,8},{4,12},{8,0},{12,4},{1,9},{5,13},{9,1},{13,5},{2,10},{6,14},... | collective-permute-start | bytes 1572872 | tf_op jit(solution)/shard_map/ppermute | solution.py:16
  71.0 32.0 %collective-permute-start.7 = (f32[512,256]{1,0:T(8,128)S(1)}, f32[512,256]{1,0:T(8,128)S(1)}, u32[]{:S(2)}, u32[]{:S(2)}) collective-permute-start(f32[512,256]{1,0:T(8,128)S(1)} %get-tuple-element.163.refs_0_), channel_id=1, source_target_pairs={{0,4},{4,0},{8,12},{12,8},{1,5},{5,1},{9,13},{13,9},{2,6},{6,2},{1... | collective-permute-start | bytes 1572872 | tf_op jit(solution)/shard_map/ppermute | solution.py:16
  107.1 40.2 %collective-permute-start.11 = (f32[2,512,512]{2,1,0:T(8,128)}, f32[2,512,512]{2,1,0:T(8,128)}, u32[]{:S(2)}, u32[]{:S(2)}) collective-permute-start(f32[2,512,512]{2,1,0:T(8,128)} %pad_maximum_fusion), channel_id=1, source_target_pairs={{0,2},{5,7},{10,8},{15,13},{16,18},{21,23},{26,24},{31,29}} | collective-permute-start | bytes 6291464 | tf_op jit(solution)/shard_map/ppermute | solution.py:151
  112.6 32.7 %collective-permute-start.13 = (f32[1,512,256]{2,1,0:T(8,128)}, f32[1,512,256]{2,1,0:T(8,128)}, u32[]{:S(2)}, u32[]{:S(2)}) collective-permute-start(f32[1,512,256]{2,1,0:T(8,128)} %slice_bitcast_fusion.13), channel_id=1, source_target_pairs={{0,2},{1,3},{2,0},{3,1},{4,6},{5,7},{6,4},{7,5},{8,10},{9,11},{10,... | collective-permute-start | bytes 1572872 | tf_op jit(solution)/shard_map/ppermute | solution.py:16
  113.0 37.9 %collective-permute-start.10 = (f32[512,256]{1,0:T(8,128)S(1)}, f32[512,256]{1,0:T(8,128)S(1)}, u32[]{:S(2)}, u32[]{:S(2)}) collective-permute-start(f32[512,256]{1,0:T(8,128)S(1)} %get-tuple-element.184.refs_0_), channel_id=1, source_target_pairs={{0,4},{4,0},{8,12},{12,8},{1,5},{5,1},{9,13},{13,9},{2,6},{6,2},{1... | collective-permute-start | bytes 1572872 | tf_op jit(solution)/shard_map/ppermute | solution.py:16
  113.0 37.9 %collective-permute-start.9 = (f32[512,256]{1,0:T(8,128)S(1)}, f32[512,256]{1,0:T(8,128)S(1)}, u32[]{:S(2)}, u32[]{:S(2)}) collective-permute-start(f32[512,256]{1,0:T(8,128)S(1)} %get-tuple-element.184.refs_0_), channel_id=1, source_target_pairs={{0,8},{4,12},{8,0},{12,4},{1,9},{5,13},{9,1},{13,5},{2,10},{6,14},... | collective-permute-start | bytes 1572872 | tf_op jit(solution)/shard_map/ppermute | solution.py:16
  115.1 35.8 %collective-permute-start.8 = (f32[512,256]{1,0:T(8,128)}, f32[512,256]{1,0:T(8,128)S(1)}, u32[]{:S(2)}, u32[]{:S(2)}) collective-permute-start(f32[512,256]{1,0:T(8,128)} %copy-done.5), channel_id=1, source_target_pairs={{0,4},{4,0},{8,12},{12,8},{1,5},{5,1},{9,13},{13,9},{2,6},{6,2},{1... | collective-permute-start | bytes 1572872 | tf_op jit(solution)/shard_map/ppermute | solution.py:16
  151.0 22.4 %collective-permute-start.14 = (f32[1,512,512]{2,1,0:T(8,128)}, f32[1,512,512]{2,1,0:T(8,128)}, u32[]{:S(2)}, u32[]{:S(2)}) collective-permute-start(f32[1,512,512]{2,1,0:T(8,128)} %bitcast.21), channel_id=1, source_target_pairs={{0,1},{2,3},{5,4},{7,6},{8,9},{10,11},{13,12},{15,14},{16,17},{18,... | collective-permute-start | bytes 3145736 | tf_op jit(solution)/shard_map/ppermute | solution.py:151
  155.4 22.6 %collective-permute-start.16 = (f32[2,512,256]{2,1,0:T(8,128)}, f32[2,512,256]{2,1,0:T(8,128)}, u32[]{:S(2)}, u32[]{:S(2)}) collective-permute-start(f32[2,512,256]{2,1,0:T(8,128)} %pad_maximum_fusion.1), channel_id=1, source_target_pairs={{0,2},{5,7},{10,8},{15,13},{16,18},{21,23},{26,24},{31,29}} | collective-permute-start | bytes 3145736 | tf_op jit(solution)/shard_map/ppermute | solution.py:151
  160.8 22.9 %collective-permute-start.15 = (f32[512,256]{1,0:T(8,128)S(1)}, f32[512,256]{1,0:T(8,128)S(1)}, u32[]{:S(2)}, u32[]{:S(2)}) collective-permute-start(f32[512,256]{1,0:T(8,128)S(1)} %collective-permute-done.9.refs_2_), channel_id=1, source_target_pairs={{0,4},{4,0},{8,12},{12,8},{1,5},{5,1},{9,13},{13,9},{2,6},{6,2},{1... | collective-permute-start | bytes 1572872 | tf_op jit(solution)/shard_map/ppermute | solution.py:16
  162.6 20.9 %collective-permute-start.18 = (f32[1,512,256]{2,1,0:T(8,128)S(1)}, f32[1,512,256]{2,1,0:T(8,128)S(1)}, u32[]{:S(2)}, u32[]{:S(2)}) collective-permute-start(f32[1,512,256]{2,1,0:T(8,128)S(1)} %slice_bitcast_fusion.9), channel_id=1, source_target_pairs={{0,2},{1,3},{2,0},{3,1},{4,6},{5,7},{6,4},{7,5},{8,10},{9,11},{10,... | collective-permute-start | bytes 1572872 | tf_op jit(solution)/shard_map/ppermute | solution.py:16
  183.7 14.8 %collective-permute-start.21 = (f32[2,512,256]{2,1,0:T(8,128)}, f32[2,512,256]{2,1,0:T(8,128)}, u32[]{:S(2)}, u32[]{:S(2)}) collective-permute-start(f32[2,512,256]{2,1,0:T(8,128)} %get-tuple-element.183), channel_id=1, source_target_pairs={{0,1},{1,0},{2,3},{3,2},{4,5},{5,4},{6,7},{7,6},{8,9},{9,8},{10,11... | collective-permute-start | bytes 3145736 | tf_op jit(solution)/shard_map/ppermute | solution.py:16
  188.3 23.5 %collective-permute-start.20 = (f32[2,512,256]{2,1,0:T(8,128)}, f32[2,512,256]{2,1,0:T(8,128)}, u32[]{:S(2)}, u32[]{:S(2)}) collective-permute-start(f32[2,512,256]{2,1,0:T(8,128)} %pad_maximum_fusion.2), channel_id=1, source_target_pairs={{0,2},{5,7},{10,8},{15,13},{16,18},{21,23},{26,24},{31,29}} | collective-permute-start | bytes 3145736 | tf_op jit(solution)/shard_map/ppermute | solution.py:151
  200.3 16.2 %collective-permute-start.22 = (f32[1,512,256]{2,1,0:T(8,128)S(1)}, f32[1,512,256]{2,1,0:T(8,128)S(1)}, u32[]{:S(2)}, u32[]{:S(2)}) collective-permute-start(f32[1,512,256]{2,1,0:T(8,128)S(1)} %slice_bitcast_fusion.5), channel_id=1, source_target_pairs={{0,2},{1,3},{2,0},{3,1},{4,6},{5,7},{6,4},{7,5},{8,10},{9,11},{10,... | collective-permute-start | bytes 1572872 | tf_op jit(solution)/shard_map/ppermute | solution.py:16
  217.3 15.0 %collective-permute-start.24 = (f32[1,512,256]{2,1,0:T(8,128)}, f32[1,512,256]{2,1,0:T(8,128)}, u32[]{:S(2)}, u32[]{:S(2)}) collective-permute-start(f32[1,512,256]{2,1,0:T(8,128)} %bitcast.42), channel_id=1, source_target_pairs={{0,1},{2,3},{5,4},{7,6},{8,9},{10,11},{13,12},{15,14},{16,17},{18,... | collective-permute-start | bytes 1572872 | tf_op jit(solution)/shard_map/ppermute | solution.py:151
  222.0 14.2 %collective-permute-start.27 = (f32[2,512,256]{2,1,0:T(8,128)S(1)}, f32[2,512,256]{2,1,0:T(8,128)}, u32[]{:S(2)}, u32[]{:S(2)}) collective-permute-start(f32[2,512,256]{2,1,0:T(8,128)S(1)} %copy-done.17), channel_id=1, source_target_pairs={{0,1},{1,0},{2,3},{3,2},{4,5},{5,4},{6,7},{7,6},{8,9},{9,8},{10,11... | collective-permute-start | bytes 3145736 | tf_op jit(solution)/shard_map/ppermute | solution.py:16
  229.4 11.8 %collective-permute-start.26 = (f32[1,1,128,256]{2,3,1,0:T(8,128)}, f32[1,1,128,256]{2,3,1,0:T(8,128)}, u32[]{:S(2)}, u32[]{:S(2)}) collective-permute-start(f32[1,1,128,256]{2,3,1,0:T(8,128)} %constant_dynamic-slice_fusion.18), channel_id=1, source_target_pairs={{0,8},{4,12},{8,0},{12,4},{1,9},{5,13},{9,1},{13,5},{2,10},{6,14},... | collective-permute-start | bytes 393224 | tf_op jit(solution)/shard_map/ppermute | solution.py:16
  238.4 14.6 %collective-permute-start.28 = (f32[1,512,256]{2,1,0:T(8,128)}, f32[1,512,256]{2,1,0:T(8,128)}, u32[]{:S(2)}, u32[]{:S(2)}) collective-permute-start(f32[1,512,256]{2,1,0:T(8,128)} %slice_bitcast_fusion.3), channel_id=1, source_target_pairs={{0,2},{1,3},{2,0},{3,1},{4,6},{5,7},{6,4},{7,5},{8,10},{9,11},{10,... | collective-permute-start | bytes 1572872 | tf_op jit(solution)/shard_map/ppermute | solution.py:16
  (61 other events, 441.0 us)

commit v11 on v8

--- a/solution.py
+++ b/solution.py
@@ -144,11 +144,8 @@
 
 
 def spread_step(held):
-    rows, cols = lax.axis_size("row"), lax.axis_size("col")
     bit = len(held) // 2
-    pairs = [(r * cols + c, r * cols + (c ^ bit)) for r in range(rows) for c in range(cols)
-             if (c ^ source_col(r)) % (2 * bit) == 0]
-    moved = lax.ppermute(jnp.stack(held[bit:]), ("row", "col"), pairs)
+    moved = swap(jnp.stack(held[bit:]), "col", bit)
     offset = lax.axis_index("col") ^ source_col(lax.axis_index("row"))
     return [jnp.where(offset & bit != 0, moved[j], held[j]) for j in range(bit)]
 

time: 268 us -> 281 us (1.049)
  waiting for transfers between devices: 111 us -> 141 us
  starting transfers between devices: 49.4 us -> 31.6 us
    ppermute x28 -> x36, waiting for transfers between devices: 104 us -> 141 us  [swap(): return lax.ppermute(block, axis, pairs)]
    ppermute x8 -> x0, starting transfers between devices: 25.3 us -> none  [spread_step(): moved = lax.ppermute(jnp.stack(held[bit:]), ('row', 'col'), pairs)]
    ppermute x28 -> x36, starting transfers between devices: 24.1 us -> 31.6 us  [swap(): return lax.ppermute(block, axis, pairs)]
    ppermute x8 -> x0, waiting for transfers between devices: 6.22 us -> none  [spread_step(): moved = lax.ppermute(jnp.stack(held[bit:]), ('row', 'col'), pairs)]
  transfers between devices with their start and end apart: 36 -> 36, of which waited for: 18 -> 21; matrix products, arithmetic and copies ran while one was open for 14% -> 13% of each run, Pallas kernels for 19% -> 18%
where the time goes in v11:
time: 281 us; the launch traced here: 280 us
  waiting for transfers between devices  141 us (50%)
  Pallas kernels  51.2 us (18%)
  starting transfers between devices  31.6 us (11%)
  other arithmetic  26.6 us (9%)
  local copies, waits for them, and re-layouts  16.1 us (6%)
  matrix products  12.3 us (4%)
    ppermute x36, waiting for transfers between devices, swap(): return lax.ppermute(block, axis, pairs)  141 us
    pallas_call x4, Pallas kernels, product(): pl.pallas_call(product_kernel, in_specs=[pl.BlockSpec(memory_space=pltpu....  44 us
    ppermute x36, starting transfers between devices, swap(): return lax.ppermute(block, axis, pairs)  31.6 us
    select_n x8, other arithmetic, spread_step(): return [jnp.where(offset & bit != 0, moved[j], held[j]) for j in range(bit)]  10.3 us
    unnamed x53, local copies, waits for them, and re-layouts  10.3 us
    dot_general x7, matrix products, dot_tn(): return lax.dot_general(a, b, (((0,), (0,)), ((), ())), precision=precision)  10 us
    pallas_call x1, Pallas kernels, split(): pl.pallas_call(split_kernel, grid=(rows // step,), in_specs=[pl.BlockSpec...  7.11 us
    another operation x4, other arithmetic, spread_step(): moved = swap(jnp.stack(held[bit:]), 'col', bit)  5.77 us
  transfers between devices with their start and end apart: 36, of which 21 were waited for; matrix products, arithmetic and copies ran while one was open for 13% of the time, Pallas kernels for 18%

profile of v11, /device:TPU:0, one launch (start us, length us, event | category | flops | bytes accessed | tf_op | source)
XLA Modules:
  0.0 280.3 jit_solution(17290625732449882627)
XLA Ops:
  3.2 4.1 %collective-permute-start = (f32[512,256]{1,0:T(8,128)S(1)}, f32[512,256]{1,0:T(8,128)}, u32[]{:S(2)}, u32[]{:S(2)}) collective-permute-start(f32[512,256]{1,0:T(8,128)S(1)} %get-tuple-element.122.refs_0_), channel_id=1, source_target_pairs={{0,8},{4,12},{8,0},{12,4},{1,9},{5,13},{9,1},{13,5},{2,10},{6,14},... | collective-permute-start | bytes 1572872 | tf_op jit(solution)/shard_map/ppermute | solution.py:16
  10.8 5.8 %copy-done.2 = f32[2048,2048]{1,0:T(8,128)S(1)} copy-done((f32[2048,2048]{1,0:T(8,128)S(1)}, f32[2048,2048]{1,0:T(8,128)}, u32[]{:S(2)}) %copy-start.2) | copy-done | bytes 16777240
  16.6 7.1 %shard_map.79 = bf16[6,2048,2048]{2,1,0:T(8,128)(2,1)} custom-call(f32[2048,2048]{1,0:T(8,128)S(1)} %copy-done.2), custom_call_target="tpu_custom_call" | custom-call | tf_op jit(solution)/shard_map/pallas_call | solution.py:34
  23.8 6.9 %collective-permute-done.refs_2_ = f32[512,256]{1,0:T(8,128)} collective-permute-done((f32[512,256]{1,0:T(8,128)S(1)}, f32[512,256]{1,0:T(8,128)}, u32[]{:S(2)}, u32[]{:S(2)}) %collective-permute-start) | collective-permute-done | bytes 524320 | tf_op jit(solution)/shard_map/ppermute | solution.py:16
  32.9 2.5 collective-permute-start.4
  38.0 18.8 %collective-permute-done.3.refs_2_ = f32[512,256]{1,0:T(8,128)} collective-permute-done((f32[512,256]{1,0:T(8,128)S(1)}, f32[512,256]{1,0:T(8,128)}, u32[]{:S(2)}, u32[]{:S(2)}) %collective-permute-start.3) | collective-permute-done | bytes 524320 | tf_op jit(solution)/shard_map/ppermute | solution.py:16
  57.9 10.3 %collective-permute-done.2.refs_3_ = f32[512,256]{1,0:T(8,128)} collective-permute-done((f32[512,256]{1,0:T(8,128)}, f32[512,256]{1,0:T(8,128)}, u32[]{:S(2)}, u32[]{:S(2)}) %collective-permute-start.2) | collective-permute-done | bytes 524320 | tf_op jit(solution)/shard_map/ppermute | solution.py:16
  77.2 11.2 %shard_map.80 = (f32[2,512,256]{2,1,0:T(8,128)}, f32[2,512,256]{2,1,0:T(8,128)S(1)}) custom-call(s32[5]{0:T(128)S(1)} %pad_add_fusion.place, bf16[6,4,512,2048]{3,2,1,0:T(8,128)(2,1)} %bitcast.199, f32[512,256]{1,0:T(8,128)S(1)} %get-tuple-element.122.refs_0_, f32[512,256]{1,0:T(8,128)S(1)} %copy-done.6, f32[512,256]{1,0:T(8,128)} %collective-permute-done.refs_2_, ...), custom_call_target="tpu_custom_call" | custom-call | tf_op jit(solution)/shard_map/pallas_call | solution.py:83
  88.4 6.5 %collective-permute-done.8 = f32[2,512,256]{2,1,0:T(8,128)} collective-permute-done((f32[2,512,256]{2,1,0:T(8,128)}, f32[2,512,256]{2,1,0:T(8,128)}, u32[]{:S(2)}, u32[]{:S(2)}) %collective-permute-start.8) | collective-permute-done | bytes 1048608 | tf_op jit(solution)/shard_map/ppermute | solution.py:16
  97.3 11.1 %collective-permute-done.5.refs_3_ = f32[512,256]{1,0:T(8,128)} collective-permute-done((f32[512,256]{1,0:T(8,128)}, f32[512,256]{1,0:T(8,128)}, u32[]{:S(2)}, u32[]{:S(2)}) %collective-permute-start.5) | collective-permute-done | bytes 524320 | tf_op jit(solution)/shard_map/ppermute | solution.py:16
  108.5 2.4 pad_maximum_fusion.1
  119.1 11.4 %shard_map.81 = (f32[2,512,256]{2,1,0:T(8,128)S(1)}, f32[2,512,256]{2,1,0:T(8,128)S(1)}) custom-call(s32[5]{0:T(128)S(1)} %pad_add_fusion.place, bf16[6,4,512,2048]{3,2,1,0:T(8,128)(2,1)} %bitcast.200, f32[512,256]{1,0:T(8,128)S(1)} %get-tuple-element.149.refs_0_, f32[512,256]{1,0:T(8,128)} %collective-permute-done.4.refs_1_, ...), custom_call_target="tpu_custom_call" | custom-call | tf_op jit(solution)/shard_map/pallas_call | solution.py:83
  130.5 6.7 %collective-permute-done.13 = f32[2,512,256]{2,1,0:T(8,128)} collective-permute-done((f32[2,512,256]{2,1,0:T(8,128)}, f32[2,512,256]{2,1,0:T(8,128)}, u32[]{:S(2)}, u32[]{:S(2)}) %collective-permute-start.13) | collective-permute-done | bytes 1048608 | tf_op jit(solution)/shard_map/ppermute | solution.py:16
  138.7 9.1 %collective-permute-done.15 = f32[1,512,256]{2,1,0:T(8,128)S(1)} collective-permute-done((f32[1,512,256]{2,1,0:T(8,128)S(1)}, f32[1,512,256]{2,1,0:T(8,128)S(1)}, u32[]{:S(2)}, u32[]{:S(2)}) %collective-permute-start.15) | collective-permute-done | bytes 524320 | tf_op jit(solution)/shard_map/ppermute | solution.py:16
  153.6 10.6 %shard_map.82 = (f32[2,512,256]{2,1,0:T(8,128)}, f32[2,512,256]{2,1,0:T(8,128)S(1)}) custom-call(s32[5]{0:T(128)S(1)} %pad_add_fusion.place, bf16[6,4,512,2048]{3,2,1,0:T(8,128)(2,1)} %bitcast.201, f32[512,256]{1,0:T(8,128)S(1)} %get-tuple-element.172.refs_0_, f32[512,256]{1,0:T(8,128)S(1)} %collective-permute-done.7.refs_1_, f32[512,256]{1,0:T(8,128)S(1)} %copy-done.4, ...), custom_call_target="tpu_custom_call" | custom-call | tf_op jit(solution)/shard_map/pallas_call | solution.py:83
  164.2 10.6 %collective-permute-done.18 = f32[2,512,256]{2,1,0:T(8,128)S(1)} collective-permute-done((f32[2,512,256]{2,1,0:T(8,128)S(1)}, f32[2,512,256]{2,1,0:T(8,128)S(1)}, u32[]{:S(2)}, u32[]{:S(2)}) %collective-permute-start.18) | collective-permute-done | bytes 1048608 | tf_op jit(solution)/shard_map/ppermute | solution.py:16
  176.0 9.7 %collective-permute-done.20 = f32[1,512,256]{2,1,0:T(8,128)S(1)} collective-permute-done((f32[1,512,256]{2,1,0:T(8,128)S(1)}, f32[1,512,256]{2,1,0:T(8,128)S(1)}, u32[]{:S(2)}, u32[]{:S(2)}) %collective-permute-start.20) | collective-permute-done | bytes 524320 | tf_op jit(solution)/shard_map/ppermute | solution.py:16
  192.8 10.8 %shard_map.83 = (f32[2,512,256]{2,1,0:T(8,128)S(1)}, f32[2,512,256]{2,1,0:T(8,128)S(1)}) custom-call(s32[5]{0:T(128)S(1)} %pad_add_fusion.place, bf16[6,4,512,2048]{3,2,1,0:T(8,128)(2,1)} %bitcast.202, f32[512,256]{1,0:T(8,128)S(1)} %get-tuple-element.194.refs_0_, f32[512,256]{1,0:T(8,128)S(1)} %collective-permute-done.12.refs_1_, ...), custom_call_target="tpu_custom_call" | custom-call | tf_op jit(solution)/shard_map/pallas_call | solution.py:83
  203.7 9.5 %collective-permute-done.22 = f32[2,512,256]{2,1,0:T(8,128)} collective-permute-done((f32[2,512,256]{2,1,0:T(8,128)}, f32[2,512,256]{2,1,0:T(8,128)}, u32[]{:S(2)}, u32[]{:S(2)}) %collective-permute-start.22) | collective-permute-done | bytes 1048608 | tf_op jit(solution)/shard_map/ppermute | solution.py:16
  214.6 9.4 %collective-permute-done.24 = f32[1,512,256]{2,1,0:T(8,128)S(1)} collective-permute-done((f32[1,512,256]{2,1,0:T(8,128)S(1)}, f32[1,512,256]{2,1,0:T(8,128)S(1)}, u32[]{:S(2)}, u32[]{:S(2)}) %collective-permute-start.24) | collective-permute-done | bytes 524320 | tf_op jit(solution)/shard_map/ppermute | solution.py:16
  232.2 12.6 %collective-permute-done.27 = f32[1,512,256]{2,1,0:T(8,128)S(1)} collective-permute-done((f32[1,512,256]{2,1,0:T(8,128)S(1)}, f32[1,512,256]{2,1,0:T(8,128)S(1)}, u32[]{:S(2)}, u32[]{:S(2)}) %collective-permute-start.27) | collective-permute-done | bytes 524320 | tf_op jit(solution)/shard_map/ppermute | solution.py:16
  257.6 8.8 %collective-permute-done.30 = f32[1,2,128,256]{3,2,1,0:T(8,128)} collective-permute-done((f32[1,2,128,256]{3,2,1,0:T(8,128)}, f32[1,2,128,256]{3,2,1,0:T(8,128)}, u32[]{:S(2)}, u32[]{:S(2)}) %collective-permute-start.30) | collective-permute-done | bytes 262176 | tf_op jit(solution)/shard_map/ppermute | solution.py:16
  270.4 2.8 %collective-permute-done.31 = f32[1,256,128]{2,1,0:T(8,128)S(1)} collective-permute-done((f32[1,256,128]{2,1,0:T(8,128)S(1)}, f32[1,256,128]{2,1,0:T(8,128)S(1)}, u32[]{:S(2)}, u32[]{:S(2)}) %collective-permute-start.31) | collective-permute-done | bytes 131104 | tf_op jit(solution)/shard_map/ppermute | solution.py:16
  275.7 3.9 %collective-permute-done.35 = f32[1,1,128,128]{3,2,1,0:T(8,128)S(1)} collective-permute-done((f32[1,1,128,128]{3,2,1,0:T(8,128)S(1)}, f32[1,1,128,128]{3,2,1,0:T(8,128)S(1)}, u32[]{:S(2)}, u32[]{:S(2)}) %collective-permute-start.35) | collective-permute-done | bytes 65568 | tf_op jit(solution)/shard_map/ppermute | solution.py:16
  (178 shorter events, 76.2 us)
Async XLA Ops:
  3.2 27.5 %collective-permute-start = (f32[512,256]{1,0:T(8,128)S(1)}, f32[512,256]{1,0:T(8,128)}, u32[]{:S(2)}, u32[]{:S(2)}) collective-permute-start(f32[512,256]{1,0:T(8,128)S(1)} %get-tuple-element.122.refs_0_), channel_id=1, source_target_pairs={{0,8},{4,12},{8,0},{12,4},{1,9},{5,13},{9,1},{13,5},{2,10},{6,14},... | collective-permute-start | bytes 1572872 | tf_op jit(solution)/shard_map/ppermute | solution.py:16
  7.3 23.5 %collective-permute-start.1 = (f32[512,256]{1,0:T(8,128)S(1)}, f32[512,256]{1,0:T(8,128)S(1)}, u32[]{:S(2)}, u32[]{:S(2)}) collective-permute-start(f32[512,256]{1,0:T(8,128)S(1)} %get-tuple-element.122.refs_0_), channel_id=1, source_target_pairs={{0,4},{4,0},{8,12},{12,8},{1,5},{5,1},{9,13},{13,9},{2,6},{6,2},{1... | collective-permute-start | bytes 1572872 | tf_op jit(solution)/shard_map/ppermute | solution.py:16
  31.5 25.3 %collective-permute-start.3 = (f32[512,256]{1,0:T(8,128)S(1)}, f32[512,256]{1,0:T(8,128)}, u32[]{:S(2)}, u32[]{:S(2)}) collective-permute-start(f32[512,256]{1,0:T(8,128)S(1)} %get-tuple-element.149.refs_0_), channel_id=1, source_target_pairs={{0,8},{4,12},{8,0},{12,4},{1,9},{5,13},{9,1},{13,5},{2,10},{6,14},... | collective-permute-start | bytes 1572872 | tf_op jit(solution)/shard_map/ppermute | solution.py:16
  32.9 24.9 %collective-permute-start.4 = (f32[512,256]{1,0:T(8,128)S(1)}, f32[512,256]{1,0:T(8,128)}, u32[]{:S(2)}, u32[]{:S(2)}) collective-permute-start(f32[512,256]{1,0:T(8,128)S(1)} %get-tuple-element.149.refs_0_), channel_id=1, source_target_pairs={{0,4},{4,0},{8,12},{12,8},{1,5},{5,1},{9,13},{13,9},{2,6},{6,2},{1... | collective-permute-start | bytes 1572872 | tf_op jit(solution)/shard_map/ppermute | solution.py:16
  35.5 32.7 %collective-permute-start.2 = (f32[512,256]{1,0:T(8,128)}, f32[512,256]{1,0:T(8,128)}, u32[]{:S(2)}, u32[]{:S(2)}) collective-permute-start(f32[512,256]{1,0:T(8,128)} %collective-permute-done.refs_2_), channel_id=1, source_target_pairs={{0,4},{4,0},{8,12},{12,8},{1,5},{5,1},{9,13},{13,9},{2,6},{6,2},{1... | collective-permute-start | bytes 1572872 | tf_op jit(solution)/shard_map/ppermute | solution.py:16
  70.4 24.6 %collective-permute-start.8 = (f32[2,512,256]{2,1,0:T(8,128)}, f32[2,512,256]{2,1,0:T(8,128)}, u32[]{:S(2)}, u32[]{:S(2)}) collective-permute-start(f32[2,512,256]{2,1,0:T(8,128)} %pad_maximum_fusion), channel_id=1, source_target_pairs={{0,2},{1,3},{2,0},{3,1},{4,6},{5,7},{6,4},{7,5},{8,10},{9,11},{10,... | collective-permute-start | bytes 3145736 | tf_op jit(solution)/shard_map/ppermute | solution.py:16
  71.7 36.7 %collective-permute-start.6 = (f32[512,256]{1,0:T(8,128)S(1)}, f32[512,256]{1,0:T(8,128)S(1)}, u32[]{:S(2)}, u32[]{:S(2)}) collective-permute-start(f32[512,256]{1,0:T(8,128)S(1)} %get-tuple-element.172.refs_0_), channel_id=1, source_target_pairs={{0,8},{4,12},{8,0},{12,4},{1,9},{5,13},{9,1},{13,5},{2,10},{6,14},... | collective-permute-start | bytes 1572872 | tf_op jit(solution)/shard_map/ppermute | solution.py:16
  73.9 34.5 %collective-permute-start.7 = (f32[512,256]{1,0:T(8,128)S(1)}, f32[512,256]{1,0:T(8,128)S(1)}, u32[]{:S(2)}, u32[]{:S(2)}) collective-permute-start(f32[512,256]{1,0:T(8,128)S(1)} %get-tuple-element.172.refs_0_), channel_id=1, source_target_pairs={{0,4},{4,0},{8,12},{12,8},{1,5},{5,1},{9,13},{13,9},{2,6},{6,2},{1... | collective-permute-start | bytes 1572872 | tf_op jit(solution)/shard_map/ppermute | solution.py:16
  75.6 32.8 %collective-permute-start.5 = (f32[512,256]{1,0:T(8,128)}, f32[512,256]{1,0:T(8,128)}, u32[]{:S(2)}, u32[]{:S(2)}) collective-permute-start(f32[512,256]{1,0:T(8,128)} %collective-permute-done.3.refs_2_), channel_id=1, source_target_pairs={{0,4},{4,0},{8,12},{12,8},{1,5},{5,1},{9,13},{13,9},{2,6},{6,2},{1... | collective-permute-start | bytes 1572872 | tf_op jit(solution)/shard_map/ppermute | solution.py:16
  110.9 26.3 %collective-permute-start.13 = (f32[2,512,256]{2,1,0:T(8,128)}, f32[2,512,256]{2,1,0:T(8,128)}, u32[]{:S(2)}, u32[]{:S(2)}) collective-permute-start(f32[2,512,256]{2,1,0:T(8,128)} %pad_maximum_fusion.1), channel_id=1, source_target_pairs={{0,2},{1,3},{2,0},{3,1},{4,6},{5,7},{6,4},{7,5},{8,10},{9,11},{10,... | collective-permute-start | bytes 3145736 | tf_op jit(solution)/shard_map/ppermute | solution.py:16
  111.8 36.9 %collective-permute-start.11 = (f32[512,256]{1,0:T(8,128)S(1)}, f32[512,256]{1,0:T(8,128)S(1)}, u32[]{:S(2)}, u32[]{:S(2)}) collective-permute-start(f32[512,256]{1,0:T(8,128)S(1)} %get-tuple-element.194.refs_0_), channel_id=1, source_target_pairs={{0,8},{4,12},{8,0},{12,4},{1,9},{5,13},{9,1},{13,5},{2,10},{6,14},... | collective-permute-start | bytes 1572872 | tf_op jit(solution)/shard_map/ppermute | solution.py:16
  111.8 36.8 %collective-permute-start.12 = (f32[512,256]{1,0:T(8,128)S(1)}, f32[512,256]{1,0:T(8,128)S(1)}, u32[]{:S(2)}, u32[]{:S(2)}) collective-permute-start(f32[512,256]{1,0:T(8,128)S(1)} %get-tuple-element.194.refs_0_), channel_id=1, source_target_pairs={{0,4},{4,0},{8,12},{12,8},{1,5},{5,1},{9,13},{13,9},{2,6},{6,2},{1... | collective-permute-start | bytes 1572872 | tf_op jit(solution)/shard_map/ppermute | solution.py:16
  113.5 35.1 %collective-permute-start.10 = (f32[512,256]{1,0:T(8,128)}, f32[512,256]{1,0:T(8,128)S(1)}, u32[]{:S(2)}, u32[]{:S(2)}) collective-permute-start(f32[512,256]{1,0:T(8,128)} %copy-done.3), channel_id=1, source_target_pairs={{0,4},{4,0},{8,12},{12,8},{1,5},{5,1},{9,13},{13,9},{2,6},{6,2},{1... | collective-permute-start | bytes 1572872 | tf_op jit(solution)/shard_map/ppermute | solution.py:16
  115.6 32.1 %collective-permute-start.15 = (f32[1,512,256]{2,1,0:T(8,128)S(1)}, f32[1,512,256]{2,1,0:T(8,128)S(1)}, u32[]{:S(2)}, u32[]{:S(2)}) collective-permute-start(f32[1,512,256]{2,1,0:T(8,128)S(1)} %slice_bitcast_fusion.11), channel_id=1, source_target_pairs={{0,2},{1,3},{2,0},{3,1},{4,6},{5,7},{6,4},{7,5},{8,10},{9,11},{10,... | collective-permute-start | bytes 1572872 | tf_op jit(solution)/shard_map/ppermute | solution.py:16
  148.8 26.0 %collective-permute-start.18 = (f32[2,512,256]{2,1,0:T(8,128)S(1)}, f32[2,512,256]{2,1,0:T(8,128)S(1)}, u32[]{:S(2)}, u32[]{:S(2)}) collective-permute-start(f32[2,512,256]{2,1,0:T(8,128)S(1)} %pad_maximum_fusion.2), channel_id=1, source_target_pairs={{0,2},{1,3},{2,0},{3,1},{4,6},{5,7},{6,4},{7,5},{8,10},{9,11},{10,... | collective-permute-start | bytes 3145736 | tf_op jit(solution)/shard_map/ppermute | solution.py:16
  150.2 35.6 %collective-permute-start.17 = (f32[512,256]{1,0:T(8,128)S(1)}, f32[512,256]{1,0:T(8,128)S(1)}, u32[]{:S(2)}, u32[]{:S(2)}) collective-permute-start(f32[512,256]{1,0:T(8,128)S(1)} %collective-permute-done.11.refs_2_), channel_id=1, source_target_pairs={{0,4},{4,0},{8,12},{12,8},{1,5},{5,1},{9,13},{13,9},{2,6},{6,2},{1... | collective-permute-start | bytes 1572872 | tf_op jit(solution)/shard_map/ppermute | solution.py:16
  151.6 34.1 %collective-permute-start.20 = (f32[1,512,256]{2,1,0:T(8,128)S(1)}, f32[1,512,256]{2,1,0:T(8,128)S(1)}, u32[]{:S(2)}, u32[]{:S(2)}) collective-permute-start(f32[1,512,256]{2,1,0:T(8,128)S(1)} %slice_bitcast_fusion.7), channel_id=1, source_target_pairs={{0,2},{1,3},{2,0},{3,1},{4,6},{5,7},{6,4},{7,5},{8,10},{9,11},{10,... | collective-permute-start | bytes 1572872 | tf_op jit(solution)/shard_map/ppermute | solution.py:16
  186.9 26.3 %collective-permute-start.22 = (f32[2,512,256]{2,1,0:T(8,128)}, f32[2,512,256]{2,1,0:T(8,128)}, u32[]{:S(2)}, u32[]{:S(2)}) collective-permute-start(f32[2,512,256]{2,1,0:T(8,128)} %pad_maximum_fusion.3), channel_id=1, source_target_pairs={{0,2},{1,3},{2,0},{3,1},{4,6},{5,7},{6,4},{7,5},{8,10},{9,11},{10,... | collective-permute-start | bytes 3145736 | tf_op jit(solution)/shard_map/ppermute | solution.py:16
  190.6 33.4 %collective-permute-start.24 = (f32[1,512,256]{2,1,0:T(8,128)S(1)}, f32[1,512,256]{2,1,0:T(8,128)S(1)}, u32[]{:S(2)}, u32[]{:S(2)}) collective-permute-start(f32[1,512,256]{2,1,0:T(8,128)S(1)} %slice_bitcast_fusion.3), channel_id=1, source_target_pairs={{0,2},{1,3},{2,0},{3,1},{4,6},{5,7},{6,4},{7,5},{8,10},{9,11},{10,... | collective-permute-start | bytes 1572872 | tf_op jit(solution)/shard_map/ppermute | solution.py:16
  224.3 5.8 %collective-permute-start.26 = (f32[2,512,256]{2,1,0:T(8,128)S(1)}, f32[2,512,256]{2,1,0:T(8,128)S(1)}, u32[]{:S(2)}, u32[]{:S(2)}) collective-permute-start(f32[2,512,256]{2,1,0:T(8,128)S(1)} %get-tuple-element.212), channel_id=1, source_target_pairs={{0,1},{1,0},{2,3},{3,2},{4,5},{5,4},{6,7},{7,6},{8,9},{9,8},{10,11... | collective-permute-start | bytes 3145736 | tf_op jit(solution)/shard_map/ppermute | solution.py:16
  230.3 14.4 %collective-permute-start.27 = (f32[1,512,256]{2,1,0:T(8,128)S(1)}, f32[1,512,256]{2,1,0:T(8,128)S(1)}, u32[]{:S(2)}, u32[]{:S(2)}) collective-permute-start(f32[1,512,256]{2,1,0:T(8,128)S(1)} %slice_bitcast_fusion.1), channel_id=1, source_target_pairs={{0,2},{1,3},{2,0},{3,1},{4,6},{5,7},{6,4},{7,5},{8,10},{9,11},{10,... | collective-permute-start | bytes 1572872 | tf_op jit(solution)/shard_map/ppermute | solution.py:16
  231.8 14.1 %collective-permute-start.29 = (f32[2,2,128,256]{3,2,1,0:T(8,128)S(1)}, f32[2,2,128,256]{3,2,1,0:T(8,128)S(1)}, u32[]{:S(2)}, u32[]{:S(2)}) collective-permute-start(f32[2,2,128,256]{3,2,1,0:T(8,128)S(1)} %bitcast.216), channel_id=1, source_target_pairs={{0,4},{4,0},{8,12},{12,8},{1,5},{5,1},{9,13},{13,9},{2,6},{6,2},{1... | collective-permute-start | bytes 1572872 | tf_op jit(solution)/shard_map/ppermute | solution.py:16
  250.9 15.6 %collective-permute-start.30 = (f32[1,2,128,256]{3,2,1,0:T(8,128)}, f32[1,2,128,256]{3,2,1,0:T(8,128)}, u32[]{:S(2)}, u32[]{:S(2)}) collective-permute-start(f32[1,2,128,256]{3,2,1,0:T(8,128)} %constant_dynamic-slice_fusion.9), channel_id=1, source_target_pairs={{0,8},{4,12},{8,0},{12,4},{1,9},{5,13},{9,1},{13,5},{2,10},{6,14},... | collective-permute-start | bytes 786440 | tf_op jit(solution)/shard_map/ppermute | solution.py:16
  257.1 11.7 %collective-permute-start.33 = (f32[1,512,128]{2,1,0:T(8,128)}, f32[1,512,128]{2,1,0:T(8,128)S(1)}, u32[]{:S(2)}, u32[]{:S(2)}) collective-permute-start(f32[1,512,128]{2,1,0:T(8,128)} %bitcast.73), channel_id=1, source_target_pairs={{0,2},{1,3},{2,0},{3,1},{4,6},{5,7},{6,4},{7,5},{8,10},{9,11},{10,... | collective-permute-start | bytes 786440 | tf_op jit(solution)/shard_map/ppermute | solution.py:16
  (35 other events, 258.5 us)

commit v12 on v11

--- a/solution.py
+++ b/solution.py
@@ -143,9 +143,15 @@
     return held
 
 
-def spread_step(held):
+def spread_step(held, one_way=False):
+    rows, cols = lax.axis_size("row"), lax.axis_size("col")
     bit = len(held) // 2
-    moved = swap(jnp.stack(held[bit:]), "col", bit)
+    if one_way:
+        pairs = [(r * cols + c, r * cols + (c ^ bit)) for r in range(rows) for c in range(cols)
+                 if (c ^ source_col(r)) % (2 * bit) == 0]
+        moved = lax.ppermute(jnp.stack(held[bit:]), ("row", "col"), pairs)
+    else:
+        moved = swap(jnp.stack(held[bit:]), "col", bit)
     offset = lax.axis_index("col") ^ source_col(lax.axis_index("row"))
     return [jnp.where(offset & bit != 0, moved[j], held[j]) for j in range(bit)]
 
@@ -199,8 +205,7 @@
             live["out", k] = -sum_scatter(live.pop(("sums", k)), "col", 2)
 
         def collect(k):
-            live["own", k] = blocks_to_send(blocks(k))
-            spread(k)
+            live["own", k] = spread_step(blocks_to_send(blocks(k)), one_way=k >= count_first)
 
         def spread(k):
             live["own", k] = spread_step(live["own", k])

time: 281 us -> 263 us (0.936)
  waiting for transfers between devices: 141 us -> 119 us
  starting transfers between devices: 31.6 us -> 35.1 us
    ppermute x36 -> x34, waiting for transfers between devices: 141 us -> 112 us  [swap(): return lax.ppermute(block, axis, pairs)]
    ppermute x0 -> x2, starting transfers between devices: none -> 8.42 us  [spread_step(): moved = lax.ppermute(jnp.stack(held[bit:]), ('row', 'col'), pairs)]
    ppermute x0 -> x2, waiting for transfers between devices: none -> 7.4 us  [spread_step(): moved = lax.ppermute(jnp.stack(held[bit:]), ('row', 'col'), pairs)]
    ppermute x36 -> x34, starting transfers between devices: 31.6 us -> 26.7 us  [swap(): return lax.ppermute(block, axis, pairs)]
    another operation x4 -> x2, other arithmetic: 5.77 us -> 4.62 us  [spread_step(): moved = swap(jnp.stack(held[bit:]), 'col', bit)]
  transfers between devices with their start and end apart: 36 -> 36, of which waited for: 21 -> 21; matrix products, arithmetic and copies ran while one was open for 13% -> 14% of each run, Pallas kernels for 18% -> 20%
where the time goes in v12:
time: 263 us; the launch traced here: 262 us
  waiting for transfers between devices  119 us (45%)
  Pallas kernels  51.2 us (19%)
  starting transfers between devices  35.1 us (13%)
  other arithmetic  26.7 us (10%)
  local copies, waits for them, and re-layouts  16.1 us (6%)
  matrix products  12.3 us (5%)
    ppermute x34, waiting for transfers between devices, swap(): return lax.ppermute(block, axis, pairs)  112 us
    pallas_call x4, Pallas kernels, product(): pl.pallas_call(product_kernel, in_specs=[pl.BlockSpec(memory_space=pltpu....  44 us
    ppermute x34, starting transfers between devices, swap(): return lax.ppermute(block, axis, pairs)  26.7 us
    select_n x8, other arithmetic, spread_step(): return [jnp.where(offset & bit != 0, moved[j], held[j]) for j in range(bit)]  10.3 us
    unnamed x53, local copies, waits for them, and re-layouts  10.3 us
    dot_general x7, matrix products, dot_tn(): return lax.dot_general(a, b, (((0,), (0,)), ((), ())), precision=precision)  10 us
    ppermute x2, starting transfers between devices, spread_step(): moved = lax.ppermute(jnp.stack(held[bit:]), ('row', 'col'), pairs)  8.42 us
    ppermute x2, waiting for transfers between devices, spread_step(): moved = lax.ppermute(jnp.stack(held[bit:]), ('row', 'col'), pairs)  7.4 us
  transfers between devices with their start and end apart: 36, of which 21 were waited for; matrix products, arithmetic and copies ran while one was open for 14% of the time, Pallas kernels for 20%

profile of v12, /device:TPU:0, one launch (start us, length us, event | category | flops | bytes accessed | tf_op | source)
XLA Modules:
  0.0 261.8 jit_solution(11176172988486491901)
XLA Ops:
  3.2 4.1 %collective-permute-start = (f32[512,256]{1,0:T(8,128)S(1)}, f32[512,256]{1,0:T(8,128)}, u32[]{:S(2)}, u32[]{:S(2)}) collective-permute-start(f32[512,256]{1,0:T(8,128)S(1)} %get-tuple-element.122.refs_0_), channel_id=1, source_target_pairs={{0,8},{4,12},{8,0},{12,4},{1,9},{5,13},{9,1},{13,5},{2,10},{6,14},... | collective-permute-start | bytes 1572872 | tf_op jit(solution)/shard_map/ppermute | solution.py:16
  10.8 5.8 %copy-done.2 = f32[2048,2048]{1,0:T(8,128)S(1)} copy-done((f32[2048,2048]{1,0:T(8,128)S(1)}, f32[2048,2048]{1,0:T(8,128)}, u32[]{:S(2)}) %copy-start.2) | copy-done | bytes 16777240
  16.6 7.1 %shard_map.79 = bf16[6,2048,2048]{2,1,0:T(8,128)(2,1)} custom-call(f32[2048,2048]{1,0:T(8,128)S(1)} %copy-done.2), custom_call_target="tpu_custom_call" | custom-call | tf_op jit(solution)/shard_map/pallas_call | solution.py:34
  23.8 6.9 %collective-permute-done.refs_2_ = f32[512,256]{1,0:T(8,128)} collective-permute-done((f32[512,256]{1,0:T(8,128)S(1)}, f32[512,256]{1,0:T(8,128)}, u32[]{:S(2)}, u32[]{:S(2)}) %collective-permute-start) | collective-permute-done | bytes 524320 | tf_op jit(solution)/shard_map/ppermute | solution.py:16
  38.0 18.8 %collective-permute-done.3.refs_2_ = f32[512,256]{1,0:T(8,128)} collective-permute-done((f32[512,256]{1,0:T(8,128)S(1)}, f32[512,256]{1,0:T(8,128)}, u32[]{:S(2)}, u32[]{:S(2)}) %collective-permute-start.3) | collective-permute-done | bytes 524320 | tf_op jit(solution)/shard_map/ppermute | solution.py:16
  57.9 10.3 %collective-permute-done.2.refs_3_ = f32[512,256]{1,0:T(8,128)} collective-permute-done((f32[512,256]{1,0:T(8,128)}, f32[512,256]{1,0:T(8,128)}, u32[]{:S(2)}, u32[]{:S(2)}) %collective-permute-start.2) | collective-permute-done | bytes 524320 | tf_op jit(solution)/shard_map/ppermute | solution.py:16
  77.2 11.2 %shard_map.80 = (f32[2,512,256]{2,1,0:T(8,128)}, f32[2,512,256]{2,1,0:T(8,128)S(1)}) custom-call(s32[5]{0:T(128)S(1)} %pad_add_fusion.place, bf16[6,4,512,2048]{3,2,1,0:T(8,128)(2,1)} %bitcast.199, f32[512,256]{1,0:T(8,128)S(1)} %get-tuple-element.122.refs_0_, f32[512,256]{1,0:T(8,128)S(1)} %copy-done.6, f32[512,256]{1,0:T(8,128)} %collective-permute-done.refs_2_, ...), custom_call_target="tpu_custom_call" | custom-call | tf_op jit(solution)/shard_map/pallas_call | solution.py:83
  88.4 6.5 %collective-permute-done.8 = f32[2,512,256]{2,1,0:T(8,128)} collective-permute-done((f32[2,512,256]{2,1,0:T(8,128)}, f32[2,512,256]{2,1,0:T(8,128)}, u32[]{:S(2)}, u32[]{:S(2)}) %collective-permute-start.8) | collective-permute-done | bytes 1048608 | tf_op jit(solution)/shard_map/ppermute | solution.py:16
  97.3 11.1 %collective-permute-done.5.refs_3_ = f32[512,256]{1,0:T(8,128)} collective-permute-done((f32[512,256]{1,0:T(8,128)}, f32[512,256]{1,0:T(8,128)}, u32[]{:S(2)}, u32[]{:S(2)}) %collective-permute-start.5) | collective-permute-done | bytes 524320 | tf_op jit(solution)/shard_map/ppermute | solution.py:16
  119.1 11.4 %shard_map.81 = (f32[2,512,256]{2,1,0:T(8,128)S(1)}, f32[2,512,256]{2,1,0:T(8,128)S(1)}) custom-call(s32[5]{0:T(128)S(1)} %pad_add_fusion.place, bf16[6,4,512,2048]{3,2,1,0:T(8,128)(2,1)} %bitcast.200, f32[512,256]{1,0:T(8,128)S(1)} %get-tuple-element.149.refs_0_, f32[512,256]{1,0:T(8,128)} %collective-permute-done.4.refs_1_, ...), custom_call_target="tpu_custom_call" | custom-call | tf_op jit(solution)/shard_map/pallas_call | solution.py:83
  130.5 6.7 %collective-permute-done.13 = f32[2,512,256]{2,1,0:T(8,128)} collective-permute-done((f32[2,512,256]{2,1,0:T(8,128)}, f32[2,512,256]{2,1,0:T(8,128)}, u32[]{:S(2)}, u32[]{:S(2)}) %collective-permute-start.13) | collective-permute-done | bytes 1048608 | tf_op jit(solution)/shard_map/ppermute | solution.py:16
  138.7 9.1 %collective-permute-done.15 = f32[1,512,256]{2,1,0:T(8,128)S(1)} collective-permute-done((f32[1,512,256]{2,1,0:T(8,128)S(1)}, f32[1,512,256]{2,1,0:T(8,128)S(1)}, u32[]{:S(2)}, u32[]{:S(2)}) %collective-permute-start.15) | collective-permute-done | bytes 524320 | tf_op jit(solution)/shard_map/ppermute | solution.py:16
  148.8 3.1 %collective-permute-start.18 = (f32[2,512,256]{2,1,0:T(8,128)S(1)}, f32[2,512,256]{2,1,0:T(8,128)S(1)}, u32[]{:S(2)}, u32[]{:S(2)}) collective-permute-start(f32[2,512,256]{2,1,0:T(8,128)S(1)} %pad_maximum_fusion.2), channel_id=1, source_target_pairs={{0,2},{5,7},{10,8},{15,13},{16,18},{21,23},{26,24},{31,29}} | collective-permute-start | bytes 3145736 | tf_op jit(solution)/shard_map/ppermute | solution.py:152
  154.8 10.6 %shard_map.82 = (f32[2,512,256]{2,1,0:T(8,128)}, f32[2,512,256]{2,1,0:T(8,128)S(1)}) custom-call(s32[5]{0:T(128)S(1)} %pad_add_fusion.place, bf16[6,4,512,2048]{3,2,1,0:T(8,128)(2,1)} %bitcast.201, f32[512,256]{1,0:T(8,128)S(1)} %get-tuple-element.172.refs_0_, f32[512,256]{1,0:T(8,128)S(1)} %collective-permute-done.7.refs_1_, f32[512,256]{1,0:T(8,128)S(1)} %copy-done.4, ...), custom_call_target="tpu_custom_call" | custom-call | tf_op jit(solution)/shard_map/pallas_call | solution.py:83
  165.4 4.4 %collective-permute-done.18 = f32[2,512,256]{2,1,0:T(8,128)S(1)} collective-permute-done((f32[2,512,256]{2,1,0:T(8,128)S(1)}, f32[2,512,256]{2,1,0:T(8,128)S(1)}, u32[]{:S(2)}, u32[]{:S(2)}) %collective-permute-start.18) | collective-permute-done | bytes 1048608 | tf_op jit(solution)/shard_map/ppermute | solution.py:152
  170.9 4.5 %collective-permute-done.20 = f32[1,512,256]{2,1,0:T(8,128)S(1)} collective-permute-done((f32[1,512,256]{2,1,0:T(8,128)S(1)}, f32[1,512,256]{2,1,0:T(8,128)S(1)}, u32[]{:S(2)}, u32[]{:S(2)}) %collective-permute-start.20) | collective-permute-done | bytes 524320 | tf_op jit(solution)/shard_map/ppermute | solution.py:16
  176.6 5.4 %collective-permute-start.22 = (f32[2,512,256]{2,1,0:T(8,128)}, f32[2,512,256]{2,1,0:T(8,128)}, u32[]{:S(2)}, u32[]{:S(2)}) collective-permute-start(f32[2,512,256]{2,1,0:T(8,128)} %pad_maximum_fusion.3), channel_id=1, source_target_pairs={{0,2},{5,7},{10,8},{15,13},{16,18},{21,23},{26,24},{31,29}} | collective-permute-start | bytes 3145736 | tf_op jit(solution)/shard_map/ppermute | solution.py:152
  185.4 10.8 %shard_map.83 = (f32[2,512,256]{2,1,0:T(8,128)S(1)}, f32[2,512,256]{2,1,0:T(8,128)S(1)}) custom-call(s32[5]{0:T(128)S(1)} %pad_add_fusion.place, bf16[6,4,512,2048]{3,2,1,0:T(8,128)(2,1)} %bitcast.202, f32[512,256]{1,0:T(8,128)S(1)} %get-tuple-element.194.refs_0_, f32[512,256]{1,0:T(8,128)S(1)} %collective-permute-done.12.refs_1_, ...), custom_call_target="tpu_custom_call" | custom-call | tf_op jit(solution)/shard_map/pallas_call | solution.py:83
  196.2 3.0 %collective-permute-done.22 = f32[2,512,256]{2,1,0:T(8,128)} collective-permute-done((f32[2,512,256]{2,1,0:T(8,128)}, f32[2,512,256]{2,1,0:T(8,128)}, u32[]{:S(2)}, u32[]{:S(2)}) %collective-permute-start.22) | collective-permute-done | bytes 1048608 | tf_op jit(solution)/shard_map/ppermute | solution.py:152
  200.6 4.2 %collective-permute-done.24 = f32[1,512,256]{2,1,0:T(8,128)S(1)} collective-permute-done((f32[1,512,256]{2,1,0:T(8,128)S(1)}, f32[1,512,256]{2,1,0:T(8,128)S(1)}, u32[]{:S(2)}, u32[]{:S(2)}) %collective-permute-start.24) | collective-permute-done | bytes 524320 | tf_op jit(solution)/shard_map/ppermute | solution.py:16
  214.1 12.2 %collective-permute-done.27 = f32[1,512,256]{2,1,0:T(8,128)S(1)} collective-permute-done((f32[1,512,256]{2,1,0:T(8,128)S(1)}, f32[1,512,256]{2,1,0:T(8,128)S(1)}, u32[]{:S(2)}, u32[]{:S(2)}) %collective-permute-start.27) | collective-permute-done | bytes 524320 | tf_op jit(solution)/shard_map/ppermute | solution.py:16
  239.8 8.5 %collective-permute-done.30 = f32[1,2,128,256]{3,2,1,0:T(8,128)} collective-permute-done((f32[1,2,128,256]{3,2,1,0:T(8,128)}, f32[1,2,128,256]{3,2,1,0:T(8,128)}, u32[]{:S(2)}, u32[]{:S(2)}) %collective-permute-start.30) | collective-permute-done | bytes 262176 | tf_op jit(solution)/shard_map/ppermute | solution.py:16
  251.7 3.5 %collective-permute-done.31 = f32[1,256,128]{2,1,0:T(8,128)S(1)} collective-permute-done((f32[1,256,128]{2,1,0:T(8,128)S(1)}, f32[1,256,128]{2,1,0:T(8,128)S(1)}, u32[]{:S(2)}, u32[]{:S(2)}) %collective-permute-start.31) | collective-permute-done | bytes 131104 | tf_op jit(solution)/shard_map/ppermute | solution.py:16
  256.4 4.7 %collective-permute-done.35 = f32[1,1,128,128]{3,2,1,0:T(8,128)S(1)} collective-permute-done((f32[1,1,128,128]{3,2,1,0:T(8,128)S(1)}, f32[1,1,128,128]{3,2,1,0:T(8,128)S(1)}, u32[]{:S(2)}, u32[]{:S(2)}) %collective-permute-start.35) | collective-permute-done | bytes 65568 | tf_op jit(solution)/shard_map/ppermute | solution.py:16
  (178 shorter events, 76.5 us)
Async XLA Ops:
  3.2 27.5 %collective-permute-start = (f32[512,256]{1,0:T(8,128)S(1)}, f32[512,256]{1,0:T(8,128)}, u32[]{:S(2)}, u32[]{:S(2)}) collective-permute-start(f32[512,256]{1,0:T(8,128)S(1)} %get-tuple-element.122.refs_0_), channel_id=1, source_target_pairs={{0,8},{4,12},{8,0},{12,4},{1,9},{5,13},{9,1},{13,5},{2,10},{6,14},... | collective-permute-start | bytes 1572872 | tf_op jit(solution)/shard_map/ppermute | solution.py:16
  7.3 23.5 %collective-permute-start.1 = (f32[512,256]{1,0:T(8,128)S(1)}, f32[512,256]{1,0:T(8,128)S(1)}, u32[]{:S(2)}, u32[]{:S(2)}) collective-permute-start(f32[512,256]{1,0:T(8,128)S(1)} %get-tuple-element.122.refs_0_), channel_id=1, source_target_pairs={{0,4},{4,0},{8,12},{12,8},{1,5},{5,1},{9,13},{13,9},{2,6},{6,2},{1... | collective-permute-start | bytes 1572872 | tf_op jit(solution)/shard_map/ppermute | solution.py:16
  31.5 25.3 %collective-permute-start.3 = (f32[512,256]{1,0:T(8,128)S(1)}, f32[512,256]{1,0:T(8,128)}, u32[]{:S(2)}, u32[]{:S(2)}) collective-permute-start(f32[512,256]{1,0:T(8,128)S(1)} %get-tuple-element.149.refs_0_), channel_id=1, source_target_pairs={{0,8},{4,12},{8,0},{12,4},{1,9},{5,13},{9,1},{13,5},{2,10},{6,14},... | collective-permute-start | bytes 1572872 | tf_op jit(solution)/shard_map/ppermute | solution.py:16
  32.9 24.9 %collective-permute-start.4 = (f32[512,256]{1,0:T(8,128)S(1)}, f32[512,256]{1,0:T(8,128)}, u32[]{:S(2)}, u32[]{:S(2)}) collective-permute-start(f32[512,256]{1,0:T(8,128)S(1)} %get-tuple-element.149.refs_0_), channel_id=1, source_target_pairs={{0,4},{4,0},{8,12},{12,8},{1,5},{5,1},{9,13},{13,9},{2,6},{6,2},{1... | collective-permute-start | bytes 1572872 | tf_op jit(solution)/shard_map/ppermute | solution.py:16
  35.5 32.7 %collective-permute-start.2 = (f32[512,256]{1,0:T(8,128)}, f32[512,256]{1,0:T(8,128)}, u32[]{:S(2)}, u32[]{:S(2)}) collective-permute-start(f32[512,256]{1,0:T(8,128)} %collective-permute-done.refs_2_), channel_id=1, source_target_pairs={{0,4},{4,0},{8,12},{12,8},{1,5},{5,1},{9,13},{13,9},{2,6},{6,2},{1... | collective-permute-start | bytes 1572872 | tf_op jit(solution)/shard_map/ppermute | solution.py:16
  70.4 24.6 %collective-permute-start.8 = (f32[2,512,256]{2,1,0:T(8,128)}, f32[2,512,256]{2,1,0:T(8,128)}, u32[]{:S(2)}, u32[]{:S(2)}) collective-permute-start(f32[2,512,256]{2,1,0:T(8,128)} %pad_maximum_fusion), channel_id=1, source_target_pairs={{0,2},{1,3},{2,0},{3,1},{4,6},{5,7},{6,4},{7,5},{8,10},{9,11},{10,... | collective-permute-start | bytes 3145736 | tf_op jit(solution)/shard_map/ppermute | solution.py:16
  71.7 36.7 %collective-permute-start.6 = (f32[512,256]{1,0:T(8,128)S(1)}, f32[512,256]{1,0:T(8,128)S(1)}, u32[]{:S(2)}, u32[]{:S(2)}) collective-permute-start(f32[512,256]{1,0:T(8,128)S(1)} %get-tuple-element.172.refs_0_), channel_id=1, source_target_pairs={{0,8},{4,12},{8,0},{12,4},{1,9},{5,13},{9,1},{13,5},{2,10},{6,14},... | collective-permute-start | bytes 1572872 | tf_op jit(solution)/shard_map/ppermute | solution.py:16
  73.9 34.5 %collective-permute-start.7 = (f32[512,256]{1,0:T(8,128)S(1)}, f32[512,256]{1,0:T(8,128)S(1)}, u32[]{:S(2)}, u32[]{:S(2)}) collective-permute-start(f32[512,256]{1,0:T(8,128)S(1)} %get-tuple-element.172.refs_0_), channel_id=1, source_target_pairs={{0,4},{4,0},{8,12},{12,8},{1,5},{5,1},{9,13},{13,9},{2,6},{6,2},{1... | collective-permute-start | bytes 1572872 | tf_op jit(solution)/shard_map/ppermute | solution.py:16
  75.6 32.8 %collective-permute-start.5 = (f32[512,256]{1,0:T(8,128)}, f32[512,256]{1,0:T(8,128)}, u32[]{:S(2)}, u32[]{:S(2)}) collective-permute-start(f32[512,256]{1,0:T(8,128)} %collective-permute-done.3.refs_2_), channel_id=1, source_target_pairs={{0,4},{4,0},{8,12},{12,8},{1,5},{5,1},{9,13},{13,9},{2,6},{6,2},{1... | collective-permute-start | bytes 1572872 | tf_op jit(solution)/shard_map/ppermute | solution.py:16
  110.9 26.3 %collective-permute-start.13 = (f32[2,512,256]{2,1,0:T(8,128)}, f32[2,512,256]{2,1,0:T(8,128)}, u32[]{:S(2)}, u32[]{:S(2)}) collective-permute-start(f32[2,512,256]{2,1,0:T(8,128)} %pad_maximum_fusion.1), channel_id=1, source_target_pairs={{0,2},{1,3},{2,0},{3,1},{4,6},{5,7},{6,4},{7,5},{8,10},{9,11},{10,... | collective-permute-start | bytes 3145736 | tf_op jit(solution)/shard_map/ppermute | solution.py:16
  111.8 36.9 %collective-permute-start.11 = (f32[512,256]{1,0:T(8,128)S(1)}, f32[512,256]{1,0:T(8,128)S(1)}, u32[]{:S(2)}, u32[]{:S(2)}) collective-permute-start(f32[512,256]{1,0:T(8,128)S(1)} %get-tuple-element.194.refs_0_), channel_id=1, source_target_pairs={{0,8},{4,12},{8,0},{12,4},{1,9},{5,13},{9,1},{13,5},{2,10},{6,14},... | collective-permute-start | bytes 1572872 | tf_op jit(solution)/shard_map/ppermute | solution.py:16
  111.8 36.8 %collective-permute-start.12 = (f32[512,256]{1,0:T(8,128)S(1)}, f32[512,256]{1,0:T(8,128)S(1)}, u32[]{:S(2)}, u32[]{:S(2)}) collective-permute-start(f32[512,256]{1,0:T(8,128)S(1)} %get-tuple-element.194.refs_0_), channel_id=1, source_target_pairs={{0,4},{4,0},{8,12},{12,8},{1,5},{5,1},{9,13},{13,9},{2,6},{6,2},{1... | collective-permute-start | bytes 1572872 | tf_op jit(solution)/shard_map/ppermute | solution.py:16
  113.5 35.1 %collective-permute-start.10 = (f32[512,256]{1,0:T(8,128)}, f32[512,256]{1,0:T(8,128)S(1)}, u32[]{:S(2)}, u32[]{:S(2)}) collective-permute-start(f32[512,256]{1,0:T(8,128)} %copy-done.3), channel_id=1, source_target_pairs={{0,4},{4,0},{8,12},{12,8},{1,5},{5,1},{9,13},{13,9},{2,6},{6,2},{1... | collective-permute-start | bytes 1572872 | tf_op jit(solution)/shard_map/ppermute | solution.py:16
  115.6 32.1 %collective-permute-start.15 = (f32[1,512,256]{2,1,0:T(8,128)S(1)}, f32[1,512,256]{2,1,0:T(8,128)S(1)}, u32[]{:S(2)}, u32[]{:S(2)}) collective-permute-start(f32[1,512,256]{2,1,0:T(8,128)S(1)} %slice_bitcast_fusion.11), channel_id=1, source_target_pairs={{0,2},{1,3},{2,0},{3,1},{4,6},{5,7},{6,4},{7,5},{8,10},{9,11},{10,... | collective-permute-start | bytes 1572872 | tf_op jit(solution)/shard_map/ppermute | solution.py:16
  148.8 20.9 %collective-permute-start.18 = (f32[2,512,256]{2,1,0:T(8,128)S(1)}, f32[2,512,256]{2,1,0:T(8,128)S(1)}, u32[]{:S(2)}, u32[]{:S(2)}) collective-permute-start(f32[2,512,256]{2,1,0:T(8,128)S(1)} %pad_maximum_fusion.2), channel_id=1, source_target_pairs={{0,2},{5,7},{10,8},{15,13},{16,18},{21,23},{26,24},{31,29}} | collective-permute-start | bytes 3145736 | tf_op jit(solution)/shard_map/ppermute | solution.py:152
  152.0 23.5 %collective-permute-start.17 = (f32[512,256]{1,0:T(8,128)S(1)}, f32[512,256]{1,0:T(8,128)S(1)}, u32[]{:S(2)}, u32[]{:S(2)}) collective-permute-start(f32[512,256]{1,0:T(8,128)S(1)} %collective-permute-done.11.refs_2_), channel_id=1, source_target_pairs={{0,4},{4,0},{8,12},{12,8},{1,5},{5,1},{9,13},{13,9},{2,6},{6,2},{1... | collective-permute-start | bytes 1572872 | tf_op jit(solution)/shard_map/ppermute | solution.py:16
  152.6 22.7 %collective-permute-start.20 = (f32[1,512,256]{2,1,0:T(8,128)S(1)}, f32[1,512,256]{2,1,0:T(8,128)S(1)}, u32[]{:S(2)}, u32[]{:S(2)}) collective-permute-start(f32[1,512,256]{2,1,0:T(8,128)S(1)} %slice_bitcast_fusion.7), channel_id=1, source_target_pairs={{0,2},{1,3},{2,0},{3,1},{4,6},{5,7},{6,4},{7,5},{8,10},{9,11},{10,... | collective-permute-start | bytes 1572872 | tf_op jit(solution)/shard_map/ppermute | solution.py:16
  175.4 6.5 %collective-permute-start.23 = (f32[2,512,256]{2,1,0:T(8,128)}, f32[2,512,256]{2,1,0:T(8,128)}, u32[]{:S(2)}, u32[]{:S(2)}) collective-permute-start(f32[2,512,256]{2,1,0:T(8,128)} %get-tuple-element.193), channel_id=1, source_target_pairs={{0,1},{1,0},{2,3},{3,2},{4,5},{5,4},{6,7},{7,6},{8,9},{9,8},{10,11... | collective-permute-start | bytes 3145736 | tf_op jit(solution)/shard_map/ppermute | solution.py:16
  176.6 22.6 %collective-permute-start.22 = (f32[2,512,256]{2,1,0:T(8,128)}, f32[2,512,256]{2,1,0:T(8,128)}, u32[]{:S(2)}, u32[]{:S(2)}) collective-permute-start(f32[2,512,256]{2,1,0:T(8,128)} %pad_maximum_fusion.3), channel_id=1, source_target_pairs={{0,2},{5,7},{10,8},{15,13},{16,18},{21,23},{26,24},{31,29}} | collective-permute-start | bytes 3145736 | tf_op jit(solution)/shard_map/ppermute | solution.py:152
  183.8 21.0 %collective-permute-start.24 = (f32[1,512,256]{2,1,0:T(8,128)S(1)}, f32[1,512,256]{2,1,0:T(8,128)S(1)}, u32[]{:S(2)}, u32[]{:S(2)}) collective-permute-start(f32[1,512,256]{2,1,0:T(8,128)S(1)} %slice_bitcast_fusion.3), channel_id=1, source_target_pairs={{0,2},{1,3},{2,0},{3,1},{4,6},{5,7},{6,4},{7,5},{8,10},{9,11},{10,... | collective-permute-start | bytes 1572872 | tf_op jit(solution)/shard_map/ppermute | solution.py:16
  211.1 15.2 %collective-permute-start.27 = (f32[1,512,256]{2,1,0:T(8,128)S(1)}, f32[1,512,256]{2,1,0:T(8,128)S(1)}, u32[]{:S(2)}, u32[]{:S(2)}) collective-permute-start(f32[1,512,256]{2,1,0:T(8,128)S(1)} %slice_bitcast_fusion.1), channel_id=1, source_target_pairs={{0,2},{1,3},{2,0},{3,1},{4,6},{5,7},{6,4},{7,5},{8,10},{9,11},{10,... | collective-permute-start | bytes 1572872 | tf_op jit(solution)/shard_map/ppermute | solution.py:16
  214.0 14.1 %collective-permute-start.29 = (f32[2,2,128,256]{3,2,1,0:T(8,128)S(1)}, f32[2,2,128,256]{3,2,1,0:T(8,128)S(1)}, u32[]{:S(2)}, u32[]{:S(2)}) collective-permute-start(f32[2,2,128,256]{3,2,1,0:T(8,128)S(1)} %bitcast.216), channel_id=1, source_target_pairs={{0,4},{4,0},{8,12},{12,8},{1,5},{5,1},{9,13},{13,9},{2,6},{6,2},{1... | collective-permute-start | bytes 1572872 | tf_op jit(solution)/shard_map/ppermute | solution.py:16
  233.1 15.3 %collective-permute-start.30 = (f32[1,2,128,256]{3,2,1,0:T(8,128)}, f32[1,2,128,256]{3,2,1,0:T(8,128)}, u32[]{:S(2)}, u32[]{:S(2)}) collective-permute-start(f32[1,2,128,256]{3,2,1,0:T(8,128)} %constant_dynamic-slice_fusion.9), channel_id=1, source_target_pairs={{0,8},{4,12},{8,0},{12,4},{1,9},{5,13},{9,1},{13,5},{2,10},{6,14},... | collective-permute-start | bytes 786440 | tf_op jit(solution)/shard_map/ppermute | solution.py:16
  238.1 11.9 %collective-permute-start.33 = (f32[1,512,128]{2,1,0:T(8,128)}, f32[1,512,128]{2,1,0:T(8,128)S(1)}, u32[]{:S(2)}, u32[]{:S(2)}) collective-permute-start(f32[1,512,128]{2,1,0:T(8,128)} %bitcast.73), channel_id=1, source_target_pairs={{0,2},{1,3},{2,0},{3,1},{4,6},{5,7},{6,4},{7,5},{8,10},{9,11},{10,... | collective-permute-start | bytes 786440 | tf_op jit(solution)/shard_map/ppermute | solution.py:16
  (35 other events, 225.9 us)

commit v13 on v12

--- a/solution.py
+++ b/solution.py
@@ -226,6 +226,8 @@
             given = dot(live["given"], link_cols, precise)
             live["link_cross"] = lax.dynamic_update_slice_in_dim(jnp.zeros_like(link), given, row_id * height, 0)
             live["link_second"] = -dot_tn(link_rows, given, precise)
+            for name in ("link_cross", "link_second"):
+                live[name] = [by_parity(live[name], odd) for odd in (0, 1)]
 
         def core_sum(terms):
             sent = swap(terms(1), "col", 1)
@@ -243,9 +245,10 @@
         def first_terms():
             out_first = outs(0, count_first)
             own_first, own_second = owns(0, count_first), owns(count_first, len(pieces))
+            live["own_second"] = [by_parity(own_second, odd) for odd in (0, 1)]
 
             def terms(odd):
-                cross = dot_tn(out_first, by_parity(own_second, odd), three_pass) + by_parity(live["link_cross"], odd)
+                cross = dot_tn(out_first, live["own_second"][odd], three_pass) + live["link_cross"][odd]
                 return jnp.concatenate([dot_tn(out_first, by_parity(own_first, odd), three_pass), cross])
 
             live["first_sums"] = sum_step(by_rows(core_sum(terms)), "row", 1)
@@ -255,10 +258,10 @@
             live["first_sums"] = rest_of_cols(sums.reshape(-1, sums.shape[2])).reshape(-1, height, span)
 
         def second_terms():
-            out_second, own_second = outs(count_first, len(pieces)), owns(count_first, len(pieces))
+            out_second = outs(count_first, len(pieces))
 
             def terms(odd):
-                return dot_tn(out_second, by_parity(own_second, odd), three_pass) + by_parity(live["link_second"], odd)
+                return dot_tn(out_second, live["own_second"][odd], three_pass) + live["link_second"][odd]
 
             live["second_sum"] = sum_rows(by_rows(rest_of_cols(core_sum(terms))), "row")[0]
 

time: 263 us -> 262 us (level)
  other arithmetic: 26.7 us -> 30.5 us
  waiting for transfers between devices: 119 us -> 116 us
    ppermute x34, waiting for transfers between devices: 112 us -> 108 us  [swap(): return lax.ppermute(block, axis, pairs)]
    concatenate x0 -> x4, other arithmetic: none -> 2.98 us  [by_parity(): return jnp.concatenate(columns_by_xor(array, odd), axis=1)]
    unnamed x53 -> x62, local copies, waits for them, and re-layouts: 10.3 us -> 10.1 us
  transfers between devices with their start and end apart: 36 -> 36, of which waited for: 21 -> 24; matrix products, arithmetic and copies ran while one was open for 14% -> 16% of each run, Pallas kernels for 20% -> 20%
where the time goes in v13:
time: 262 us; the launch traced here: 261 us
  waiting for transfers between devices  116 us (44%)
  Pallas kernels  51.1 us (20%)
  starting transfers between devices  34.9 us (13%)
  other arithmetic  30.5 us (12%)
  local copies, waits for them, and re-layouts  15.9 us (6%)
  matrix products  11.4 us (4%)
    ppermute x34, waiting for transfers between devices, swap(): return lax.ppermute(block, axis, pairs)  108 us
    pallas_call x4, Pallas kernels, product(): pl.pallas_call(product_kernel, in_specs=[pl.BlockSpec(memory_space=pltpu....  44 us
    ppermute x34, starting transfers between devices, swap(): return lax.ppermute(block, axis, pairs)  26.3 us
    unnamed x62, local copies, waits for them, and re-layouts  10.1 us
    select_n x8, other arithmetic, spread_step(): return [jnp.where(offset & bit != 0, moved[j], held[j]) for j in range(bit)]  9.19 us
    ppermute x2, starting transfers between devices, spread_step(): moved = lax.ppermute(jnp.stack(held[bit:]), ('row', 'col'), pairs)  8.61 us
    dot_general x7, matrix products, dot_tn(): return lax.dot_general(a, b, (((0,), (0,)), ((), ())), precision=precision)  8.17 us
    ppermute x2, waiting for transfers between devices, spread_step(): moved = lax.ppermute(jnp.stack(held[bit:]), ('row', 'col'), pairs)  7.74 us
  transfers between devices with their start and end apart: 36, of which 24 were waited for; matrix products, arithmetic and copies ran while one was open for 16% of the time, Pallas kernels for 20%

profile of v13, /device:TPU:0, one launch (start us, length us, event | category | flops | bytes accessed | tf_op | source)
XLA Modules:
  0.0 261.2 jit_solution(8019169423090635742)
XLA Ops:
  3.2 4.1 %collective-permute-start = (f32[512,256]{1,0:T(8,128)S(1)}, f32[512,256]{1,0:T(8,128)}, u32[]{:S(2)}, u32[]{:S(2)}) collective-permute-start(f32[512,256]{1,0:T(8,128)S(1)} %get-tuple-element.133.refs_0_), channel_id=1, source_target_pairs={{0,8},{4,12},{8,0},{12,4},{1,9},{5,13},{9,1},{13,5},{2,10},{6,14},... | collective-permute-start | bytes 1572872 | tf_op jit(solution)/shard_map/ppermute | solution.py:16
  8.9 2.9 %convolution_subtract_fusion = f32[512,512]{1,0:T(8,128)} fusion(f32[1,512,512]{2,1,0:T(8,128)S(1)} %copy-done, f32[1,2,512,512]{3,2,1,0:T(8,128)S(1)} %copy-done.16, f32[512]{0:T(512)S(1)} %bitcast.223, f32[512]{0:T(512)S(1)} %bitcast.224), kind=kOutput, calls=%fused_computation.10 | convolution fusion | flops 1611399168 | bytes 4198400 | tf_op jit(solution)/shard_map/dot_general | solution.py:95
  11.8 5.8 %copy-done.2 = f32[2048,2048]{1,0:T(8,128)S(1)} copy-done((f32[2048,2048]{1,0:T(8,128)S(1)}, f32[2048,2048]{1,0:T(8,128)}, u32[]{:S(2)}) %copy-start.2) | copy-done | bytes 16777240
  17.6 7.1 %shard_map.79 = bf16[6,2048,2048]{2,1,0:T(8,128)(2,1)} custom-call(f32[2048,2048]{1,0:T(8,128)S(1)} %copy-done.2), custom_call_target="tpu_custom_call" | custom-call | tf_op jit(solution)/shard_map/pallas_call | solution.py:34
  25.9 4.7 %collective-permute-done.refs_2_ = f32[512,256]{1,0:T(8,128)} collective-permute-done((f32[512,256]{1,0:T(8,128)S(1)}, f32[512,256]{1,0:T(8,128)}, u32[]{:S(2)}, u32[]{:S(2)}) %collective-permute-start) | collective-permute-done | bytes 524320 | tf_op jit(solution)/shard_map/ppermute | solution.py:16
  38.6 17.4 %collective-permute-done.3.refs_2_ = f32[512,256]{1,0:T(8,128)} collective-permute-done((f32[512,256]{1,0:T(8,128)S(1)}, f32[512,256]{1,0:T(8,128)}, u32[]{:S(2)}, u32[]{:S(2)}) %collective-permute-start.3) | collective-permute-done | bytes 524320 | tf_op jit(solution)/shard_map/ppermute | solution.py:16
  57.0 10.3 %collective-permute-done.2.refs_3_ = f32[512,256]{1,0:T(8,128)S(1)} collective-permute-done((f32[512,256]{1,0:T(8,128)}, f32[512,256]{1,0:T(8,128)S(1)}, u32[]{:S(2)}, u32[]{:S(2)}) %collective-permute-start.2) | collective-permute-done | bytes 524320 | tf_op jit(solution)/shard_map/ppermute | solution.py:16
  76.3 11.2 %shard_map.80 = (f32[2,512,256]{2,1,0:T(8,128)}, f32[2,512,256]{2,1,0:T(8,128)S(1)}) custom-call(s32[5]{0:T(128)S(1)} %pad_add_fusion.place, bf16[6,4,512,2048]{3,2,1,0:T(8,128)(2,1)} %bitcast.202, f32[512,256]{1,0:T(8,128)S(1)} %get-tuple-element.133.refs_0_, f32[512,256]{1,0:T(8,128)} %collective-permute-done.1.refs_1_, ...), custom_call_target="tpu_custom_call" | custom-call | tf_op jit(solution)/shard_map/pallas_call | solution.py:83
  87.5 6.6 %collective-permute-done.8 = f32[2,512,256]{2,1,0:T(8,128)} collective-permute-done((f32[2,512,256]{2,1,0:T(8,128)}, f32[2,512,256]{2,1,0:T(8,128)}, u32[]{:S(2)}, u32[]{:S(2)}) %collective-permute-start.8) | collective-permute-done | bytes 1048608 | tf_op jit(solution)/shard_map/ppermute | solution.py:16
  96.6 10.9 %collective-permute-done.5.refs_3_ = f32[512,256]{1,0:T(8,128)S(1)} collective-permute-done((f32[512,256]{1,0:T(8,128)}, f32[512,256]{1,0:T(8,128)S(1)}, u32[]{:S(2)}, u32[]{:S(2)}) %collective-permute-start.5) | collective-permute-done | bytes 524320 | tf_op jit(solution)/shard_map/ppermute | solution.py:16
  117.8 11.1 %shard_map.81 = (f32[2,512,256]{2,1,0:T(8,128)S(1)}, f32[2,512,256]{2,1,0:T(8,128)S(1)}) custom-call(s32[5]{0:T(128)S(1)} %pad_add_fusion.place, bf16[6,4,512,2048]{3,2,1,0:T(8,128)(2,1)} %bitcast.203, f32[512,256]{1,0:T(8,128)S(1)} %get-tuple-element.164.refs_0_, f32[512,256]{1,0:T(8,128)S(1)} %copy-done.4, f32[512,256]{1,0:T(8,128)} %collective-permute-done.3.refs_2_, ...), custom_call_target="tpu_custom_call" | custom-call | tf_op jit(solution)/shard_map/pallas_call | solution.py:83
  128.9 7.1 %collective-permute-done.13 = f32[2,512,256]{2,1,0:T(8,128)} collective-permute-done((f32[2,512,256]{2,1,0:T(8,128)}, f32[2,512,256]{2,1,0:T(8,128)}, u32[]{:S(2)}, u32[]{:S(2)}) %collective-permute-start.13) | collective-permute-done | bytes 1048608 | tf_op jit(solution)/shard_map/ppermute | solution.py:16
  137.3 9.2 %collective-permute-done.15 = f32[1,512,256]{2,1,0:T(8,128)S(1)} collective-permute-done((f32[1,512,256]{2,1,0:T(8,128)S(1)}, f32[1,512,256]{2,1,0:T(8,128)S(1)}, u32[]{:S(2)}, u32[]{:S(2)}) %collective-permute-start.15) | collective-permute-done | bytes 524320 | tf_op jit(solution)/shard_map/ppermute | solution.py:16
  148.6 3.2 %collective-permute-start.18 = (f32[2,512,256]{2,1,0:T(8,128)S(1)}, f32[2,512,256]{2,1,0:T(8,128)S(1)}, u32[]{:S(2)}, u32[]{:S(2)}) collective-permute-start(f32[2,512,256]{2,1,0:T(8,128)S(1)} %pad_maximum_fusion.2), channel_id=1, source_target_pairs={{0,2},{5,7},{10,8},{15,13},{16,18},{21,23},{26,24},{31,29}} | collective-permute-start | bytes 3145736 | tf_op jit(solution)/shard_map/ppermute | solution.py:152
  154.7 11.1 %shard_map.82 = (f32[2,512,256]{2,1,0:T(8,128)}, f32[2,512,256]{2,1,0:T(8,128)S(1)}) custom-call(s32[5]{0:T(128)S(1)} %pad_add_fusion.place, bf16[6,4,512,2048]{3,2,1,0:T(8,128)(2,1)} %bitcast.204, f32[512,256]{1,0:T(8,128)S(1)} %get-tuple-element.189.refs_0_, f32[512,256]{1,0:T(8,128)S(1)} %collective-permute-done.7.refs_1_, ...), custom_call_target="tpu_custom_call" | custom-call | tf_op jit(solution)/shard_map/pallas_call | solution.py:83
  165.8 3.9 %collective-permute-done.18 = f32[2,512,256]{2,1,0:T(8,128)S(1)} collective-permute-done((f32[2,512,256]{2,1,0:T(8,128)S(1)}, f32[2,512,256]{2,1,0:T(8,128)S(1)}, u32[]{:S(2)}, u32[]{:S(2)}) %collective-permute-start.18) | collective-permute-done | bytes 1048608 | tf_op jit(solution)/shard_map/ppermute | solution.py:152
  170.9 4.5 %collective-permute-done.20 = f32[1,512,256]{2,1,0:T(8,128)S(1)} collective-permute-done((f32[1,512,256]{2,1,0:T(8,128)S(1)}, f32[1,512,256]{2,1,0:T(8,128)S(1)}, u32[]{:S(2)}, u32[]{:S(2)}) %collective-permute-start.20) | collective-permute-done | bytes 524320 | tf_op jit(solution)/shard_map/ppermute | solution.py:16
  176.5 5.4 %collective-permute-start.22 = (f32[2,512,256]{2,1,0:T(8,128)}, f32[2,512,256]{2,1,0:T(8,128)}, u32[]{:S(2)}, u32[]{:S(2)}) collective-permute-start(f32[2,512,256]{2,1,0:T(8,128)} %pad_maximum_fusion.3), channel_id=1, source_target_pairs={{0,2},{5,7},{10,8},{15,13},{16,18},{21,23},{26,24},{31,29}} | collective-permute-start | bytes 3145736 | tf_op jit(solution)/shard_map/ppermute | solution.py:152
  184.7 10.6 %shard_map.83 = (f32[2,512,256]{2,1,0:T(8,128)S(1)}, f32[2,512,256]{2,1,0:T(8,128)S(1)}) custom-call(s32[5]{0:T(128)S(1)} %pad_add_fusion.place, bf16[6,4,512,2048]{3,2,1,0:T(8,128)(2,1)} %bitcast.205, f32[512,256]{1,0:T(8,128)S(1)} %get-tuple-element.213.refs_0_, f32[512,256]{1,0:T(8,128)S(1)} %collective-permute-done.12.refs_1_, f32[512,256]{1,0:T(8,128)S(1)} %copy-done.6, ...), custom_call_target="tpu_custom_call" | custom-call | tf_op jit(solution)/shard_map/pallas_call | solution.py:83
  195.3 3.9 %collective-permute-done.22 = f32[2,512,256]{2,1,0:T(8,128)} collective-permute-done((f32[2,512,256]{2,1,0:T(8,128)}, f32[2,512,256]{2,1,0:T(8,128)}, u32[]{:S(2)}, u32[]{:S(2)}) %collective-permute-start.22) | collective-permute-done | bytes 1048608 | tf_op jit(solution)/shard_map/ppermute | solution.py:152
  200.5 4.2 %collective-permute-done.24 = f32[1,512,256]{2,1,0:T(8,128)S(1)} collective-permute-done((f32[1,512,256]{2,1,0:T(8,128)S(1)}, f32[1,512,256]{2,1,0:T(8,128)S(1)}, u32[]{:S(2)}, u32[]{:S(2)}) %collective-permute-start.24) | collective-permute-done | bytes 524320 | tf_op jit(solution)/shard_map/ppermute | solution.py:16
  215.2 11.3 %collective-permute-done.27 = f32[1,512,256]{2,1,0:T(8,128)S(1)} collective-permute-done((f32[1,512,256]{2,1,0:T(8,128)S(1)}, f32[1,512,256]{2,1,0:T(8,128)S(1)}, u32[]{:S(2)}, u32[]{:S(2)}) %collective-permute-start.27) | collective-permute-done | bytes 524320 | tf_op jit(solution)/shard_map/ppermute | solution.py:16
  235.6 9.4 %collective-permute-done.30 = f32[1,2,128,256]{3,2,1,0:T(8,128)S(1)} collective-permute-done((f32[1,2,128,256]{3,2,1,0:T(8,128)S(1)}, f32[1,2,128,256]{3,2,1,0:T(8,128)S(1)}, u32[]{:S(2)}, u32[]{:S(2)}) %collective-permute-start.30) | collective-permute-done | bytes 262176 | tf_op jit(solution)/shard_map/ppermute | solution.py:16
  255.9 4.7 %collective-permute-done.35 = f32[1,1,128,128]{3,2,1,0:T(8,128)S(1)} collective-permute-done((f32[1,1,128,128]{3,2,1,0:T(8,128)S(1)}, f32[1,1,128,128]{3,2,1,0:T(8,128)S(1)}, u32[]{:S(2)}, u32[]{:S(2)}) %collective-permute-start.35) | collective-permute-done | bytes 65568 | tf_op jit(solution)/shard_map/ppermute | solution.py:16
  (189 shorter events, 79.5 us)
Async XLA Ops:
  3.2 27.5 %collective-permute-start = (f32[512,256]{1,0:T(8,128)S(1)}, f32[512,256]{1,0:T(8,128)}, u32[]{:S(2)}, u32[]{:S(2)}) collective-permute-start(f32[512,256]{1,0:T(8,128)S(1)} %get-tuple-element.133.refs_0_), channel_id=1, source_target_pairs={{0,8},{4,12},{8,0},{12,4},{1,9},{5,13},{9,1},{13,5},{2,10},{6,14},... | collective-permute-start | bytes 1572872 | tf_op jit(solution)/shard_map/ppermute | solution.py:16
  7.3 23.6 %collective-permute-start.1 = (f32[512,256]{1,0:T(8,128)S(1)}, f32[512,256]{1,0:T(8,128)}, u32[]{:S(2)}, u32[]{:S(2)}) collective-permute-start(f32[512,256]{1,0:T(8,128)S(1)} %get-tuple-element.133.refs_0_), channel_id=1, source_target_pairs={{0,4},{4,0},{8,12},{12,8},{1,5},{5,1},{9,13},{13,9},{2,6},{6,2},{1... | collective-permute-start | bytes 1572872 | tf_op jit(solution)/shard_map/ppermute | solution.py:16
  30.9 25.2 %collective-permute-start.3 = (f32[512,256]{1,0:T(8,128)S(1)}, f32[512,256]{1,0:T(8,128)}, u32[]{:S(2)}, u32[]{:S(2)}) collective-permute-start(f32[512,256]{1,0:T(8,128)S(1)} %get-tuple-element.164.refs_0_), channel_id=1, source_target_pairs={{0,8},{4,12},{8,0},{12,4},{1,9},{5,13},{9,1},{13,5},{2,10},{6,14},... | collective-permute-start | bytes 1572872 | tf_op jit(solution)/shard_map/ppermute | solution.py:16
  32.2 24.7 %collective-permute-start.4 = (f32[512,256]{1,0:T(8,128)S(1)}, f32[512,256]{1,0:T(8,128)S(1)}, u32[]{:S(2)}, u32[]{:S(2)}) collective-permute-start(f32[512,256]{1,0:T(8,128)S(1)} %get-tuple-element.164.refs_0_), channel_id=1, source_target_pairs={{0,4},{4,0},{8,12},{12,8},{1,5},{5,1},{9,13},{13,9},{2,6},{6,2},{1... | collective-permute-start | bytes 1572872 | tf_op jit(solution)/shard_map/ppermute | solution.py:16
  36.2 31.1 %collective-permute-start.2 = (f32[512,256]{1,0:T(8,128)}, f32[512,256]{1,0:T(8,128)S(1)}, u32[]{:S(2)}, u32[]{:S(2)}) collective-permute-start(f32[512,256]{1,0:T(8,128)} %collective-permute-done.refs_2_), channel_id=1, source_target_pairs={{0,4},{4,0},{8,12},{12,8},{1,5},{5,1},{9,13},{13,9},{2,6},{6,2},{1... | collective-permute-start | bytes 1572872 | tf_op jit(solution)/shard_map/ppermute | solution.py:16
  69.5 24.6 %collective-permute-start.8 = (f32[2,512,256]{2,1,0:T(8,128)}, f32[2,512,256]{2,1,0:T(8,128)}, u32[]{:S(2)}, u32[]{:S(2)}) collective-permute-start(f32[2,512,256]{2,1,0:T(8,128)} %pad_maximum_fusion), channel_id=1, source_target_pairs={{0,2},{1,3},{2,0},{3,1},{4,6},{5,7},{6,4},{7,5},{8,10},{9,11},{10,... | collective-permute-start | bytes 3145736 | tf_op jit(solution)/shard_map/ppermute | solution.py:16
  70.8 36.6 %collective-permute-start.6 = (f32[512,256]{1,0:T(8,128)S(1)}, f32[512,256]{1,0:T(8,128)}, u32[]{:S(2)}, u32[]{:S(2)}) collective-permute-start(f32[512,256]{1,0:T(8,128)S(1)} %get-tuple-element.189.refs_0_), channel_id=1, source_target_pairs={{0,8},{4,12},{8,0},{12,4},{1,9},{5,13},{9,1},{13,5},{2,10},{6,14},... | collective-permute-start | bytes 1572872 | tf_op jit(solution)/shard_map/ppermute | solution.py:16
  73.1 34.4 %collective-permute-start.7 = (f32[512,256]{1,0:T(8,128)S(1)}, f32[512,256]{1,0:T(8,128)S(1)}, u32[]{:S(2)}, u32[]{:S(2)}) collective-permute-start(f32[512,256]{1,0:T(8,128)S(1)} %get-tuple-element.189.refs_0_), channel_id=1, source_target_pairs={{0,4},{4,0},{8,12},{12,8},{1,5},{5,1},{9,13},{13,9},{2,6},{6,2},{1... | collective-permute-start | bytes 1572872 | tf_op jit(solution)/shard_map/ppermute | solution.py:16
  74.8 32.6 %collective-permute-start.5 = (f32[512,256]{1,0:T(8,128)}, f32[512,256]{1,0:T(8,128)S(1)}, u32[]{:S(2)}, u32[]{:S(2)}) collective-permute-start(f32[512,256]{1,0:T(8,128)} %collective-permute-done.3.refs_2_), channel_id=1, source_target_pairs={{0,4},{4,0},{8,12},{12,8},{1,5},{5,1},{9,13},{13,9},{2,6},{6,2},{1... | collective-permute-start | bytes 1572872 | tf_op jit(solution)/shard_map/ppermute | solution.py:16
  109.7 26.3 %collective-permute-start.13 = (f32[2,512,256]{2,1,0:T(8,128)}, f32[2,512,256]{2,1,0:T(8,128)}, u32[]{:S(2)}, u32[]{:S(2)}) collective-permute-start(f32[2,512,256]{2,1,0:T(8,128)} %pad_maximum_fusion.1), channel_id=1, source_target_pairs={{0,2},{1,3},{2,0},{3,1},{4,6},{5,7},{6,4},{7,5},{8,10},{9,11},{10,... | collective-permute-start | bytes 3145736 | tf_op jit(solution)/shard_map/ppermute | solution.py:16
  110.5 36.8 %collective-permute-start.11 = (f32[512,256]{1,0:T(8,128)S(1)}, f32[512,256]{1,0:T(8,128)S(1)}, u32[]{:S(2)}, u32[]{:S(2)}) collective-permute-start(f32[512,256]{1,0:T(8,128)S(1)} %get-tuple-element.213.refs_0_), channel_id=1, source_target_pairs={{0,8},{4,12},{8,0},{12,4},{1,9},{5,13},{9,1},{13,5},{2,10},{6,14},... | collective-permute-start | bytes 1572872 | tf_op jit(solution)/shard_map/ppermute | solution.py:16
  110.6 36.7 %collective-permute-start.12 = (f32[512,256]{1,0:T(8,128)S(1)}, f32[512,256]{1,0:T(8,128)S(1)}, u32[]{:S(2)}, u32[]{:S(2)}) collective-permute-start(f32[512,256]{1,0:T(8,128)S(1)} %get-tuple-element.213.refs_0_), channel_id=1, source_target_pairs={{0,4},{4,0},{8,12},{12,8},{1,5},{5,1},{9,13},{13,9},{2,6},{6,2},{1... | collective-permute-start | bytes 1572872 | tf_op jit(solution)/shard_map/ppermute | solution.py:16
  112.3 35.0 %collective-permute-start.10 = (f32[512,256]{1,0:T(8,128)}, f32[512,256]{1,0:T(8,128)S(1)}, u32[]{:S(2)}, u32[]{:S(2)}) collective-permute-start(f32[512,256]{1,0:T(8,128)} %collective-permute-done.6.refs_2_), channel_id=1, source_target_pairs={{0,4},{4,0},{8,12},{12,8},{1,5},{5,1},{9,13},{13,9},{2,6},{6,2},{1... | collective-permute-start | bytes 1572872 | tf_op jit(solution)/shard_map/ppermute | solution.py:16
  114.3 32.2 %collective-permute-start.15 = (f32[1,512,256]{2,1,0:T(8,128)S(1)}, f32[1,512,256]{2,1,0:T(8,128)S(1)}, u32[]{:S(2)}, u32[]{:S(2)}) collective-permute-start(f32[1,512,256]{2,1,0:T(8,128)S(1)} %slice_bitcast_fusion.11), channel_id=1, source_target_pairs={{0,2},{1,3},{2,0},{3,1},{4,6},{5,7},{6,4},{7,5},{8,10},{9,11},{10,... | collective-permute-start | bytes 1572872 | tf_op jit(solution)/shard_map/ppermute | solution.py:16
  148.6 21.1 %collective-permute-start.18 = (f32[2,512,256]{2,1,0:T(8,128)S(1)}, f32[2,512,256]{2,1,0:T(8,128)S(1)}, u32[]{:S(2)}, u32[]{:S(2)}) collective-permute-start(f32[2,512,256]{2,1,0:T(8,128)S(1)} %pad_maximum_fusion.2), channel_id=1, source_target_pairs={{0,2},{5,7},{10,8},{15,13},{16,18},{21,23},{26,24},{31,29}} | collective-permute-start | bytes 3145736 | tf_op jit(solution)/shard_map/ppermute | solution.py:152
  151.9 23.5 %collective-permute-start.17 = (f32[512,256]{1,0:T(8,128)S(1)}, f32[512,256]{1,0:T(8,128)S(1)}, u32[]{:S(2)}, u32[]{:S(2)}) collective-permute-start(f32[512,256]{1,0:T(8,128)S(1)} %collective-permute-done.11.refs_2_), channel_id=1, source_target_pairs={{0,4},{4,0},{8,12},{12,8},{1,5},{5,1},{9,13},{13,9},{2,6},{6,2},{1... | collective-permute-start | bytes 1572872 | tf_op jit(solution)/shard_map/ppermute | solution.py:16
  152.5 22.8 %collective-permute-start.20 = (f32[1,512,256]{2,1,0:T(8,128)S(1)}, f32[1,512,256]{2,1,0:T(8,128)S(1)}, u32[]{:S(2)}, u32[]{:S(2)}) collective-permute-start(f32[1,512,256]{2,1,0:T(8,128)S(1)} %slice_bitcast_fusion.7), channel_id=1, source_target_pairs={{0,2},{1,3},{2,0},{3,1},{4,6},{5,7},{6,4},{7,5},{8,10},{9,11},{10,... | collective-permute-start | bytes 1572872 | tf_op jit(solution)/shard_map/ppermute | solution.py:16
  175.4 6.5 %collective-permute-start.23 = (f32[2,512,256]{2,1,0:T(8,128)}, f32[2,512,256]{2,1,0:T(8,128)}, u32[]{:S(2)}, u32[]{:S(2)}) collective-permute-start(f32[2,512,256]{2,1,0:T(8,128)} %get-tuple-element.212), channel_id=1, source_target_pairs={{0,1},{1,0},{2,3},{3,2},{4,5},{5,4},{6,7},{7,6},{8,9},{9,8},{10,11... | collective-permute-start | bytes 3145736 | tf_op jit(solution)/shard_map/ppermute | solution.py:16
  176.5 22.6 %collective-permute-start.22 = (f32[2,512,256]{2,1,0:T(8,128)}, f32[2,512,256]{2,1,0:T(8,128)}, u32[]{:S(2)}, u32[]{:S(2)}) collective-permute-start(f32[2,512,256]{2,1,0:T(8,128)} %pad_maximum_fusion.3), channel_id=1, source_target_pairs={{0,2},{5,7},{10,8},{15,13},{16,18},{21,23},{26,24},{31,29}} | collective-permute-start | bytes 3145736 | tf_op jit(solution)/shard_map/ppermute | solution.py:152
  183.7 21.0 %collective-permute-start.24 = (f32[1,512,256]{2,1,0:T(8,128)S(1)}, f32[1,512,256]{2,1,0:T(8,128)S(1)}, u32[]{:S(2)}, u32[]{:S(2)}) collective-permute-start(f32[1,512,256]{2,1,0:T(8,128)S(1)} %slice_bitcast_fusion.3), channel_id=1, source_target_pairs={{0,2},{1,3},{2,0},{3,1},{4,6},{5,7},{6,4},{7,5},{8,10},{9,11},{10,... | collective-permute-start | bytes 1572872 | tf_op jit(solution)/shard_map/ppermute | solution.py:16
  211.4 15.1 %collective-permute-start.27 = (f32[1,512,256]{2,1,0:T(8,128)S(1)}, f32[1,512,256]{2,1,0:T(8,128)S(1)}, u32[]{:S(2)}, u32[]{:S(2)}) collective-permute-start(f32[1,512,256]{2,1,0:T(8,128)S(1)} %slice_bitcast_fusion.1), channel_id=1, source_target_pairs={{0,2},{1,3},{2,0},{3,1},{4,6},{5,7},{6,4},{7,5},{8,10},{9,11},{10,... | collective-permute-start | bytes 1572872 | tf_op jit(solution)/shard_map/ppermute | solution.py:16
  214.2 14.1 %collective-permute-start.29 = (f32[2,2,128,256]{3,2,1,0:T(8,128)S(1)}, f32[2,2,128,256]{3,2,1,0:T(8,128)S(1)}, u32[]{:S(2)}, u32[]{:S(2)}) collective-permute-start(f32[2,2,128,256]{3,2,1,0:T(8,128)S(1)} %bitcast.217), channel_id=1, source_target_pairs={{0,4},{4,0},{8,12},{12,8},{1,5},{5,1},{9,13},{13,9},{2,6},{6,2},{1... | collective-permute-start | bytes 1572872 | tf_op jit(solution)/shard_map/ppermute | solution.py:16
  229.9 15.0 %collective-permute-start.30 = (f32[1,2,128,256]{3,2,1,0:T(8,128)S(1)}, f32[1,2,128,256]{3,2,1,0:T(8,128)S(1)}, u32[]{:S(2)}, u32[]{:S(2)}) collective-permute-start(f32[1,2,128,256]{3,2,1,0:T(8,128)S(1)} %constant_dynamic-slice_fusion.3), channel_id=1, source_target_pairs={{0,8},{4,12},{8,0},{12,4},{1,9},{5,13},{9,1},{13,5},{2,10},{6,14},... | collective-permute-start | bytes 786440 | tf_op jit(solution)/shard_map/ppermute | solution.py:16
  234.6 11.7 %collective-permute-start.33 = (f32[1,512,128]{1,2,0:T(8,128)}, f32[1,512,128]{1,2,0:T(8,128)}, u32[]{:S(2)}, u32[]{:S(2)}) collective-permute-start(f32[1,512,128]{1,2,0:T(8,128)} %slice_bitcast_fusion.17), channel_id=1, source_target_pairs={{0,2},{1,3},{2,0},{3,1},{4,6},{5,7},{6,4},{7,5},{8,10},{9,11},{10,... | collective-permute-start | bytes 786440 | tf_op jit(solution)/shard_map/ppermute | solution.py:16
  (39 other events, 289.5 us)
